TPU v7x, 32 devices: a whole 2x2x4 slice. The times are simulated.
32 devices in a mesh: grp: 2 (over x), row: 8 (over z, y), col: 2 (over core).
Axes of the slice: x: 2, y: 2, z: 4, core: 2. Of those that a mesh axis runs over, the one named last changes fastest.
Arguments:
- queries: bfloat16 [8192, 2048], P(('grp', 'row'), 'col'), parts along dimension 0, may hold values from -34 to 34
- keys: bfloat16 [8192, 1024], P(('grp', 'row'), 'col'), parts along dimension 0, may hold values from -34 to 34
- values: bfloat16 [8192, 1024], P(('grp', 'row'), 'col'), parts along dimension 0, may hold values from -6 to 6
- out_proj: bfloat16 [2048, 5376], P(('col', 'row'))
- post_gain: float32 [5376], P('col'), may hold values from 0.1 to 1.9
- mean_vec: float32 [5376], P('col'), may hold values from -5 to 5
- erase_in: float32 [5376, 64], P('col'), may hold values from -0.078125 to 0.078125
- erase_out: float32 [5376, 64], P('col'), may hold values from -0.375 to 0.375
Outputs:
- erased: bfloat16 [8192, 5376], P(('grp', 'row'), 'col'), parts along dimension 0
There are 2 independent parts, one for each index of `grp`. A program takes and returns all parts, laid end to end along the dimension named above; an argument that names none is the same for every part. Nothing has to cross between parts.
All inputs are finite; a program needn't handle non-finite values.
Results may differ from a plain program's by a relative error of at most 0.012.
The roundings to bfloat16 on the way count: a program that leaves them out, or rounds other values in their place, can miss the bound.
Values may be sent and summed in bfloat16 or wider, within the bound.
No kernel may reach another device: no remote copies, remote signals or barrier semaphores. Data moves between devices by JAX's collectives and lax.ppermute only.
A program may use at most 128 MiB of HBM per device.

v0:
```python
import jax
import jax.numpy as jnp
from jax import lax
from jax.sharding import PartitionSpec as P

D = 5376
HD = 128
WINDOW = 1024


query_scale = 168.0 ** (-0.5)
norm_eps = 1e-06
rope_base = 10000.0


def shifted(block, axis, distance):
    devices = range(lax.axis_size(axis))
    route = [(i - distance, i) for i in devices if i - distance in devices]
    return lax.ppermute(block, axis, route)


def rotate(field, positions):
    half_dim = HD // 2
    inverse = jnp.exp(
        -(2.0 * jnp.arange(half_dim, dtype=jnp.float32) / HD) * jnp.log(jnp.float32(rope_base))
    )
    angles = positions[:, None] * inverse[None, :]
    cosine = jnp.cos(angles)[:, None, :]
    sine = jnp.sin(angles)[:, None, :]
    wide = field.astype(jnp.float32)
    first = wide[..., :half_dim]
    second = wide[..., half_dim:]
    return jnp.concatenate(
        [first * cosine - second * sine, second * cosine + first * sine], -1
    ).astype(jnp.bfloat16)


def on_device(queries, keys, values, out_proj, post_gain, mean_vec, erase_in, erase_out):
    tok_rows = queries.shape[0]
    head_local = queries.shape[1] // HD
    kv_local = keys.shape[1] // HD
    group = head_local // kv_local
    first_row = lax.axis_index("row") * tok_rows
    positions = (first_row + jnp.arange(tok_rows, dtype=jnp.int32)).astype(jnp.float32)
    q_rot = rotate(queries.reshape(tok_rows, head_local, HD), positions)
    k_rot = rotate(keys.reshape(tok_rows, kv_local, HD), positions).reshape(tok_rows, kv_local * HD)
    hop_count = WINDOW // tok_rows
    received = []
    for hop_index in range(1, hop_count + 1):
        received.append(shifted((k_rot, values), "row", hop_index))
    key_all = jnp.concatenate([pair[0] for pair in reversed(received)] + [k_rot], 0)
    val_all = jnp.concatenate([pair[1] for pair in reversed(received)] + [values], 0)
    key_count = key_all.shape[0]
    key_pos = first_row - hop_count * tok_rows + jnp.arange(key_count, dtype=jnp.int32)
    query_pos = first_row + jnp.arange(tok_rows, dtype=jnp.int32)
    offsets = query_pos[:, None] - key_pos[None, :]
    allowed = ((key_pos >= 0)[None, :] & (offsets >= 0) & (offsets < WINDOW))[None]
    outputs = []
    for kv_slot in range(kv_local):
        query_group = q_rot[:, kv_slot * group : (kv_slot + 1) * group, :]
        key_group = key_all[:, kv_slot * HD : (kv_slot + 1) * HD]
        val_group = val_all[:, kv_slot * HD : (kv_slot + 1) * HD]
        scores = (
            jnp.einsum("tgd,sd->gts", query_group, key_group, preferred_element_type=jnp.float32)
            * query_scale
        )
        scores = jnp.where(allowed, scores, -1e30)
        row_max = jnp.max(scores, axis=-1, keepdims=True)
        weights = jnp.where(allowed, jnp.exp(scores - row_max), 0.0)
        probs = (weights / jnp.sum(weights, axis=-1, keepdims=True)).astype(jnp.bfloat16)
        mixed = jnp.einsum("gts,sd->tgd", probs, val_group, preferred_element_type=jnp.float32)
        outputs.append(mixed.reshape(tok_rows, group * HD))
    attended = jnp.concatenate(outputs, 1).astype(jnp.bfloat16)
    partial_sum = jnp.dot(
        attended,
        lax.all_gather(out_proj, "row", axis=0, tiled=True),
        preferred_element_type=jnp.float32,
    )
    hidden = lax.psum_scatter(partial_sum, "col", scatter_dimension=1, tiled=True)
    gained = jnp.dot(hidden * post_gain[None, :], erase_in, precision=lax.Precision.HIGHEST)
    mean_code = jnp.dot(mean_vec[None, :], erase_in, precision=lax.Precision.HIGHEST)
    total_sq, gained_sum, mean_sum = lax.psum(
        (jnp.sum(hidden * hidden, axis=1), gained, mean_code), "col"
    )
    inv_rms = lax.rsqrt(total_sq / D + norm_eps)
    normed = hidden * inv_rms[:, None] * post_gain[None, :]
    erase_code = inv_rms[:, None] * gained_sum - mean_sum
    return (normed - jnp.dot(erase_code, erase_out.T, precision=lax.Precision.HIGHEST)).astype(
        jnp.bfloat16
    )


def solution(mesh):
    placed = (
        P(("grp", "row"), "col"),
        P(("grp", "row"), "col"),
        P(("grp", "row"), "col"),
        P(("col", "row"), None),
        P("col"),
        P("col"),
        P("col", None),
        P("col", None),
    )
    return jax.shard_map(
        on_device, mesh=mesh, in_specs=placed, out_specs=P(("grp", "row"), "col"), check_vma=False
    )
```

profile of v0, /device:TPU:0, one launch (start us, length us, event | category | flops | bytes accessed | tf_op | source)
XLA Modules:
  0.0 279.7 jit_solution(11931267085919414568)
XLA Ops:
  12.2 5.7 %collective-permute-start.2 = (bf16[512,512]{1,0:T(8,128)(2,1)}, bf16[512,512]{1,0:T(8,128)(2,1)}, u32[]{:S(2)}, u32[]{:S(2)}) collective-permute-start(bf16[512,512]{1,0:T(8,128)(2,1)} %bitcast.102), channel_id=1, source_target_pairs={{0,4},{2,6},{4,8},{6,10},{8,12},{10,14},{1,5},{3,7},{5,9},{7,11},{... | collective-permute-start | bytes 1572872 | tf_op jit(solution)/shard_map/ppermute | solution.py:19
  17.9 4.2 %collective-permute-start.3 = (bf16[512,512]{1,0:T(8,128)(2,1)}, bf16[512,512]{1,0:T(8,128)(2,1)}, u32[]{:S(2)}, u32[]{:S(2)}) collective-permute-start(bf16[512,512]{1,0:T(8,128)(2,1)} %bitcast.102), channel_id=1, source_target_pairs={{0,2},{2,4},{4,6},{6,8},{8,10},{10,12},{12,14},{1,3},{3,5},{5,7},{... | collective-permute-start | bytes 1572872 | tf_op jit(solution)/shard_map/ppermute | solution.py:19
  23.2 2.7 collective-permute-start
  25.9 4.2 %collective-permute-start.1 = (bf16[512,512]{0,1:T(8,128)(2,1)}, bf16[512,512]{0,1:T(8,128)(2,1)}, u32[]{:S(2)}, u32[]{:S(2)}) collective-permute-start(bf16[512,512]{0,1:T(8,128)(2,1)} %copy.16), channel_id=1, source_target_pairs={{0,2},{2,4},{4,6},{6,8},{8,10},{10,12},{12,14},{1,3},{3,5},{5,7},{... | collective-permute-start | bytes 1572872 | tf_op jit(solution)/shard_map/ppermute | solution.py:19
  30.7 2.0 fusion.19
  32.7 1.6 fusion.79
  34.3 1.8 copy.30
  36.1 3.2 %copy.31 = f32[512,8,64]{2,0,1:T(8,128)} copy(f32[512,8,64]{0,2,1:T(8,128)} %get-tuple-element.11) | data formatting | bytes 2097152
  39.3 3.6 %subtract_convert_fusion.1 = (bf16[512,8,64]{2,0,1:T(8,128)(2,1)}, bf16[512,8,64]{2,0,1:T(8,128)(2,1)}) fusion(f32[512,8,64]{2,0,1:T(8,128)} %copy.31, f32[512,8,64]{2,0,1:T(8,128)S(1)} %copy.30, f32[512,64]{1,0:T(8,128)} %copy-done.3, f32[512,64]{1,0:T(8,128)} %copy-done.2), kind=kLoop, calls=%fused_computation.46 | loop fusion | flops 2097152 | bytes 3407872 | tf_op jit(solution)/shard_map/convert.14
  46.0 12.5 %collective-permute-done = bf16[512,512]{0,1:T(8,128)(2,1)} collective-permute-done((bf16[512,512]{0,1:T(8,128)(2,1)}, bf16[512,512]{0,1:T(8,128)(2,1)}, u32[]{:S(2)}, u32[]{:S(2)}) %collective-permute-start) | collective-permute-done | bytes 524320 | tf_op jit(solution)/shard_map/ppermute | solution.py:19
  58.5 1.5 pad_maximum_fusion
  60.0 7.4 %fusion.80 = (f32[2,512]{1,0:T(2,128)S(1)}, f32[2,512,1536]{1,2,0:T(8,128)}) fusion(pred[512,1536]{0,1:T(8,128)(4,1)} %fusion.19, bf16[1536,512]{1,0:T(8,128)(2,1)} %copy-done.7, bf16[512,8,64]{2,0,1:T(8,128)(2,1)} %get-tuple-element.8, bf16[512,8,64]{2,0,1:T(8,128)(2,1)S(1)} %copy-done.5), kind=kOutput, calls=%fused_computation.116 | convolution fusion | flops 411043328 | bytes 9834496 | tf_op jit(solution)/shard_map/sub | solution.py:69
  67.4 7.4 %fusion.87 = (f32[2,512]{1,0:T(2,128)S(1)}, f32[2,512,1536]{1,2,0:T(8,128)}) fusion(pred[512,1536]{0,1:T(8,128)(4,1)} %fusion.19, bf16[1536,512]{1,0:T(8,128)(2,1)} %copy-done.7, bf16[512,8,64]{2,0,1:T(8,128)(2,1)S(1)} %copy-done.5, bf16[512,8,64]{2,0,1:T(8,128)(2,1)} %get-tuple-element.8), kind=kOutput, calls=%fused_computation.119 | convolution fusion | flops 411043328 | bytes 9834496 | tf_op jit(solution)/shard_map/sub | solution.py:69
  74.8 7.4 %fusion.84 = (f32[2,512]{1,0:T(2,128)S(1)}, f32[2,512,1536]{1,2,0:T(8,128)}) fusion(pred[512,1536]{0,1:T(8,128)(4,1)} %fusion.19, bf16[1536,512]{1,0:T(8,128)(2,1)} %copy-done.7, bf16[512,8,64]{2,0,1:T(8,128)(2,1)S(1)} %copy-done.5, bf16[512,8,64]{2,0,1:T(8,128)(2,1)} %get-tuple-element.8), kind=kOutput, calls=%fused_computation.118 | convolution fusion | flops 411043328 | bytes 9834496 | tf_op jit(solution)/shard_map/sub | solution.py:69
  82.2 7.6 %fusion.81 = (f32[2,512]{1,0:T(2,128)S(1)}, f32[2,512,1536]{1,2,0:T(8,128)}) fusion(pred[512,1536]{0,1:T(8,128)(4,1)} %fusion.19, bf16[1536,512]{1,0:T(8,128)(2,1)} %copy-done.7, bf16[512,8,64]{2,0,1:T(8,128)(2,1)S(1)} %copy-done.5, bf16[512,8,64]{2,0,1:T(8,128)(2,1)} %get-tuple-element.8), kind=kOutput, calls=%fused_computation.117 | convolution fusion | flops 411043328 | bytes 9834496 | tf_op jit(solution)/shard_map/sub | solution.py:69
  89.9 3.5 %fusion.32 = bf16[128,2,512]{2,0,1:T(8,128)(2,1)S(1)} fusion(f32[2,512,1536]{1,2,0:T(8,128)} %get-tuple-element.22, f32[2,512]{1,0:T(2,128)S(1)} %get-tuple-element.21, bf16[1536,512]{0,1:T(8,128)(2,1)S(1)} %pad_maximum_fusion), kind=kOutput, calls=%fused_computation.51 | convolution fusion | flops 405929984 | bytes 6950912 | tf_op jit(solution)/shard_map/gts,sd->tgd/dot_general | solution.py:71
  99.0 108.1 %all-gather.2.cloned.1.call-done = bf16[1024,5376]{1,0:T(8,128)(2,1)} async-done(((bf16[128,5376]{1,0:T(8,128)(2,1)}), bf16[1024,5376]{1,0:T(8,128)(2,1)}) %all-gather.2.cloned.1.call-update) | async-done | bytes 11010064 | tf_op jit(solution)/shard_map/all_gather | solution.py:76
  207.1 12.6 %fusion.41 = f32[512,5376]{1,0:T(8,128)} fusion(bf16[1024,5376]{1,0:T(8,128)(2,1)} %all-gather.2.cloned.1.call-done, bf16[512,256]{0,1:T(8,128)(2,1)S(1)} %bitcast.109, bf16[512,256]{0,1:T(8,128)(2,1)S(1)} %bitcast.108, bf16[512,256]{0,1:T(8,128)(2,1)S(1)} %bitcast.107, bf16[512,256]{0,1:T(8,128)(2,1)S(1)} %bitcast.106), kind=kOutput, calls=%fused_computation.57 | convolution fusion | flops 5641338880 | bytes 23068672 | tf_op jit(solution)/shard_map/dot_general | solution.py:74
  221.5 16.2 %reduce-scatter.2.cloned.1.call-done = f32[512,2688]{1,0:T(8,128)} async-done(((f32[512,5376]{1,0:T(8,128)}), f32[512,2688]{1,0:T(8,128)}) %reduce-scatter.2.cloned.1.call-update) | async-done | bytes 5505040 | tf_op jit(solution)/shard_map/reduce_scatter | solution.py:79
  237.7 7.8 %fusion.4 = f32[512,64]{1,0:T(8,128)} fusion(f32[2688,64]{0,1:T(8,128)S(1)} %copy-done.1, f32[512,2688]{1,0:T(8,128)} %reduce-scatter.2.cloned.1.call-done, f32[2688]{0:T(1024)S(1)} %copy-done.8), kind=kOutput, calls=%fused_computation.17 | convolution fusion | flops 1058340864 | bytes 6334976 | tf_op jit(solution)/shard_map/dot_general | solution.py:80
  245.5 3.0 %multiply_reduce_fusion = f32[512]{0:T(512)S(1)} fusion(f32[512,2688]{1,0:T(8,128)} %reduce-scatter.2.cloned.1.call-done), kind=kLoop, calls=%fused_computation.19 | loop fusion | flops 2752000 | bytes 5507072 | tf_op jit(solution)/shard_map/reduce_sum | solution.py:83
  248.5 2.5 all-reduce
  251.0 14.2 %all-reduce.3.cloned.1.call-done = f32[512,64]{1,0:T(8,128)} async-done(((f32[512,64]{1,0:T(8,128)}), f32[512,64]{1,0:T(8,128)}) %all-reduce.3.cloned.1.call-update) | async-done | bytes 131088 | tf_op jit(solution)/shard_map/psum | solution.py:82
  265.2 8.0 %subtract_convert_fusion = bf16[512,2688]{1,0:T(8,128)(2,1)} fusion(f32[512,2688]{1,0:T(8,128)} %reduce-scatter.2.cloned.1.call-done, f32[2688,64]{0,1:T(8,128)S(1)} %copy-done, f32[2688]{0:T(1024)S(1)} %copy-done.8, f32[512]{0:T(512)S(1)} %add_rsqrt_fusion, f32[512,64]{1,0:T(8,128)} %all-reduce.3.cloned.1.call-done, f32[64]{0:T(128)S(1)} %get-tuple-element.6), kind=kOutput, calls=%fused_computation.16 | convolution fusion | flops 1062535168 | bytes 9089792 | tf_op jit(solution)/shard_map/dot_general | solution.py:88
  (62 shorter events, 17.7 us)
Async XLA Ops:
  6.5 258.6 %copy-start = (f32[2688,64]{0,1:T(8,128)S(1)}, f32[2688,64]{0,1:T(8,128)}, u32[]{:S(2)}) copy-start(f32[2688,64]{0,1:T(8,128)} %param.15) | copy-start | bytes 2064388
  6.5 15.7 %copy-start.6 = (bf16[512,512]{1,0:T(8,128)(2,1)S(1)}, bf16[512,512]{1,0:T(8,128)(2,1)}, u32[]{:S(2)}) copy-start(bf16[512,512]{1,0:T(8,128)(2,1)} %param.10) | copy-start | bytes 1572868
  6.5 23.5 %copy-start.4 = (bf16[512,1024]{1,0:T(8,128)(2,1)S(1)}, bf16[512,1024]{1,0:T(8,128)(2,1)}, u32[]{:S(2)}) copy-start(bf16[512,1024]{1,0:T(8,128)(2,1)} %param.8) | copy-start | bytes 3145732
  6.5 200.5 %all-gather.2.cloned.1.call-start = ((), (), s32[]{:S(2)}) async-start(), calls=%async_computation.1 | async-start | bytes 12386304 | tf_op jit(solution)/shard_map/all_gather | solution.py:76
  7.3 230.4 %reduce-scatter.2.cloned.1.call-start = ((), (), s32[]{:S(2)}) async-start(), calls=%async_computation.2 | async-start | bytes 16515072 | tf_op jit(solution)/shard_map/reduce_scatter | solution.py:79
  9.7 0.9 copy-start.2
  9.7 0.9 copy-start.3
  12.2 30.6 %collective-permute-start.2 = (bf16[512,512]{1,0:T(8,128)(2,1)}, bf16[512,512]{1,0:T(8,128)(2,1)}, u32[]{:S(2)}, u32[]{:S(2)}) collective-permute-start(bf16[512,512]{1,0:T(8,128)(2,1)} %bitcast.102), channel_id=1, source_target_pairs={{0,4},{2,6},{4,8},{6,10},{8,12},{10,14},{1,5},{3,7},{5,9},{7,11},{... | collective-permute-start | bytes 1572872 | tf_op jit(solution)/shard_map/ppermute | solution.py:19
  17.9 26.9 %collective-permute-start.3 = (bf16[512,512]{1,0:T(8,128)(2,1)}, bf16[512,512]{1,0:T(8,128)(2,1)}, u32[]{:S(2)}, u32[]{:S(2)}) collective-permute-start(bf16[512,512]{1,0:T(8,128)(2,1)} %bitcast.102), channel_id=1, source_target_pairs={{0,2},{2,4},{4,6},{6,8},{8,10},{10,12},{12,14},{1,3},{3,5},{5,7},{... | collective-permute-start | bytes 1572872 | tf_op jit(solution)/shard_map/ppermute | solution.py:19
  23.2 35.3 %collective-permute-start = (bf16[512,512]{0,1:T(8,128)(2,1)}, bf16[512,512]{0,1:T(8,128)(2,1)}, u32[]{:S(2)}, u32[]{:S(2)}) collective-permute-start(bf16[512,512]{0,1:T(8,128)(2,1)} %copy.16), channel_id=1, source_target_pairs={{0,4},{2,6},{4,8},{6,10},{8,12},{10,14},{1,5},{3,7},{5,9},{7,11},{... | collective-permute-start | bytes 1572872 | tf_op jit(solution)/shard_map/ppermute | solution.py:19
  25.9 32.7 %collective-permute-start.1 = (bf16[512,512]{0,1:T(8,128)(2,1)}, bf16[512,512]{0,1:T(8,128)(2,1)}, u32[]{:S(2)}, u32[]{:S(2)}) collective-permute-start(bf16[512,512]{0,1:T(8,128)(2,1)} %copy.16), channel_id=1, source_target_pairs={{0,2},{2,4},{4,6},{6,8},{8,10},{10,12},{12,14},{1,3},{3,5},{5,7},{... | collective-permute-start | bytes 1572872 | tf_op jit(solution)/shard_map/ppermute | solution.py:19
  42.8 17.2 %copy-start.5 = (bf16[512,8,64]{2,0,1:T(8,128)(2,1)S(1)}, bf16[512,8,64]{2,0,1:T(8,128)(2,1)}, u32[]{:S(2)}) copy-start(bf16[512,8,64]{2,0,1:T(8,128)(2,1)} %get-tuple-element.7) | copy-start | bytes 1572868
  46.0 12.6 %copy-start.7 = (bf16[1536,512]{1,0:T(8,128)(2,1)}, bf16[1536,512]{1,0:T(8,128)(2,1)S(1)}, u32[]{:S(2)}) copy-start(bf16[1536,512]{1,0:T(8,128)(2,1)S(1)} %constant_dynamic-update-slice_fusion) | copy-start | bytes 4718596
  89.9 4.6 %copy-start.10 = (f32[2,512,1536]{1,2,0:T(8,128)S(1)}, f32[2,512,1536]{1,2,0:T(8,128)}, u32[]{:S(2)}) copy-start(f32[2,512,1536]{1,2,0:T(8,128)} %get-tuple-element.20) | copy-start | bytes 18874372
  89.9 5.8 %slice-start.2 = ((s8[6291456]{0:T(1024)(128)(4,1)}), s8[4194304]{0:T(1024)(128)(4,1)S(1)}, s32[]{:S(2)}) async-start(s8[6291456]{0:T(1024)(128)(4,1)} %bitcast.112), calls=%async_computation.6 | async-start | bytes 8388608
  94.5 2.1 slice-start.3
  94.5 3.3 %slice-start = ((s8[6291456]{0:T(1024)(128)(4,1)}), s8[4194304]{0:T(1024)(128)(4,1)S(1)}, s32[]{:S(2)}) async-start(s8[6291456]{0:T(1024)(128)(4,1)} %bitcast.110), calls=%async_computation.4 | async-start | bytes 8388608
  96.6 1.8 slice-start.1
  219.7 0.7 copy-start.9
  219.7 1.1 copy-start.1
  219.7 18.0 %copy-start.8 = (f32[2688]{0:T(1024)S(1)}, f32[2688]{0:T(1024)}, u32[]{:S(2)}) copy-start(f32[2688]{0:T(1024)} %param.12) | copy-start | bytes 32260
  219.7 45.4 %all-reduce.3.cloned.1.call-start = ((), (), s32[]{:S(2)}) async-start(), calls=%async_computation.3 | async-start | bytes 524288 | tf_op jit(solution)/shard_map/psum | solution.py:82
Sparse Core Ops, SparseCore 0:
  9.5 197.4 all-gather.1
  219.9 17.7 reduce-scatter.1
  245.6 19.4 all-reduce.2
where the time goes:
time: 280 us
  waiting for transfers between devices  153 us (55%)
  matrix products  64.2 us (23%)
  local copies, waits for them, and re-layouts  17.3 us (6%)
  starting transfers between devices  17.2 us (6%)
  between operations  13.3 us (5%)
  other arithmetic  12.6 us (4%)
    all_gather x1, waiting for transfers between devices, on_device(): lax.all_gather(out_proj, 'row', axis=0, tiled=True)  108 us
    sub x4, matrix products, on_device(): weights = jnp.where(allowed, jnp.exp(scores - row_max), 0.0)  29.8 us
    ppermute x4, starting transfers between devices, shifted(): return lax.ppermute(block, axis, route)  16.8 us
    reduce_scatter x1, waiting for transfers between devices, on_device(): lax.psum_scatter(partial_sum, 'col', scatter_dimension=1, tiled=True)  16.2 us
    unnamed x38, local copies, waits for them, and re-layouts  14.3 us
    psum x1, waiting for transfers between devices, on_device(): lax.psum((jnp.sum(hidden * hidden, axis=1), gained, mean_code), 'col')  14.2 us
    ppermute x4, waiting for transfers between devices, shifted(): return lax.ppermute(block, axis, route)  13.4 us
    dot_general x1, matrix products, on_device(): jnp.dot(attended, lax.all_gather(out_proj, 'row', axis=0, tiled=True), pr...  12.6 us
  transfers between devices with their start and end apart: 7, of which 5 were waited for; matrix products, arithmetic and copies ran while one was open for 22% of the time, Pallas kernels for 0%

commit v1 on v0

v1 whole, which is shorter than its diff:
```python
import functools

import jax
import jax.numpy as jnp
from jax import lax
from jax.experimental import pallas as pl
from jax.experimental.pallas import tpu as pltpu
from jax.sharding import Mesh
from jax.sharding import PartitionSpec as P

HD = 128
WINDOW = 1024
RANK = 64

query_scale = 168.0 ** (-0.5)
norm_eps = 1e-06
rope_base = 10000.0
log2_e = 1.4426950408889634

CHUNKS = ((2, "B"), (3, "D"), (2, "B"))
TILE = 384

NT = (((1,), (1,)), ((), ()))


def split_high_low(value):
    high = lax.reduce_precision(value, 8, 7)
    return high.astype(jnp.bfloat16), (value - high).astype(jnp.bfloat16)


def rope_tables(first_position, count):
    half_dim = HD // 2
    inverse = jnp.exp(
        -(2.0 * jnp.arange(half_dim, dtype=jnp.float32) / HD) * jnp.log(jnp.float32(rope_base))
    )
    positions = (first_position + jnp.arange(count, dtype=jnp.int32)).astype(jnp.float32)
    angles = positions[:, None] * inverse[None, :]
    cosine, sine = jnp.cos(angles), jnp.sin(angles)
    return jnp.concatenate([cosine, cosine], 1), jnp.concatenate([-sine, sine], 1)


def attend_kernel(tok, group, direct, row_ref, q_ref, k0, k1, k2, v0, v1, v2, cos_ref, sin_ref, out_ref):
    tile = 256

    def turned(field, at):
        wide = field.astype(jnp.float32)
        cos, sin = cos_ref[at : at + tok, :], sin_ref[at : at + tok, :]
        return (wide * cos + pltpu.roll(wide, HD // 2, 1) * sin).astype(jnp.bfloat16)

    row = row_ref[0]
    bias0 = jnp.where(row >= 2, 0.0, -1e30).astype(jnp.float32)
    bias1 = jnp.where(row >= 1, 0.0, -1e30).astype(jnp.float32)
    key0, key1, key2 = turned(k0[...], 0), turned(k1[...], tok), turned(k2[...], 2 * tok)
    heads = [turned(q_ref[:, h * HD : (h + 1) * HD], 2 * tok) for h in range(group)]
    scale = query_scale * log2_e
    stacked = group * tile
    inner = lax.rem(lax.broadcasted_iota(jnp.int32, (stacked, tile), 0), tile)
    newer = lax.broadcasted_iota(jnp.int32, (stacked, tile), 1) > inner

    def dot_nt(a, b):
        return lax.dot_general(a, b, NT, preferred_element_type=jnp.float32)

    def dot(a, b):
        return jnp.dot(a, b, preferred_element_type=jnp.float32)

    for t in range(tok // tile):
        lo, hi = t * tile, (t + 1) * tile
        query = jnp.concatenate([h[lo:hi] for h in heads], 0)
        parts = [(dot_nt(query, key1) + bias1, v1[...])]
        if hi < tok:
            parts.append((dot_nt(query, key0[hi:]) + bias0, v0[hi:, :]))
        if lo > 0:
            parts.append((dot_nt(query, key2[:lo]), v2[:lo, :]))
        mixed = jnp.where(newer, dot_nt(query, key0[lo:hi]) + bias0, dot_nt(query, key2[lo:hi]))
        top = jnp.max(mixed, axis=1, keepdims=True)
        for part, _ in parts:
            top = jnp.maximum(top, jnp.max(part, axis=1, keepdims=True))
        top = top * scale
        weights = jnp.exp2(mixed * scale - top)
        total = jnp.sum(weights, axis=1, keepdims=True)
        older = jnp.where(newer, weights, 0.0)
        result = dot(older.astype(jnp.bfloat16), v0[lo:hi, :])
        result += dot((weights - older).astype(jnp.bfloat16), v2[lo:hi, :])
        for part, value in parts:
            weights = jnp.exp2(part * scale - top)
            total += jnp.sum(weights, axis=1, keepdims=True)
            result += dot(weights.astype(jnp.bfloat16), value)
        result = (result / total).astype(jnp.bfloat16)
        for h in range(group):
            block = result[h * tile : (h + 1) * tile]
            if direct:
                out_ref[h, lo:hi, :] = block
            else:
                out_ref[lo:hi, h * HD : (h + 1) * HD] = block


def attend(row, queries, key_blocks, val_blocks, cos, sin, direct):
    tok, kv_local = queries.shape[0], key_blocks[0].shape[1] // HD
    group = queries.shape[1] // HD // kv_local
    head_block = pl.BlockSpec((tok, HD), lambda g, r: (0, g))
    table = pl.BlockSpec((3 * tok, HD), lambda g, r: (0, 0))
    if direct:
        out_shape = (group, tok, kv_local * HD)
        out_spec = pl.BlockSpec((group, tok, HD), lambda g, r: (0, 0, g))
    else:
        out_shape = queries.shape
        out_spec = pl.BlockSpec((tok, group * HD), lambda g, r: (0, g))
    heads = kv_local * group
    return pl.pallas_call(
        functools.partial(attend_kernel, tok, group, direct),
        grid_spec=pltpu.PrefetchScalarGridSpec(
            num_scalar_prefetch=1,
            grid=(kv_local,),
            in_specs=[pl.BlockSpec((tok, group * HD), lambda g, r: (0, g))] + [head_block] * 6 + [table] * 2,
            out_specs=out_spec,
        ),
        out_shape=jax.ShapeDtypeStruct(out_shape, jnp.bfloat16),
        compiler_params=pltpu.CompilerParams(vmem_limit_bytes=48 * 2**20),
        cost_estimate=pl.CostEstimate(
            flops=heads * tok * 10 * tok * HD, bytes_accessed=6 * 2**20, transcendentals=heads * tok * 2 * tok
        ),
    )(row, queries, *key_blocks, *val_blocks, cos, sin)


def project_kernel(pick_ref, att_ref, w0, w1, w2, w3, gain_ref, in_a, in_b, hidden_ref, stat_ref):
    step = pl.program_id(0)
    total = None
    for n, piece in enumerate((w0, w1, w2, w3)):
        part = jnp.dot(
            att_ref[pick_ref[2 * n], pick_ref[2 * n + 1]], piece[...], preferred_element_type=jnp.float32
        )
        total = part if total is None else total + part
    hidden_ref[...] = total
    gained = total * gain_ref[...]
    high = gained.astype(jnp.bfloat16)
    low = (gained - high.astype(jnp.float32)).astype(jnp.bfloat16)
    code = jnp.dot(high, in_a[...], preferred_element_type=jnp.float32)
    code += jnp.dot(low, in_b[...], preferred_element_type=jnp.float32)
    code = code + pltpu.roll(code, RANK, 1)
    square = jnp.sum(total * total, axis=1, keepdims=True)
    lane = lax.broadcasted_iota(jnp.int32, code.shape, 1)
    stat = jnp.where(lane < RANK, code, square)

    @pl.when(step == 0)
    def _():
        stat_ref[...] = stat

    @pl.when(step > 0)
    def _():
        stat_ref[...] += stat


def project(pick, att, pieces, gain, in_a, in_b):
    tok, depth = att.shape[2], att.shape[3]
    count = pieces[0].shape[1]
    return pl.pallas_call(
        project_kernel,
        grid_spec=pltpu.PrefetchScalarGridSpec(
            num_scalar_prefetch=1,
            grid=(count // TILE,),
            in_specs=[pl.BlockSpec(att.shape, lambda j, r: (0, 0, 0, 0))]
            + [pl.BlockSpec((depth, TILE), lambda j, r: (0, j))] * 4
            + [pl.BlockSpec((1, TILE), lambda j, r: (0, j))]
            + [pl.BlockSpec((TILE, 2 * RANK), lambda j, r: (j, 0))] * 2,
            out_specs=[
                pl.BlockSpec((tok, TILE), lambda j, r: (0, j)),
                pl.BlockSpec((tok, 2 * RANK), lambda j, r: (0, 0)),
            ],
        ),
        out_shape=[
            jax.ShapeDtypeStruct((tok, count), jnp.float32),
            jax.ShapeDtypeStruct((tok, 2 * RANK), jnp.float32),
        ],
        compiler_params=pltpu.CompilerParams(vmem_limit_bytes=48 * 2**20),
        cost_estimate=pl.CostEstimate(
            flops=2 * tok * 4 * depth * count, bytes_accessed=8 * depth * count, transcendentals=0
        ),
    )(pick, att, *pieces, gain, in_a, in_b)


def finish_kernel(model_width, counts, stat_ref, mean_ref, gain_ref, out_w_ref, *refs):
    hidden_refs, erased_ref = refs[:-1], refs[-1]
    stat = stat_ref[...]
    inv_rms = lax.rsqrt(stat[:, RANK : RANK + 1] / model_width + norm_eps)
    lane = lax.broadcasted_iota(jnp.int32, stat.shape, 1)
    code = jnp.where(lane < RANK, stat * inv_rms - mean_ref[...], 0.0)
    high = code.astype(jnp.bfloat16).astype(jnp.float32)
    low = code - high
    packed = jnp.concatenate([high + pltpu.roll(low, RANK, 1), high], 1).astype(jnp.bfloat16)
    at = 0
    for count, hidden in zip(counts, hidden_refs):
        for j in range(0, count, TILE):
            here = slice(at + j, at + j + TILE)
            removed = lax.dot_general(packed, out_w_ref[here, :], NT, preferred_element_type=jnp.float32)
            normed = hidden[:, j : j + TILE] * inv_rms * gain_ref[:, here]
            erased_ref[:, here] = (normed - removed).astype(jnp.bfloat16)
        at += count


def finish(model_width, stat, mean_code, gain, out_w, hiddens):
    tok, width = stat.shape[0], gain.shape[1]
    counts = [h.shape[1] for h in hiddens]
    rows = 128
    whole = lambda shape: pl.BlockSpec(shape, lambda i: (0, 0))
    return pl.pallas_call(
        functools.partial(finish_kernel, model_width, counts),
        grid=(tok // rows,),
        in_specs=[
            pl.BlockSpec((rows, 2 * RANK), lambda i: (i, 0)),
            whole(mean_code.shape),
            whole(gain.shape),
            whole(out_w.shape),
        ]
        + [pl.BlockSpec((rows, count), lambda i: (i, 0)) for count in counts],
        out_specs=pl.BlockSpec((rows, width), lambda i: (i, 0)),
        out_shape=jax.ShapeDtypeStruct((tok, width), jnp.bfloat16),
        compiler_params=pltpu.CompilerParams(vmem_limit_bytes=48 * 2**20),
        cost_estimate=pl.CostEstimate(
            flops=2 * tok * 256 * width, bytes_accessed=6 * tok * width, transcendentals=0
        ),
    )(stat, mean_code, gain, out_w, *hiddens)


def swapped(block, axis):
    return lax.ppermute(block, axis, [(0, 1), (1, 0)])


def on_device(queries, keys, values, out_proj, post_gain, mean_vec, erase_in, erase_out):
    tok = queries.shape[0]
    outer, inner = lax.axis_size("far"), lax.axis_size("near")
    grp, far, near, col = (lax.axis_index(a) for a in ("grp", "far", "near", "col"))
    row = far * inner + near
    depth, model_width = out_proj.shape
    width = model_width // 2

    mine = lax.dynamic_slice_in_dim(out_proj, col * width, width, 1)
    theirs = swapped(lax.dynamic_slice_in_dim(out_proj, (1 - col) * width, width, 1), "col")
    share = jnp.where(grp == col, mine, theirs)

    ahead = [(i, i + 1) for i in range(outer - 1)]
    blocks = []
    for own in (keys, values):
        second = lax.ppermute(own, "far", ahead)
        first = swapped(jnp.where(near == 0, own, second), "near")
        blocks.append((second, first, own))

    pieces = []
    at = 0
    bounds = []
    for tiles, order in CHUNKS:
        count = tiles * TILE
        along_far = lax.all_gather(share[:, at : at + count], "far", axis=0, tiled=True)
        along_near = swapped(along_far, "near")
        other = swapped(along_far, "grp")
        last = swapped(along_near, "grp") if order == "B" else swapped(other, "near")
        pieces.append((along_far, along_near, other, last))
        bounds.append((at, at + count))
        at += count

    mean_code = jnp.dot(mean_vec[None, :], erase_in, precision=lax.Precision.HIGHEST)
    mean_code = jnp.pad(mean_code, ((0, 7), (0, RANK)))
    mean_code = (mean_code + swapped(mean_code, "col"))[:1]

    cos, sin = rope_tables((row - 2) * tok, 3 * tok)
    kv_local = keys.shape[1] // HD
    group = queries.shape[1] // HD // kv_local
    direct = depth == HD and group == inner
    attended = attend(row[None], queries, *blocks_of(blocks), cos, sin, direct)
    if not direct:
        attended = attended.reshape(tok, outer, inner, depth).transpose(2, 0, 1, 3)
        attended = attended.reshape(inner, tok, outer * depth)
    att = jnp.stack([attended, swapped(attended, "col")])

    in_high, in_low = split_high_low(erase_in)
    in_a = jnp.concatenate([in_high, in_low], 1)
    in_b = jnp.concatenate([in_high, jnp.zeros_like(in_low)], 1)
    out_high, out_low = split_high_low(erase_out)
    out_w = jnp.concatenate([out_high, out_high, out_low, jnp.zeros_like(out_low)], 1)
    gain = post_gain[None, :]

    here = jnp.where(grp == col, 0, 1)
    pick = jnp.stack([here, near, here, 1 - near, 1 - here, near, 1 - here, 1 - near]).astype(jnp.int32)
    hiddens, stats = [], None
    for (lo, hi), piece in zip(bounds, pieces):
        hidden, stat = project(pick, att, piece, gain[:, lo:hi], in_a[lo:hi], in_b[lo:hi])
        hiddens.append(hidden)
        stats = stat if stats is None else stats + stat
    stats = stats + swapped(stats, "col")
    return finish(model_width, stats, mean_code, gain, out_w, hiddens)


def blocks_of(blocks):
    return blocks[0], blocks[1]


def solution(mesh):
    grp, row, col = (mesh.shape[a] for a in ("grp", "row", "col"))
    fine = Mesh(mesh.devices.reshape(grp, row // 2, 2, col), ("grp", "far", "near", "col"))
    tokens = P(("grp", "far", "near"), "col")
    placed = (tokens, tokens, tokens, P(("col", "far", "near"), None), P("col"), P("col"), P("col", None), P("col", None))
    return jax.shard_map(on_device, mesh=fine, in_specs=placed, out_specs=tokens, check_vma=False)
```

time: 280 us -> 196 us (0.70)
  waiting for transfers between devices: 153 us -> 39.4 us
  matrix products: 64.2 us -> 0.66 us
  blocking collectives: 2.47 us -> 45.5 us
  Pallas kernels: 0 us -> 37.3 us
  other arithmetic: 12.6 us -> 20.9 us
  starting transfers between devices: 17.2 us -> 20 us
    all_gather x1, waiting for transfers between devices: 108 us -> 0.01 us  [on_device(): lax.all_gather(share[:, at:at + count], 'far', axis=0, tiled=True)]
    all_gather x0 -> x2, blocking collectives: none -> 45.5 us  [on_device(): lax.all_gather(share[:, at:at + count], 'far', axis=0, tiled=True)]
    pallas_call x0 -> x5, Pallas kernels: none -> 37.3 us  [the longest x3 20.3 us: project(): pl.pallas_call(project_kernel, grid_spec=pltpu.PrefetchScalarGridSpec(num...]
    dot_general x7 -> x0, matrix products: 33.7 us -> none  [the longest x1 12.6 us: on_device(): jnp.dot(attended, lax.all_gather(out_proj, 'row', axis=0, tiled=True), pr...]
    sub x4 -> x0, matrix products: 29.8 us -> none  [on_device(): weights = jnp.where(allowed, jnp.exp(scores - row_max), 0.0)]
    ppermute x4 -> x17, waiting for transfers between devices: 13.4 us -> 39.3 us  [the longest x15 39.3 us: swapped(): return lax.ppermute(block, axis, [(0, 1), (1, 0)])]
    reduce_scatter x1 -> x0, waiting for transfers between devices: 16.2 us -> none  [on_device(): lax.psum_scatter(partial_sum, 'col', scatter_dimension=1, tiled=True)]
    psum x1 -> x0, waiting for transfers between devices: 14.2 us -> none  [on_device(): lax.psum((jnp.sum(hidden * hidden, axis=1), gained, mean_code), 'col')]
  transfers between devices with their start and end apart: 7 -> 18, of which waited for: 5 -> 4; matrix products, arithmetic and copies ran while one was open for 22% -> 16% of each run, Pallas kernels for 0% -> 16%
where the time goes in v1:
time: 196 us; the launch traced here: 195 us
  blocking collectives  45.5 us (23%)
  waiting for transfers between devices  39.4 us (20%)
  Pallas kernels  37.3 us (19%)
  other arithmetic  20.9 us (11%)
  starting transfers between devices  20 us (10%)
  local copies, waits for them, and re-layouts  17.4 us (9%)
  between operations  13.7 us (7%)
    all_gather x2, blocking collectives, on_device(): lax.all_gather(share[:, at:at + count], 'far', axis=0, tiled=True)  45.5 us
    ppermute x15, waiting for transfers between devices, swapped(): return lax.ppermute(block, axis, [(0, 1), (1, 0)])  39.3 us
    pallas_call x3, Pallas kernels, project(): pl.pallas_call(project_kernel, grid_spec=pltpu.PrefetchScalarGridSpec(num...  20.3 us
    pallas_call x1, Pallas kernels, attend(): pl.pallas_call(functools.partial(attend_kernel, tok, group, direct), grid...  11.8 us
    ppermute x15, starting transfers between devices, swapped(): return lax.ppermute(block, axis, [(0, 1), (1, 0)])  11.4 us
    unnamed x49, local copies, waits for them, and re-layouts  9.17 us
    ppermute x2, starting transfers between devices, on_device(): second = lax.ppermute(own, 'far', ahead)  8.57 us
    reduce_precision x2, local copies, waits for them, and re-layouts, split_high_low(): high = lax.reduce_precision(value, 8, 7)  5.28 us
  transfers between devices with their start and end apart: 18, of which 4 were waited for; matrix products, arithmetic and copies ran while one was open for 16% of the time, Pallas kernels for 16%

profile of v1, /device:TPU:0, one launch (start us, length us, event | category | flops | bytes accessed | tf_op | source)
XLA Modules:
  0.0 194.9 jit_solution(2935371267901129934)
XLA Ops:
  6.5 5.1 %collective-permute-start = (bf16[512,512]{1,0:T(8,128)(2,1)}, bf16[512,512]{1,0:T(8,128)(2,1)S(1)}, u32[]{:S(2)}, u32[]{:S(2)}) collective-permute-start(bf16[512,512]{1,0:T(8,128)(2,1)} %k2.1), channel_id=1, source_target_pairs={{0,4},{4,8},{8,12},{1,5},{5,9},{9,13},{2,6},{6,10},{10,14},{3,7},{... | collective-permute-start | bytes 1572872 | tf_op jit(solution)/shard_map/ppermute | solution.py:243
  11.6 3.5 %collective-permute-start.2 = (bf16[512,512]{1,0:T(8,128)(2,1)}, bf16[512,512]{1,0:T(8,128)(2,1)S(1)}, u32[]{:S(2)}, u32[]{:S(2)}) collective-permute-start(bf16[512,512]{1,0:T(8,128)(2,1)} %v2.1), channel_id=1, source_target_pairs={{0,4},{4,8},{8,12},{1,5},{5,9},{9,13},{2,6},{6,10},{10,14},{3,7},{... | collective-permute-start | bytes 1572872 | tf_op jit(solution)/shard_map/ppermute | solution.py:243
  15.1 2.0 %constant_dynamic-slice_fusion = bf16[128,2688]{1,0:T(8,128)(2,1)} fusion(bf16[128,5376]{1,0:T(8,128)(2,1)} %param.11, s32[]{:T(128)S(6)} %select_n.36), kind=kLoop, calls=%fused_computation.22 | loop fusion | bytes 1376260 | tf_op jit(solution)/shard_map/dynamic_slice | solution.py:237
  18.5 2.6 %copy.13 = f32[2688,64]{1,0:T(8,128)} copy(f32[2688,64]{0,1:T(8,128)} %reduce_precision.6) | data formatting | bytes 1376256 | tf_op jit(solution)/shard_map/reduce_precision | solution.py:27
  21.2 3.2 %fusion.2 = (bf16[2688,64]{1,0:T(8,128)(2,1)}, bf16[2688,64]{1,0:T(8,128)(2,1)}) fusion(f32[2688,64]{1,0:T(8,128)} %copy.13, f32[2688,64]{1,0:T(8,128)S(1)} %copy.14), kind=kLoop, calls=%fused_computation.24 | loop fusion | flops 516096 | bytes 2064384 | tf_op jit(solution)/shard_map/convert_element_type | solution.py:28
  26.1 4.2 %fusion = (f32[1536,64]{1,0:T(8,128)S(1)}, f32[1536,64]{1,0:T(8,128)S(1)}, f32[1536,64]{1,0:T(8,128)}) fusion(f32[64]{0:T(128)S(1)} %multiply_exponential_fusion, f32[1536]{0:T(1024)S(1)} %add_convert_fusion), kind=kLoop, calls=%fused_computation.16 | loop fusion | flops 196608 | bytes 1186048 | tf_op jit(solution)/shard_map/neg | solution.py:39
  31.2 1.5 copy.17
  32.8 2.7 %copy.16 = f32[2688,64]{1,0:T(8,128)} copy(f32[2688,64]{0,1:T(8,128)} %reduce_precision.7) | data formatting | bytes 1376256 | tf_op jit(solution)/shard_map/reduce_precision | solution.py:27
  35.4 2.8 %pad_maximum_fusion.1 = (f32[1536,128]{1,0:T(8,128)S(1)}, f32[1536,128]{1,0:T(8,128)}) fusion(f32[1536,64]{1,0:T(8,128)} %get-tuple-element.35, f32[1536,64]{1,0:T(8,128)S(1)} %get-tuple-element.34, f32[1536,64]{1,0:T(8,128)S(1)} %get-tuple-element.33), kind=kLoop, calls=%fused_computation.6 | loop fusion | flops 393216 | bytes 2752512 | tf_op jit(solution)/shard_map/concatenate | solution.py:39
  42.2 27.5 %all_gather.9.w0 = bf16[512,768]{1,0:T(8,128)(2,1)S(1)} all-gather(bf16[128,768]{1,0:T(8,128)(2,1)S(1)} %get-tuple-element.29), channel_id=1, replica_groups=mesh['grp'=2,'far'=4,'near'=2,'col'=2] {'far'}, dimensions={0}, use_global_device_ids=true | all-gather | bytes 983040 | tf_op jit(solution)/shard_map/all_gather | solution.py:252
  69.7 1.5 collective-permute-start.6
  71.2 1.7 collective-permute-start.7
  73.2 18.1 %all_gather.11.w0 = bf16[512,768]{1,0:T(8,128)(2,1)S(1)} all-gather(bf16[128,768]{1,0:T(8,128)(2,1)S(1)} %get-tuple-element.30), channel_id=1, replica_groups=mesh['grp'=2,'far'=4,'near'=2,'col'=2] {'far'}, dimensions={0}, use_global_device_ids=true | all-gather | bytes 983040 | tf_op jit(solution)/shard_map/all_gather | solution.py:252
  97.1 11.8 %shard_map.82 = bf16[2,512,512]{2,1,0:T(8,128)(2,1)S(1)} custom-call(s32[1]{0:T(128)} %bitcast.4.row_ref, bf16[512,1024]{1,0:T(8,128)(2,1)} %q_ref.1, bf16[512,512]{1,0:T(8,128)(2,1)S(1)} %copy-done.6, bf16[512,512]{1,0:T(8,128)(2,1)} %collective-permute-done.1.k1, bf16[512,512]{1,0:T(8,128)(2,1)S(1)} %copy-done.2, bf16[512,512]{1,0:T(8,128)(2,1)S(1)} %copy-done.8, ...), custom_call_target="tpu_custom_call" | custom-call | flops 2684354560 | bytes 6291456 | tf_op jit(solution)/shard_map/pallas_call | solution.py:109
  113.1 4.0 %collective-permute-done.10.w2 = bf16[512,1152]{1,0:T(8,128)(2,1)} collective-permute-done((bf16[512,1152]{1,0:T(8,128)(2,1)}, bf16[512,1152]{1,0:T(8,128)(2,1)}, u32[]{:S(2)}, u32[]{:S(2)}) %collective-permute-start.10) | collective-permute-done | bytes 1179680 | tf_op jit(solution)/shard_map/ppermute | solution.py:225
  118.3 1.7 pad_slice_fusion.2
  122.3 2.7 %pad_maximum_fusion.att_ref = bf16[2,2,512,512]{3,2,1,0:T(8,128)(2,1)} fusion(bf16[1,2,512,512]{3,2,1,0:T(8,128)(2,1)} %bitcast.6, bf16[1,2,512,512]{3,2,1,0:T(8,128)(2,1)S(1)} %bitcast.10), kind=kLoop, calls=%fused_computation | loop fusion | flops 1048576 | bytes 4194304 | tf_op jit(solution)/shard_map/stack | solution.py:272
  125.1 8.7 %collective-permute-done.8.w3 = bf16[512,768]{1,0:T(8,128)(2,1)S(1)} collective-permute-done((bf16[512,768]{1,0:T(8,128)(2,1)}, bf16[512,768]{1,0:T(8,128)(2,1)S(1)}, u32[]{:S(2)}, u32[]{:S(2)}) %collective-permute-start.8) | collective-permute-done | bytes 786464 | tf_op jit(solution)/shard_map/ppermute | solution.py:225
  133.8 5.9 %shard_map.83 = (f32[512,768]{1,0:T(8,128)S(1)}, f32[512,128]{1,0:T(8,128)S(1)}) custom-call(s32[8]{0:T(128)S(1)} %stack.32.pick_ref, bf16[2,2,512,512]{3,2,1,0:T(8,128)(2,1)} %pad_maximum_fusion.att_ref, bf16[512,768]{1,0:T(8,128)(2,1)S(1)} %all_gather.9.w0, bf16[512,768]{1,0:T(8,128)(2,1)} %collective-permute-done.6.w1, ...), custom_call_target="tpu_custom_call" | custom-call | flops 1610612736 | bytes 3145728 | tf_op jit(solution)/shard_map/pallas_call | solution.py:156
  139.7 11.0 %collective-permute-done.13.w2 = bf16[512,768]{1,0:T(8,128)(2,1)S(1)} collective-permute-done((bf16[512,768]{1,0:T(8,128)(2,1)S(1)}, bf16[512,768]{1,0:T(8,128)(2,1)S(1)}, u32[]{:S(2)}, u32[]{:S(2)}) %collective-permute-start.13) | collective-permute-done | bytes 786464 | tf_op jit(solution)/shard_map/ppermute | solution.py:225
  150.6 15.7 %collective-permute-done.14.w3 = bf16[512,768]{1,0:T(8,128)(2,1)S(1)} collective-permute-done((bf16[512,768]{1,0:T(8,128)(2,1)}, bf16[512,768]{1,0:T(8,128)(2,1)S(1)}, u32[]{:S(2)}, u32[]{:S(2)}) %collective-permute-start.14) | collective-permute-done | bytes 786464 | tf_op jit(solution)/shard_map/ppermute | solution.py:225
  166.3 5.7 %shard_map.85 = (f32[512,768]{1,0:T(8,128)S(1)}, f32[512,128]{1,0:T(8,128)S(1)}) custom-call(s32[8]{0:T(128)S(1)} %stack.32.pick_ref, bf16[2,2,512,512]{3,2,1,0:T(8,128)(2,1)} %pad_maximum_fusion.att_ref, bf16[512,768]{1,0:T(8,128)(2,1)S(1)} %all_gather.11.w0, bf16[512,768]{1,0:T(8,128)(2,1)} %collective-permute-done.12.w1, ...), custom_call_target="tpu_custom_call" | custom-call | flops 1610612736 | bytes 3145728 | tf_op jit(solution)/shard_map/pallas_call | solution.py:156
  172.1 8.7 %shard_map.84 = (f32[512,1152]{1,0:T(8,128)}, f32[512,128]{1,0:T(8,128)S(1)}) custom-call(s32[8]{0:T(128)S(1)} %stack.32.pick_ref, bf16[2,2,512,512]{3,2,1,0:T(8,128)(2,1)} %pad_maximum_fusion.att_ref, bf16[512,1152]{1,0:T(8,128)(2,1)} %all-gather.2.cloned.1.call-done.w0, bf16[512,1152]{1,0:T(8,128)(2,1)} %collective-permute-done.9.w1, ...), custom_call_target="tpu_custom_call" | custom-call | flops 2415919104 | bytes 4718592 | tf_op jit(solution)/shard_map/pallas_call | solution.py:156
  182.9 5.2 %shard_map.86 = bf16[512,2688]{1,0:T(8,128)(2,1)} custom-call(f32[512,128]{1,0:T(8,128)S(1)} %add.43.stat_ref, f32[1,128]{1,0:T(1,128)S(1)} %slice.51.mean_ref, f32[1,2688]{1,0:T(1,128)S(1)} %broadcast_in_dim.10.gain_ref, bf16[2688,256]{1,0:T(8,128)(2,1)S(1)} %maximum_maximum_fusion.out_w_ref, f32[512,768]{1,0:T(8,128)S(1)} %get-tuple-element.14.refs_0_, ...), custom_call_target="tpu_custom_call" | custom-call | flops 704643072 | bytes 8257536 | tf_op jit(solution)/shard_map/pallas_call | solution.py:205
  (101 shorter events, 23.7 us)
Async XLA Ops:
  6.5 10.6 %copy-start.9 = (f32[2688,64]{0,1:T(8,128)S(1)}, f32[2688,64]{0,1:T(8,128)}, u32[]{:S(2)}) copy-start(f32[2688,64]{0,1:T(8,128)} %param.14) | copy-start | bytes 2064388
  6.5 66.4 %all-gather.2.cloned.1.call-start = ((), (), s32[]{:S(2)}) async-start(), calls=%async_computation | async-start | bytes 1474560 | tf_op jit(solution)/shard_map/all_gather | solution.py:252
  6.5 31.7 %collective-permute-start = (bf16[512,512]{1,0:T(8,128)(2,1)}, bf16[512,512]{1,0:T(8,128)(2,1)S(1)}, u32[]{:S(2)}, u32[]{:S(2)}) collective-permute-start(bf16[512,512]{1,0:T(8,128)(2,1)} %k2.1), channel_id=1, source_target_pairs={{0,4},{4,8},{8,12},{1,5},{5,9},{9,13},{2,6},{6,10},{10,14},{3,7},{... | collective-permute-start | bytes 1572872 | tf_op jit(solution)/shard_map/ppermute | solution.py:243
  11.6 29.1 %collective-permute-start.2 = (bf16[512,512]{1,0:T(8,128)(2,1)}, bf16[512,512]{1,0:T(8,128)(2,1)S(1)}, u32[]{:S(2)}, u32[]{:S(2)}) collective-permute-start(bf16[512,512]{1,0:T(8,128)(2,1)} %v2.1), channel_id=1, source_target_pairs={{0,4},{4,8},{8,12},{1,5},{5,9},{9,13},{2,6},{6,10},{10,14},{3,7},{... | collective-permute-start | bytes 1572872 | tf_op jit(solution)/shard_map/ppermute | solution.py:243
  17.2 7.2 %collective-permute-start.5 = (bf16[128,2688]{1,0:T(8,128)(2,1)}, bf16[128,2688]{1,0:T(8,128)(2,1)}, u32[]{:S(2)}, u32[]{:S(2)}) collective-permute-start(bf16[128,2688]{1,0:T(8,128)(2,1)} %constant_dynamic-slice_fusion), channel_id=1, source_target_pairs={{0,1},{1,0},{2,3},{3,2},{4,5},{5,4},{6,7},{7,6},{8,9},{9,8},{10,11... | collective-permute-start | bytes 2064392 | tf_op jit(solution)/shard_map/ppermute | solution.py:225
  39.2 52.1 %collective-permute-start.1 = (bf16[512,512]{1,0:T(8,128)(2,1)}, bf16[512,512]{1,0:T(8,128)(2,1)}, u32[]{:S(2)}, u32[]{:S(2)}) collective-permute-start(bf16[512,512]{1,0:T(8,128)(2,1)} %broadcast_select_fusion.1), channel_id=1, source_target_pairs={{0,2},{2,0},{1,3},{3,1},{4,6},{6,4},{5,7},{7,5},{8,10},{10,8},{9,1... | collective-permute-start | bytes 1572872 | tf_op jit(solution)/shard_map/ppermute | solution.py:225
  40.7 29.0 %copy-start.7 = (bf16[512,512]{1,0:T(8,128)(2,1)}, bf16[512,512]{1,0:T(8,128)(2,1)S(1)}, u32[]{:S(2)}) copy-start(bf16[512,512]{1,0:T(8,128)(2,1)S(1)} %collective-permute-done.2.v0) | copy-start | bytes 1572868
  41.6 50.1 %collective-permute-start.3 = (bf16[512,512]{1,0:T(8,128)(2,1)}, bf16[512,512]{1,0:T(8,128)(2,1)}, u32[]{:S(2)}, u32[]{:S(2)}) collective-permute-start(bf16[512,512]{1,0:T(8,128)(2,1)} %broadcast_select_fusion), channel_id=1, source_target_pairs={{0,2},{2,0},{1,3},{3,1},{4,6},{6,4},{5,7},{7,5},{8,10},{10,8},{9,1... | collective-permute-start | bytes 1572872 | tf_op jit(solution)/shard_map/ppermute | solution.py:225
  69.7 40.7 %collective-permute-start.6 = (bf16[512,768]{1,0:T(8,128)(2,1)S(1)}, bf16[512,768]{1,0:T(8,128)(2,1)}, u32[]{:S(2)}, u32[]{:S(2)}) collective-permute-start(bf16[512,768]{1,0:T(8,128)(2,1)S(1)} %all_gather.9.w0), channel_id=1, source_target_pairs={{0,2},{2,0},{1,3},{3,1},{4,6},{6,4},{5,7},{7,5},{8,10},{10,8},{9,1... | collective-permute-start | bytes 2359304 | tf_op jit(solution)/shard_map/ppermute | solution.py:225
  71.2 40.4 %collective-permute-start.7 = (bf16[512,768]{1,0:T(8,128)(2,1)S(1)}, bf16[512,768]{1,0:T(8,128)(2,1)}, u32[]{:S(2)}, u32[]{:S(2)}) collective-permute-start(bf16[512,768]{1,0:T(8,128)(2,1)S(1)} %all_gather.9.w0), channel_id=1, source_target_pairs={{0,16},{16,0},{1,17},{17,1},{2,18},{18,2},{3,19},{19,3},{4,20},{20... | collective-permute-start | bytes 2359304 | tf_op jit(solution)/shard_map/ppermute | solution.py:225
  72.9 44.1 %collective-permute-start.10 = (bf16[512,1152]{1,0:T(8,128)(2,1)}, bf16[512,1152]{1,0:T(8,128)(2,1)}, u32[]{:S(2)}, u32[]{:S(2)}) collective-permute-start(bf16[512,1152]{1,0:T(8,128)(2,1)} %all-gather.2.cloned.1.call-done.w0), channel_id=1, source_target_pairs={{0,16},{16,0},{1,17},{17,1},{2,18},{18,2},{3,19},{19,3},{4,20},{20... | collective-permute-start | bytes 3538952 | tf_op jit(solution)/shard_map/ppermute | solution.py:225
  91.3 28.7 %collective-permute-start.12 = (bf16[512,768]{1,0:T(8,128)(2,1)S(1)}, bf16[512,768]{1,0:T(8,128)(2,1)}, u32[]{:S(2)}, u32[]{:S(2)}) collective-permute-start(bf16[512,768]{1,0:T(8,128)(2,1)S(1)} %all_gather.11.w0), channel_id=1, source_target_pairs={{0,2},{2,0},{1,3},{3,1},{4,6},{6,4},{5,7},{7,5},{8,10},{10,8},{9,1... | collective-permute-start | bytes 2359304 | tf_op jit(solution)/shard_map/ppermute | solution.py:225
  97.1 11.9 %copy-start.13 = (f32[2688,64]{1,0:T(8,128)S(1)}, f32[2688,64]{1,0:T(8,128)}, u32[]{:S(2)}) copy-start(f32[2688,64]{1,0:T(8,128)} %copy.17) | copy-start | bytes 2064388
  97.1 11.9 %copy-start.14 = (f32[2688,64]{1,0:T(8,128)S(1)}, f32[2688,64]{1,0:T(8,128)}, u32[]{:S(2)}) copy-start(f32[2688,64]{1,0:T(8,128)} %copy.16) | copy-start | bytes 2064388
  108.9 9.1 %copy-start.22 = (f32[2688]{0:T(1024)S(1)}, f32[2688]{0:T(1024)}, u32[]{:S(2)}) copy-start(f32[2688]{0:T(1024)} %param.12) | copy-start | bytes 32260
  108.9 12.0 %collective-permute-start.4 = (bf16[2,512,512]{2,1,0:T(8,128)(2,1)S(1)}, bf16[2,512,512]{2,1,0:T(8,128)(2,1)}, u32[]{:S(2)}, u32[]{:S(2)}) collective-permute-start(bf16[2,512,512]{2,1,0:T(8,128)(2,1)S(1)} %shard_map.82), channel_id=1, source_target_pairs={{0,1},{1,0},{2,3},{3,2},{4,5},{5,4},{6,7},{7,6},{8,9},{9,8},{10,11... | collective-permute-start | bytes 3145736 | tf_op jit(solution)/shard_map/ppermute | solution.py:225
  110.3 23.4 %collective-permute-start.8 = (bf16[512,768]{1,0:T(8,128)(2,1)}, bf16[512,768]{1,0:T(8,128)(2,1)S(1)}, u32[]{:S(2)}, u32[]{:S(2)}) collective-permute-start(bf16[512,768]{1,0:T(8,128)(2,1)} %collective-permute-done.6.w1), channel_id=1, source_target_pairs={{0,16},{16,0},{1,17},{17,1},{2,18},{18,2},{3,19},{19,3},{4,20},{20... | collective-permute-start | bytes 2359304 | tf_op jit(solution)/shard_map/ppermute | solution.py:225
  111.6 60.4 %collective-permute-start.9 = (bf16[512,1152]{1,0:T(8,128)(2,1)}, bf16[512,1152]{1,0:T(8,128)(2,1)}, u32[]{:S(2)}, u32[]{:S(2)}) collective-permute-start(bf16[512,1152]{1,0:T(8,128)(2,1)} %all-gather.2.cloned.1.call-done.w0), channel_id=1, source_target_pairs={{0,2},{2,0},{1,3},{3,1},{4,6},{6,4},{5,7},{7,5},{8,10},{10,8},{9,1... | collective-permute-start | bytes 3538952 | tf_op jit(solution)/shard_map/ppermute | solution.py:225
  117.0 55.1 %collective-permute-start.11 = (bf16[512,1152]{1,0:T(8,128)(2,1)}, bf16[512,1152]{1,0:T(8,128)(2,1)}, u32[]{:S(2)}, u32[]{:S(2)}) collective-permute-start(bf16[512,1152]{1,0:T(8,128)(2,1)} %collective-permute-done.10.w2), channel_id=1, source_target_pairs={{0,2},{2,0},{1,3},{3,1},{4,6},{6,4},{5,7},{7,5},{8,10},{10,8},{9,1... | collective-permute-start | bytes 3538952 | tf_op jit(solution)/shard_map/ppermute | solution.py:225
  120.0 30.6 %collective-permute-start.13 = (bf16[512,768]{1,0:T(8,128)(2,1)S(1)}, bf16[512,768]{1,0:T(8,128)(2,1)S(1)}, u32[]{:S(2)}, u32[]{:S(2)}) collective-permute-start(bf16[512,768]{1,0:T(8,128)(2,1)S(1)} %all_gather.11.w0), channel_id=1, source_target_pairs={{0,16},{16,0},{1,17},{17,1},{2,18},{18,2},{3,19},{19,3},{4,20},{20... | collective-permute-start | bytes 2359304 | tf_op jit(solution)/shard_map/ppermute | solution.py:225
  120.9 45.4 %collective-permute-start.14 = (bf16[512,768]{1,0:T(8,128)(2,1)}, bf16[512,768]{1,0:T(8,128)(2,1)S(1)}, u32[]{:S(2)}, u32[]{:S(2)}) collective-permute-start(bf16[512,768]{1,0:T(8,128)(2,1)} %collective-permute-done.12.w1), channel_id=1, source_target_pairs={{0,16},{16,0},{1,17},{17,1},{2,18},{18,2},{3,19},{19,3},{4,20},{20... | collective-permute-start | bytes 2359304 | tf_op jit(solution)/shard_map/ppermute | solution.py:225
  133.8 49.0 %collective-permute-start.16 = (f32[8,128]{1,0:T(8,128)S(1)}, f32[8,128]{1,0:T(8,128)S(1)}, u32[]{:S(2)}, u32[]{:S(2)}) collective-permute-start(f32[8,128]{1,0:T(8,128)S(1)} %pad.5), channel_id=1, source_target_pairs={{0,1},{1,0},{2,3},{3,2},{4,5},{5,4},{6,7},{7,6},{8,9},{9,8},{10,11... | collective-permute-start | bytes 12296 | tf_op jit(solution)/shard_map/ppermute | solution.py:225
  172.1 8.8 %copy-start.19 = (bf16[2688,64]{1,0:T(8,128)(2,1)S(1)}, bf16[2688,64]{1,0:T(8,128)(2,1)}, u32[]{:S(2)}) copy-start(bf16[2688,64]{1,0:T(8,128)(2,1)} %get-tuple-element.18) | copy-start | bytes 1032196
  180.8 2.0 %collective-permute-start.15 = (f32[512,128]{1,0:T(8,128)S(1)}, f32[512,128]{1,0:T(8,128)S(1)}, u32[]{:S(2)}, u32[]{:S(2)}) collective-permute-start(f32[512,128]{1,0:T(8,128)S(1)} %add_add_fusion), channel_id=1, source_target_pairs={{0,1},{1,0},{2,3},{3,2},{4,5},{5,4},{6,7},{7,6},{8,9},{9,8},{10,11... | collective-permute-start | bytes 786440 | tf_op jit(solution)/shard_map/ppermute | solution.py:225
  (17 other events, 45.9 us)
Sparse Core Ops, SparseCore 0:
  26.3 40.4 all-gather.1

commit v2 on v1

v2 whole, which is shorter than its diff:
```python
import functools

import jax
import jax.numpy as jnp
from jax import lax
from jax.experimental import pallas as pl
from jax.experimental.pallas import tpu as pltpu
from jax.sharding import Mesh
from jax.sharding import PartitionSpec as P

HD = 128
WINDOW = 1024
RANK = 64

query_scale = 168.0 ** (-0.5)
norm_eps = 1e-06
rope_base = 10000.0
log2_e = 1.4426950408889634

TILE = 384
VMEM_LIMIT = 60 * 2**20

NT = (((1,), (1,)), ((), ()))


def split_high_low(value):
    high = lax.reduce_precision(value, 8, 7)
    return high.astype(jnp.bfloat16), (value - high).astype(jnp.bfloat16)


def rope_tables(first_position, count):
    half_dim = HD // 2
    inverse = jnp.exp(
        -(2.0 * jnp.arange(half_dim, dtype=jnp.float32) / HD) * jnp.log(jnp.float32(rope_base))
    )
    positions = (first_position + jnp.arange(count, dtype=jnp.int32)).astype(jnp.float32)
    angles = positions[:, None] * inverse[None, :]
    cosine, sine = jnp.cos(angles), jnp.sin(angles)
    return jnp.concatenate([cosine, cosine], 1), jnp.concatenate([-sine, sine], 1)


def attend_kernel(tok, group, direct, row_ref, q_ref, k0, k1, k2, v0, v1, v2, cos_ref, sin_ref, out_ref):
    tile = 256

    def turned(field, at):
        wide = field.astype(jnp.float32)
        cos, sin = cos_ref[at : at + tok, :], sin_ref[at : at + tok, :]
        return (wide * cos + pltpu.roll(wide, HD // 2, 1) * sin).astype(jnp.bfloat16)

    row = row_ref[0]
    bias0 = jnp.where(row >= 2, 0.0, -1e30).astype(jnp.float32)
    bias1 = jnp.where(row >= 1, 0.0, -1e30).astype(jnp.float32)
    key0, key1, key2 = turned(k0[...], 0), turned(k1[...], tok), turned(k2[...], 2 * tok)
    heads = [turned(q_ref[:, h * HD : (h + 1) * HD], 2 * tok) for h in range(group)]
    scale = query_scale * log2_e
    stacked = group * tile
    inner = lax.rem(lax.broadcasted_iota(jnp.int32, (stacked, tile), 0), tile)
    newer = lax.broadcasted_iota(jnp.int32, (stacked, tile), 1) > inner

    def dot_nt(a, b):
        return lax.dot_general(a, b, NT, preferred_element_type=jnp.float32)

    def dot(a, b):
        return jnp.dot(a, b, preferred_element_type=jnp.float32)

    for t in range(tok // tile):
        lo, hi = t * tile, (t + 1) * tile
        query = jnp.concatenate([h[lo:hi] for h in heads], 0)
        parts = [(dot_nt(query, key1) + bias1, v1[...])]
        if hi < tok:
            parts.append((dot_nt(query, key0[hi:]) + bias0, v0[hi:, :]))
        if lo > 0:
            parts.append((dot_nt(query, key2[:lo]), v2[:lo, :]))
        mixed = jnp.where(newer, dot_nt(query, key0[lo:hi]) + bias0, dot_nt(query, key2[lo:hi]))
        top = jnp.max(mixed, axis=1, keepdims=True)
        for part, _ in parts:
            top = jnp.maximum(top, jnp.max(part, axis=1, keepdims=True))
        top = top * scale
        weights = jnp.exp2(mixed * scale - top)
        total = jnp.sum(weights, axis=1, keepdims=True)
        older = jnp.where(newer, weights, 0.0)
        result = dot(older.astype(jnp.bfloat16), v0[lo:hi, :])
        result += dot((weights - older).astype(jnp.bfloat16), v2[lo:hi, :])
        for part, value in parts:
            weights = jnp.exp2(part * scale - top)
            total += jnp.sum(weights, axis=1, keepdims=True)
            result += dot(weights.astype(jnp.bfloat16), value)
        result = (result / total).astype(jnp.bfloat16)
        for h in range(group):
            block = result[h * tile : (h + 1) * tile]
            if direct:
                out_ref[h, lo:hi, :] = block
            else:
                out_ref[lo:hi, h * HD : (h + 1) * HD] = block


def attend(row, queries, key_blocks, val_blocks, cos, sin, direct):
    tok, kv_local = queries.shape[0], key_blocks[0].shape[1] // HD
    group = queries.shape[1] // HD // kv_local
    head_block = pl.BlockSpec((tok, HD), lambda g, r: (0, g))
    table = pl.BlockSpec((3 * tok, HD), lambda g, r: (0, 0))
    if direct:
        out_shape = (kv_local * group, tok, HD)
        out_spec = pl.BlockSpec((group, tok, HD), lambda g, r: (g, 0, 0))
    else:
        out_shape = queries.shape
        out_spec = pl.BlockSpec((tok, group * HD), lambda g, r: (0, g))
    heads = kv_local * group
    return pl.pallas_call(
        functools.partial(attend_kernel, tok, group, direct),
        grid_spec=pltpu.PrefetchScalarGridSpec(
            num_scalar_prefetch=1,
            grid=(kv_local,),
            in_specs=[pl.BlockSpec((tok, group * HD), lambda g, r: (0, g))] + [head_block] * 6 + [table] * 2,
            out_specs=out_spec,
        ),
        out_shape=jax.ShapeDtypeStruct(out_shape, jnp.bfloat16),
        compiler_params=pltpu.CompilerParams(vmem_limit_bytes=VMEM_LIMIT),
        cost_estimate=pl.CostEstimate(
            flops=heads * tok * 10 * tok * HD, bytes_accessed=6 * 2**20, transcendentals=heads * tok * 2 * tok
        ),
    )(row, queries, *key_blocks, *val_blocks, cos, sin)


def project_kernel(count, first, last, pick_ref, own_ref, other_ref, *refs):
    weights, refs = refs[:count], refs[count:]
    if not first:
        partial_ref, refs = refs[0], refs[1:]
    if last:
        gain_ref, in_ref, mean_ref, refs = *refs[:3], refs[3:]
    hidden_ref, refs = refs[0], refs[1:]
    if last:
        stat_ref, refs = refs[0], refs[1:]
    heads, sems = refs
    step = pl.program_id(0)
    depth = weights[0].shape[0]
    slots = own_ref.shape[0]

    @pl.when(step == 0)
    def _():
        for n in range(count):
            slot = pick_ref[n]
            place = heads.at[:, n * depth : (n + 1) * depth]

            @pl.when(slot < slots)
            def _():
                pltpu.make_async_copy(own_ref.at[slot], place, sems.at[n]).start()

            @pl.when(slot >= slots)
            def _():
                pltpu.make_async_copy(other_ref.at[slot - slots], place, sems.at[n]).start()

        for n in range(count):
            place = heads.at[:, n * depth : (n + 1) * depth]
            pltpu.make_async_copy(own_ref.at[0], place, sems.at[n]).wait()

    weight = jnp.concatenate([w[...] for w in weights], 0)
    total = jnp.dot(heads[...], weight, preferred_element_type=jnp.float32)
    if not first:
        total += partial_ref[...]
    hidden_ref[...] = total
    if last:
        wide = jnp.concatenate([in_ref[...], jnp.zeros_like(in_ref)], 1)
        wide_high = wide.astype(jnp.bfloat16)
        wide_low = wide - wide_high.astype(jnp.float32)
        in_a = (wide_high.astype(jnp.float32) + pltpu.roll(wide_low, RANK, 1)).astype(jnp.bfloat16)

        def coded(field):
            high = field.astype(jnp.bfloat16)
            low = (field - high.astype(jnp.float32)).astype(jnp.bfloat16)
            code = jnp.dot(high, in_a, preferred_element_type=jnp.float32)
            code += jnp.dot(low, wide_high, preferred_element_type=jnp.float32)
            return code + pltpu.roll(code, RANK, 1)

        code = coded(total * gain_ref[...])
        square = jnp.sum(total * total, axis=1, keepdims=True)
        lane = lax.broadcasted_iota(jnp.int32, code.shape, 1)
        stat = jnp.where(lane < RANK, code, square)
        tok = stat.shape[0]
        mean_code = coded(jnp.broadcast_to(mean_ref[...], (8, mean_ref.shape[1])))

        @pl.when(step == 0)
        def _():
            stat_ref[:tok, :] = stat
            stat_ref[tok:, :] = mean_code

        @pl.when(step > 0)
        def _():
            stat_ref[:tok, :] += stat
            stat_ref[tok:, :] += mean_code


def project(pick, own, other, weights, partial=None, last_terms=None):
    tok = own.shape[1]
    depth, width = weights[0].shape
    count = len(weights)
    first, last = partial is None, last_terms is not None
    columns = lambda rows: pl.BlockSpec((rows, TILE), lambda j, r: (0, j))
    anywhere = pl.BlockSpec(memory_space=pl.ANY)
    in_specs = [anywhere] * 2 + [columns(depth)] * count
    operands = [pick, own, other, *weights]
    out_specs = [columns(tok)]
    out_shape = [jax.ShapeDtypeStruct((tok, width), jnp.float32)]
    if not first:
        in_specs.append(columns(tok))
        operands.append(partial)
    if last:
        gain, erase_in, mean = last_terms
        in_specs += [columns(1), pl.BlockSpec((TILE, RANK), lambda j, r: (j, 0)), columns(1)]
        operands += [gain, erase_in, mean]
        out_specs.append(pl.BlockSpec((tok + 8, 2 * RANK), lambda j, r: (0, 0)))
        out_shape.append(jax.ShapeDtypeStruct((tok + 8, 2 * RANK), jnp.float32))
    return pl.pallas_call(
        functools.partial(project_kernel, count, first, last),
        grid_spec=pltpu.PrefetchScalarGridSpec(
            num_scalar_prefetch=1,
            grid=(width // TILE,),
            in_specs=in_specs,
            out_specs=out_specs,
            scratch_shapes=[
                pltpu.VMEM((tok, count * depth), jnp.bfloat16),
                pltpu.SemaphoreType.DMA((count,)),
            ],
        ),
        out_shape=out_shape,
        compiler_params=pltpu.CompilerParams(vmem_limit_bytes=VMEM_LIMIT),
        cost_estimate=pl.CostEstimate(
            flops=2 * tok * count * depth * width, bytes_accessed=2 * count * depth * width, transcendentals=0
        ),
    )(*operands)


def finish_kernel(model_width, own_ref, other_ref, own_mean, other_mean, gain_ref, out_w_ref, hidden_ref, erased_ref):
    stat = own_ref[...] + other_ref[...]
    mean_code = own_mean[0:1, :] + other_mean[0:1, :]
    inv_rms = lax.rsqrt(stat[:, RANK : RANK + 1] / model_width + norm_eps)
    lane = lax.broadcasted_iota(jnp.int32, stat.shape, 1)
    code = jnp.where(lane < RANK, stat * inv_rms - mean_code, 0.0)
    high = code.astype(jnp.bfloat16).astype(jnp.float32)
    low = code - high
    packed = jnp.concatenate([high + pltpu.roll(low, RANK, 1), high], 1).astype(jnp.bfloat16)
    for at in range(0, hidden_ref.shape[1], TILE):
        here = slice(at, at + TILE)
        removed = lax.dot_general(packed, out_w_ref[here, :], NT, preferred_element_type=jnp.float32)
        normed = hidden_ref[:, here] * inv_rms * gain_ref[:, here]
        erased_ref[:, here] = (normed - removed).astype(jnp.bfloat16)


def finish(model_width, stat, stat_other, gain, out_w, hidden):
    tok, width = hidden.shape
    rows = 128
    whole = lambda shape: pl.BlockSpec(shape, lambda i: (0, 0))
    stats = pl.BlockSpec((rows, 2 * RANK), lambda i: (i, 0))
    mean = pl.BlockSpec((8, 2 * RANK), lambda i: (tok // 8, 0))
    return pl.pallas_call(
        functools.partial(finish_kernel, model_width),
        grid=(tok // rows,),
        in_specs=[
            stats,
            stats,
            mean,
            mean,
            whole(gain.shape),
            whole(out_w.shape),
            pl.BlockSpec((rows, width), lambda i: (i, 0)),
        ],
        out_specs=pl.BlockSpec((rows, width), lambda i: (i, 0)),
        out_shape=jax.ShapeDtypeStruct((tok, width), jnp.bfloat16),
        compiler_params=pltpu.CompilerParams(vmem_limit_bytes=VMEM_LIMIT),
        cost_estimate=pl.CostEstimate(
            flops=2 * tok * 256 * width, bytes_accessed=6 * tok * width, transcendentals=0
        ),
    )(stat, stat_other, stat, stat_other, gain, out_w, hidden)


def swapped(block, axis):
    return lax.ppermute(block, axis, [(0, 1), (1, 0)])


def ring_order(size):
    return list(range(0, 1)) + list(range(1, size, 2)) + [i for i in range(size - 1, 0, -1) if i % 2 == 0]


def on_device(queries, keys, values, out_proj, post_gain, mean_vec, erase_in, erase_out):
    tok = queries.shape[0]
    outer, inner = lax.axis_size("far"), lax.axis_size("near")
    grp, far, near, col = (lax.axis_index(a) for a in ("grp", "far", "near", "col"))
    row = far * inner + near
    depth, model_width = out_proj.shape
    width = model_width // 2
    kv_local = keys.shape[1] // HD
    heads = queries.shape[1] // HD
    direct = depth == HD and outer * inner == heads

    mine = lax.dynamic_slice_in_dim(out_proj, col * width, width, 1)
    theirs = swapped(lax.dynamic_slice_in_dim(out_proj, (1 - col) * width, width, 1), "col")

    ahead = [(i, i + 1) for i in range(outer - 1)]
    blocks = []
    for own in (keys, values):
        second = lax.ppermute(own, "far", ahead)
        first = swapped(jnp.where(near == 0, own, second), "near")
        blocks.append((second, first, own))

    if direct:
        order = ring_order(outer)
        places = jnp.array(order, jnp.int32)
        position = jnp.argmax(places == far).astype(jnp.int32)
        hops = [(order[i], order[(i + 1) % outer]) for i in range(outer)]
        ring = lambda block: lax.ppermute(block, "far", hops)
        is_mine = grp == col
        main = [jnp.where(is_mine, mine, theirs)]
        across = [jnp.where(is_mine, theirs, mine)]
        beside = [swapped(main[0], "near")]
        corner = [swapped(beside[0], "grp")]
        for k in range(1, outer):
            main.append(ring(main[-1]))
            across.append(swapped(main[-1], "grp") if k % 2 else ring(across[-1]))
            beside.append(swapped(main[-1], "near"))
            corner.append(swapped(beside[-1], "grp"))
        here = jnp.where(is_mine, 0, heads)
        there = heads - here
        weights, pick = [], []
        for k in range(outer):
            far_k = places[lax.rem(position - k + outer, outer)]
            for piece, base, side in (
                (main[k], here, near),
                (beside[k], here, 1 - near),
                (across[k], there, near),
                (corner[k], there, 1 - near),
            ):
                weights.append(piece)
                pick.append(base + far_k * inner + side)
    else:
        weights = [lax.all_gather(w, ("far", "near"), axis=0, tiled=True) for w in (mine, theirs)]
        pick = [jnp.int32(0), jnp.int32(1)]
    pick = jnp.stack(pick).astype(jnp.int32)

    cos, sin = rope_tables((row - 2) * tok, 3 * tok)
    attended = attend(row[None], queries, blocks[0], blocks[1], cos, sin, direct)
    if not direct:
        attended = attended[None]
    att_other = swapped(attended, "col")

    out_high, out_low = split_high_low(erase_out)
    out_w = jnp.concatenate([out_high, out_high, out_low, jnp.zeros_like(out_low)], 1)
    gain = post_gain[None, :]

    half = len(weights) // 2
    (partial,) = project(pick[:half], attended, att_other, weights[:half])
    hidden, stat = project(
        pick[half:], attended, att_other, weights[half:], partial, (gain, erase_in, mean_vec[None, :])
    )
    return finish(model_width, stat, swapped(stat, "col"), gain, out_w, hidden)


def solution(mesh):
    grp, row, col = (mesh.shape[a] for a in ("grp", "row", "col"))
    fine = Mesh(mesh.devices.reshape(grp, row // 2, 2, col), ("grp", "far", "near", "col"))
    tokens = P(("grp", "far", "near"), "col")
    placed = (tokens, tokens, tokens, P(("col", "far", "near"), None), P("col"), P("col"), P("col", None), P("col", None))
    return jax.shard_map(on_device, mesh=fine, in_specs=placed, out_specs=tokens, check_vma=False)
```

time: 196 us -> 194 us (0.990)
  waiting for transfers between devices: 39.4 us -> 91.2 us
  blocking collectives: 45.5 us -> 0 us
  starting transfers between devices: 20 us -> 31.7 us
  other arithmetic: 20.9 us -> 10.6 us
  between operations: 13.7 us -> 5.04 us
  local copies, waits for them, and re-layouts: 17.4 us -> 8.83 us
  Pallas kernels: 37.3 us -> 45.5 us
    all_gather x2 -> x0, blocking collectives: 45.5 us -> none  [on_device(): lax.all_gather(share[:, at:at + count], 'far', axis=0, tiled=True)]
    ppermute x0 -> x4, waiting for transfers between devices: none -> 19.7 us  [on_device(): ring = lambda block: lax.ppermute(block, 'far', hops)]
    ppermute x15, waiting for transfers between devices: 39.3 us -> 56.1 us  [swapped(): return lax.ppermute(block, axis, [(0, 1), (1, 0)])]
    ppermute x2, waiting for transfers between devices: 0.01 us -> 15.4 us  [on_device(): second = lax.ppermute(own, 'far', ahead)]
    ppermute x0 -> x4, starting transfers between devices: none -> 8.45 us  [on_device(): ring = lambda block: lax.ppermute(block, 'far', hops)]
    pallas_call x4 -> x3, Pallas kernels: 25.5 us -> 32.5 us  [the longest x2 26 us: project(): pl.pallas_call(functools.partial(project_kernel, count, first, last), gri...]
    unnamed x49 -> x28, local copies, waits for them, and re-layouts: 9.17 us -> 3.91 us
    reduce_precision x2 -> x1, local copies, waits for them, and re-layouts: 5.28 us -> 0.43 us  [split_high_low(): high = lax.reduce_precision(value, 8, 7)]
  transfers between devices with their start and end apart: 18 -> 21, of which waited for: 4 -> 11; matrix products, arithmetic and copies ran while one was open for 16% -> 8% of each run, Pallas kernels for 16% -> 13%
where the time goes in v2:
time: 194 us; the launch traced here: 193 us
  waiting for transfers between devices  91.2 us (47%)
  Pallas kernels  45.5 us (23%)
  starting transfers between devices  31.7 us (16%)
  other arithmetic  10.6 us (5%)
  local copies, waits for them, and re-layouts  8.83 us (5%)
  between operations  5.04 us (3%)
    ppermute x15, waiting for transfers between devices, swapped(): return lax.ppermute(block, axis, [(0, 1), (1, 0)])  56.1 us
    pallas_call x2, Pallas kernels, project(): pl.pallas_call(functools.partial(project_kernel, count, first, last), gri...  26 us
    ppermute x4, waiting for transfers between devices, on_device(): ring = lambda block: lax.ppermute(block, 'far', hops)  19.7 us
    ppermute x2, waiting for transfers between devices, on_device(): second = lax.ppermute(own, 'far', ahead)  15.4 us
    ppermute x15, starting transfers between devices, swapped(): return lax.ppermute(block, axis, [(0, 1), (1, 0)])  14.8 us
    pallas_call x1, Pallas kernels, attend(): pl.pallas_call(functools.partial(attend_kernel, tok, group, direct), grid...  13.1 us
    ppermute x4, starting transfers between devices, on_device(): ring = lambda block: lax.ppermute(block, 'far', hops)  8.45 us
    ppermute x2, starting transfers between devices, on_device(): second = lax.ppermute(own, 'far', ahead)  8.44 us
  transfers between devices with their start and end apart: 21, of which 11 were waited for; matrix products, arithmetic and copies ran while one was open for 8% of the time, Pallas kernels for 13%

profile of v2, /device:TPU:0, one launch (start us, length us, event | category | flops | bytes accessed | tf_op | source)
XLA Modules:
  0.0 192.9 jit_solution(1969148945934829843)
XLA Ops:
  1.8 5.3 %collective-permute-start = (bf16[512,512]{1,0:T(8,128)(2,1)}, bf16[512,512]{1,0:T(8,128)(2,1)}, u32[]{:S(2)}, u32[]{:S(2)}) collective-permute-start(bf16[512,512]{1,0:T(8,128)(2,1)} %k2.1), channel_id=1, source_target_pairs={{0,4},{4,8},{8,12},{1,5},{5,9},{9,13},{2,6},{6,10},{10,14},{3,7},{... | collective-permute-start | bytes 1572872 | tf_op jit(solution)/shard_map/ppermute | solution.py:301
  9.0 3.1 %collective-permute-start.2 = (bf16[512,512]{1,0:T(8,128)(2,1)}, bf16[512,512]{1,0:T(8,128)(2,1)S(1)}, u32[]{:S(2)}, u32[]{:S(2)}) collective-permute-start(bf16[512,512]{1,0:T(8,128)(2,1)} %v2.1), channel_id=1, source_target_pairs={{0,4},{4,8},{8,12},{1,5},{5,9},{9,13},{2,6},{6,10},{10,14},{3,7},{... | collective-permute-start | bytes 1572872 | tf_op jit(solution)/shard_map/ppermute | solution.py:301
  12.2 6.7 %collective-permute-done.k0 = bf16[512,512]{1,0:T(8,128)(2,1)} collective-permute-done((bf16[512,512]{1,0:T(8,128)(2,1)}, bf16[512,512]{1,0:T(8,128)(2,1)}, u32[]{:S(2)}, u32[]{:S(2)}) %collective-permute-start) | collective-permute-done | bytes 524320 | tf_op jit(solution)/shard_map/ppermute | solution.py:301
  18.9 2.6 %collective-permute-start.1 = (bf16[512,512]{1,0:T(8,128)(2,1)S(1)}, bf16[512,512]{1,0:T(8,128)(2,1)S(1)}, u32[]{:S(2)}, u32[]{:S(2)}) collective-permute-start(bf16[512,512]{1,0:T(8,128)(2,1)S(1)} %broadcast_select_fusion.3), channel_id=1, source_target_pairs={{0,2},{2,0},{1,3},{3,1},{4,6},{6,4},{5,7},{7,5},{8,10},{10,8},{9,1... | collective-permute-start | bytes 1572872 | tf_op jit(solution)/shard_map/ppermute | solution.py:277
  21.5 12.0 %collective-permute-done.6.refs_4_ = bf16[128,2688]{1,0:T(8,128)(2,1)} collective-permute-done((bf16[128,2688]{1,0:T(8,128)(2,1)S(1)}, bf16[128,2688]{1,0:T(8,128)(2,1)}, u32[]{:S(2)}, u32[]{:S(2)}) %collective-permute-start.6) | collective-permute-done | bytes 688160 | tf_op jit(solution)/shard_map/ppermute | solution.py:310
  33.5 2.6 %collective-permute-start.7 = (bf16[128,2688]{1,0:T(8,128)(2,1)}, bf16[128,2688]{1,0:T(8,128)(2,1)}, u32[]{:S(2)}, u32[]{:S(2)}) collective-permute-start(bf16[128,2688]{1,0:T(8,128)(2,1)} %collective-permute-done.6.refs_4_), channel_id=1, source_target_pairs={{0,4},{4,12},{12,8},{8,0},{1,5},{5,13},{13,9},{9,1},{2,6},{6,14},{... | collective-permute-start | bytes 2064392 | tf_op jit(solution)/shard_map/ppermute | solution.py:310
  36.0 8.8 %collective-permute-done.2.v0 = bf16[512,512]{1,0:T(8,128)(2,1)S(1)} collective-permute-done((bf16[512,512]{1,0:T(8,128)(2,1)}, bf16[512,512]{1,0:T(8,128)(2,1)S(1)}, u32[]{:S(2)}, u32[]{:S(2)}) %collective-permute-start.2) | collective-permute-done | bytes 524320 | tf_op jit(solution)/shard_map/ppermute | solution.py:301
  46.4 2.8 %fusion = (f32[1536,64]{1,0:T(8,128)S(1)}, f32[1536,64]{1,0:T(8,128)S(1)}, f32[1536,64]{1,0:T(8,128)S(1)}) fusion(f32[64]{0:T(128)S(1)} %multiply_exponential_fusion, f32[1536]{0:T(1024)S(1)} %add_convert_fusion), kind=kLoop, calls=%fused_computation.10 | loop fusion | flops 196608 | bytes 1186048 | tf_op jit(solution)/shard_map/neg | solution.py:39
  49.3 1.8 collective-permute-start.16
  51.4 7.8 %collective-permute-done.7.refs_0_ = bf16[128,2688]{1,0:T(8,128)(2,1)} collective-permute-done((bf16[128,2688]{1,0:T(8,128)(2,1)}, bf16[128,2688]{1,0:T(8,128)(2,1)}, u32[]{:S(2)}, u32[]{:S(2)}) %collective-permute-start.7) | collective-permute-done | bytes 688160 | tf_op jit(solution)/shard_map/ppermute | solution.py:310
  59.1 2.5 %collective-permute-start.12 = (bf16[128,2688]{1,0:T(8,128)(2,1)}, bf16[128,2688]{1,0:T(8,128)(2,1)}, u32[]{:S(2)}, u32[]{:S(2)}) collective-permute-start(bf16[128,2688]{1,0:T(8,128)(2,1)} %collective-permute-done.7.refs_0_), channel_id=1, source_target_pairs={{0,4},{4,12},{12,8},{8,0},{1,5},{5,13},{13,9},{9,1},{2,6},{6,14},{... | collective-permute-start | bytes 2064392 | tf_op jit(solution)/shard_map/ppermute | solution.py:310
  64.2 13.1 %shard_map.91.own_ref = bf16[8,512,128]{2,1,0:T(8,128)(2,1)} custom-call(s32[1]{0:T(128)} %bitcast.10.row_ref, bf16[512,1024]{1,0:T(8,128)(2,1)} %q_ref.1, bf16[512,512]{1,0:T(8,128)(2,1)} %collective-permute-done.k0, bf16[512,512]{1,0:T(8,128)(2,1)} %copy-done.11, bf16[512,512]{1,0:T(8,128)(2,1)} %k2.1, bf16[512,512]{1,0:T(8,128)(2,1)} %copy-done.7, ...), custom_call_target="tpu_custom_call" | custom-call | flops 2684354560 | bytes 6291456 | tf_op jit(solution)/shard_map/pallas_call | solution.py:109
  79.4 9.5 %collective-permute-done.18.refs_5_ = bf16[128,2688]{1,0:T(8,128)(2,1)} collective-permute-done((bf16[128,2688]{1,0:T(8,128)(2,1)}, bf16[128,2688]{1,0:T(8,128)(2,1)}, u32[]{:S(2)}, u32[]{:S(2)}) %collective-permute-start.18) | collective-permute-done | bytes 688160 | tf_op jit(solution)/shard_map/ppermute | solution.py:277
  103.9 6.8 %collective-permute-done.17.refs_3_ = bf16[128,2688]{1,0:T(8,128)(2,1)} collective-permute-done((bf16[128,2688]{1,0:T(8,128)(2,1)}, bf16[128,2688]{1,0:T(8,128)(2,1)}, u32[]{:S(2)}, u32[]{:S(2)}) %collective-permute-start.17) | collective-permute-done | bytes 688160 | tf_op jit(solution)/shard_map/ppermute | solution.py:277
  110.7 2.6 %collective-permute-start.10 = (bf16[128,2688]{1,0:T(8,128)(2,1)}, bf16[128,2688]{1,0:T(8,128)(2,1)}, u32[]{:S(2)}, u32[]{:S(2)}) collective-permute-start(bf16[128,2688]{1,0:T(8,128)(2,1)} %collective-permute-done.9.refs_6_), channel_id=1, source_target_pairs={{0,4},{4,12},{12,8},{8,0},{1,5},{5,13},{13,9},{9,1},{2,6},{6,14},{... | collective-permute-start | bytes 2064392 | tf_op jit(solution)/shard_map/ppermute | solution.py:310
  115.3 4.4 %collective-permute-done.13.refs_5_ = bf16[128,2688]{1,0:T(8,128)(2,1)} collective-permute-done((bf16[128,2688]{1,0:T(8,128)(2,1)}, bf16[128,2688]{1,0:T(8,128)(2,1)}, u32[]{:S(2)}, u32[]{:S(2)}) %collective-permute-start.13) | collective-permute-done | bytes 688160 | tf_op jit(solution)/shard_map/ppermute | solution.py:277
  122.2 3.2 %collective-permute-done.19.refs_7_ = bf16[128,2688]{1,0:T(8,128)(2,1)} collective-permute-done((bf16[128,2688]{1,0:T(8,128)(2,1)}, bf16[128,2688]{1,0:T(8,128)(2,1)}, u32[]{:S(2)}, u32[]{:S(2)}) %collective-permute-start.19) | collective-permute-done | bytes 688160 | tf_op jit(solution)/shard_map/ppermute | solution.py:277
  125.4 11.5 %shard_map.92.refs_8_ = f32[512,2688]{1,0:T(8,128)} custom-call(s32[8]{0:T(128)} %stack.70.pick_ref, bf16[8,512,128]{2,1,0:T(8,128)(2,1)} %shard_map.91.own_ref, bf16[8,512,128]{2,1,0:T(8,128)(2,1)} %collective-permute-done.4.other_ref, bf16[128,2688]{1,0:T(8,128)(2,1)} %copy-done.1, bf16[128,2688]{1,0:T(8,128)(2,1)} %collective-permute-done.16.refs_1_, ...), custom_call_target="tpu_custom_call" | custom-call | flops 2818572288 | bytes 5505024 | tf_op jit(solution)/shard_map/pallas_call | solution.py:213
  136.9 3.2 %collective-permute-done.14.refs_6_ = bf16[128,2688]{1,0:T(8,128)(2,1)} collective-permute-done((bf16[128,2688]{1,0:T(8,128)(2,1)}, bf16[128,2688]{1,0:T(8,128)(2,1)}, u32[]{:S(2)}, u32[]{:S(2)}) %collective-permute-start.14) | collective-permute-done | bytes 688160 | tf_op jit(solution)/shard_map/ppermute | solution.py:277
  140.1 14.7 %collective-permute-done.11.refs_3_ = bf16[128,2688]{1,0:T(8,128)(2,1)} collective-permute-done((bf16[128,2688]{1,0:T(8,128)(2,1)}, bf16[128,2688]{1,0:T(8,128)(2,1)}, u32[]{:S(2)}, u32[]{:S(2)}) %collective-permute-start.11) | collective-permute-done | bytes 688160 | tf_op jit(solution)/shard_map/ppermute | solution.py:277
  154.9 14.3 %collective-permute-done.15.refs_7_ = bf16[128,2688]{1,0:T(8,128)(2,1)} collective-permute-done((bf16[128,2688]{1,0:T(8,128)(2,1)}, bf16[128,2688]{1,0:T(8,128)(2,1)}, u32[]{:S(2)}, u32[]{:S(2)}) %collective-permute-start.15) | collective-permute-done | bytes 688160 | tf_op jit(solution)/shard_map/ppermute | solution.py:277
  169.2 14.5 %shard_map.93 = (f32[512,2688]{1,0:T(8,128)}, f32[520,128]{1,0:T(8,128)}) custom-call(s32[8]{0:T(128)} %stack.61.pick_ref, bf16[8,512,128]{2,1,0:T(8,128)(2,1)} %shard_map.91.own_ref, bf16[8,512,128]{2,1,0:T(8,128)(2,1)} %collective-permute-done.4.other_ref, bf16[128,2688]{1,0:T(8,128)(2,1)} %collective-permute-done.7.refs_0_, ...), custom_call_target="tpu_custom_call" | custom-call | flops 2818572288 | bytes 5505024 | tf_op jit(solution)/shard_map/pallas_call | solution.py:213
  183.8 2.0 %maximum_maximum_fusion.out_w_ref = bf16[2688,256]{1,0:T(8,128)(2,1)} fusion(bf16[2688,64]{1,0:T(8,128)(2,1)S(1)} %copy-done.2, bf16[2688,64]{1,0:T(8,128)(2,1)S(1)} %get-tuple-element.13, bf16[256]{0:T(256)(128)(2,1)S(1)} %pad.3.clone), kind=kLoop, calls=%fused_computation | loop fusion | flops 5505024 | bytes 2064896 | tf_op jit(solution)/shard_map/concatenate | solution.py:346
  186.4 6.5 %shard_map.94 = bf16[512,2688]{1,0:T(8,128)(2,1)} custom-call(f32[520,128]{1,0:T(8,128)} %get-tuple-element.9.own_ref.own_mean, f32[520,128]{1,0:T(8,128)} %copy-done.4, f32[520,128]{1,0:T(8,128)} %get-tuple-element.9.own_ref.own_mean, f32[520,128]{1,0:T(8,128)} %copy-done.4, f32[1,2688]{1,0:T(1,128)} %broadcast_in_dim.15.refs_9_.gain_ref, ...), custom_call_target="tpu_custom_call" | custom-call | flops 704643072 | bytes 8257536 | tf_op jit(solution)/shard_map/pallas_call | solution.py:255
  (70 shorter events, 25.8 us)
Async XLA Ops:
  1.3 5.9 %collective-permute-start.5 = (bf16[128,2688]{1,0:T(8,128)(2,1)S(1)}, bf16[128,2688]{1,0:T(8,128)(2,1)S(1)}, u32[]{:S(2)}, u32[]{:S(2)}) collective-permute-start(bf16[128,2688]{1,0:T(8,128)(2,1)S(1)} %constant_dynamic-slice_fusion), channel_id=1, source_target_pairs={{0,1},{1,0},{2,3},{3,2},{4,5},{5,4},{6,7},{7,6},{8,9},{9,8},{10,11... | collective-permute-start | bytes 2064392 | tf_op jit(solution)/shard_map/ppermute | solution.py:277
  1.8 17.0 %collective-permute-start = (bf16[512,512]{1,0:T(8,128)(2,1)}, bf16[512,512]{1,0:T(8,128)(2,1)}, u32[]{:S(2)}, u32[]{:S(2)}) collective-permute-start(bf16[512,512]{1,0:T(8,128)(2,1)} %k2.1), channel_id=1, source_target_pairs={{0,4},{4,8},{8,12},{1,5},{5,9},{9,13},{2,6},{6,10},{10,14},{3,7},{... | collective-permute-start | bytes 1572872 | tf_op jit(solution)/shard_map/ppermute | solution.py:301
  8.2 41.1 %copy-start.1 = (bf16[128,2688]{1,0:T(8,128)(2,1)}, bf16[128,2688]{1,0:T(8,128)(2,1)S(1)}, u32[]{:S(2)}) copy-start(bf16[128,2688]{1,0:T(8,128)(2,1)S(1)} %get-tuple-element.12.refs_0_) | copy-start | bytes 2064388
  8.2 25.2 %collective-permute-start.6 = (bf16[128,2688]{1,0:T(8,128)(2,1)S(1)}, bf16[128,2688]{1,0:T(8,128)(2,1)}, u32[]{:S(2)}, u32[]{:S(2)}) collective-permute-start(bf16[128,2688]{1,0:T(8,128)(2,1)S(1)} %get-tuple-element.12.refs_0_), channel_id=1, source_target_pairs={{0,4},{4,12},{12,8},{8,0},{1,5},{5,13},{13,9},{9,1},{2,6},{6,14},{... | collective-permute-start | bytes 2064392 | tf_op jit(solution)/shard_map/ppermute | solution.py:310
  9.0 35.8 %collective-permute-start.2 = (bf16[512,512]{1,0:T(8,128)(2,1)}, bf16[512,512]{1,0:T(8,128)(2,1)S(1)}, u32[]{:S(2)}, u32[]{:S(2)}) collective-permute-start(bf16[512,512]{1,0:T(8,128)(2,1)} %v2.1), channel_id=1, source_target_pairs={{0,4},{4,8},{8,12},{1,5},{5,9},{9,13},{2,6},{6,10},{10,14},{3,7},{... | collective-permute-start | bytes 1572872 | tf_op jit(solution)/shard_map/ppermute | solution.py:301
  18.9 44.4 %collective-permute-start.1 = (bf16[512,512]{1,0:T(8,128)(2,1)S(1)}, bf16[512,512]{1,0:T(8,128)(2,1)S(1)}, u32[]{:S(2)}, u32[]{:S(2)}) collective-permute-start(bf16[512,512]{1,0:T(8,128)(2,1)S(1)} %broadcast_select_fusion.3), channel_id=1, source_target_pairs={{0,2},{2,0},{1,3},{3,1},{4,6},{6,4},{5,7},{7,5},{8,10},{10,8},{9,1... | collective-permute-start | bytes 1572872 | tf_op jit(solution)/shard_map/ppermute | solution.py:277
  33.5 25.7 %collective-permute-start.7 = (bf16[128,2688]{1,0:T(8,128)(2,1)}, bf16[128,2688]{1,0:T(8,128)(2,1)}, u32[]{:S(2)}, u32[]{:S(2)}) collective-permute-start(bf16[128,2688]{1,0:T(8,128)(2,1)} %collective-permute-done.6.refs_4_), channel_id=1, source_target_pairs={{0,4},{4,12},{12,8},{8,0},{1,5},{5,13},{13,9},{9,1},{2,6},{6,14},{... | collective-permute-start | bytes 2064392 | tf_op jit(solution)/shard_map/ppermute | solution.py:310
  46.1 17.2 %collective-permute-start.3 = (bf16[512,512]{1,0:T(8,128)(2,1)S(1)}, bf16[512,512]{1,0:T(8,128)(2,1)S(1)}, u32[]{:S(2)}, u32[]{:S(2)}) collective-permute-start(bf16[512,512]{1,0:T(8,128)(2,1)S(1)} %broadcast_select_fusion.2), channel_id=1, source_target_pairs={{0,2},{2,0},{1,3},{3,1},{4,6},{6,4},{5,7},{7,5},{8,10},{10,8},{9,1... | collective-permute-start | bytes 1572872 | tf_op jit(solution)/shard_map/ppermute | solution.py:277
  49.3 29.6 %collective-permute-start.16 = (bf16[128,2688]{1,0:T(8,128)(2,1)S(1)}, bf16[128,2688]{1,0:T(8,128)(2,1)}, u32[]{:S(2)}, u32[]{:S(2)}) collective-permute-start(bf16[128,2688]{1,0:T(8,128)(2,1)S(1)} %get-tuple-element.12.refs_0_), channel_id=1, source_target_pairs={{0,2},{2,0},{1,3},{3,1},{4,6},{6,4},{5,7},{7,5},{8,10},{10,8},{9,1... | collective-permute-start | bytes 2064392 | tf_op jit(solution)/shard_map/ppermute | solution.py:277
  51.1 37.8 %collective-permute-start.18 = (bf16[128,2688]{1,0:T(8,128)(2,1)}, bf16[128,2688]{1,0:T(8,128)(2,1)}, u32[]{:S(2)}, u32[]{:S(2)}) collective-permute-start(bf16[128,2688]{1,0:T(8,128)(2,1)} %collective-permute-done.6.refs_4_), channel_id=1, source_target_pairs={{0,2},{2,0},{1,3},{3,1},{4,6},{6,4},{5,7},{7,5},{8,10},{10,8},{9,1... | collective-permute-start | bytes 2064392 | tf_op jit(solution)/shard_map/ppermute | solution.py:277
  59.1 30.0 %collective-permute-start.12 = (bf16[128,2688]{1,0:T(8,128)(2,1)}, bf16[128,2688]{1,0:T(8,128)(2,1)}, u32[]{:S(2)}, u32[]{:S(2)}) collective-permute-start(bf16[128,2688]{1,0:T(8,128)(2,1)} %collective-permute-done.7.refs_0_), channel_id=1, source_target_pairs={{0,4},{4,12},{12,8},{8,0},{1,5},{5,13},{13,9},{9,1},{2,6},{6,14},{... | collective-permute-start | bytes 2064392 | tf_op jit(solution)/shard_map/ppermute | solution.py:310
  64.2 32.9 %copy-start = (f32[2688,64]{0,1:T(8,128)S(1)}, f32[2688,64]{0,1:T(8,128)}, u32[]{:S(2)}) copy-start(f32[2688,64]{0,1:T(8,128)} %param.16) | copy-start | bytes 2064388
  77.3 36.0 %collective-permute-start.4 = (bf16[8,512,128]{2,1,0:T(8,128)(2,1)}, bf16[8,512,128]{2,1,0:T(8,128)(2,1)}, u32[]{:S(2)}, u32[]{:S(2)}) collective-permute-start(bf16[8,512,128]{2,1,0:T(8,128)(2,1)} %shard_map.91.own_ref), channel_id=1, source_target_pairs={{0,1},{1,0},{2,3},{3,2},{4,5},{5,4},{6,7},{7,6},{8,9},{9,8},{10,11... | collective-permute-start | bytes 3145736 | tf_op jit(solution)/shard_map/ppermute | solution.py:277
  77.3 25.1 %collective-permute-start.9 = (bf16[128,2688]{1,0:T(8,128)(2,1)}, bf16[128,2688]{1,0:T(8,128)(2,1)}, u32[]{:S(2)}, u32[]{:S(2)}) collective-permute-start(bf16[128,2688]{1,0:T(8,128)(2,1)} %collective-permute-done.6.refs_4_), channel_id=1, source_target_pairs={{0,16},{16,0},{1,17},{17,1},{2,18},{18,2},{3,19},{19,3},{4,20},{20... | collective-permute-start | bytes 2064392 | tf_op jit(solution)/shard_map/ppermute | solution.py:277
  78.8 31.8 %collective-permute-start.17 = (bf16[128,2688]{1,0:T(8,128)(2,1)}, bf16[128,2688]{1,0:T(8,128)(2,1)}, u32[]{:S(2)}, u32[]{:S(2)}) collective-permute-start(bf16[128,2688]{1,0:T(8,128)(2,1)} %collective-permute-done.16.refs_1_), channel_id=1, source_target_pairs={{0,16},{16,0},{1,17},{17,1},{2,18},{18,2},{3,19},{19,3},{4,20},{20... | collective-permute-start | bytes 2064392 | tf_op jit(solution)/shard_map/ppermute | solution.py:277
  88.9 25.9 %collective-permute-start.8 = (bf16[128,2688]{1,0:T(8,128)(2,1)}, bf16[128,2688]{1,0:T(8,128)(2,1)}, u32[]{:S(2)}, u32[]{:S(2)}) collective-permute-start(bf16[128,2688]{1,0:T(8,128)(2,1)} %collective-permute-done.7.refs_0_), channel_id=1, source_target_pairs={{0,2},{2,0},{1,3},{3,1},{4,6},{6,4},{5,7},{7,5},{8,10},{10,8},{9,1... | collective-permute-start | bytes 2064392 | tf_op jit(solution)/shard_map/ppermute | solution.py:277
  89.2 30.5 %collective-permute-start.13 = (bf16[128,2688]{1,0:T(8,128)(2,1)}, bf16[128,2688]{1,0:T(8,128)(2,1)}, u32[]{:S(2)}, u32[]{:S(2)}) collective-permute-start(bf16[128,2688]{1,0:T(8,128)(2,1)} %collective-permute-done.12.refs_4_), channel_id=1, source_target_pairs={{0,2},{2,0},{1,3},{3,1},{4,6},{6,4},{5,7},{7,5},{8,10},{10,8},{9,1... | collective-permute-start | bytes 2064392 | tf_op jit(solution)/shard_map/ppermute | solution.py:277
  102.4 23.0 %collective-permute-start.19 = (bf16[128,2688]{1,0:T(8,128)(2,1)}, bf16[128,2688]{1,0:T(8,128)(2,1)}, u32[]{:S(2)}, u32[]{:S(2)}) collective-permute-start(bf16[128,2688]{1,0:T(8,128)(2,1)} %collective-permute-done.18.refs_5_), channel_id=1, source_target_pairs={{0,16},{16,0},{1,17},{17,1},{2,18},{18,2},{3,19},{19,3},{4,20},{20... | collective-permute-start | bytes 2064392 | tf_op jit(solution)/shard_map/ppermute | solution.py:277
  110.7 26.3 %collective-permute-start.10 = (bf16[128,2688]{1,0:T(8,128)(2,1)}, bf16[128,2688]{1,0:T(8,128)(2,1)}, u32[]{:S(2)}, u32[]{:S(2)}) collective-permute-start(bf16[128,2688]{1,0:T(8,128)(2,1)} %collective-permute-done.9.refs_6_), channel_id=1, source_target_pairs={{0,4},{4,12},{12,8},{8,0},{1,5},{5,13},{13,9},{9,1},{2,6},{6,14},{... | collective-permute-start | bytes 2064392 | tf_op jit(solution)/shard_map/ppermute | solution.py:310
  113.3 26.9 %collective-permute-start.14 = (bf16[128,2688]{1,0:T(8,128)(2,1)}, bf16[128,2688]{1,0:T(8,128)(2,1)}, u32[]{:S(2)}, u32[]{:S(2)}) collective-permute-start(bf16[128,2688]{1,0:T(8,128)(2,1)} %collective-permute-done.12.refs_4_), channel_id=1, source_target_pairs={{0,16},{16,0},{1,17},{17,1},{2,18},{18,2},{3,19},{19,3},{4,20},{20... | collective-permute-start | bytes 2064392 | tf_op jit(solution)/shard_map/ppermute | solution.py:277
  114.7 40.2 %collective-permute-start.11 = (bf16[128,2688]{1,0:T(8,128)(2,1)}, bf16[128,2688]{1,0:T(8,128)(2,1)}, u32[]{:S(2)}, u32[]{:S(2)}) collective-permute-start(bf16[128,2688]{1,0:T(8,128)(2,1)} %collective-permute-done.8.refs_1_), channel_id=1, source_target_pairs={{0,16},{16,0},{1,17},{17,1},{2,18},{18,2},{3,19},{19,3},{4,20},{20... | collective-permute-start | bytes 2064392 | tf_op jit(solution)/shard_map/ppermute | solution.py:277
  119.7 49.5 %collective-permute-start.15 = (bf16[128,2688]{1,0:T(8,128)(2,1)}, bf16[128,2688]{1,0:T(8,128)(2,1)}, u32[]{:S(2)}, u32[]{:S(2)}) collective-permute-start(bf16[128,2688]{1,0:T(8,128)(2,1)} %collective-permute-done.13.refs_5_), channel_id=1, source_target_pairs={{0,16},{16,0},{1,17},{17,1},{2,18},{18,2},{3,19},{19,3},{4,20},{20... | collective-permute-start | bytes 2064392 | tf_op jit(solution)/shard_map/ppermute | solution.py:277
  136.9 46.8 %copy-start.2 = (bf16[2688,64]{1,0:T(8,128)(2,1)S(1)}, bf16[2688,64]{1,0:T(8,128)(2,1)}, u32[]{:S(2)}) copy-start(bf16[2688,64]{1,0:T(8,128)(2,1)} %get-tuple-element.14) | copy-start | bytes 1032196
  183.7 2.1 %collective-permute-start.20 = (f32[520,128]{1,0:T(8,128)}, f32[520,128]{1,0:T(8,128)S(1)}, u32[]{:S(2)}, u32[]{:S(2)}) collective-permute-start(f32[520,128]{1,0:T(8,128)} %get-tuple-element.9.own_ref.own_mean), channel_id=1, source_target_pairs={{0,1},{1,0},{2,3},{3,2},{4,5},{5,4},{6,7},{7,6},{8,9},{9,8},{10,11... | collective-permute-start | bytes 798728 | tf_op jit(solution)/shard_map/ppermute | solution.py:277
  (10 other events, 56.6 us)

commit v3 on v2

--- a/solution.py
+++ b/solution.py
@@ -296,11 +296,14 @@
     theirs = swapped(lax.dynamic_slice_in_dim(out_proj, (1 - col) * width, width, 1), "col")
 
     ahead = [(i, i + 1) for i in range(outer - 1)]
-    blocks = []
-    for own in (keys, values):
-        second = lax.ppermute(own, "far", ahead)
-        first = swapped(jnp.where(near == 0, own, second), "near")
-        blocks.append((second, first, own))
+    from_behind = lambda block: lax.ppermute(block, "far", ahead)
+    hold = lax.optimization_barrier
+    cos, sin = rope_tables((row - 2) * tok, 3 * tok)
+    out_high, out_low = split_high_low(erase_out)
+    out_w = jnp.concatenate([out_high, out_high, out_low, jnp.zeros_like(out_low)], 1)
+
+    def for_next(second):
+        return [swapped(jnp.where(near == 0, own, old), "near") for own, old in zip((keys, values), second)]
 
     if direct:
         order = ring_order(outer)
@@ -308,19 +311,32 @@
         position = jnp.argmax(places == far).astype(jnp.int32)
         hops = [(order[i], order[(i + 1) % outer]) for i in range(outer)]
         ring = lambda block: lax.ppermute(block, "far", hops)
+        beyond = lambda block: swapped(block, "near")
+        facing = lambda block: swapped(block, "grp")
         is_mine = grp == col
-        main = [jnp.where(is_mine, mine, theirs)]
-        across = [jnp.where(is_mine, theirs, mine)]
-        beside = [swapped(main[0], "near")]
-        corner = [swapped(beside[0], "grp")]
-        for k in range(1, outer):
-            main.append(ring(main[-1]))
-            across.append(swapped(main[-1], "grp") if k % 2 else ring(across[-1]))
-            beside.append(swapped(main[-1], "near"))
-            corner.append(swapped(beside[-1], "grp"))
+        main, beside, across, corner = ([None] * outer for _ in range(4))
+        main[0] = jnp.where(is_mine, mine, theirs)
+        across[0] = jnp.where(is_mine, theirs, mine)
+        main[1], beside[0] = ring(main[0]), beyond(main[0])
+        main[1], beside[0], keys, values, cos, sin, out_w = hold((main[1], beside[0], keys, values, cos, sin, out_w))
+        second = [from_behind(keys), from_behind(values)]
+        beside[1], across[1] = beyond(main[1]), facing(main[1])
+        second, beside[1], across[1], main[1] = hold((second, beside[1], across[1], main[1]))
+        first = for_next(second)
+        main[2], corner[1] = ring(main[1]), facing(beside[1])
+        first, main[2], corner[1] = hold((first, main[2], corner[1]))
+        main[3], beside[2], across[2] = ring(main[2]), beyond(main[2]), facing(main[2])
+        attended = attend(row[None], queries, (second[0], first[0], keys), (second[1], first[1], values), cos, sin, True)
+        main[3], beside[2], across[2], attended = hold((main[3], beside[2], across[2], attended))
+        across[3], beside[3], corner[2] = ring(across[2]), beyond(main[3]), facing(beside[2])
+        att_other = swapped(attended, "col")
+        across[3], beside[3], corner[2], att_other, across[0] = hold(
+            (across[3], beside[3], corner[2], att_other, across[0])
+        )
+        corner[0], corner[3] = beyond(across[0]), facing(beside[3])
         here = jnp.where(is_mine, 0, heads)
         there = heads - here
-        weights, pick = [], []
+        weights, pick, late, late_pick = [], [], [], []
         for k in range(outer):
             far_k = places[lax.rem(position - k + outer, outer)]
             for piece, base, side in (
@@ -329,27 +345,22 @@
                 (across[k], there, near),
                 (corner[k], there, 1 - near),
             ):
-                weights.append(piece)
-                pick.append(base + far_k * inner + side)
+                is_late = piece is corner[0] or piece is corner[3]
+                (late if is_late else weights).append(piece)
+                (late_pick if is_late else pick).append(base + far_k * inner + side)
     else:
-        weights = [lax.all_gather(w, ("far", "near"), axis=0, tiled=True) for w in (mine, theirs)]
-        pick = [jnp.int32(0), jnp.int32(1)]
-    pick = jnp.stack(pick).astype(jnp.int32)
-
-    cos, sin = rope_tables((row - 2) * tok, 3 * tok)
-    attended = attend(row[None], queries, blocks[0], blocks[1], cos, sin, direct)
-    if not direct:
+        second = [from_behind(keys), from_behind(values)]
+        first = for_next(second)
+        attended = attend(row[None], queries, (second[0], first[0], keys), (second[1], first[1], values), cos, sin, False)
         attended = attended[None]
-    att_other = swapped(attended, "col")
-
-    out_high, out_low = split_high_low(erase_out)
-    out_w = jnp.concatenate([out_high, out_high, out_low, jnp.zeros_like(out_low)], 1)
+        att_other = swapped(attended, "col")
+        weights, late = ([lax.all_gather(w, ("far", "near"), axis=0, tiled=True)] for w in (mine, theirs))
+        pick, late_pick = [jnp.int32(0)], [jnp.int32(1)]
+
     gain = post_gain[None, :]
-
-    half = len(weights) // 2
-    (partial,) = project(pick[:half], attended, att_other, weights[:half])
+    (partial,) = project(jnp.stack(pick).astype(jnp.int32), attended, att_other, weights)
     hidden, stat = project(
-        pick[half:], attended, att_other, weights[half:], partial, (gain, erase_in, mean_vec[None, :])
+        jnp.stack(late_pick).astype(jnp.int32), attended, att_other, late, partial, (gain, erase_in, mean_vec[None, :])
     )
     return finish(model_width, stat, swapped(stat, "col"), gain, out_w, hidden)
 

time: 194 us -> 174 us (0.90)
  waiting for transfers between devices: 91.2 us -> 69.6 us
  other arithmetic: 10.6 us -> 12.6 us
    ppermute x15, waiting for transfers between devices: 56.1 us -> 21.8 us  [swapped(): return lax.ppermute(block, axis, [(0, 1), (1, 0)])]
    ppermute x4, waiting for transfers between devices: 19.7 us -> 28.4 us  [on_device(): ring = lambda block: lax.ppermute(block, 'far', hops)]
    ppermute x2, waiting for transfers between devices: 15.4 us -> 19.4 us  [on_device(): from_behind = lambda block: lax.ppermute(block, 'far', ahead)]
    ppermute x2, starting transfers between devices: 8.44 us -> 6.44 us  [on_device(): from_behind = lambda block: lax.ppermute(block, 'far', ahead)]
    unnamed x28 -> x50, local copies, waits for them, and re-layouts: 3.91 us -> 4.91 us
  transfers between devices with their start and end apart: 21 -> 21, of which waited for: 11 -> 10; matrix products, arithmetic and copies ran while one was open for 8% -> 9% of each run, Pallas kernels for 13% -> 16%
where the time goes in v3:
time: 174 us; the launch traced here: 173 us
  waiting for transfers between devices  69.6 us (40%)
  Pallas kernels  45.2 us (26%)
  starting transfers between devices  30 us (17%)
  other arithmetic  12.6 us (7%)
  local copies, waits for them, and re-layouts  9.95 us (6%)
  between operations  5.25 us (3%)
    ppermute x4, waiting for transfers between devices, on_device(): ring = lambda block: lax.ppermute(block, 'far', hops)  28.4 us
    pallas_call x2, Pallas kernels, project(): pl.pallas_call(functools.partial(project_kernel, count, first, last), gri...  25.7 us
    ppermute x15, waiting for transfers between devices, swapped(): return lax.ppermute(block, axis, [(0, 1), (1, 0)])  21.8 us
    ppermute x2, waiting for transfers between devices, on_device(): from_behind = lambda block: lax.ppermute(block, 'far', ahead)  19.4 us
    ppermute x15, starting transfers between devices, swapped(): return lax.ppermute(block, axis, [(0, 1), (1, 0)])  14.1 us
    pallas_call x1, Pallas kernels, attend(): pl.pallas_call(functools.partial(attend_kernel, tok, group, direct), grid...  13 us
    ppermute x4, starting transfers between devices, on_device(): ring = lambda block: lax.ppermute(block, 'far', hops)  9.53 us
    pallas_call x1, Pallas kernels, finish(): pl.pallas_call(functools.partial(finish_kernel, model_width), grid=(tok /...  6.46 us
  transfers between devices with their start and end apart: 21, of which 10 were waited for; matrix products, arithmetic and copies ran while one was open for 9% of the time, Pallas kernels for 16%

profile of v3, /device:TPU:0, one launch (start us, length us, event | category | flops | bytes accessed | tf_op | source)
XLA Modules:
  0.0 172.6 jit_solution(14883849543403317103)
XLA Ops:
  0.0 2.1 %constant_dynamic-slice_fusion = bf16[128,2688]{1,0:T(8,128)(2,1)} fusion(bf16[128,5376]{1,0:T(8,128)(2,1)} %param.12, s32[]{:T(128)S(6)} %select_n.56), kind=kLoop, calls=%fused_computation.15 | loop fusion | bytes 1376260 | tf_op jit(solution)/shard_map/dynamic_slice | solution.py:296
  3.5 4.3 %fusion = (f32[1536,64]{1,0:T(8,128)S(1)}, f32[1536,64]{1,0:T(8,128)}, f32[1536,64]{1,0:T(8,128)}) fusion(f32[64]{0:T(128)S(1)} %multiply_exponential_fusion, f32[1536]{0:T(1024)S(1)} %add_convert_fusion), kind=kLoop, calls=%fused_computation.10 | loop fusion | flops 196608 | bytes 1186048 | tf_op jit(solution)/shard_map/neg | solution.py:39
  7.9 3.3 %pad_maximum_fusion = (f32[1536,128]{1,0:T(8,128)}, f32[1536,128]{1,0:T(8,128)}) fusion(f32[1536,64]{1,0:T(8,128)} %get-tuple-element.67, f32[1536,64]{1,0:T(8,128)} %get-tuple-element.66, f32[1536,64]{1,0:T(8,128)S(1)} %get-tuple-element.65), kind=kLoop, calls=%fused_computation.4 | loop fusion | flops 393216 | bytes 2752512 | tf_op jit(solution)/shard_map/concatenate | solution.py:39
  13.9 2.6 %collective-permute-start.1 = (bf16[128,2688]{1,0:T(8,128)(2,1)S(1)}, bf16[128,2688]{1,0:T(8,128)(2,1)S(1)}, u32[]{:S(2)}, u32[]{:S(2)}) collective-permute-start(bf16[128,2688]{1,0:T(8,128)(2,1)S(1)} %get-tuple-element.62.refs_0_), channel_id=1, source_target_pairs={{0,4},{4,12},{12,8},{8,0},{1,5},{5,13},{13,9},{9,1},{2,6},{6,14},{... | collective-permute-start | bytes 2064392 | tf_op jit(solution)/shard_map/ppermute | solution.py:313
  16.5 1.5 collective-permute-start.2
  18.0 2.0 %maximum_maximum_fusion.out_w_ref = bf16[2688,256]{1,0:T(8,128)(2,1)} fusion(bf16[2688,64]{1,0:T(8,128)(2,1)S(1)} %get-tuple-element.64, bf16[2688,64]{1,0:T(8,128)(2,1)S(1)} %get-tuple-element.63, bf16[256]{0:T(256)(128)(2,1)S(1)} %pad.3.clone), kind=kLoop, calls=%fused_computation | loop fusion | flops 5505024 | bytes 2064896 | tf_op jit(solution)/shard_map/concatenate | solution.py:303
  20.0 13.6 %collective-permute-done.1.refs_3_ = bf16[128,2688]{1,0:T(8,128)(2,1)S(1)} collective-permute-done((bf16[128,2688]{1,0:T(8,128)(2,1)S(1)}, bf16[128,2688]{1,0:T(8,128)(2,1)S(1)}, u32[]{:S(2)}, u32[]{:S(2)}) %collective-permute-start.1) | collective-permute-done | bytes 688160 | tf_op jit(solution)/shard_map/ppermute | solution.py:313
  34.0 1.5 collective-permute-start.5
  37.1 4.5 %collective-permute-start.3 = (bf16[512,512]{1,0:T(8,128)(2,1)S(1)}, bf16[512,512]{1,0:T(8,128)(2,1)S(1)}, u32[]{:S(2)}, u32[]{:S(2)}) collective-permute-start(bf16[512,512]{1,0:T(8,128)(2,1)S(1)} %copy-done.8), channel_id=1, source_target_pairs={{0,4},{4,8},{8,12},{1,5},{5,9},{9,13},{2,6},{6,10},{10,14},{3,7},{... | collective-permute-start | bytes 1572872 | tf_op jit(solution)/shard_map/ppermute | solution.py:299
  41.6 1.9 %collective-permute-start.4 = (bf16[512,512]{1,0:T(8,128)(2,1)S(1)}, bf16[512,512]{1,0:T(8,128)(2,1)S(1)}, u32[]{:S(2)}, u32[]{:S(2)}) collective-permute-start(bf16[512,512]{1,0:T(8,128)(2,1)S(1)} %copy-done.9), channel_id=1, source_target_pairs={{0,4},{4,8},{8,12},{1,5},{5,9},{9,13},{2,6},{6,10},{10,14},{3,7},{... | collective-permute-start | bytes 1572872 | tf_op jit(solution)/shard_map/ppermute | solution.py:299
  43.5 10.4 %collective-permute-done.3.k0 = bf16[512,512]{1,0:T(8,128)(2,1)S(1)} collective-permute-done((bf16[512,512]{1,0:T(8,128)(2,1)S(1)}, bf16[512,512]{1,0:T(8,128)(2,1)S(1)}, u32[]{:S(2)}, u32[]{:S(2)}) %collective-permute-start.3) | collective-permute-done | bytes 524320 | tf_op jit(solution)/shard_map/ppermute | solution.py:299
  53.9 9.0 %collective-permute-done.4.v0 = bf16[512,512]{1,0:T(8,128)(2,1)S(1)} collective-permute-done((bf16[512,512]{1,0:T(8,128)(2,1)S(1)}, bf16[512,512]{1,0:T(8,128)(2,1)S(1)}, u32[]{:S(2)}, u32[]{:S(2)}) %collective-permute-start.4) | collective-permute-done | bytes 524320 | tf_op jit(solution)/shard_map/ppermute | solution.py:299
  64.6 2.5 %collective-permute-start.9 = (bf16[128,2688]{1,0:T(8,128)(2,1)S(1)}, bf16[128,2688]{1,0:T(8,128)(2,1)}, u32[]{:S(2)}, u32[]{:S(2)}) collective-permute-start(bf16[128,2688]{1,0:T(8,128)(2,1)S(1)} %copy-done.16), channel_id=1, source_target_pairs={{0,4},{4,12},{12,8},{8,0},{1,5},{5,13},{13,9},{9,1},{2,6},{6,14},{... | collective-permute-start | bytes 2064392 | tf_op jit(solution)/shard_map/ppermute | solution.py:313
  68.3 9.7 %collective-permute-done.8.v1 = bf16[512,512]{1,0:T(8,128)(2,1)S(1)} collective-permute-done((bf16[512,512]{1,0:T(8,128)(2,1)S(1)}, bf16[512,512]{1,0:T(8,128)(2,1)S(1)}, u32[]{:S(2)}, u32[]{:S(2)}) %collective-permute-start.8) | collective-permute-done | bytes 524320 | tf_op jit(solution)/shard_map/ppermute | solution.py:277
  78.0 8.1 %collective-permute-done.7.k1 = bf16[512,512]{1,0:T(8,128)(2,1)S(1)} collective-permute-done((bf16[512,512]{1,0:T(8,128)(2,1)S(1)}, bf16[512,512]{1,0:T(8,128)(2,1)S(1)}, u32[]{:S(2)}, u32[]{:S(2)}) %collective-permute-start.7) | collective-permute-done | bytes 524320 | tf_op jit(solution)/shard_map/ppermute | solution.py:277
  86.1 2.5 %collective-permute-start.11 = (bf16[128,2688]{1,0:T(8,128)(2,1)}, bf16[128,2688]{1,0:T(8,128)(2,1)S(1)}, u32[]{:S(2)}, u32[]{:S(2)}) collective-permute-start(bf16[128,2688]{1,0:T(8,128)(2,1)} %collective-permute-done.9.refs_7_), channel_id=1, source_target_pairs={{0,4},{4,12},{12,8},{8,0},{1,5},{5,13},{13,9},{9,1},{2,6},{6,14},{... | collective-permute-start | bytes 2064392 | tf_op jit(solution)/shard_map/ppermute | solution.py:313
  90.5 13.0 %shard_map.91.own_ref = bf16[8,512,128]{2,1,0:T(8,128)(2,1)} custom-call(s32[1]{0:T(128)} %bitcast.4.row_ref, bf16[512,1024]{1,0:T(8,128)(2,1)} %q_ref.1, bf16[512,512]{1,0:T(8,128)(2,1)} %copy-done.10, bf16[512,512]{1,0:T(8,128)(2,1)} %copy-done.23, bf16[512,512]{1,0:T(8,128)(2,1)} %k2, bf16[512,512]{1,0:T(8,128)(2,1)} %copy-done.11, ...), custom_call_target="tpu_custom_call" | custom-call | flops 2684354560 | bytes 6291456 | tf_op jit(solution)/shard_map/pallas_call | solution.py:109
  103.7 1.9 %collective-permute-start.14 = (bf16[128,2688]{1,0:T(8,128)(2,1)}, bf16[128,2688]{1,0:T(8,128)(2,1)S(1)}, u32[]{:S(2)}, u32[]{:S(2)}) collective-permute-start(bf16[128,2688]{1,0:T(8,128)(2,1)} %collective-permute-done.13.refs_9_), channel_id=1, source_target_pairs={{0,4},{4,12},{12,8},{8,0},{1,5},{5,13},{13,9},{9,1},{2,6},{6,14},{... | collective-permute-start | bytes 2064392 | tf_op jit(solution)/shard_map/ppermute | solution.py:313
  107.8 14.8 %collective-permute-done.14.refs_13_ = bf16[128,2688]{1,0:T(8,128)(2,1)S(1)} collective-permute-done((bf16[128,2688]{1,0:T(8,128)(2,1)}, bf16[128,2688]{1,0:T(8,128)(2,1)S(1)}, u32[]{:S(2)}, u32[]{:S(2)}) %collective-permute-start.14) | collective-permute-done | bytes 688160 | tf_op jit(solution)/shard_map/ppermute | solution.py:313
  133.7 1.5 copy.16.refs_4_
  137.0 14.1 %shard_map.92.refs_2_ = f32[512,2688]{1,0:T(8,128)} custom-call(s32[14]{0:T(128)} %stack.71.pick_ref, bf16[8,512,128]{2,1,0:T(8,128)(2,1)} %shard_map.91.own_ref, bf16[8,512,128]{2,1,0:T(8,128)(2,1)} %copy-done.3, bf16[128,2688]{1,0:T(8,128)(2,1)} %copy-done.6, bf16[128,2688]{1,0:T(8,128)(2,1)} %copy-done.17, bf16[128,2688]{1,0:T(8,128)(2,1)} %copy-done.5, ...), custom_call_target="tpu_custom_call" | custom-call | flops 4932501504 | bytes 9633792 | tf_op jit(solution)/shard_map/pallas_call | solution.py:213
  152.0 11.6 %shard_map.93 = (f32[512,2688]{1,0:T(8,128)}, f32[520,128]{1,0:T(8,128)}) custom-call(s32[2]{0:T(128)} %pad_add_fusion.pick_ref, bf16[8,512,128]{2,1,0:T(8,128)(2,1)} %shard_map.91.own_ref, bf16[8,512,128]{2,1,0:T(8,128)(2,1)} %copy-done.3, bf16[128,2688]{1,0:T(8,128)(2,1)} %copy-done.7, bf16[128,2688]{1,0:T(8,128)(2,1)} %collective-permute-done.19.refs_1_, ...), custom_call_target="tpu_custom_call" | custom-call | flops 704643072 | bytes 1376256 | tf_op jit(solution)/shard_map/pallas_call | solution.py:213
  163.7 1.7 %collective-permute-done.20.other_ref.other_mean = f32[520,128]{1,0:T(8,128)S(1)} collective-permute-done((f32[520,128]{1,0:T(8,128)}, f32[520,128]{1,0:T(8,128)S(1)}, u32[]{:S(2)}, u32[]{:S(2)}) %collective-permute-start.20) | collective-permute-done | bytes 266272 | tf_op jit(solution)/shard_map/ppermute | solution.py:277
  166.1 6.5 %shard_map.94 = bf16[512,2688]{1,0:T(8,128)(2,1)} custom-call(f32[520,128]{1,0:T(8,128)} %get-tuple-element.58.own_ref.own_mean, f32[520,128]{1,0:T(8,128)} %copy-done.2, f32[520,128]{1,0:T(8,128)} %get-tuple-element.58.own_ref.own_mean, f32[520,128]{1,0:T(8,128)} %copy-done.2, f32[1,2688]{1,0:T(1,128)} %broadcast_in_dim.16.refs_3_.gain_ref, ...), custom_call_target="tpu_custom_call" | custom-call | flops 704643072 | bytes 8257536 | tf_op jit(solution)/shard_map/pallas_call | solution.py:255
  (92 shorter events, 22.6 us)
Async XLA Ops:
  2.1 9.3 %collective-permute-start = (bf16[128,2688]{1,0:T(8,128)(2,1)}, bf16[128,2688]{1,0:T(8,128)(2,1)}, u32[]{:S(2)}, u32[]{:S(2)}) collective-permute-start(bf16[128,2688]{1,0:T(8,128)(2,1)} %constant_dynamic-slice_fusion), channel_id=1, source_target_pairs={{0,1},{1,0},{2,3},{3,2},{4,5},{5,4},{6,7},{7,6},{8,9},{9,8},{10,11... | collective-permute-start | bytes 2064392 | tf_op jit(solution)/shard_map/ppermute | solution.py:277
  13.8 110.6 %copy-start.5 = (bf16[128,2688]{1,0:T(8,128)(2,1)}, bf16[128,2688]{1,0:T(8,128)(2,1)S(1)}, u32[]{:S(2)}) copy-start(bf16[128,2688]{1,0:T(8,128)(2,1)S(1)} %get-tuple-element.51.refs_2_) | copy-start | bytes 2064388
  13.9 19.7 %collective-permute-start.1 = (bf16[128,2688]{1,0:T(8,128)(2,1)S(1)}, bf16[128,2688]{1,0:T(8,128)(2,1)S(1)}, u32[]{:S(2)}, u32[]{:S(2)}) collective-permute-start(bf16[128,2688]{1,0:T(8,128)(2,1)S(1)} %get-tuple-element.62.refs_0_), channel_id=1, source_target_pairs={{0,4},{4,12},{12,8},{8,0},{1,5},{5,13},{13,9},{9,1},{2,6},{6,14},{... | collective-permute-start | bytes 2064392 | tf_op jit(solution)/shard_map/ppermute | solution.py:313
  16.5 17.5 %collective-permute-start.2 = (bf16[128,2688]{1,0:T(8,128)(2,1)S(1)}, bf16[128,2688]{1,0:T(8,128)(2,1)S(1)}, u32[]{:S(2)}, u32[]{:S(2)}) collective-permute-start(bf16[128,2688]{1,0:T(8,128)(2,1)S(1)} %get-tuple-element.62.refs_0_), channel_id=1, source_target_pairs={{0,2},{2,0},{1,3},{3,1},{4,6},{6,4},{5,7},{7,5},{8,10},{10,8},{9,1... | collective-permute-start | bytes 2064392 | tf_op jit(solution)/shard_map/ppermute | solution.py:277
  34.0 28.9 %collective-permute-start.5 = (bf16[128,2688]{1,0:T(8,128)(2,1)S(1)}, bf16[128,2688]{1,0:T(8,128)(2,1)}, u32[]{:S(2)}, u32[]{:S(2)}) collective-permute-start(bf16[128,2688]{1,0:T(8,128)(2,1)S(1)} %collective-permute-done.1.refs_3_), channel_id=1, source_target_pairs={{0,2},{2,0},{1,3},{3,1},{4,6},{6,4},{5,7},{7,5},{8,10},{10,8},{9,1... | collective-permute-start | bytes 2064392 | tf_op jit(solution)/shard_map/ppermute | solution.py:277
  35.6 27.4 %collective-permute-start.6 = (bf16[128,2688]{1,0:T(8,128)(2,1)S(1)}, bf16[128,2688]{1,0:T(8,128)(2,1)}, u32[]{:S(2)}, u32[]{:S(2)}) collective-permute-start(bf16[128,2688]{1,0:T(8,128)(2,1)S(1)} %collective-permute-done.1.refs_3_), channel_id=1, source_target_pairs={{0,16},{16,0},{1,17},{17,1},{2,18},{18,2},{3,19},{19,3},{4,20},{20... | collective-permute-start | bytes 2064392 | tf_op jit(solution)/shard_map/ppermute | solution.py:277
  37.1 16.9 %collective-permute-start.3 = (bf16[512,512]{1,0:T(8,128)(2,1)S(1)}, bf16[512,512]{1,0:T(8,128)(2,1)S(1)}, u32[]{:S(2)}, u32[]{:S(2)}) collective-permute-start(bf16[512,512]{1,0:T(8,128)(2,1)S(1)} %copy-done.8), channel_id=1, source_target_pairs={{0,4},{4,8},{8,12},{1,5},{5,9},{9,13},{2,6},{6,10},{10,14},{3,7},{... | collective-permute-start | bytes 1572872 | tf_op jit(solution)/shard_map/ppermute | solution.py:299
  41.6 21.3 %collective-permute-start.4 = (bf16[512,512]{1,0:T(8,128)(2,1)S(1)}, bf16[512,512]{1,0:T(8,128)(2,1)S(1)}, u32[]{:S(2)}, u32[]{:S(2)}) collective-permute-start(bf16[512,512]{1,0:T(8,128)(2,1)S(1)} %copy-done.9), channel_id=1, source_target_pairs={{0,4},{4,8},{8,12},{1,5},{5,9},{9,13},{2,6},{6,10},{10,14},{3,7},{... | collective-permute-start | bytes 1572872 | tf_op jit(solution)/shard_map/ppermute | solution.py:299
  63.0 14.9 %collective-permute-start.8 = (bf16[512,512]{1,0:T(8,128)(2,1)S(1)}, bf16[512,512]{1,0:T(8,128)(2,1)S(1)}, u32[]{:S(2)}, u32[]{:S(2)}) collective-permute-start(bf16[512,512]{1,0:T(8,128)(2,1)S(1)} %broadcast_select_fusion.2), channel_id=1, source_target_pairs={{0,2},{2,0},{1,3},{3,1},{4,6},{6,4},{5,7},{7,5},{8,10},{10,8},{9,1... | collective-permute-start | bytes 1572872 | tf_op jit(solution)/shard_map/ppermute | solution.py:277
  63.6 22.5 %collective-permute-start.10 = (bf16[128,2688]{1,0:T(8,128)(2,1)}, bf16[128,2688]{1,0:T(8,128)(2,1)S(1)}, u32[]{:S(2)}, u32[]{:S(2)}) collective-permute-start(bf16[128,2688]{1,0:T(8,128)(2,1)} %collective-permute-done.5.refs_4_), channel_id=1, source_target_pairs={{0,16},{16,0},{1,17},{17,1},{2,18},{18,2},{3,19},{19,3},{4,20},{20... | collective-permute-start | bytes 2064392 | tf_op jit(solution)/shard_map/ppermute | solution.py:277
  64.6 21.5 %collective-permute-start.9 = (bf16[128,2688]{1,0:T(8,128)(2,1)S(1)}, bf16[128,2688]{1,0:T(8,128)(2,1)}, u32[]{:S(2)}, u32[]{:S(2)}) collective-permute-start(bf16[128,2688]{1,0:T(8,128)(2,1)S(1)} %copy-done.16), channel_id=1, source_target_pairs={{0,4},{4,12},{12,8},{8,0},{1,5},{5,13},{13,9},{9,1},{2,6},{6,14},{... | collective-permute-start | bytes 2064392 | tf_op jit(solution)/shard_map/ppermute | solution.py:313
  67.1 18.9 %collective-permute-start.7 = (bf16[512,512]{1,0:T(8,128)(2,1)S(1)}, bf16[512,512]{1,0:T(8,128)(2,1)S(1)}, u32[]{:S(2)}, u32[]{:S(2)}) collective-permute-start(bf16[512,512]{1,0:T(8,128)(2,1)S(1)} %broadcast_select_fusion.3), channel_id=1, source_target_pairs={{0,2},{2,0},{1,3},{3,1},{4,6},{6,4},{5,7},{7,5},{8,10},{10,8},{9,1... | collective-permute-start | bytes 1572872 | tf_op jit(solution)/shard_map/ppermute | solution.py:277
  86.1 17.5 %collective-permute-start.11 = (bf16[128,2688]{1,0:T(8,128)(2,1)}, bf16[128,2688]{1,0:T(8,128)(2,1)S(1)}, u32[]{:S(2)}, u32[]{:S(2)}) collective-permute-start(bf16[128,2688]{1,0:T(8,128)(2,1)} %collective-permute-done.9.refs_7_), channel_id=1, source_target_pairs={{0,4},{4,12},{12,8},{8,0},{1,5},{5,13},{13,9},{9,1},{2,6},{6,14},{... | collective-permute-start | bytes 2064392 | tf_op jit(solution)/shard_map/ppermute | solution.py:313
  88.6 15.0 %collective-permute-start.12 = (bf16[128,2688]{1,0:T(8,128)(2,1)}, bf16[128,2688]{1,0:T(8,128)(2,1)}, u32[]{:S(2)}, u32[]{:S(2)}) collective-permute-start(bf16[128,2688]{1,0:T(8,128)(2,1)} %collective-permute-done.9.refs_7_), channel_id=1, source_target_pairs={{0,2},{2,0},{1,3},{3,1},{4,6},{6,4},{5,7},{7,5},{8,10},{10,8},{9,1... | collective-permute-start | bytes 2064392 | tf_op jit(solution)/shard_map/ppermute | solution.py:277
  89.1 14.5 %collective-permute-start.13 = (bf16[128,2688]{1,0:T(8,128)(2,1)}, bf16[128,2688]{1,0:T(8,128)(2,1)}, u32[]{:S(2)}, u32[]{:S(2)}) collective-permute-start(bf16[128,2688]{1,0:T(8,128)(2,1)} %collective-permute-done.9.refs_7_), channel_id=1, source_target_pairs={{0,16},{16,0},{1,17},{17,1},{2,18},{18,2},{3,19},{19,3},{4,20},{20... | collective-permute-start | bytes 2064392 | tf_op jit(solution)/shard_map/ppermute | solution.py:277
  90.5 42.5 %copy-start.13 = (f32[2688]{0:T(1024)S(1)}, f32[2688]{0:T(1024)}, u32[]{:S(2)}) copy-start(f32[2688]{0:T(1024)} %param.13) | copy-start | bytes 32260
  90.5 43.1 %copy-start.4 = (f32[2688,64]{0,1:T(8,128)S(1)}, f32[2688,64]{0,1:T(8,128)}, u32[]{:S(2)}) copy-start(f32[2688,64]{0,1:T(8,128)} %param.15) | copy-start | bytes 2064388
  103.6 20.8 %collective-permute-start.17 = (bf16[8,512,128]{2,1,0:T(8,128)(2,1)}, bf16[8,512,128]{2,1,0:T(8,128)(2,1)S(1)}, u32[]{:S(2)}, u32[]{:S(2)}) collective-permute-start(bf16[8,512,128]{2,1,0:T(8,128)(2,1)} %shard_map.91.own_ref), channel_id=1, source_target_pairs={{0,1},{1,0},{2,3},{3,2},{4,5},{5,4},{6,7},{7,6},{8,9},{9,8},{10,11... | collective-permute-start | bytes 3145736 | tf_op jit(solution)/shard_map/ppermute | solution.py:277
  103.7 18.9 %collective-permute-start.14 = (bf16[128,2688]{1,0:T(8,128)(2,1)}, bf16[128,2688]{1,0:T(8,128)(2,1)S(1)}, u32[]{:S(2)}, u32[]{:S(2)}) collective-permute-start(bf16[128,2688]{1,0:T(8,128)(2,1)} %collective-permute-done.13.refs_9_), channel_id=1, source_target_pairs={{0,4},{4,12},{12,8},{8,0},{1,5},{5,13},{13,9},{9,1},{2,6},{6,14},{... | collective-permute-start | bytes 2064392 | tf_op jit(solution)/shard_map/ppermute | solution.py:313
  105.6 17.6 %collective-permute-start.15 = (bf16[128,2688]{1,0:T(8,128)(2,1)S(1)}, bf16[128,2688]{1,0:T(8,128)(2,1)}, u32[]{:S(2)}, u32[]{:S(2)}) collective-permute-start(bf16[128,2688]{1,0:T(8,128)(2,1)S(1)} %collective-permute-done.11.refs_11_), channel_id=1, source_target_pairs={{0,2},{2,0},{1,3},{3,1},{4,6},{6,4},{5,7},{7,5},{8,10},{10,8},{9,1... | collective-permute-start | bytes 2064392 | tf_op jit(solution)/shard_map/ppermute | solution.py:277
  106.9 17.5 %collective-permute-start.16 = (bf16[128,2688]{1,0:T(8,128)(2,1)}, bf16[128,2688]{1,0:T(8,128)(2,1)S(1)}, u32[]{:S(2)}, u32[]{:S(2)}) collective-permute-start(bf16[128,2688]{1,0:T(8,128)(2,1)} %collective-permute-done.12.refs_8_), channel_id=1, source_target_pairs={{0,16},{16,0},{1,17},{17,1},{2,18},{18,2},{3,19},{19,3},{4,20},{20... | collective-permute-start | bytes 2064392 | tf_op jit(solution)/shard_map/ppermute | solution.py:277
  124.5 26.6 %collective-permute-start.18 = (bf16[128,2688]{1,0:T(8,128)(2,1)S(1)}, bf16[128,2688]{1,0:T(8,128)(2,1)S(1)}, u32[]{:S(2)}, u32[]{:S(2)}) collective-permute-start(bf16[128,2688]{1,0:T(8,128)(2,1)S(1)} %get-tuple-element.51.refs_2_), channel_id=1, source_target_pairs={{0,2},{2,0},{1,3},{3,1},{4,6},{6,4},{5,7},{7,5},{8,10},{10,8},{9,1... | collective-permute-start | bytes 2064392 | tf_op jit(solution)/shard_map/ppermute | solution.py:277
  125.3 25.8 %collective-permute-start.19 = (bf16[128,2688]{1,0:T(8,128)(2,1)}, bf16[128,2688]{1,0:T(8,128)(2,1)}, u32[]{:S(2)}, u32[]{:S(2)}) collective-permute-start(bf16[128,2688]{1,0:T(8,128)(2,1)} %collective-permute-done.15.refs_12_), channel_id=1, source_target_pairs={{0,16},{16,0},{1,17},{17,1},{2,18},{18,2},{3,19},{19,3},{4,20},{20... | collective-permute-start | bytes 2064392 | tf_op jit(solution)/shard_map/ppermute | solution.py:277
  163.6 1.8 %collective-permute-start.20 = (f32[520,128]{1,0:T(8,128)}, f32[520,128]{1,0:T(8,128)S(1)}, u32[]{:S(2)}, u32[]{:S(2)}) collective-permute-start(f32[520,128]{1,0:T(8,128)} %get-tuple-element.58.own_ref.own_mean), channel_id=1, source_target_pairs={{0,1},{1,0},{2,3},{3,2},{4,5},{5,4},{6,7},{7,6},{8,9},{9,8},{10,11... | collective-permute-start | bytes 798728 | tf_op jit(solution)/shard_map/ppermute | solution.py:277
  (21 other events, 231.6 us)

commit v4 on v3

--- a/solution.py
+++ b/solution.py
@@ -17,8 +17,8 @@
 rope_base = 10000.0
 log2_e = 1.4426950408889634
 
-TILE = 384
-VMEM_LIMIT = 60 * 2**20
+TILE = 896
+VMEM_LIMIT = 32 * 2**20
 
 NT = (((1,), (1,)), ((), ()))
 
@@ -122,7 +122,26 @@
     )(row, queries, *key_blocks, *val_blocks, cos, sin)
 
 
-def project_kernel(count, first, last, pick_ref, own_ref, other_ref, *refs):
+def ring_place(position, size):
+    return jnp.where(position <= size // 2, jnp.maximum(2 * position - 1, 0), 2 * (size - position))
+
+
+def ring_position(place, size):
+    return jnp.where(place % 2 == 1, (place + 1) // 2, (size - place // 2) % size)
+
+
+def slot_of(kind, step, where_ref, slots):
+    if kind is None:
+        return step * slots
+    is_mine, far, near, outer = where_ref[0], where_ref[1], where_ref[2], where_ref[3]
+    from_far = ring_place((ring_position(far, outer) - step + outer) % outer, outer)
+    side = near if kind in ("main", "across") else 1 - near
+    other = 1 - is_mine if kind in ("main", "beside") else is_mine
+    return other * slots + from_far * 2 + side
+
+
+def project_kernel(kinds, first, last, where_ref, own_ref, other_ref, *refs):
+    count = len(kinds)
     weights, refs = refs[:count], refs[count:]
     if not first:
         partial_ref, refs = refs[0], refs[1:]
@@ -138,8 +157,8 @@
 
     @pl.when(step == 0)
     def _():
-        for n in range(count):
-            slot = pick_ref[n]
+        for n, (kind, k) in enumerate(kinds):
+            slot = slot_of(kind, k, where_ref, slots)
             place = heads.at[:, n * depth : (n + 1) * depth]
 
             @pl.when(slot < slots)
@@ -166,10 +185,7 @@
         in_a = (wide_high.astype(jnp.float32) + pltpu.roll(wide_low, RANK, 1)).astype(jnp.bfloat16)
 
         def coded(field):
-            high = field.astype(jnp.bfloat16)
-            low = (field - high.astype(jnp.float32)).astype(jnp.bfloat16)
-            code = jnp.dot(high, in_a, preferred_element_type=jnp.float32)
-            code += jnp.dot(low, wide_high, preferred_element_type=jnp.float32)
+            code = jnp.dot(field.astype(jnp.bfloat16), in_a, preferred_element_type=jnp.float32)
             return code + pltpu.roll(code, RANK, 1)
 
         code = coded(total * gain_ref[...])
@@ -177,7 +193,9 @@
         lane = lax.broadcasted_iota(jnp.int32, code.shape, 1)
         stat = jnp.where(lane < RANK, code, square)
         tok = stat.shape[0]
-        mean_code = coded(jnp.broadcast_to(mean_ref[...], (8, mean_ref.shape[1])))
+        mean = jnp.broadcast_to(mean_ref[...], (8, mean_ref.shape[1]))
+        mean_high = mean.astype(jnp.bfloat16).astype(jnp.float32)
+        mean_code = coded(mean_high) + coded(mean - mean_high)
 
         @pl.when(step == 0)
         def _():
@@ -190,7 +208,7 @@
             stat_ref[tok:, :] += mean_code
 
 
-def project(pick, own, other, weights, partial=None, last_terms=None):
+def project(where, kinds, own, other, weights, partial=None, last_terms=None):
     tok = own.shape[1]
     depth, width = weights[0].shape
     count = len(weights)
@@ -198,7 +216,7 @@
     columns = lambda rows: pl.BlockSpec((rows, TILE), lambda j, r: (0, j))
     anywhere = pl.BlockSpec(memory_space=pl.ANY)
     in_specs = [anywhere] * 2 + [columns(depth)] * count
-    operands = [pick, own, other, *weights]
+    operands = [where, own, other, *weights]
     out_specs = [columns(tok)]
     out_shape = [jax.ShapeDtypeStruct((tok, width), jnp.float32)]
     if not first:
@@ -211,7 +229,7 @@
         out_specs.append(pl.BlockSpec((tok + 8, 2 * RANK), lambda j, r: (0, 0)))
         out_shape.append(jax.ShapeDtypeStruct((tok + 8, 2 * RANK), jnp.float32))
     return pl.pallas_call(
-        functools.partial(project_kernel, count, first, last),
+        functools.partial(project_kernel, kinds, first, last),
         grid_spec=pltpu.PrefetchScalarGridSpec(
             num_scalar_prefetch=1,
             grid=(width // TILE,),
@@ -230,47 +248,47 @@
     )(*operands)
 
 
-def finish_kernel(model_width, own_ref, other_ref, own_mean, other_mean, gain_ref, out_w_ref, hidden_ref, erased_ref):
-    stat = own_ref[...] + other_ref[...]
-    mean_code = own_mean[0:1, :] + other_mean[0:1, :]
-    inv_rms = lax.rsqrt(stat[:, RANK : RANK + 1] / model_width + norm_eps)
-    lane = lax.broadcasted_iota(jnp.int32, stat.shape, 1)
-    code = jnp.where(lane < RANK, stat * inv_rms - mean_code, 0.0)
-    high = code.astype(jnp.bfloat16).astype(jnp.float32)
-    low = code - high
-    packed = jnp.concatenate([high + pltpu.roll(low, RANK, 1), high], 1).astype(jnp.bfloat16)
-    for at in range(0, hidden_ref.shape[1], TILE):
-        here = slice(at, at + TILE)
-        removed = lax.dot_general(packed, out_w_ref[here, :], NT, preferred_element_type=jnp.float32)
-        normed = hidden_ref[:, here] * inv_rms * gain_ref[:, here]
-        erased_ref[:, here] = (normed - removed).astype(jnp.bfloat16)
+def finish_kernel(model_width, own_ref, other_ref, gain_ref, out_w_ref, hidden_ref, erased_ref, packed_ref, inv_ref):
+    tok = hidden_ref.shape[0]
+
+    @pl.when(pl.program_id(0) == 0)
+    def _():
+        stat = own_ref[:tok, :] + other_ref[:tok, :]
+        mean_code = own_ref[tok : tok + 1, :] + other_ref[tok : tok + 1, :]
+        inv_rms = lax.rsqrt(stat[:, RANK : RANK + 1] / model_width + norm_eps)
+        lane = lax.broadcasted_iota(jnp.int32, stat.shape, 1)
+        code = jnp.where(lane < RANK, stat * inv_rms - mean_code, 0.0)
+        high = code.astype(jnp.bfloat16).astype(jnp.float32)
+        low = code - high
+        packed_ref[...] = jnp.concatenate([high + pltpu.roll(low, RANK, 1), high], 1).astype(jnp.bfloat16)
+        inv_ref[...] = jnp.broadcast_to(inv_rms, inv_ref.shape)
+
+    removed = lax.dot_general(packed_ref[...], out_w_ref[...], NT, preferred_element_type=jnp.float32)
+    normed = hidden_ref[...] * inv_ref[:, :1] * gain_ref[...]
+    erased_ref[...] = (normed - removed).astype(jnp.bfloat16)
 
 
 def finish(model_width, stat, stat_other, gain, out_w, hidden):
     tok, width = hidden.shape
-    rows = 128
-    whole = lambda shape: pl.BlockSpec(shape, lambda i: (0, 0))
-    stats = pl.BlockSpec((rows, 2 * RANK), lambda i: (i, 0))
-    mean = pl.BlockSpec((8, 2 * RANK), lambda i: (tok // 8, 0))
+    whole = pl.BlockSpec(stat.shape, lambda j: (0, 0))
     return pl.pallas_call(
         functools.partial(finish_kernel, model_width),
-        grid=(tok // rows,),
+        grid=(width // TILE,),
         in_specs=[
-            stats,
-            stats,
-            mean,
-            mean,
-            whole(gain.shape),
-            whole(out_w.shape),
-            pl.BlockSpec((rows, width), lambda i: (i, 0)),
+            whole,
+            whole,
+            pl.BlockSpec((1, TILE), lambda j: (0, j)),
+            pl.BlockSpec((TILE, 4 * RANK), lambda j: (j, 0)),
+            pl.BlockSpec((tok, TILE), lambda j: (0, j)),
         ],
-        out_specs=pl.BlockSpec((rows, width), lambda i: (i, 0)),
+        out_specs=pl.BlockSpec((tok, TILE), lambda j: (0, j)),
         out_shape=jax.ShapeDtypeStruct((tok, width), jnp.bfloat16),
+        scratch_shapes=[pltpu.VMEM((tok, 4 * RANK), jnp.bfloat16), pltpu.VMEM((tok, 2 * RANK), jnp.float32)],
         compiler_params=pltpu.CompilerParams(vmem_limit_bytes=VMEM_LIMIT),
         cost_estimate=pl.CostEstimate(
             flops=2 * tok * 256 * width, bytes_accessed=6 * tok * width, transcendentals=0
         ),
-    )(stat, stat_other, stat, stat_other, gain, out_w, hidden)
+    )(stat, stat_other, gain, out_w, hidden)
 
 
 def swapped(block, axis):
@@ -290,78 +308,65 @@
     width = model_width // 2
     kv_local = keys.shape[1] // HD
     heads = queries.shape[1] // HD
-    direct = depth == HD and outer * inner == heads
-
-    mine = lax.dynamic_slice_in_dim(out_proj, col * width, width, 1)
-    theirs = swapped(lax.dynamic_slice_in_dim(out_proj, (1 - col) * width, width, 1), "col")
+    direct = depth == HD and outer * inner == heads and outer == 4
 
     ahead = [(i, i + 1) for i in range(outer - 1)]
     from_behind = lambda block: lax.ppermute(block, "far", ahead)
     hold = lax.optimization_barrier
+
+    def for_next(second):
+        return [swapped(jnp.where(near == 0, own, old), "near") for own, old in zip((keys, values), second)]
+
+    second = [from_behind(keys), from_behind(values)]
+    theirs = swapped(lax.dynamic_slice_in_dim(out_proj, (1 - col) * width, width, 1), "col")
+    mine = lax.dynamic_slice_in_dim(out_proj, col * width, width, 1)
     cos, sin = rope_tables((row - 2) * tok, 3 * tok)
     out_high, out_low = split_high_low(erase_out)
     out_w = jnp.concatenate([out_high, out_high, out_low, jnp.zeros_like(out_low)], 1)
-
-    def for_next(second):
-        return [swapped(jnp.where(near == 0, own, old), "near") for own, old in zip((keys, values), second)]
+    gain, mean = post_gain[None, :], mean_vec[None, :]
+    is_mine = grp == col
+    where = jnp.stack([is_mine.astype(jnp.int32), far, near, jnp.int32(outer)])
 
     if direct:
         order = ring_order(outer)
-        places = jnp.array(order, jnp.int32)
-        position = jnp.argmax(places == far).astype(jnp.int32)
         hops = [(order[i], order[(i + 1) % outer]) for i in range(outer)]
         ring = lambda block: lax.ppermute(block, "far", hops)
         beyond = lambda block: swapped(block, "near")
         facing = lambda block: swapped(block, "grp")
-        is_mine = grp == col
-        main, beside, across, corner = ([None] * outer for _ in range(4))
+        main, beside, across, corner = ({} for _ in range(4))
         main[0] = jnp.where(is_mine, mine, theirs)
         across[0] = jnp.where(is_mine, theirs, mine)
-        main[1], beside[0] = ring(main[0]), beyond(main[0])
-        main[1], beside[0], keys, values, cos, sin, out_w = hold((main[1], beside[0], keys, values, cos, sin, out_w))
-        second = [from_behind(keys), from_behind(values)]
-        beside[1], across[1] = beyond(main[1]), facing(main[1])
-        second, beside[1], across[1], main[1] = hold((second, beside[1], across[1], main[1]))
-        first = for_next(second)
-        main[2], corner[1] = ring(main[1]), facing(beside[1])
-        first, main[2], corner[1] = hold((first, main[2], corner[1]))
-        main[3], beside[2], across[2] = ring(main[2]), beyond(main[2]), facing(main[2])
+        beside[0] = beyond(main[0])
+        second, beside[0], main[0], keys, values, cos, sin, out_w, where, gain, mean, erase_in = hold(
+            (second, beside[0], main[0], keys, values, cos, sin, out_w, where, gain, mean, erase_in)
+        )
+        main[1], first, corner[0] = ring(main[0]), for_next(second), facing(beside[0])
+        main[1], first, corner[0] = hold((main[1], first, corner[0]))
+        main[2], beside[1], across[1] = ring(main[1]), beyond(main[1]), facing(main[1])
         attended = attend(row[None], queries, (second[0], first[0], keys), (second[1], first[1], values), cos, sin, True)
-        main[3], beside[2], across[2], attended = hold((main[3], beside[2], across[2], attended))
-        across[3], beside[3], corner[2] = ring(across[2]), beyond(main[3]), facing(beside[2])
+        main[2], beside[1], across[1], attended = hold((main[2], beside[1], across[1], attended))
+        main[3], beside[2], corner[1] = ring(main[2]), beyond(main[2]), facing(beside[1])
         att_other = swapped(attended, "col")
-        across[3], beside[3], corner[2], att_other, across[0] = hold(
-            (across[3], beside[3], corner[2], att_other, across[0])
-        )
-        corner[0], corner[3] = beyond(across[0]), facing(beside[3])
-        here = jnp.where(is_mine, 0, heads)
-        there = heads - here
-        weights, pick, late, late_pick = [], [], [], []
-        for k in range(outer):
-            far_k = places[lax.rem(position - k + outer, outer)]
-            for piece, base, side in (
-                (main[k], here, near),
-                (beside[k], here, 1 - near),
-                (across[k], there, near),
-                (corner[k], there, 1 - near),
-            ):
-                is_late = piece is corner[0] or piece is corner[3]
-                (late if is_late else weights).append(piece)
-                (late_pick if is_late else pick).append(base + far_k * inner + side)
+        main[3], beside[2], corner[1], att_other = hold((main[3], beside[2], corner[1], att_other))
+        across[2], beside[3], corner[2] = ring(across[1]), beyond(main[3]), facing(beside[2])
+        across[2], beside[3], corner[2] = hold((across[2], beside[3], corner[2]))
+        across[3], corner[3] = ring(across[2]), facing(beside[3])
+        weights, kinds, late, late_kinds = [], [], [], []
+        for name, pieces in (("main", main), ("beside", beside), ("across", across), ("corner", corner)):
+            for k in range(outer):
+                is_late = k == 3 and name in ("across", "corner")
+                (late if is_late else weights).append(pieces[k])
+                (late_kinds if is_late else kinds).append((name, k))
     else:
-        second = [from_behind(keys), from_behind(values)]
         first = for_next(second)
         attended = attend(row[None], queries, (second[0], first[0], keys), (second[1], first[1], values), cos, sin, False)
         attended = attended[None]
         att_other = swapped(attended, "col")
         weights, late = ([lax.all_gather(w, ("far", "near"), axis=0, tiled=True)] for w in (mine, theirs))
-        pick, late_pick = [jnp.int32(0)], [jnp.int32(1)]
-
-    gain = post_gain[None, :]
-    (partial,) = project(jnp.stack(pick).astype(jnp.int32), attended, att_other, weights)
-    hidden, stat = project(
-        jnp.stack(late_pick).astype(jnp.int32), attended, att_other, late, partial, (gain, erase_in, mean_vec[None, :])
-    )
+        kinds, late_kinds = [(None, 0)], [(None, 1)]
+
+    (partial,) = project(where, kinds, attended, att_other, weights)
+    hidden, stat = project(where, late_kinds, attended, att_other, late, partial, (gain, erase_in, mean))
     return finish(model_width, stat, swapped(stat, "col"), gain, out_w, hidden)
 
 

time: 174 us -> 165 us (0.948)
  local copies, waits for them, and re-layouts: 9.95 us -> 32.4 us
  Pallas kernels: 45.2 us -> 29.3 us
  other arithmetic: 12.6 us -> 6.8 us
  between operations: 5.25 us -> 0.28 us
  starting transfers between devices: 30 us -> 27.4 us
  waiting for transfers between devices: 69.6 us -> 67.6 us
    ppermute x15 -> x14, waiting for transfers between devices: 21.8 us -> 51.8 us  [swapped(): return lax.ppermute(block, axis, [(0, 1), (1, 0)])]
    unnamed x50 -> x69, local copies, waits for them, and re-layouts: 4.91 us -> 26.1 us
    ppermute x4 -> x5, waiting for transfers between devices: 28.4 us -> 12.4 us  [on_device(): ring = lambda block: lax.ppermute(block, 'far', hops)]
    ppermute x2, waiting for transfers between devices: 19.4 us -> 3.46 us  [on_device(): from_behind = lambda block: lax.ppermute(block, 'far', ahead)]
    pallas_call x3, Pallas kernels: 32.2 us -> 18.1 us  [the longest x2 14.8 us: project(): pl.pallas_call(functools.partial(project_kernel, kinds, first, last), gri...]
    ppermute x4 -> x5, starting transfers between devices: 9.53 us -> 4.93 us  [on_device(): ring = lambda block: lax.ppermute(block, 'far', hops)]
    concatenate x1, other arithmetic: 3.27 us -> 0.48 us  [rope_tables(): jnp.concatenate([cosine, cosine], 1)]
    reduce_precision x1, local copies, waits for them, and re-layouts: 0.44 us -> 2.62 us  [split_high_low(): high = lax.reduce_precision(value, 8, 7)]
  transfers between devices with their start and end apart: 21 -> 21, of which waited for: 10 -> 14; matrix products, arithmetic and copies ran while one was open for 9% -> 8% of each run, Pallas kernels for 16% -> 13%
where the time goes in v4:
time: 165 us; the launch traced here: 164 us
  waiting for transfers between devices  67.6 us (41%)
  local copies, waits for them, and re-layouts  32.4 us (20%)
  Pallas kernels  29.3 us (18%)
  starting transfers between devices  27.4 us (17%)
  other arithmetic  6.8 us (4%)
    ppermute x14, waiting for transfers between devices, swapped(): return lax.ppermute(block, axis, [(0, 1), (1, 0)])  51.8 us
    unnamed x69, local copies, waits for them, and re-layouts  26.1 us
    pallas_call x2, Pallas kernels, project(): pl.pallas_call(functools.partial(project_kernel, kinds, first, last), gri...  14.8 us
    ppermute x14, starting transfers between devices, swapped(): return lax.ppermute(block, axis, [(0, 1), (1, 0)])  13.9 us
    ppermute x5, waiting for transfers between devices, on_device(): ring = lambda block: lax.ppermute(block, 'far', hops)  12.4 us
    pallas_call x1, Pallas kernels, attend(): pl.pallas_call(functools.partial(attend_kernel, tok, group, direct), grid...  11.3 us
    ppermute x2, starting transfers between devices, on_device(): from_behind = lambda block: lax.ppermute(block, 'far', ahead)  8.57 us
    ppermute x5, starting transfers between devices, on_device(): ring = lambda block: lax.ppermute(block, 'far', hops)  4.93 us
  transfers between devices with their start and end apart: 21, of which 14 were waited for; matrix products, arithmetic and copies ran while one was open for 8% of the time, Pallas kernels for 13%

profile of v4, /device:TPU:0, one launch (start us, length us, event | category | flops | bytes accessed | tf_op | source)
XLA Modules:
  0.0 163.8 jit_solution(733933568416571192)
XLA Ops:
  0.0 5.1 %collective-permute-start = (bf16[512,512]{1,0:T(8,128)(2,1)}, bf16[512,512]{1,0:T(8,128)(2,1)S(1)}, u32[]{:S(2)}, u32[]{:S(2)}) collective-permute-start(bf16[512,512]{1,0:T(8,128)(2,1)} %k2), channel_id=1, source_target_pairs={{0,4},{4,8},{8,12},{1,5},{5,9},{9,13},{2,6},{6,10},{10,14},{3,7},{... | collective-permute-start | bytes 1572872 | tf_op jit(solution)/shard_map/ppermute | solution.py:314
  5.1 3.5 %collective-permute-start.1 = (bf16[512,512]{1,0:T(8,128)(2,1)}, bf16[512,512]{1,0:T(8,128)(2,1)S(1)}, u32[]{:S(2)}, u32[]{:S(2)}) collective-permute-start(bf16[512,512]{1,0:T(8,128)(2,1)} %v2), channel_id=1, source_target_pairs={{0,4},{4,8},{8,12},{1,5},{5,9},{9,13},{2,6},{6,10},{10,14},{3,7},{... | collective-permute-start | bytes 1572872 | tf_op jit(solution)/shard_map/ppermute | solution.py:314
  8.6 2.0 %constant_dynamic-slice_fusion = bf16[128,2688]{1,0:T(8,128)(2,1)} fusion(bf16[128,5376]{1,0:T(8,128)(2,1)} %param.11, s32[]{:T(128)S(6)} %select_n.32), kind=kLoop, calls=%fused_computation.14 | loop fusion | bytes 1376260 | tf_op jit(solution)/shard_map/dynamic_slice | solution.py:321
  12.3 2.6 %copy.12 = f32[2688,64]{1,0:T(8,128)} copy(f32[2688,64]{0,1:T(8,128)} %reduce_precision.3) | data formatting | bytes 1376256 | tf_op jit(solution)/shard_map/reduce_precision | solution.py:27
  15.0 2.8 %fusion = (f32[1536,64]{1,0:T(8,128)S(1)}, f32[1536,64]{1,0:T(8,128)S(1)}, f32[1536,64]{1,0:T(8,128)S(1)}) fusion(f32[64]{0:T(128)S(1)} %multiply_exponential_fusion, f32[1536]{0:T(1024)S(1)} %add_convert_fusion), kind=kLoop, calls=%fused_computation.10 | loop fusion | flops 196608 | bytes 1186048 | tf_op jit(solution)/shard_map/neg | solution.py:39
  21.8 1.6 collective-permute-start.3
  24.3 3.5 %collective-permute-done.1.v0 = bf16[512,512]{1,0:T(8,128)(2,1)S(1)} collective-permute-done((bf16[512,512]{1,0:T(8,128)(2,1)}, bf16[512,512]{1,0:T(8,128)(2,1)S(1)}, u32[]{:S(2)}, u32[]{:S(2)}) %collective-permute-start.1) | collective-permute-done | bytes 524320 | tf_op jit(solution)/shard_map/ppermute | solution.py:314
  27.8 11.9 %collective-permute-done.3.refs_4_ = bf16[128,2688]{1,0:T(8,128)(2,1)S(1)} collective-permute-done((bf16[128,2688]{1,0:T(8,128)(2,1)S(1)}, bf16[128,2688]{1,0:T(8,128)(2,1)S(1)}, u32[]{:S(2)}, u32[]{:S(2)}) %collective-permute-start.3) | collective-permute-done | bytes 688160 | tf_op jit(solution)/shard_map/ppermute | solution.py:295
  39.8 1.6 collective-permute-start.6
  41.4 1.5 collective-permute-start.4
  45.1 9.6 %collective-permute-done.6.v1 = bf16[512,512]{1,0:T(8,128)(2,1)S(1)} collective-permute-done((bf16[512,512]{1,0:T(8,128)(2,1)S(1)}, bf16[512,512]{1,0:T(8,128)(2,1)S(1)}, u32[]{:S(2)}, u32[]{:S(2)}) %collective-permute-start.6) | collective-permute-done | bytes 524320 | tf_op jit(solution)/shard_map/ppermute | solution.py:295
  54.7 9.9 %collective-permute-done.5.k1 = bf16[512,512]{1,0:T(8,128)(2,1)S(1)} collective-permute-done((bf16[512,512]{1,0:T(8,128)(2,1)S(1)}, bf16[512,512]{1,0:T(8,128)(2,1)S(1)}, u32[]{:S(2)}, u32[]{:S(2)}) %collective-permute-start.5) | collective-permute-done | bytes 524320 | tf_op jit(solution)/shard_map/ppermute | solution.py:295
  68.5 1.5 collective-permute-start.8
  70.1 11.3 %shard_map.82.own_ref = bf16[8,512,128]{2,1,0:T(8,128)(2,1)S(1)} custom-call(s32[1]{0:T(128)} %bitcast.3.row_ref, bf16[512,1024]{1,0:T(8,128)(2,1)S(1)} %copy-done.8, bf16[512,512]{1,0:T(8,128)(2,1)S(1)} %collective-permute-done.k0, bf16[512,512]{1,0:T(8,128)(2,1)S(1)} %collective-permute-done.5.k1, bf16[512,512]{1,0:T(8,128)(2,1)S(1)} %copy-done.6, ...), custom_call_target="tpu_custom_call" | custom-call | flops 2684354560 | bytes 6291456 | tf_op jit(solution)/shard_map/pallas_call | solution.py:109
  82.9 2.1 %collective-permute-done.8.refs_2_ = bf16[128,2688]{1,0:T(8,128)(2,1)S(1)} collective-permute-done((bf16[128,2688]{1,0:T(8,128)(2,1)S(1)}, bf16[128,2688]{1,0:T(8,128)(2,1)S(1)}, u32[]{:S(2)}, u32[]{:S(2)}) %collective-permute-start.8) | collective-permute-done | bytes 688160 | tf_op jit(solution)/shard_map/ppermute | solution.py:333
  91.5 12.4 %collective-permute-done.13.refs_12_ = bf16[128,2688]{1,0:T(8,128)(2,1)S(1)} collective-permute-done((bf16[128,2688]{1,0:T(8,128)(2,1)S(1)}, bf16[128,2688]{1,0:T(8,128)(2,1)S(1)}, u32[]{:S(2)}, u32[]{:S(2)}) %collective-permute-start.13) | collective-permute-done | bytes 688160 | tf_op jit(solution)/shard_map/ppermute | solution.py:295
  105.0 2.1 %collective-permute-done.11.refs_3_ = bf16[128,2688]{1,0:T(8,128)(2,1)S(1)} collective-permute-done((bf16[128,2688]{1,0:T(8,128)(2,1)S(1)}, bf16[128,2688]{1,0:T(8,128)(2,1)S(1)}, u32[]{:S(2)}, u32[]{:S(2)}) %collective-permute-start.11) | collective-permute-done | bytes 688160 | tf_op jit(solution)/shard_map/ppermute | solution.py:333
  112.9 8.1 %collective-permute-done.15.refs_10_ = bf16[128,2688]{1,0:T(8,128)(2,1)} collective-permute-done((bf16[128,2688]{1,0:T(8,128)(2,1)S(1)}, bf16[128,2688]{1,0:T(8,128)(2,1)}, u32[]{:S(2)}, u32[]{:S(2)}) %collective-permute-start.15) | collective-permute-done | bytes 688160 | tf_op jit(solution)/shard_map/ppermute | solution.py:333
  121.0 2.7 %collective-permute-done.16.refs_7_ = bf16[128,2688]{1,0:T(8,128)(2,1)} collective-permute-done((bf16[128,2688]{1,0:T(8,128)(2,1)S(1)}, bf16[128,2688]{1,0:T(8,128)(2,1)}, u32[]{:S(2)}, u32[]{:S(2)}) %collective-permute-start.16) | collective-permute-done | bytes 688160 | tf_op jit(solution)/shard_map/ppermute | solution.py:295
  123.7 2.0 %collective-permute-done.17.refs_13_ = bf16[128,2688]{1,0:T(8,128)(2,1)S(1)} collective-permute-done((bf16[128,2688]{1,0:T(8,128)(2,1)S(1)}, bf16[128,2688]{1,0:T(8,128)(2,1)S(1)}, u32[]{:S(2)}, u32[]{:S(2)}) %collective-permute-start.17) | collective-permute-done | bytes 688160 | tf_op jit(solution)/shard_map/ppermute | solution.py:295
  128.0 1.5 copy.15.refs_4_
  144.1 9.8 %shard_map.83.refs_2_ = f32[512,2688]{1,0:T(8,128)S(1)} custom-call(s32[4]{0:T(128)S(1)} %pad_add_fusion.where_ref, bf16[8,512,128]{2,1,0:T(8,128)(2,1)S(1)} %copy-done.1, bf16[8,512,128]{2,1,0:T(8,128)(2,1)S(1)} %copy-done.3, bf16[128,2688]{1,0:T(8,128)(2,1)S(1)} %copy-done.5, bf16[128,2688]{1,0:T(8,128)(2,1)S(1)} %copy-done.12, ...), custom_call_target="tpu_custom_call" | custom-call | flops 4932501504 | bytes 9633792 | tf_op jit(solution)/shard_map/pallas_call | solution.py:231
  153.9 5.0 %shard_map.84 = (f32[512,2688]{1,0:T(8,128)S(1)}, f32[520,128]{1,0:T(8,128)S(1)}) custom-call(s32[4]{0:T(128)S(1)} %pad_add_fusion.where_ref, bf16[8,512,128]{2,1,0:T(8,128)(2,1)S(1)} %copy-done.1, bf16[8,512,128]{2,1,0:T(8,128)(2,1)S(1)} %copy-done.3, bf16[128,2688]{1,0:T(8,128)(2,1)} %collective-permute-done.18.refs_0_, ...), custom_call_target="tpu_custom_call" | custom-call | flops 704643072 | bytes 1376256 | tf_op jit(solution)/shard_map/pallas_call | solution.py:231
  160.5 3.3 %shard_map.85 = bf16[512,2688]{1,0:T(8,128)(2,1)} custom-call(f32[520,128]{1,0:T(8,128)S(1)} %get-tuple-element.62.own_ref, f32[520,128]{1,0:T(8,128)S(1)} %collective-permute-done.20.other_ref, f32[1,2688]{1,0:T(1,128)S(1)} %broadcast_in_dim.15.refs_3_.gain_ref, bf16[2688,256]{1,0:T(8,128)(2,1)S(1)} %maximum_maximum_fusion.out_w_ref, ...), custom_call_target="tpu_custom_call" | custom-call | flops 704643072 | bytes 8257536 | tf_op jit(solution)/shard_map/pallas_call | solution.py:274
  (109 shorter events, 46.0 us)
Async XLA Ops:
  0.0 24.3 %collective-permute-start = (bf16[512,512]{1,0:T(8,128)(2,1)}, bf16[512,512]{1,0:T(8,128)(2,1)S(1)}, u32[]{:S(2)}, u32[]{:S(2)}) collective-permute-start(bf16[512,512]{1,0:T(8,128)(2,1)} %k2), channel_id=1, source_target_pairs={{0,4},{4,8},{8,12},{1,5},{5,9},{9,13},{2,6},{6,10},{10,14},{3,7},{... | collective-permute-start | bytes 1572872 | tf_op jit(solution)/shard_map/ppermute | solution.py:314
  5.1 22.7 %collective-permute-start.1 = (bf16[512,512]{1,0:T(8,128)(2,1)}, bf16[512,512]{1,0:T(8,128)(2,1)S(1)}, u32[]{:S(2)}, u32[]{:S(2)}) collective-permute-start(bf16[512,512]{1,0:T(8,128)(2,1)} %v2), channel_id=1, source_target_pairs={{0,4},{4,8},{8,12},{1,5},{5,9},{9,13},{2,6},{6,10},{10,14},{3,7},{... | collective-permute-start | bytes 1572872 | tf_op jit(solution)/shard_map/ppermute | solution.py:314
  10.6 8.7 %collective-permute-start.2 = (bf16[128,2688]{1,0:T(8,128)(2,1)}, bf16[128,2688]{1,0:T(8,128)(2,1)}, u32[]{:S(2)}, u32[]{:S(2)}) collective-permute-start(bf16[128,2688]{1,0:T(8,128)(2,1)} %constant_dynamic-slice_fusion), channel_id=1, source_target_pairs={{0,1},{1,0},{2,3},{3,2},{4,5},{5,4},{6,7},{7,6},{8,9},{9,8},{10,11... | collective-permute-start | bytes 2064392 | tf_op jit(solution)/shard_map/ppermute | solution.py:295
  21.8 19.6 %copy-start.4 = (bf16[128,2688]{1,0:T(8,128)(2,1)}, bf16[128,2688]{1,0:T(8,128)(2,1)S(1)}, u32[]{:S(2)}) copy-start(bf16[128,2688]{1,0:T(8,128)(2,1)S(1)} %get-tuple-element.36.refs_0_) | copy-start | bytes 2064388
  21.8 17.9 %collective-permute-start.3 = (bf16[128,2688]{1,0:T(8,128)(2,1)S(1)}, bf16[128,2688]{1,0:T(8,128)(2,1)S(1)}, u32[]{:S(2)}, u32[]{:S(2)}) collective-permute-start(bf16[128,2688]{1,0:T(8,128)(2,1)S(1)} %get-tuple-element.36.refs_0_), channel_id=1, source_target_pairs={{0,2},{2,0},{1,3},{3,1},{4,6},{6,4},{5,7},{7,5},{8,10},{10,8},{9,1... | collective-permute-start | bytes 2064392 | tf_op jit(solution)/shard_map/ppermute | solution.py:295
  24.3 20.1 %copy-start.6 = (bf16[512,512]{1,0:T(8,128)(2,1)S(1)}, bf16[512,512]{1,0:T(8,128)(2,1)}, u32[]{:S(2)}) copy-start(bf16[512,512]{1,0:T(8,128)(2,1)} %k2) | copy-start | bytes 1572868
  39.7 30.4 %copy-start.8 = (bf16[512,1024]{1,0:T(8,128)(2,1)S(1)}, bf16[512,1024]{1,0:T(8,128)(2,1)}, u32[]{:S(2)}) copy-start(bf16[512,1024]{1,0:T(8,128)(2,1)} %q_ref.1) | copy-start | bytes 3145732
  39.8 14.9 %collective-permute-start.6 = (bf16[512,512]{1,0:T(8,128)(2,1)S(1)}, bf16[512,512]{1,0:T(8,128)(2,1)S(1)}, u32[]{:S(2)}, u32[]{:S(2)}) collective-permute-start(bf16[512,512]{1,0:T(8,128)(2,1)S(1)} %broadcast_select_fusion.2), channel_id=1, source_target_pairs={{0,2},{2,0},{1,3},{3,1},{4,6},{6,4},{5,7},{7,5},{8,10},{10,8},{9,1... | collective-permute-start | bytes 1572872 | tf_op jit(solution)/shard_map/ppermute | solution.py:295
  41.4 23.3 %collective-permute-start.4 = (bf16[128,2688]{1,0:T(8,128)(2,1)S(1)}, bf16[128,2688]{1,0:T(8,128)(2,1)S(1)}, u32[]{:S(2)}, u32[]{:S(2)}) collective-permute-start(bf16[128,2688]{1,0:T(8,128)(2,1)S(1)} %get-tuple-element.36.refs_0_), channel_id=1, source_target_pairs={{0,4},{4,12},{12,8},{8,0},{1,5},{5,13},{13,9},{9,1},{2,6},{6,14},{... | collective-permute-start | bytes 2064392 | tf_op jit(solution)/shard_map/ppermute | solution.py:333
  42.9 21.7 %collective-permute-start.7 = (bf16[128,2688]{1,0:T(8,128)(2,1)S(1)}, bf16[128,2688]{1,0:T(8,128)(2,1)S(1)}, u32[]{:S(2)}, u32[]{:S(2)}) collective-permute-start(bf16[128,2688]{1,0:T(8,128)(2,1)S(1)} %collective-permute-done.3.refs_4_), channel_id=1, source_target_pairs={{0,16},{16,0},{1,17},{17,1},{2,18},{18,2},{3,19},{19,3},{4,20},{20... | collective-permute-start | bytes 2064392 | tf_op jit(solution)/shard_map/ppermute | solution.py:295
  44.5 20.1 %collective-permute-start.5 = (bf16[512,512]{1,0:T(8,128)(2,1)S(1)}, bf16[512,512]{1,0:T(8,128)(2,1)S(1)}, u32[]{:S(2)}, u32[]{:S(2)}) collective-permute-start(bf16[512,512]{1,0:T(8,128)(2,1)S(1)} %broadcast_select_fusion.3), channel_id=1, source_target_pairs={{0,2},{2,0},{1,3},{3,1},{4,6},{6,4},{5,7},{7,5},{8,10},{10,8},{9,1... | collective-permute-start | bytes 1572872 | tf_op jit(solution)/shard_map/ppermute | solution.py:295
  65.5 16.2 %collective-permute-start.10 = (bf16[128,2688]{1,0:T(8,128)(2,1)S(1)}, bf16[128,2688]{1,0:T(8,128)(2,1)S(1)}, u32[]{:S(2)}, u32[]{:S(2)}) collective-permute-start(bf16[128,2688]{1,0:T(8,128)(2,1)S(1)} %collective-permute-done.4.refs_1_), channel_id=1, source_target_pairs={{0,16},{16,0},{1,17},{17,1},{2,18},{18,2},{3,19},{19,3},{4,20},{20... | collective-permute-start | bytes 2064392 | tf_op jit(solution)/shard_map/ppermute | solution.py:295
  67.0 15.9 %collective-permute-start.9 = (bf16[128,2688]{1,0:T(8,128)(2,1)S(1)}, bf16[128,2688]{1,0:T(8,128)(2,1)S(1)}, u32[]{:S(2)}, u32[]{:S(2)}) collective-permute-start(bf16[128,2688]{1,0:T(8,128)(2,1)S(1)} %collective-permute-done.4.refs_1_), channel_id=1, source_target_pairs={{0,2},{2,0},{1,3},{3,1},{4,6},{6,4},{5,7},{7,5},{8,10},{10,8},{9,1... | collective-permute-start | bytes 2064392 | tf_op jit(solution)/shard_map/ppermute | solution.py:295
  68.5 16.5 %collective-permute-start.8 = (bf16[128,2688]{1,0:T(8,128)(2,1)S(1)}, bf16[128,2688]{1,0:T(8,128)(2,1)S(1)}, u32[]{:S(2)}, u32[]{:S(2)}) collective-permute-start(bf16[128,2688]{1,0:T(8,128)(2,1)S(1)} %collective-permute-done.4.refs_1_), channel_id=1, source_target_pairs={{0,4},{4,12},{12,8},{8,0},{1,5},{5,13},{13,9},{9,1},{2,6},{6,14},{... | collective-permute-start | bytes 2064392 | tf_op jit(solution)/shard_map/ppermute | solution.py:333
  85.0 22.1 %collective-permute-start.14 = (bf16[8,512,128]{2,1,0:T(8,128)(2,1)S(1)}, bf16[8,512,128]{2,1,0:T(8,128)(2,1)S(1)}, u32[]{:S(2)}, u32[]{:S(2)}) collective-permute-start(bf16[8,512,128]{2,1,0:T(8,128)(2,1)S(1)} %shard_map.82.own_ref), channel_id=1, source_target_pairs={{0,1},{1,0},{2,3},{3,2},{4,5},{5,4},{6,7},{7,6},{8,9},{9,8},{10,11... | collective-permute-start | bytes 3145736 | tf_op jit(solution)/shard_map/ppermute | solution.py:295
  86.0 17.8 %collective-permute-start.13 = (bf16[128,2688]{1,0:T(8,128)(2,1)S(1)}, bf16[128,2688]{1,0:T(8,128)(2,1)S(1)}, u32[]{:S(2)}, u32[]{:S(2)}) collective-permute-start(bf16[128,2688]{1,0:T(8,128)(2,1)S(1)} %collective-permute-done.9.refs_5_), channel_id=1, source_target_pairs={{0,16},{16,0},{1,17},{17,1},{2,18},{18,2},{3,19},{19,3},{4,20},{20... | collective-permute-start | bytes 2064392 | tf_op jit(solution)/shard_map/ppermute | solution.py:295
  87.4 17.6 %collective-permute-start.12 = (bf16[128,2688]{1,0:T(8,128)(2,1)S(1)}, bf16[128,2688]{1,0:T(8,128)(2,1)S(1)}, u32[]{:S(2)}, u32[]{:S(2)}) collective-permute-start(bf16[128,2688]{1,0:T(8,128)(2,1)S(1)} %collective-permute-done.8.refs_2_), channel_id=1, source_target_pairs={{0,2},{2,0},{1,3},{3,1},{4,6},{6,4},{5,7},{7,5},{8,10},{10,8},{9,1... | collective-permute-start | bytes 2064392 | tf_op jit(solution)/shard_map/ppermute | solution.py:295
  87.9 19.2 %collective-permute-start.11 = (bf16[128,2688]{1,0:T(8,128)(2,1)S(1)}, bf16[128,2688]{1,0:T(8,128)(2,1)S(1)}, u32[]{:S(2)}, u32[]{:S(2)}) collective-permute-start(bf16[128,2688]{1,0:T(8,128)(2,1)S(1)} %collective-permute-done.8.refs_2_), channel_id=1, source_target_pairs={{0,4},{4,12},{12,8},{8,0},{1,5},{5,13},{13,9},{9,1},{2,6},{6,14},{... | collective-permute-start | bytes 2064392 | tf_op jit(solution)/shard_map/ppermute | solution.py:333
  89.4 31.5 %collective-permute-start.15 = (bf16[128,2688]{1,0:T(8,128)(2,1)S(1)}, bf16[128,2688]{1,0:T(8,128)(2,1)}, u32[]{:S(2)}, u32[]{:S(2)}) collective-permute-start(bf16[128,2688]{1,0:T(8,128)(2,1)S(1)} %collective-permute-done.10.refs_9_), channel_id=1, source_target_pairs={{0,4},{4,12},{12,8},{8,0},{1,5},{5,13},{13,9},{9,1},{2,6},{6,14},{... | collective-permute-start | bytes 2064392 | tf_op jit(solution)/shard_map/ppermute | solution.py:333
  108.2 15.5 %collective-permute-start.16 = (bf16[128,2688]{1,0:T(8,128)(2,1)S(1)}, bf16[128,2688]{1,0:T(8,128)(2,1)}, u32[]{:S(2)}, u32[]{:S(2)}) collective-permute-start(bf16[128,2688]{1,0:T(8,128)(2,1)S(1)} %collective-permute-done.11.refs_3_), channel_id=1, source_target_pairs={{0,2},{2,0},{1,3},{3,1},{4,6},{6,4},{5,7},{7,5},{8,10},{10,8},{9,1... | collective-permute-start | bytes 2064392 | tf_op jit(solution)/shard_map/ppermute | solution.py:295
  110.5 15.1 %collective-permute-start.17 = (bf16[128,2688]{1,0:T(8,128)(2,1)S(1)}, bf16[128,2688]{1,0:T(8,128)(2,1)S(1)}, u32[]{:S(2)}, u32[]{:S(2)}) collective-permute-start(bf16[128,2688]{1,0:T(8,128)(2,1)S(1)} %collective-permute-done.12.refs_6_), channel_id=1, source_target_pairs={{0,16},{16,0},{1,17},{17,1},{2,18},{18,2},{3,19},{19,3},{4,20},{20... | collective-permute-start | bytes 2064392 | tf_op jit(solution)/shard_map/ppermute | solution.py:295
  126.5 27.4 %collective-permute-start.18 = (bf16[128,2688]{1,0:T(8,128)(2,1)}, bf16[128,2688]{1,0:T(8,128)(2,1)}, u32[]{:S(2)}, u32[]{:S(2)}) collective-permute-start(bf16[128,2688]{1,0:T(8,128)(2,1)} %collective-permute-done.15.refs_10_), channel_id=1, source_target_pairs={{0,4},{4,12},{12,8},{8,0},{1,5},{5,13},{13,9},{9,1},{2,6},{6,14},{... | collective-permute-start | bytes 2064392 | tf_op jit(solution)/shard_map/ppermute | solution.py:333
  126.5 27.4 %collective-permute-start.19 = (bf16[128,2688]{1,0:T(8,128)(2,1)}, bf16[128,2688]{1,0:T(8,128)(2,1)}, u32[]{:S(2)}, u32[]{:S(2)}) collective-permute-start(bf16[128,2688]{1,0:T(8,128)(2,1)} %collective-permute-done.16.refs_7_), channel_id=1, source_target_pairs={{0,16},{16,0},{1,17},{17,1},{2,18},{18,2},{3,19},{19,3},{4,20},{20... | collective-permute-start | bytes 2064392 | tf_op jit(solution)/shard_map/ppermute | solution.py:295
  158.9 1.6 collective-permute-start.20
  (31 other events, 76.1 us)

commit v5 on v4

--- a/solution.py
+++ b/solution.py
@@ -21,11 +21,6 @@
 VMEM_LIMIT = 32 * 2**20
 
 NT = (((1,), (1,)), ((), ()))
-
-
-def split_high_low(value):
-    high = lax.reduce_precision(value, 8, 7)
-    return high.astype(jnp.bfloat16), (value - high).astype(jnp.bfloat16)
 
 
 def rope_tables(first_position, count):
@@ -94,10 +89,11 @@
                 out_ref[lo:hi, h * HD : (h + 1) * HD] = block
 
 
-def attend(row, queries, key_blocks, val_blocks, cos, sin, direct):
-    tok, kv_local = queries.shape[0], key_blocks[0].shape[1] // HD
+def attend(row, queries, blocks, cos, sin, direct):
+    tok, kv_local = queries.shape[0], blocks[0].shape[1] // HD // 2
     group = queries.shape[1] // HD // kv_local
-    head_block = pl.BlockSpec((tok, HD), lambda g, r: (0, g))
+    key_block = pl.BlockSpec((tok, HD), lambda g, r: (0, g))
+    val_block = pl.BlockSpec((tok, HD), lambda g, r: (0, g + kv_local))
     table = pl.BlockSpec((3 * tok, HD), lambda g, r: (0, 0))
     if direct:
         out_shape = (kv_local * group, tok, HD)
@@ -111,7 +107,7 @@
         grid_spec=pltpu.PrefetchScalarGridSpec(
             num_scalar_prefetch=1,
             grid=(kv_local,),
-            in_specs=[pl.BlockSpec((tok, group * HD), lambda g, r: (0, g))] + [head_block] * 6 + [table] * 2,
+            in_specs=[pl.BlockSpec((tok, group * HD), lambda g, r: (0, g))] + [key_block] * 3 + [val_block] * 3 + [table] * 2,
             out_specs=out_spec,
         ),
         out_shape=jax.ShapeDtypeStruct(out_shape, jnp.bfloat16),
@@ -119,7 +115,7 @@
         cost_estimate=pl.CostEstimate(
             flops=heads * tok * 10 * tok * HD, bytes_accessed=6 * 2**20, transcendentals=heads * tok * 2 * tok
         ),
-    )(row, queries, *key_blocks, *val_blocks, cos, sin)
+    )(row, queries, *blocks, *blocks, cos, sin)
 
 
 def ring_place(position, size):
@@ -150,9 +146,27 @@
     hidden_ref, refs = refs[0], refs[1:]
     if last:
         stat_ref, refs = refs[0], refs[1:]
-    heads, sems = refs
+    heads, sems = refs[:2]
     step = pl.program_id(0)
     depth = weights[0].shape[0]
+    if not last:
+        blocks, block_sems = refs[2:]
+        steps = pl.num_programs(0)
+
+        def columns_of(at, act):
+            slot = lax.rem(at, 2)
+            for n, piece in enumerate(weights):
+                source = piece.at[:, pl.ds(pl.multiple_of(at * TILE, TILE), TILE)]
+                act(pltpu.make_async_copy(source, blocks.at[slot, n * depth : (n + 1) * depth], block_sems.at[slot, n]))
+
+        @pl.when(step == 0)
+        def _():
+            columns_of(step, lambda copy: copy.start())
+
+        @pl.when(step + 1 < steps)
+        def _():
+            columns_of(step + 1, lambda copy: copy.start())
+
     slots = own_ref.shape[0]
 
     @pl.when(step == 0)
@@ -173,19 +187,22 @@
             place = heads.at[:, n * depth : (n + 1) * depth]
             pltpu.make_async_copy(own_ref.at[0], place, sems.at[n]).wait()
 
-    weight = jnp.concatenate([w[...] for w in weights], 0)
+    if last:
+        weight = jnp.concatenate([w[...] for w in weights], 0)
+    else:
+        columns_of(step, lambda copy: copy.wait())
+        weight = blocks[lax.rem(step, 2)]
     total = jnp.dot(heads[...], weight, preferred_element_type=jnp.float32)
     if not first:
         total += partial_ref[...]
     hidden_ref[...] = total
     if last:
-        wide = jnp.concatenate([in_ref[...], jnp.zeros_like(in_ref)], 1)
-        wide_high = wide.astype(jnp.bfloat16)
-        wide_low = wide - wide_high.astype(jnp.float32)
-        in_a = (wide_high.astype(jnp.float32) + pltpu.roll(wide_low, RANK, 1)).astype(jnp.bfloat16)
+        in_high = in_ref[...].astype(jnp.bfloat16)
+        in_low = (in_ref[...] - in_high.astype(jnp.float32)).astype(jnp.bfloat16)
+        in_parts = jnp.concatenate([in_high, in_low], 0)
 
         def coded(field):
-            code = jnp.dot(field.astype(jnp.bfloat16), in_a, preferred_element_type=jnp.float32)
+            code = lax.dot_general(field.astype(jnp.bfloat16), in_parts, NT, preferred_element_type=jnp.float32)
             return code + pltpu.roll(code, RANK, 1)
 
         code = coded(total * gain_ref[...])
@@ -214,8 +231,11 @@
     count = len(weights)
     first, last = partial is None, last_terms is not None
     columns = lambda rows: pl.BlockSpec((rows, TILE), lambda j, r: (0, j))
-    anywhere = pl.BlockSpec(memory_space=pl.ANY)
-    in_specs = [anywhere] * 2 + [columns(depth)] * count
+    in_hbm = pl.BlockSpec(memory_space=pltpu.HBM)
+    in_specs = [in_hbm] * 2 + [columns(depth) if last else in_hbm] * count
+    scratch = [pltpu.VMEM((tok, count * depth), jnp.bfloat16), pltpu.SemaphoreType.DMA((count,))]
+    if not last:
+        scratch += [pltpu.VMEM((2, count * depth, TILE), jnp.bfloat16), pltpu.SemaphoreType.DMA((2, count))]
     operands = [where, own, other, *weights]
     out_specs = [columns(tok)]
     out_shape = [jax.ShapeDtypeStruct((tok, width), jnp.float32)]
@@ -224,7 +244,7 @@
         operands.append(partial)
     if last:
         gain, erase_in, mean = last_terms
-        in_specs += [columns(1), pl.BlockSpec((TILE, RANK), lambda j, r: (j, 0)), columns(1)]
+        in_specs += [columns(1), columns(RANK), columns(1)]
         operands += [gain, erase_in, mean]
         out_specs.append(pl.BlockSpec((tok + 8, 2 * RANK), lambda j, r: (0, 0)))
         out_shape.append(jax.ShapeDtypeStruct((tok + 8, 2 * RANK), jnp.float32))
@@ -235,10 +255,7 @@
             grid=(width // TILE,),
             in_specs=in_specs,
             out_specs=out_specs,
-            scratch_shapes=[
-                pltpu.VMEM((tok, count * depth), jnp.bfloat16),
-                pltpu.SemaphoreType.DMA((count,)),
-            ],
+            scratch_shapes=scratch,
         ),
         out_shape=out_shape,
         compiler_params=pltpu.CompilerParams(vmem_limit_bytes=VMEM_LIMIT),
@@ -248,7 +265,7 @@
     )(*operands)
 
 
-def finish_kernel(model_width, own_ref, other_ref, gain_ref, out_w_ref, hidden_ref, erased_ref, packed_ref, inv_ref):
+def finish_kernel(model_width, own_ref, other_ref, gain_ref, out_ref, hidden_ref, erased_ref, packed_ref, inv_ref):
     tok = hidden_ref.shape[0]
 
     @pl.when(pl.program_id(0) == 0)
@@ -263,12 +280,15 @@
         packed_ref[...] = jnp.concatenate([high + pltpu.roll(low, RANK, 1), high], 1).astype(jnp.bfloat16)
         inv_ref[...] = jnp.broadcast_to(inv_rms, inv_ref.shape)
 
-    removed = lax.dot_general(packed_ref[...], out_w_ref[...], NT, preferred_element_type=jnp.float32)
+    out_high = out_ref[...].astype(jnp.bfloat16)
+    out_low = (out_ref[...] - out_high.astype(jnp.float32)).astype(jnp.bfloat16)
+    out_parts = jnp.concatenate([out_high, out_high, out_low, jnp.zeros_like(out_low)], 0)
+    removed = jnp.dot(packed_ref[...], out_parts, preferred_element_type=jnp.float32)
     normed = hidden_ref[...] * inv_ref[:, :1] * gain_ref[...]
     erased_ref[...] = (normed - removed).astype(jnp.bfloat16)
 
 
-def finish(model_width, stat, stat_other, gain, out_w, hidden):
+def finish(model_width, stat, stat_other, gain, erase_out, hidden):
     tok, width = hidden.shape
     whole = pl.BlockSpec(stat.shape, lambda j: (0, 0))
     return pl.pallas_call(
@@ -278,7 +298,7 @@
             whole,
             whole,
             pl.BlockSpec((1, TILE), lambda j: (0, j)),
-            pl.BlockSpec((TILE, 4 * RANK), lambda j: (j, 0)),
+            pl.BlockSpec((RANK, TILE), lambda j: (0, j)),
             pl.BlockSpec((tok, TILE), lambda j: (0, j)),
         ],
         out_specs=pl.BlockSpec((tok, TILE), lambda j: (0, j)),
@@ -288,7 +308,7 @@
         cost_estimate=pl.CostEstimate(
             flops=2 * tok * 256 * width, bytes_accessed=6 * tok * width, transcendentals=0
         ),
-    )(stat, stat_other, gain, out_w, hidden)
+    )(stat, stat_other, gain, erase_out, hidden)
 
 
 def swapped(block, axis):
@@ -315,15 +335,14 @@
     hold = lax.optimization_barrier
 
     def for_next(second):
-        return [swapped(jnp.where(near == 0, own, old), "near") for own, old in zip((keys, values), second)]
-
-    second = [from_behind(keys), from_behind(values)]
+        return swapped(jnp.where(near == 0, both, second), "near")
+
+    both = jnp.concatenate([keys, values], 1)
+    second = from_behind(both)
     theirs = swapped(lax.dynamic_slice_in_dim(out_proj, (1 - col) * width, width, 1), "col")
     mine = lax.dynamic_slice_in_dim(out_proj, col * width, width, 1)
-    cos, sin = rope_tables((row - 2) * tok, 3 * tok)
-    out_high, out_low = split_high_low(erase_out)
-    out_w = jnp.concatenate([out_high, out_high, out_low, jnp.zeros_like(out_low)], 1)
     gain, mean = post_gain[None, :], mean_vec[None, :]
+    erase_in, erase_out = erase_in.T, erase_out.T
     is_mine = grp == col
     where = jnp.stack([is_mine.astype(jnp.int32), far, near, jnp.int32(outer)])
 
@@ -337,13 +356,12 @@
         main[0] = jnp.where(is_mine, mine, theirs)
         across[0] = jnp.where(is_mine, theirs, mine)
         beside[0] = beyond(main[0])
-        second, beside[0], main[0], keys, values, cos, sin, out_w, where, gain, mean, erase_in = hold(
-            (second, beside[0], main[0], keys, values, cos, sin, out_w, where, gain, mean, erase_in)
-        )
+        second, beside[0], main[0], row, where = hold((second, beside[0], main[0], row, where))
         main[1], first, corner[0] = ring(main[0]), for_next(second), facing(beside[0])
-        main[1], first, corner[0] = hold((main[1], first, corner[0]))
+        cos, sin = rope_tables((row - 2) * tok, 3 * tok)
+        main[1], first, corner[0], cos, sin = hold((main[1], first, corner[0], cos, sin))
         main[2], beside[1], across[1] = ring(main[1]), beyond(main[1]), facing(main[1])
-        attended = attend(row[None], queries, (second[0], first[0], keys), (second[1], first[1], values), cos, sin, True)
+        attended = attend(row[None], queries, (second, first, both), cos, sin, True)
         main[2], beside[1], across[1], attended = hold((main[2], beside[1], across[1], attended))
         main[3], beside[2], corner[1] = ring(main[2]), beyond(main[2]), facing(beside[1])
         att_other = swapped(attended, "col")
@@ -359,7 +377,8 @@
                 (late_kinds if is_late else kinds).append((name, k))
     else:
         first = for_next(second)
-        attended = attend(row[None], queries, (second[0], first[0], keys), (second[1], first[1], values), cos, sin, False)
+        cos, sin = rope_tables((row - 2) * tok, 3 * tok)
+        attended = attend(row[None], queries, (second, first, both), cos, sin, False)
         attended = attended[None]
         att_other = swapped(attended, "col")
         weights, late = ([lax.all_gather(w, ("far", "near"), axis=0, tiled=True)] for w in (mine, theirs))
@@ -367,7 +386,7 @@
 
     (partial,) = project(where, kinds, attended, att_other, weights)
     hidden, stat = project(where, late_kinds, attended, att_other, late, partial, (gain, erase_in, mean))
-    return finish(model_width, stat, swapped(stat, "col"), gain, out_w, hidden)
+    return finish(model_width, stat, swapped(stat, "col"), gain, erase_out, hidden)
 
 
 def solution(mesh):

time: 165 us -> 140 us (0.85)
  local copies, waits for them, and re-layouts: 32.4 us -> 2.42 us
  waiting for transfers between devices: 67.6 us -> 73.7 us
    ppermute x14 -> x13, waiting for transfers between devices: 51.8 us -> 23.7 us  [swapped(): return lax.ppermute(block, axis, [(0, 1), (1, 0)])]
    unnamed x69 -> x19, local copies, waits for them, and re-layouts: 26.1 us -> 1.14 us
    ppermute x5, waiting for transfers between devices: 12.4 us -> 30.8 us  [on_device(): ring = lambda block: lax.ppermute(block, 'far', hops)]
    ppermute x2 -> x1, waiting for transfers between devices: 3.46 us -> 19.2 us  [on_device(): from_behind = lambda block: lax.ppermute(block, 'far', ahead)]
    ppermute x5, starting transfers between devices: 4.93 us -> 10.3 us  [on_device(): ring = lambda block: lax.ppermute(block, 'far', hops)]
    ppermute x2 -> x1, starting transfers between devices: 8.57 us -> 4.56 us  [on_device(): from_behind = lambda block: lax.ppermute(block, 'far', ahead)]
    reduce_precision x1 -> x0, local copies, waits for them, and re-layouts: 2.62 us -> none  [split_high_low(): high = lax.reduce_precision(value, 8, 7)]
    ppermute x14 -> x13, starting transfers between devices: 13.9 us -> 12.8 us  [swapped(): return lax.ppermute(block, axis, [(0, 1), (1, 0)])]
  transfers between devices with their start and end apart: 21 -> 19, of which waited for: 14 -> 16; matrix products, arithmetic and copies ran while one was open for 8% -> 5% of each run, Pallas kernels for 13% -> 15%
where the time goes in v5:
time: 140 us; the launch traced here: 139 us
  waiting for transfers between devices  73.7 us (53%)
  Pallas kernels  28.8 us (21%)
  starting transfers between devices  27.6 us (20%)
  other arithmetic  6.7 us (5%)
  local copies, waits for them, and re-layouts  2.42 us (2%)
    ppermute x5, waiting for transfers between devices, on_device(): ring = lambda block: lax.ppermute(block, 'far', hops)  30.8 us
    ppermute x13, waiting for transfers between devices, swapped(): return lax.ppermute(block, axis, [(0, 1), (1, 0)])  23.7 us
    ppermute x1, waiting for transfers between devices, on_device(): from_behind = lambda block: lax.ppermute(block, 'far', ahead)  19.2 us
    pallas_call x2, Pallas kernels, project(): pl.pallas_call(functools.partial(project_kernel, kinds, first, last), gri...  14.1 us
    ppermute x13, starting transfers between devices, swapped(): return lax.ppermute(block, axis, [(0, 1), (1, 0)])  12.8 us
    pallas_call x1, Pallas kernels, attend(): pl.pallas_call(functools.partial(attend_kernel, tok, group, direct), grid...  11.4 us
    ppermute x5, starting transfers between devices, on_device(): ring = lambda block: lax.ppermute(block, 'far', hops)  10.3 us
    ppermute x1, starting transfers between devices, on_device(): from_behind = lambda block: lax.ppermute(block, 'far', ahead)  4.56 us
  transfers between devices with their start and end apart: 19, of which 16 were waited for; matrix products, arithmetic and copies ran while one was open for 5% of the time, Pallas kernels for 15%

profile of v5, /device:TPU:0, one launch (start us, length us, event | category | flops | bytes accessed | tf_op | source)
XLA Modules:
  0.0 139.4 jit_solution(4614637457738514813)
XLA Ops:
  2.9 4.6 %collective-permute-start = (bf16[512,1024]{1,0:T(8,128)(2,1)S(1)}, bf16[512,1024]{1,0:T(8,128)(2,1)S(1)}, u32[]{:S(2)}, u32[]{:S(2)}) collective-permute-start(bf16[512,1024]{1,0:T(8,128)(2,1)S(1)} %constant_dynamic-update-slice_fusion.k2.v2), channel_id=1, source_target_pairs={{0,4},{4,8},{8,12},{1,5},{5,9},{9,13},{2,6},{6,10},{10,14},{3,7},{... | collective-permute-start | bytes 3145736 | tf_op jit(solution)/shard_map/ppermute | solution.py:334
  7.5 2.2 %broadcast_select_fusion.1 = (bf16[128,2688]{1,0:T(8,128)(2,1)}, bf16[128,2688]{1,0:T(8,128)(2,1)S(1)}) fusion(bf16[128,2688]{1,0:T(8,128)(2,1)S(1)} %collective-permute-done.1, pred[]{:T(512)S(6)} %eq.6, bf16[128,5376]{1,0:T(8,128)(2,1)} %param.11, s32[]{:T(128)S(6)} %select_n.27), kind=kLoop, calls=%fused_computation.5 | loop fusion | flops 688128 | bytes 2752517 | tf_op jit(solution)/shard_map/jit(_where)/select_n | solution.py:357
  9.7 1.5 %collective-permute-start.2 = (bf16[128,2688]{1,0:T(8,128)(2,1)S(1)}, bf16[128,2688]{1,0:T(8,128)(2,1)}, u32[]{:S(2)}, u32[]{:S(2)}) collective-permute-start(bf16[128,2688]{1,0:T(8,128)(2,1)S(1)} %get-tuple-element.29.refs_0_), channel_id=1, source_target_pairs={{0,2},{2,0},{1,3},{3,1},{4,6},{6,4},{5,7},{7,5},{8,10},{10,8},{9,1... | collective-permute-start | bytes 2064392 | tf_op jit(solution)/shard_map/ppermute | solution.py:315
  11.3 19.2 %collective-permute-done.k0.v0 = bf16[512,1024]{1,0:T(8,128)(2,1)S(1)} collective-permute-done((bf16[512,1024]{1,0:T(8,128)(2,1)S(1)}, bf16[512,1024]{1,0:T(8,128)(2,1)S(1)}, u32[]{:S(2)}, u32[]{:S(2)}) %collective-permute-start) | collective-permute-done | bytes 1048608 | tf_op jit(solution)/shard_map/ppermute | solution.py:334
  31.6 1.5 %collective-permute-start.4 = (bf16[512,1024]{1,0:T(8,128)(2,1)}, bf16[512,1024]{1,0:T(8,128)(2,1)S(1)}, u32[]{:S(2)}, u32[]{:S(2)}) collective-permute-start(bf16[512,1024]{1,0:T(8,128)(2,1)} %broadcast_select_fusion), channel_id=1, source_target_pairs={{0,2},{2,0},{1,3},{3,1},{4,6},{6,4},{5,7},{7,5},{8,10},{10,8},{9,1... | collective-permute-start | bytes 3145736 | tf_op jit(solution)/shard_map/ppermute | solution.py:315
  33.1 2.5 %collective-permute-start.3 = (bf16[128,2688]{1,0:T(8,128)(2,1)}, bf16[128,2688]{1,0:T(8,128)(2,1)}, u32[]{:S(2)}, u32[]{:S(2)}) collective-permute-start(bf16[128,2688]{1,0:T(8,128)(2,1)} %copy-done.2), channel_id=1, source_target_pairs={{0,4},{4,12},{12,8},{8,0},{1,5},{5,13},{13,9},{9,1},{2,6},{6,14},{... | collective-permute-start | bytes 2064392 | tf_op jit(solution)/shard_map/ppermute | solution.py:352
  37.1 2.8 %fusion = (f32[1536,64]{1,0:T(8,128)S(1)}, f32[1536,64]{1,0:T(8,128)S(1)}, f32[1536,64]{1,0:T(8,128)S(1)}) fusion(f32[64]{0:T(128)S(1)} %multiply_exponential_fusion, f32[1536]{0:T(1024)S(1)} %add_convert_fusion), kind=kLoop, calls=%fused_computation.7 | loop fusion | flops 196608 | bytes 1186048 | tf_op jit(solution)/shard_map/neg | solution.py:34
  40.4 11.6 %collective-permute-done.3.refs_1_ = bf16[128,2688]{1,0:T(8,128)(2,1)} collective-permute-done((bf16[128,2688]{1,0:T(8,128)(2,1)}, bf16[128,2688]{1,0:T(8,128)(2,1)}, u32[]{:S(2)}, u32[]{:S(2)}) %collective-permute-start.3) | collective-permute-done | bytes 688160 | tf_op jit(solution)/shard_map/ppermute | solution.py:352
  52.4 4.2 %collective-permute-done.4.k1.v1 = bf16[512,1024]{1,0:T(8,128)(2,1)S(1)} collective-permute-done((bf16[512,1024]{1,0:T(8,128)(2,1)}, bf16[512,1024]{1,0:T(8,128)(2,1)S(1)}, u32[]{:S(2)}, u32[]{:S(2)}) %collective-permute-start.4) | collective-permute-done | bytes 1048608 | tf_op jit(solution)/shard_map/ppermute | solution.py:315
  56.6 2.5 %collective-permute-start.6 = (bf16[128,2688]{1,0:T(8,128)(2,1)}, bf16[128,2688]{1,0:T(8,128)(2,1)S(1)}, u32[]{:S(2)}, u32[]{:S(2)}) collective-permute-start(bf16[128,2688]{1,0:T(8,128)(2,1)} %collective-permute-done.3.refs_1_), channel_id=1, source_target_pairs={{0,4},{4,12},{12,8},{8,0},{1,5},{5,13},{13,9},{9,1},{2,6},{6,14},{... | collective-permute-start | bytes 2064392 | tf_op jit(solution)/shard_map/ppermute | solution.py:352
  59.1 1.5 %collective-permute-start.7 = (bf16[128,2688]{1,0:T(8,128)(2,1)}, bf16[128,2688]{1,0:T(8,128)(2,1)S(1)}, u32[]{:S(2)}, u32[]{:S(2)}) collective-permute-start(bf16[128,2688]{1,0:T(8,128)(2,1)} %collective-permute-done.3.refs_1_), channel_id=1, source_target_pairs={{0,2},{2,0},{1,3},{3,1},{4,6},{6,4},{5,7},{7,5},{8,10},{10,8},{9,1... | collective-permute-start | bytes 2064392 | tf_op jit(solution)/shard_map/ppermute | solution.py:315
  62.1 11.4 %shard_map.82.own_ref = bf16[8,512,128]{2,1,0:T(8,128)(2,1)S(1)} custom-call(s32[1]{0:T(128)} %bitcast.3.row_ref, bf16[512,1024]{1,0:T(8,128)(2,1)S(1)} %copy-done, bf16[512,1024]{1,0:T(8,128)(2,1)S(1)} %collective-permute-done.k0.v0, bf16[512,1024]{1,0:T(8,128)(2,1)S(1)} %collective-permute-done.4.k1.v1, ...), custom_call_target="tpu_custom_call" | custom-call | flops 2684354560 | bytes 6291456 | tf_op jit(solution)/shard_map/pallas_call | solution.py:105
  78.4 2.6 %collective-permute-start.9 = (bf16[128,2688]{1,0:T(8,128)(2,1)S(1)}, bf16[128,2688]{1,0:T(8,128)(2,1)S(1)}, u32[]{:S(2)}, u32[]{:S(2)}) collective-permute-start(bf16[128,2688]{1,0:T(8,128)(2,1)S(1)} %collective-permute-done.6.refs_2_), channel_id=1, source_target_pairs={{0,4},{4,12},{12,8},{8,0},{1,5},{5,13},{13,9},{9,1},{2,6},{6,14},{... | collective-permute-start | bytes 2064392 | tf_op jit(solution)/shard_map/ppermute | solution.py:352
  82.0 12.2 %collective-permute-done.10.refs_6_ = bf16[128,2688]{1,0:T(8,128)(2,1)S(1)} collective-permute-done((bf16[128,2688]{1,0:T(8,128)(2,1)S(1)}, bf16[128,2688]{1,0:T(8,128)(2,1)S(1)}, u32[]{:S(2)}, u32[]{:S(2)}) %collective-permute-start.10) | collective-permute-done | bytes 688160 | tf_op jit(solution)/shard_map/ppermute | solution.py:315
  94.5 3.1 %collective-permute-done.9.refs_3_ = bf16[128,2688]{1,0:T(8,128)(2,1)S(1)} collective-permute-done((bf16[128,2688]{1,0:T(8,128)(2,1)S(1)}, bf16[128,2688]{1,0:T(8,128)(2,1)S(1)}, u32[]{:S(2)}, u32[]{:S(2)}) %collective-permute-start.9) | collective-permute-done | bytes 688160 | tf_op jit(solution)/shard_map/ppermute | solution.py:352
  97.6 1.5 %collective-permute-start.14 = (bf16[128,2688]{1,0:T(8,128)(2,1)S(1)}, bf16[128,2688]{1,0:T(8,128)(2,1)S(1)}, u32[]{:S(2)}, u32[]{:S(2)}) collective-permute-start(bf16[128,2688]{1,0:T(8,128)(2,1)S(1)} %collective-permute-done.9.refs_3_), channel_id=1, source_target_pairs={{0,2},{2,0},{1,3},{3,1},{4,6},{6,4},{5,7},{7,5},{8,10},{10,8},{9,1... | collective-permute-start | bytes 2064392 | tf_op jit(solution)/shard_map/ppermute | solution.py:315
  99.7 11.7 %collective-permute-done.13.refs_10_ = bf16[128,2688]{1,0:T(8,128)(2,1)S(1)} collective-permute-done((bf16[128,2688]{1,0:T(8,128)(2,1)S(1)}, bf16[128,2688]{1,0:T(8,128)(2,1)S(1)}, u32[]{:S(2)}, u32[]{:S(2)}) %collective-permute-start.13) | collective-permute-done | bytes 688160 | tf_op jit(solution)/shard_map/ppermute | solution.py:352
  111.3 1.7 %collective-permute-done.14.refs_7_ = bf16[128,2688]{1,0:T(8,128)(2,1)S(1)} collective-permute-done((bf16[128,2688]{1,0:T(8,128)(2,1)S(1)}, bf16[128,2688]{1,0:T(8,128)(2,1)S(1)}, u32[]{:S(2)}, u32[]{:S(2)}) %collective-permute-start.14) | collective-permute-done | bytes 688160 | tf_op jit(solution)/shard_map/ppermute | solution.py:315
  114.3 1.7 %collective-permute-start.16 = (bf16[128,2688]{1,0:T(8,128)(2,1)S(1)}, bf16[128,2688]{1,0:T(8,128)(2,1)S(1)}, u32[]{:S(2)}, u32[]{:S(2)}) collective-permute-start(bf16[128,2688]{1,0:T(8,128)(2,1)S(1)} %collective-permute-done.13.refs_10_), channel_id=1, source_target_pairs={{0,4},{4,12},{12,8},{8,0},{1,5},{5,13},{13,9},{9,1},{2,6},{6,14},{... | collective-permute-start | bytes 2064392 | tf_op jit(solution)/shard_map/ppermute | solution.py:352
  116.6 9.5 %shard_map.83.refs_2_ = f32[512,2688]{1,0:T(8,128)S(1)} custom-call(s32[4]{0:T(128)S(1)} %pad_add_fusion.where_ref, bf16[8,512,128]{2,1,0:T(8,128)(2,1)S(1)} %shard_map.82.own_ref, bf16[8,512,128]{2,1,0:T(8,128)(2,1)S(1)} %collective-permute-done.12.other_ref, bf16[128,2688]{1,0:T(8,128)(2,1)S(1)} %copy-done.3, ...), custom_call_target="tpu_custom_call" | custom-call | flops 4932501504 | bytes 9633792 | tf_op jit(solution)/shard_map/pallas_call | solution.py:251
  126.1 3.2 %collective-permute-done.16.refs_0_ = bf16[128,2688]{1,0:T(8,128)(2,1)S(1)} collective-permute-done((bf16[128,2688]{1,0:T(8,128)(2,1)S(1)}, bf16[128,2688]{1,0:T(8,128)(2,1)S(1)}, u32[]{:S(2)}, u32[]{:S(2)}) %collective-permute-start.16) | collective-permute-done | bytes 688160 | tf_op jit(solution)/shard_map/ppermute | solution.py:352
  129.9 4.7 %shard_map.84 = (f32[512,2688]{1,0:T(8,128)S(1)}, f32[520,128]{1,0:T(8,128)S(1)}) custom-call(s32[4]{0:T(128)S(1)} %pad_add_fusion.where_ref, bf16[8,512,128]{2,1,0:T(8,128)(2,1)S(1)} %shard_map.82.own_ref, bf16[8,512,128]{2,1,0:T(8,128)(2,1)S(1)} %collective-permute-done.12.other_ref, bf16[128,2688]{1,0:T(8,128)(2,1)S(1)} %collective-permute-done.16.refs_0_, ...), custom_call_target="tpu_custom_call" | custom-call | flops 704643072 | bytes 1376256 | tf_op jit(solution)/shard_map/pallas_call | solution.py:251
  134.6 1.5 %collective-permute-done.18.other_ref = f32[520,128]{1,0:T(8,128)S(1)} collective-permute-done((f32[520,128]{1,0:T(8,128)S(1)}, f32[520,128]{1,0:T(8,128)S(1)}, u32[]{:S(2)}, u32[]{:S(2)}) %collective-permute-start.18) | collective-permute-done | bytes 266272 | tf_op jit(solution)/shard_map/ppermute | solution.py:315
  136.2 3.2 %shard_map.85 = bf16[512,2688]{1,0:T(8,128)(2,1)} custom-call(f32[520,128]{1,0:T(8,128)S(1)} %get-tuple-element.49.own_ref, f32[520,128]{1,0:T(8,128)S(1)} %collective-permute-done.18.other_ref, f32[1,2688]{1,0:T(1,128)S(1)} %broadcast_in_dim.12.refs_3_.gain_ref, f32[64,2688]{1,0:T(8,128)S(1)} %bitcast.7, f32[512,2688]{1,0:T(8,128)S(1)} %get-tuple-element.50.hidden_ref), custom_call_target="tpu_custom_call" | custom-call | flops 704643072 | bytes 8257536 | tf_op jit(solution)/shard_map/pallas_call | solution.py:294
  (48 shorter events, 17.1 us)
Async XLA Ops:
  1.2 6.3 %collective-permute-start.1 = (bf16[128,2688]{1,0:T(8,128)(2,1)S(1)}, bf16[128,2688]{1,0:T(8,128)(2,1)S(1)}, u32[]{:S(2)}, u32[]{:S(2)}) collective-permute-start(bf16[128,2688]{1,0:T(8,128)(2,1)S(1)} %constant_dynamic-slice_fusion), channel_id=1, source_target_pairs={{0,1},{1,0},{2,3},{3,2},{4,5},{5,4},{6,7},{7,6},{8,9},{9,8},{10,11... | collective-permute-start | bytes 2064392 | tf_op jit(solution)/shard_map/ppermute | solution.py:315
  2.9 27.6 %collective-permute-start = (bf16[512,1024]{1,0:T(8,128)(2,1)S(1)}, bf16[512,1024]{1,0:T(8,128)(2,1)S(1)}, u32[]{:S(2)}, u32[]{:S(2)}) collective-permute-start(bf16[512,1024]{1,0:T(8,128)(2,1)S(1)} %constant_dynamic-update-slice_fusion.k2.v2), channel_id=1, source_target_pairs={{0,4},{4,8},{8,12},{1,5},{5,9},{9,13},{2,6},{6,10},{10,14},{3,7},{... | collective-permute-start | bytes 3145736 | tf_op jit(solution)/shard_map/ppermute | solution.py:334
  9.7 20.8 %collective-permute-start.2 = (bf16[128,2688]{1,0:T(8,128)(2,1)S(1)}, bf16[128,2688]{1,0:T(8,128)(2,1)}, u32[]{:S(2)}, u32[]{:S(2)}) collective-permute-start(bf16[128,2688]{1,0:T(8,128)(2,1)S(1)} %get-tuple-element.29.refs_0_), channel_id=1, source_target_pairs={{0,2},{2,0},{1,3},{3,1},{4,6},{6,4},{5,7},{7,5},{8,10},{10,8},{9,1... | collective-permute-start | bytes 2064392 | tf_op jit(solution)/shard_map/ppermute | solution.py:315
  31.6 25.0 %collective-permute-start.4 = (bf16[512,1024]{1,0:T(8,128)(2,1)}, bf16[512,1024]{1,0:T(8,128)(2,1)S(1)}, u32[]{:S(2)}, u32[]{:S(2)}) collective-permute-start(bf16[512,1024]{1,0:T(8,128)(2,1)} %broadcast_select_fusion), channel_id=1, source_target_pairs={{0,2},{2,0},{1,3},{3,1},{4,6},{6,4},{5,7},{7,5},{8,10},{10,8},{9,1... | collective-permute-start | bytes 3145736 | tf_op jit(solution)/shard_map/ppermute | solution.py:315
  33.1 18.8 %collective-permute-start.3 = (bf16[128,2688]{1,0:T(8,128)(2,1)}, bf16[128,2688]{1,0:T(8,128)(2,1)}, u32[]{:S(2)}, u32[]{:S(2)}) collective-permute-start(bf16[128,2688]{1,0:T(8,128)(2,1)} %copy-done.2), channel_id=1, source_target_pairs={{0,4},{4,12},{12,8},{8,0},{1,5},{5,13},{13,9},{9,1},{2,6},{6,14},{... | collective-permute-start | bytes 2064392 | tf_op jit(solution)/shard_map/ppermute | solution.py:352
  35.6 16.8 %collective-permute-start.5 = (bf16[128,2688]{1,0:T(8,128)(2,1)}, bf16[128,2688]{1,0:T(8,128)(2,1)}, u32[]{:S(2)}, u32[]{:S(2)}) collective-permute-start(bf16[128,2688]{1,0:T(8,128)(2,1)} %collective-permute-done.2.refs_4_), channel_id=1, source_target_pairs={{0,16},{16,0},{1,17},{17,1},{2,18},{18,2},{3,19},{19,3},{4,20},{20... | collective-permute-start | bytes 2064392 | tf_op jit(solution)/shard_map/ppermute | solution.py:315
  37.1 25.0 %copy-start = (bf16[512,1024]{1,0:T(8,128)(2,1)S(1)}, bf16[512,1024]{1,0:T(8,128)(2,1)}, u32[]{:S(2)}) copy-start(bf16[512,1024]{1,0:T(8,128)(2,1)} %q_ref.1) | copy-start | bytes 3145732
  56.6 18.1 %collective-permute-start.6 = (bf16[128,2688]{1,0:T(8,128)(2,1)}, bf16[128,2688]{1,0:T(8,128)(2,1)S(1)}, u32[]{:S(2)}, u32[]{:S(2)}) collective-permute-start(bf16[128,2688]{1,0:T(8,128)(2,1)} %collective-permute-done.3.refs_1_), channel_id=1, source_target_pairs={{0,4},{4,12},{12,8},{8,0},{1,5},{5,13},{13,9},{9,1},{2,6},{6,14},{... | collective-permute-start | bytes 2064392 | tf_op jit(solution)/shard_map/ppermute | solution.py:352
  59.1 16.1 %collective-permute-start.7 = (bf16[128,2688]{1,0:T(8,128)(2,1)}, bf16[128,2688]{1,0:T(8,128)(2,1)S(1)}, u32[]{:S(2)}, u32[]{:S(2)}) collective-permute-start(bf16[128,2688]{1,0:T(8,128)(2,1)} %collective-permute-done.3.refs_1_), channel_id=1, source_target_pairs={{0,2},{2,0},{1,3},{3,1},{4,6},{6,4},{5,7},{7,5},{8,10},{10,8},{9,1... | collective-permute-start | bytes 2064392 | tf_op jit(solution)/shard_map/ppermute | solution.py:315
  60.6 15.8 %collective-permute-start.8 = (bf16[128,2688]{1,0:T(8,128)(2,1)}, bf16[128,2688]{1,0:T(8,128)(2,1)S(1)}, u32[]{:S(2)}, u32[]{:S(2)}) collective-permute-start(bf16[128,2688]{1,0:T(8,128)(2,1)} %collective-permute-done.3.refs_1_), channel_id=1, source_target_pairs={{0,16},{16,0},{1,17},{17,1},{2,18},{18,2},{3,19},{19,3},{4,20},{20... | collective-permute-start | bytes 2064392 | tf_op jit(solution)/shard_map/ppermute | solution.py:315
  62.1 54.5 %copy-start.7 = (f32[2688]{0:T(1024)S(1)}, f32[2688]{0:T(1024)}, u32[]{:S(2)}) copy-start(f32[2688]{0:T(1024)} %param.12) | copy-start | bytes 32260
  62.1 54.5 %copy-start.8 = (f32[2688]{0:T(1024)S(1)}, f32[2688]{0:T(1024)}, u32[]{:S(2)}) copy-start(f32[2688]{0:T(1024)} %param.13) | copy-start | bytes 32260
  62.1 54.5 %copy-start.1 = (bf16[128,2688]{1,0:T(8,128)(2,1)S(1)}, bf16[128,2688]{1,0:T(8,128)(2,1)}, u32[]{:S(2)}) copy-start(bf16[128,2688]{1,0:T(8,128)(2,1)} %get-tuple-element.51.refs_8_) | copy-start | bytes 2064388
  62.1 54.5 %copy-start.3 = (bf16[128,2688]{1,0:T(8,128)(2,1)S(1)}, bf16[128,2688]{1,0:T(8,128)(2,1)}, u32[]{:S(2)}) copy-start(bf16[128,2688]{1,0:T(8,128)(2,1)} %copy-done.2) | copy-start | bytes 2064388
  76.4 21.2 %collective-permute-start.12 = (bf16[8,512,128]{2,1,0:T(8,128)(2,1)S(1)}, bf16[8,512,128]{2,1,0:T(8,128)(2,1)S(1)}, u32[]{:S(2)}, u32[]{:S(2)}) collective-permute-start(bf16[8,512,128]{2,1,0:T(8,128)(2,1)S(1)} %shard_map.82.own_ref), channel_id=1, source_target_pairs={{0,1},{1,0},{2,3},{3,2},{4,5},{5,4},{6,7},{7,6},{8,9},{9,8},{10,11... | collective-permute-start | bytes 3145736 | tf_op jit(solution)/shard_map/ppermute | solution.py:315
  76.4 17.8 %collective-permute-start.10 = (bf16[128,2688]{1,0:T(8,128)(2,1)S(1)}, bf16[128,2688]{1,0:T(8,128)(2,1)S(1)}, u32[]{:S(2)}, u32[]{:S(2)}) collective-permute-start(bf16[128,2688]{1,0:T(8,128)(2,1)S(1)} %collective-permute-done.6.refs_2_), channel_id=1, source_target_pairs={{0,2},{2,0},{1,3},{3,1},{4,6},{6,4},{5,7},{7,5},{8,10},{10,8},{9,1... | collective-permute-start | bytes 2064392 | tf_op jit(solution)/shard_map/ppermute | solution.py:315
  76.9 17.6 %collective-permute-start.11 = (bf16[128,2688]{1,0:T(8,128)(2,1)S(1)}, bf16[128,2688]{1,0:T(8,128)(2,1)S(1)}, u32[]{:S(2)}, u32[]{:S(2)}) collective-permute-start(bf16[128,2688]{1,0:T(8,128)(2,1)S(1)} %collective-permute-done.7.refs_5_), channel_id=1, source_target_pairs={{0,16},{16,0},{1,17},{17,1},{2,18},{18,2},{3,19},{19,3},{4,20},{20... | collective-permute-start | bytes 2064392 | tf_op jit(solution)/shard_map/ppermute | solution.py:315
  78.4 19.2 %collective-permute-start.9 = (bf16[128,2688]{1,0:T(8,128)(2,1)S(1)}, bf16[128,2688]{1,0:T(8,128)(2,1)S(1)}, u32[]{:S(2)}, u32[]{:S(2)}) collective-permute-start(bf16[128,2688]{1,0:T(8,128)(2,1)S(1)} %collective-permute-done.6.refs_2_), channel_id=1, source_target_pairs={{0,4},{4,12},{12,8},{8,0},{1,5},{5,13},{13,9},{9,1},{2,6},{6,14},{... | collective-permute-start | bytes 2064392 | tf_op jit(solution)/shard_map/ppermute | solution.py:352
  81.0 30.3 %collective-permute-start.13 = (bf16[128,2688]{1,0:T(8,128)(2,1)S(1)}, bf16[128,2688]{1,0:T(8,128)(2,1)S(1)}, u32[]{:S(2)}, u32[]{:S(2)}) collective-permute-start(bf16[128,2688]{1,0:T(8,128)(2,1)S(1)} %collective-permute-done.8.refs_9_), channel_id=1, source_target_pairs={{0,4},{4,12},{12,8},{8,0},{1,5},{5,13},{13,9},{9,1},{2,6},{6,14},{... | collective-permute-start | bytes 2064392 | tf_op jit(solution)/shard_map/ppermute | solution.py:352
  97.6 15.4 %collective-permute-start.14 = (bf16[128,2688]{1,0:T(8,128)(2,1)S(1)}, bf16[128,2688]{1,0:T(8,128)(2,1)S(1)}, u32[]{:S(2)}, u32[]{:S(2)}) collective-permute-start(bf16[128,2688]{1,0:T(8,128)(2,1)S(1)} %collective-permute-done.9.refs_3_), channel_id=1, source_target_pairs={{0,2},{2,0},{1,3},{3,1},{4,6},{6,4},{5,7},{7,5},{8,10},{10,8},{9,1... | collective-permute-start | bytes 2064392 | tf_op jit(solution)/shard_map/ppermute | solution.py:315
  99.1 15.1 %collective-permute-start.15 = (bf16[128,2688]{1,0:T(8,128)(2,1)S(1)}, bf16[128,2688]{1,0:T(8,128)(2,1)S(1)}, u32[]{:S(2)}, u32[]{:S(2)}) collective-permute-start(bf16[128,2688]{1,0:T(8,128)(2,1)S(1)} %collective-permute-done.10.refs_6_), channel_id=1, source_target_pairs={{0,16},{16,0},{1,17},{17,1},{2,18},{18,2},{3,19},{19,3},{4,20},{20... | collective-permute-start | bytes 2064392 | tf_op jit(solution)/shard_map/ppermute | solution.py:315
  114.3 15.1 %collective-permute-start.16 = (bf16[128,2688]{1,0:T(8,128)(2,1)S(1)}, bf16[128,2688]{1,0:T(8,128)(2,1)S(1)}, u32[]{:S(2)}, u32[]{:S(2)}) collective-permute-start(bf16[128,2688]{1,0:T(8,128)(2,1)S(1)} %collective-permute-done.13.refs_10_), channel_id=1, source_target_pairs={{0,4},{4,12},{12,8},{8,0},{1,5},{5,13},{13,9},{9,1},{2,6},{6,14},{... | collective-permute-start | bytes 2064392 | tf_op jit(solution)/shard_map/ppermute | solution.py:352
  116.0 13.9 %collective-permute-start.17 = (bf16[128,2688]{1,0:T(8,128)(2,1)S(1)}, bf16[128,2688]{1,0:T(8,128)(2,1)S(1)}, u32[]{:S(2)}, u32[]{:S(2)}) collective-permute-start(bf16[128,2688]{1,0:T(8,128)(2,1)S(1)} %collective-permute-done.14.refs_7_), channel_id=1, source_target_pairs={{0,16},{16,0},{1,17},{17,1},{2,18},{18,2},{3,19},{19,3},{4,20},{20... | collective-permute-start | bytes 2064392 | tf_op jit(solution)/shard_map/ppermute | solution.py:315
  134.6 1.6 %collective-permute-start.18 = (f32[520,128]{1,0:T(8,128)S(1)}, f32[520,128]{1,0:T(8,128)S(1)}, u32[]{:S(2)}, u32[]{:S(2)}) collective-permute-start(f32[520,128]{1,0:T(8,128)S(1)} %get-tuple-element.49.own_ref), channel_id=1, source_target_pairs={{0,1},{1,0},{2,3},{3,2},{4,5},{5,4},{6,7},{7,6},{8,9},{9,8},{10,11... | collective-permute-start | bytes 798728 | tf_op jit(solution)/shard_map/ppermute | solution.py:315
  (4 other events, 43.2 us)

commit v6 on v5

--- a/solution.py
+++ b/solution.py
@@ -89,11 +89,10 @@
                 out_ref[lo:hi, h * HD : (h + 1) * HD] = block
 
 
-def attend(row, queries, blocks, cos, sin, direct):
-    tok, kv_local = queries.shape[0], blocks[0].shape[1] // HD // 2
+def attend(row, queries, key_blocks, val_blocks, cos, sin, direct):
+    tok, kv_local = queries.shape[0], key_blocks[0].shape[1] // HD
     group = queries.shape[1] // HD // kv_local
-    key_block = pl.BlockSpec((tok, HD), lambda g, r: (0, g))
-    val_block = pl.BlockSpec((tok, HD), lambda g, r: (0, g + kv_local))
+    head_block = pl.BlockSpec((tok, HD), lambda g, r: (0, g))
     table = pl.BlockSpec((3 * tok, HD), lambda g, r: (0, 0))
     if direct:
         out_shape = (kv_local * group, tok, HD)
@@ -107,7 +106,7 @@
         grid_spec=pltpu.PrefetchScalarGridSpec(
             num_scalar_prefetch=1,
             grid=(kv_local,),
-            in_specs=[pl.BlockSpec((tok, group * HD), lambda g, r: (0, g))] + [key_block] * 3 + [val_block] * 3 + [table] * 2,
+            in_specs=[pl.BlockSpec((tok, group * HD), lambda g, r: (0, g))] + [head_block] * 6 + [table] * 2,
             out_specs=out_spec,
         ),
         out_shape=jax.ShapeDtypeStruct(out_shape, jnp.bfloat16),
@@ -115,7 +114,7 @@
         cost_estimate=pl.CostEstimate(
             flops=heads * tok * 10 * tok * HD, bytes_accessed=6 * 2**20, transcendentals=heads * tok * 2 * tok
         ),
-    )(row, queries, *blocks, *blocks, cos, sin)
+    )(row, queries, *key_blocks, *val_blocks, cos, sin)
 
 
 def ring_place(position, size):
@@ -334,11 +333,12 @@
     from_behind = lambda block: lax.ppermute(block, "far", ahead)
     hold = lax.optimization_barrier
 
-    def for_next(second):
-        return swapped(jnp.where(near == 0, both, second), "near")
-
-    both = jnp.concatenate([keys, values], 1)
-    second = from_behind(both)
+    def for_next(own, second):
+        return swapped(jnp.where(near == 0, own, second), "near")
+
+    def after(block, *earlier):
+        return hold((block, earlier))[0]
+
     theirs = swapped(lax.dynamic_slice_in_dim(out_proj, (1 - col) * width, width, 1), "col")
     mine = lax.dynamic_slice_in_dim(out_proj, col * width, width, 1)
     gain, mean = post_gain[None, :], mean_vec[None, :]
@@ -356,16 +356,26 @@
         main[0] = jnp.where(is_mine, mine, theirs)
         across[0] = jnp.where(is_mine, theirs, mine)
         beside[0] = beyond(main[0])
-        second, beside[0], main[0], row, where = hold((second, beside[0], main[0], row, where))
-        main[1], first, corner[0] = ring(main[0]), for_next(second), facing(beside[0])
-        cos, sin = rope_tables((row - 2) * tok, 3 * tok)
-        main[1], first, corner[0], cos, sin = hold((main[1], first, corner[0], cos, sin))
+        second_keys = from_behind(after(keys, main[0]))
+        second_values = from_behind(after(values, second_keys))
+        first_keys = for_next(keys, after(second_keys, beside[0]))
+        corner[0] = facing(beside[0])
+        main[1] = ring(after(main[0], second_values))
+        first_values = for_next(values, after(second_values, first_keys))
+        cos, sin = rope_tables((after(row, beside[0]) - 2) * tok, 3 * tok)
+        main[1], first_keys, first_values, corner[0], cos, sin, where = hold(
+            (main[1], first_keys, first_values, corner[0], cos, sin, where)
+        )
         main[2], beside[1], across[1] = ring(main[1]), beyond(main[1]), facing(main[1])
-        attended = attend(row[None], queries, (second, first, both), cos, sin, True)
+        attended = attend(
+            row[None], queries, (second_keys, first_keys, keys), (second_values, first_values, values), cos, sin, True
+        )
         main[2], beside[1], across[1], attended = hold((main[2], beside[1], across[1], attended))
         main[3], beside[2], corner[1] = ring(main[2]), beyond(main[2]), facing(beside[1])
         att_other = swapped(attended, "col")
-        main[3], beside[2], corner[1], att_other = hold((main[3], beside[2], corner[1], att_other))
+        main[3], beside[2], corner[1], att_other, across[1] = hold(
+            (main[3], beside[2], corner[1], att_other, across[1])
+        )
         across[2], beside[3], corner[2] = ring(across[1]), beyond(main[3]), facing(beside[2])
         across[2], beside[3], corner[2] = hold((across[2], beside[3], corner[2]))
         across[3], corner[3] = ring(across[2]), facing(beside[3])
@@ -376,9 +386,12 @@
                 (late if is_late else weights).append(pieces[k])
                 (late_kinds if is_late else kinds).append((name, k))
     else:
-        first = for_next(second)
+        second_keys, second_values = from_behind(keys), from_behind(values)
+        first_keys, first_values = for_next(keys, second_keys), for_next(values, second_values)
         cos, sin = rope_tables((row - 2) * tok, 3 * tok)
-        attended = attend(row[None], queries, (second, first, both), cos, sin, False)
+        attended = attend(
+            row[None], queries, (second_keys, first_keys, keys), (second_values, first_values, values), cos, sin, False
+        )
         attended = attended[None]
         att_other = swapped(attended, "col")
         weights, late = ([lax.all_gather(w, ("far", "near"), axis=0, tiled=True)] for w in (mine, theirs))

time: 140 us -> 137 us (0.979)
    ppermute x13 -> x14, waiting for transfers between devices: 23.7 us -> 7.83 us  [swapped(): return lax.ppermute(block, axis, [(0, 1), (1, 0)])]
    ppermute x5, waiting for transfers between devices: 30.8 us -> 46.2 us  [on_device(): ring = lambda block: lax.ppermute(block, 'far', hops)]
    ppermute x1 -> x2, starting transfers between devices: 4.56 us -> 7.91 us  [on_device(): from_behind = lambda block: lax.ppermute(block, 'far', ahead)]
    ppermute x5, starting transfers between devices: 10.3 us -> 7.9 us  [on_device(): ring = lambda block: lax.ppermute(block, 'far', hops)]
    ppermute x13 -> x14, starting transfers between devices: 12.8 us -> 11.8 us  [swapped(): return lax.ppermute(block, axis, [(0, 1), (1, 0)])]
    ppermute x1 -> x2, waiting for transfers between devices: 19.2 us -> 18.6 us  [on_device(): from_behind = lambda block: lax.ppermute(block, 'far', ahead)]
  transfers between devices with their start and end apart: 19 -> 21, of which waited for: 16 -> 15; matrix products, arithmetic and copies ran while one was open for 5% -> 3% of each run, Pallas kernels for 15% -> 16%
where the time goes in v6:
time: 137 us; the launch traced here: 136 us
  waiting for transfers between devices  72.6 us (53%)
  Pallas kernels  29.2 us (21%)
  starting transfers between devices  27.6 us (20%)
  other arithmetic  5.64 us (4%)
    ppermute x5, waiting for transfers between devices, on_device(): ring = lambda block: lax.ppermute(block, 'far', hops)  46.2 us
    ppermute x2, waiting for transfers between devices, on_device(): from_behind = lambda block: lax.ppermute(block, 'far', ahead)  18.6 us
    pallas_call x2, Pallas kernels, project(): pl.pallas_call(functools.partial(project_kernel, kinds, first, last), gri...  14.3 us
    ppermute x14, starting transfers between devices, swapped(): return lax.ppermute(block, axis, [(0, 1), (1, 0)])  11.8 us
    pallas_call x1, Pallas kernels, attend(): pl.pallas_call(functools.partial(attend_kernel, tok, group, direct), grid...  11.7 us
    ppermute x2, starting transfers between devices, on_device(): from_behind = lambda block: lax.ppermute(block, 'far', ahead)  7.91 us
    ppermute x5, starting transfers between devices, on_device(): ring = lambda block: lax.ppermute(block, 'far', hops)  7.9 us
    ppermute x14, waiting for transfers between devices, swapped(): return lax.ppermute(block, axis, [(0, 1), (1, 0)])  7.83 us
  transfers between devices with their start and end apart: 21, of which 15 were waited for; matrix products, arithmetic and copies ran while one was open for 3% of the time, Pallas kernels for 16%

profile of v6, /device:TPU:0, one launch (start us, length us, event | category | flops | bytes accessed | tf_op | source)
XLA Modules:
  0.0 136.4 jit_solution(14612214539355937687)
XLA Ops:
  1.8 1.8 %collective-permute-done = bf16[128,2688]{1,0:T(8,128)(2,1)S(1)} collective-permute-done((bf16[128,2688]{1,0:T(8,128)(2,1)S(1)}, bf16[128,2688]{1,0:T(8,128)(2,1)S(1)}, u32[]{:S(2)}, u32[]{:S(2)}) %collective-permute-start) | collective-permute-done | bytes 688160 | tf_op jit(solution)/shard_map/ppermute | solution.py:314
  3.5 1.3 broadcast_select_fusion
  4.9 3.0 %collective-permute-start.4 = (bf16[128,2688]{1,0:T(8,128)(2,1)S(1)}, bf16[128,2688]{1,0:T(8,128)(2,1)}, u32[]{:S(2)}, u32[]{:S(2)}) collective-permute-start(bf16[128,2688]{1,0:T(8,128)(2,1)S(1)} %get-tuple-element.34.refs_0_), channel_id=1, source_target_pairs={{0,2},{2,0},{1,3},{3,1},{4,6},{6,4},{5,7},{7,5},{8,10},{10,8},{9,1... | collective-permute-start | bytes 2064392 | tf_op jit(solution)/shard_map/ppermute | solution.py:314
  7.8 3.5 %collective-permute-start.1 = (bf16[512,512]{1,0:T(8,128)(2,1)S(1)}, bf16[512,512]{1,0:T(8,128)(2,1)S(1)}, u32[]{:S(2)}, u32[]{:S(2)}) collective-permute-start(bf16[512,512]{1,0:T(8,128)(2,1)S(1)} %copy-done.2), channel_id=1, source_target_pairs={{0,4},{4,8},{8,12},{1,5},{5,9},{9,13},{2,6},{6,10},{10,14},{3,7},{... | collective-permute-start | bytes 1572872 | tf_op jit(solution)/shard_map/ppermute | solution.py:333
  11.3 11.1 %collective-permute-done.1.k0 = bf16[512,512]{1,0:T(8,128)(2,1)S(1)} collective-permute-done((bf16[512,512]{1,0:T(8,128)(2,1)S(1)}, bf16[512,512]{1,0:T(8,128)(2,1)S(1)}, u32[]{:S(2)}, u32[]{:S(2)}) %collective-permute-start.1) | collective-permute-done | bytes 524320 | tf_op jit(solution)/shard_map/ppermute | solution.py:333
  22.5 4.4 %collective-permute-start.2 = (bf16[512,512]{1,0:T(8,128)(2,1)S(1)}, bf16[512,512]{1,0:T(8,128)(2,1)S(1)}, u32[]{:S(2)}, u32[]{:S(2)}) collective-permute-start(bf16[512,512]{1,0:T(8,128)(2,1)S(1)} %copy-done.3), channel_id=1, source_target_pairs={{0,4},{4,8},{8,12},{1,5},{5,9},{9,13},{2,6},{6,10},{10,14},{3,7},{... | collective-permute-start | bytes 1572872 | tf_op jit(solution)/shard_map/ppermute | solution.py:333
  28.4 1.5 %collective-permute-start.7 = (bf16[128,2688]{1,0:T(8,128)(2,1)}, bf16[128,2688]{1,0:T(8,128)(2,1)S(1)}, u32[]{:S(2)}, u32[]{:S(2)}) collective-permute-start(bf16[128,2688]{1,0:T(8,128)(2,1)} %collective-permute-done.4.refs_4_), channel_id=1, source_target_pairs={{0,16},{16,0},{1,17},{17,1},{2,18},{18,2},{3,19},{19,3},{4,20},{20... | collective-permute-start | bytes 2064392 | tf_op jit(solution)/shard_map/ppermute | solution.py:314
  29.9 7.4 %collective-permute-done.2.v0 = bf16[512,512]{1,0:T(8,128)(2,1)S(1)} collective-permute-done((bf16[512,512]{1,0:T(8,128)(2,1)S(1)}, bf16[512,512]{1,0:T(8,128)(2,1)S(1)}, u32[]{:S(2)}, u32[]{:S(2)}) %collective-permute-start.2) | collective-permute-done | bytes 524320 | tf_op jit(solution)/shard_map/ppermute | solution.py:333
  37.3 2.5 %collective-permute-start.3 = (bf16[128,2688]{1,0:T(8,128)(2,1)S(1)}, bf16[128,2688]{1,0:T(8,128)(2,1)S(1)}, u32[]{:S(2)}, u32[]{:S(2)}) collective-permute-start(bf16[128,2688]{1,0:T(8,128)(2,1)S(1)} %get-tuple-element.34.refs_0_), channel_id=1, source_target_pairs={{0,4},{4,12},{12,8},{8,0},{1,5},{5,13},{13,9},{9,1},{2,6},{6,14},{... | collective-permute-start | bytes 2064392 | tf_op jit(solution)/shard_map/ppermute | solution.py:352
  41.4 2.8 %fusion = (f32[1536,64]{1,0:T(8,128)S(1)}, f32[1536,64]{1,0:T(8,128)S(1)}, f32[1536,64]{1,0:T(8,128)S(1)}) fusion(f32[64]{0:T(128)S(1)} %multiply_exponential_fusion, f32[1536]{0:T(1024)S(1)} %add_convert_fusion), kind=kLoop, calls=%fused_computation.8 | loop fusion | flops 196608 | bytes 1186048 | tf_op jit(solution)/shard_map/neg | solution.py:34
  44.7 10.0 %collective-permute-done.3.refs_1_ = bf16[128,2688]{1,0:T(8,128)(2,1)S(1)} collective-permute-done((bf16[128,2688]{1,0:T(8,128)(2,1)S(1)}, bf16[128,2688]{1,0:T(8,128)(2,1)S(1)}, u32[]{:S(2)}, u32[]{:S(2)}) %collective-permute-start.3) | collective-permute-done | bytes 688160 | tf_op jit(solution)/shard_map/ppermute | solution.py:352
  54.7 1.5 %collective-permute-start.10 = (bf16[128,2688]{1,0:T(8,128)(2,1)S(1)}, bf16[128,2688]{1,0:T(8,128)(2,1)S(1)}, u32[]{:S(2)}, u32[]{:S(2)}) collective-permute-start(bf16[128,2688]{1,0:T(8,128)(2,1)S(1)} %collective-permute-done.3.refs_1_), channel_id=1, source_target_pairs={{0,16},{16,0},{1,17},{17,1},{2,18},{18,2},{3,19},{19,3},{4,20},{20... | collective-permute-start | bytes 2064392 | tf_op jit(solution)/shard_map/ppermute | solution.py:314
  57.5 11.7 %shard_map.82.own_ref = bf16[8,512,128]{2,1,0:T(8,128)(2,1)S(1)} custom-call(s32[1]{0:T(128)} %bitcast.3.row_ref, bf16[512,1024]{1,0:T(8,128)(2,1)S(1)} %copy-done.4, bf16[512,512]{1,0:T(8,128)(2,1)S(1)} %collective-permute-done.1.k0, bf16[512,512]{1,0:T(8,128)(2,1)} %collective-permute-done.5.k1, bf16[512,512]{1,0:T(8,128)(2,1)S(1)} %copy-done.2, ...), custom_call_target="tpu_custom_call" | custom-call | flops 2684354560 | bytes 6291456 | tf_op jit(solution)/shard_map/pallas_call | solution.py:104
  69.6 2.1 %collective-permute-done.8.refs_2_ = bf16[128,2688]{1,0:T(8,128)(2,1)S(1)} collective-permute-done((bf16[128,2688]{1,0:T(8,128)(2,1)S(1)}, bf16[128,2688]{1,0:T(8,128)(2,1)S(1)}, u32[]{:S(2)}, u32[]{:S(2)}) %collective-permute-start.8) | collective-permute-done | bytes 688160 | tf_op jit(solution)/shard_map/ppermute | solution.py:352
  71.7 2.8 %collective-permute-start.11 = (bf16[128,2688]{1,0:T(8,128)(2,1)S(1)}, bf16[128,2688]{1,0:T(8,128)(2,1)S(1)}, u32[]{:S(2)}, u32[]{:S(2)}) collective-permute-start(bf16[128,2688]{1,0:T(8,128)(2,1)S(1)} %collective-permute-done.8.refs_2_), channel_id=1, source_target_pairs={{0,4},{4,12},{12,8},{8,0},{1,5},{5,13},{13,9},{9,1},{2,6},{6,14},{... | collective-permute-start | bytes 2064392 | tf_op jit(solution)/shard_map/ppermute | solution.py:352
  75.5 14.9 %collective-permute-done.11.refs_3_ = bf16[128,2688]{1,0:T(8,128)(2,1)S(1)} collective-permute-done((bf16[128,2688]{1,0:T(8,128)(2,1)S(1)}, bf16[128,2688]{1,0:T(8,128)(2,1)S(1)}, u32[]{:S(2)}, u32[]{:S(2)}) %collective-permute-start.11) | collective-permute-done | bytes 688160 | tf_op jit(solution)/shard_map/ppermute | solution.py:352
  90.5 1.6 %collective-permute-done.12.refs_6_ = bf16[128,2688]{1,0:T(8,128)(2,1)S(1)} collective-permute-done((bf16[128,2688]{1,0:T(8,128)(2,1)S(1)}, bf16[128,2688]{1,0:T(8,128)(2,1)S(1)}, u32[]{:S(2)}, u32[]{:S(2)}) %collective-permute-start.12) | collective-permute-done | bytes 688160 | tf_op jit(solution)/shard_map/ppermute | solution.py:314
  93.5 1.5 %collective-permute-start.16 = (bf16[128,2688]{1,0:T(8,128)(2,1)S(1)}, bf16[128,2688]{1,0:T(8,128)(2,1)S(1)}, u32[]{:S(2)}, u32[]{:S(2)}) collective-permute-start(bf16[128,2688]{1,0:T(8,128)(2,1)S(1)} %collective-permute-done.11.refs_3_), channel_id=1, source_target_pairs={{0,2},{2,0},{1,3},{3,1},{4,6},{6,4},{5,7},{7,5},{8,10},{10,8},{9,1... | collective-permute-start | bytes 2064392 | tf_op jit(solution)/shard_map/ppermute | solution.py:314
  95.5 14.2 %collective-permute-done.15.refs_10_ = bf16[128,2688]{1,0:T(8,128)(2,1)S(1)} collective-permute-done((bf16[128,2688]{1,0:T(8,128)(2,1)S(1)}, bf16[128,2688]{1,0:T(8,128)(2,1)S(1)}, u32[]{:S(2)}, u32[]{:S(2)}) %collective-permute-start.15) | collective-permute-done | bytes 688160 | tf_op jit(solution)/shard_map/ppermute | solution.py:352
  112.1 9.6 %shard_map.83.refs_2_ = f32[512,2688]{1,0:T(8,128)S(1)} custom-call(s32[4]{0:T(128)S(1)} %pad_add_fusion.where_ref, bf16[8,512,128]{2,1,0:T(8,128)(2,1)S(1)} %shard_map.82.own_ref, bf16[8,512,128]{2,1,0:T(8,128)(2,1)S(1)} %collective-permute-done.14.other_ref, bf16[128,2688]{1,0:T(8,128)(2,1)S(1)} %get-tuple-element.34.refs_0_, ...), custom_call_target="tpu_custom_call" | custom-call | flops 4932501504 | bytes 9633792 | tf_op jit(solution)/shard_map/pallas_call | solution.py:250
  121.7 5.0 %collective-permute-done.18.refs_0_ = bf16[128,2688]{1,0:T(8,128)(2,1)S(1)} collective-permute-done((bf16[128,2688]{1,0:T(8,128)(2,1)S(1)}, bf16[128,2688]{1,0:T(8,128)(2,1)S(1)}, u32[]{:S(2)}, u32[]{:S(2)}) %collective-permute-start.18) | collective-permute-done | bytes 688160 | tf_op jit(solution)/shard_map/ppermute | solution.py:352
  126.9 4.7 %shard_map.84 = (f32[512,2688]{1,0:T(8,128)S(1)}, f32[520,128]{1,0:T(8,128)S(1)}) custom-call(s32[4]{0:T(128)S(1)} %pad_add_fusion.where_ref, bf16[8,512,128]{2,1,0:T(8,128)(2,1)S(1)} %shard_map.82.own_ref, bf16[8,512,128]{2,1,0:T(8,128)(2,1)S(1)} %collective-permute-done.14.other_ref, bf16[128,2688]{1,0:T(8,128)(2,1)S(1)} %collective-permute-done.18.refs_0_, ...), custom_call_target="tpu_custom_call" | custom-call | flops 704643072 | bytes 1376256 | tf_op jit(solution)/shard_map/pallas_call | solution.py:250
  131.6 1.5 %collective-permute-done.20.other_ref = f32[520,128]{1,0:T(8,128)S(1)} collective-permute-done((f32[520,128]{1,0:T(8,128)S(1)}, f32[520,128]{1,0:T(8,128)S(1)}, u32[]{:S(2)}, u32[]{:S(2)}) %collective-permute-start.20) | collective-permute-done | bytes 266272 | tf_op jit(solution)/shard_map/ppermute | solution.py:314
  133.1 3.2 %shard_map.85 = bf16[512,2688]{1,0:T(8,128)(2,1)} custom-call(f32[520,128]{1,0:T(8,128)S(1)} %get-tuple-element.57.own_ref, f32[520,128]{1,0:T(8,128)S(1)} %collective-permute-done.20.other_ref, f32[1,2688]{1,0:T(1,128)S(1)} %broadcast_in_dim.12.refs_3_.gain_ref, f32[64,2688]{1,0:T(8,128)S(1)} %bitcast.7, f32[512,2688]{1,0:T(8,128)S(1)} %get-tuple-element.58.hidden_ref), custom_call_target="tpu_custom_call" | custom-call | flops 704643072 | bytes 8257536 | tf_op jit(solution)/shard_map/pallas_call | solution.py:293
  (47 shorter events, 12.7 us)
Async XLA Ops:
  0.0 22.5 %copy-start.3 = (bf16[512,512]{1,0:T(8,128)(2,1)S(1)}, bf16[512,512]{1,0:T(8,128)(2,1)}, u32[]{:S(2)}) copy-start(bf16[512,512]{1,0:T(8,128)(2,1)} %v2.1) | copy-start | bytes 1572868
  1.2 2.3 %collective-permute-start = (bf16[128,2688]{1,0:T(8,128)(2,1)S(1)}, bf16[128,2688]{1,0:T(8,128)(2,1)S(1)}, u32[]{:S(2)}, u32[]{:S(2)}) collective-permute-start(bf16[128,2688]{1,0:T(8,128)(2,1)S(1)} %constant_dynamic-slice_fusion), channel_id=1, source_target_pairs={{0,1},{1,0},{2,3},{3,2},{4,5},{5,4},{6,7},{7,6},{8,9},{9,8},{10,11... | collective-permute-start | bytes 2064392 | tf_op jit(solution)/shard_map/ppermute | solution.py:314
  4.9 22.0 %collective-permute-start.4 = (bf16[128,2688]{1,0:T(8,128)(2,1)S(1)}, bf16[128,2688]{1,0:T(8,128)(2,1)}, u32[]{:S(2)}, u32[]{:S(2)}) collective-permute-start(bf16[128,2688]{1,0:T(8,128)(2,1)S(1)} %get-tuple-element.34.refs_0_), channel_id=1, source_target_pairs={{0,2},{2,0},{1,3},{3,1},{4,6},{6,4},{5,7},{7,5},{8,10},{10,8},{9,1... | collective-permute-start | bytes 2064392 | tf_op jit(solution)/shard_map/ppermute | solution.py:314
  7.8 14.7 %collective-permute-start.1 = (bf16[512,512]{1,0:T(8,128)(2,1)S(1)}, bf16[512,512]{1,0:T(8,128)(2,1)S(1)}, u32[]{:S(2)}, u32[]{:S(2)}) collective-permute-start(bf16[512,512]{1,0:T(8,128)(2,1)S(1)} %copy-done.2), channel_id=1, source_target_pairs={{0,4},{4,8},{8,12},{1,5},{5,9},{9,13},{2,6},{6,10},{10,14},{3,7},{... | collective-permute-start | bytes 1572872 | tf_op jit(solution)/shard_map/ppermute | solution.py:333
  22.5 14.8 %collective-permute-start.2 = (bf16[512,512]{1,0:T(8,128)(2,1)S(1)}, bf16[512,512]{1,0:T(8,128)(2,1)S(1)}, u32[]{:S(2)}, u32[]{:S(2)}) collective-permute-start(bf16[512,512]{1,0:T(8,128)(2,1)S(1)} %copy-done.3), channel_id=1, source_target_pairs={{0,4},{4,8},{8,12},{1,5},{5,9},{9,13},{2,6},{6,10},{10,14},{3,7},{... | collective-permute-start | bytes 1572872 | tf_op jit(solution)/shard_map/ppermute | solution.py:333
  27.8 13.0 %collective-permute-start.5 = (bf16[512,512]{1,0:T(8,128)(2,1)}, bf16[512,512]{1,0:T(8,128)(2,1)}, u32[]{:S(2)}, u32[]{:S(2)}) collective-permute-start(bf16[512,512]{1,0:T(8,128)(2,1)} %broadcast_select_fusion.3), channel_id=1, source_target_pairs={{0,2},{2,0},{1,3},{3,1},{4,6},{6,4},{5,7},{7,5},{8,10},{10,8},{9,1... | collective-permute-start | bytes 1572872 | tf_op jit(solution)/shard_map/ppermute | solution.py:314
  28.4 16.3 %collective-permute-start.7 = (bf16[128,2688]{1,0:T(8,128)(2,1)}, bf16[128,2688]{1,0:T(8,128)(2,1)S(1)}, u32[]{:S(2)}, u32[]{:S(2)}) collective-permute-start(bf16[128,2688]{1,0:T(8,128)(2,1)} %collective-permute-done.4.refs_4_), channel_id=1, source_target_pairs={{0,16},{16,0},{1,17},{17,1},{2,18},{18,2},{3,19},{19,3},{4,20},{20... | collective-permute-start | bytes 2064392 | tf_op jit(solution)/shard_map/ppermute | solution.py:314
  37.3 17.4 %collective-permute-start.3 = (bf16[128,2688]{1,0:T(8,128)(2,1)S(1)}, bf16[128,2688]{1,0:T(8,128)(2,1)S(1)}, u32[]{:S(2)}, u32[]{:S(2)}) collective-permute-start(bf16[128,2688]{1,0:T(8,128)(2,1)S(1)} %get-tuple-element.34.refs_0_), channel_id=1, source_target_pairs={{0,4},{4,12},{12,8},{8,0},{1,5},{5,13},{13,9},{9,1},{2,6},{6,14},{... | collective-permute-start | bytes 2064392 | tf_op jit(solution)/shard_map/ppermute | solution.py:352
  40.8 13.8 %collective-permute-start.6 = (bf16[512,512]{1,0:T(8,128)(2,1)S(1)}, bf16[512,512]{1,0:T(8,128)(2,1)S(1)}, u32[]{:S(2)}, u32[]{:S(2)}) collective-permute-start(bf16[512,512]{1,0:T(8,128)(2,1)S(1)} %broadcast_select_fusion.2), channel_id=1, source_target_pairs={{0,2},{2,0},{1,3},{3,1},{4,6},{6,4},{5,7},{7,5},{8,10},{10,8},{9,1... | collective-permute-start | bytes 1572872 | tf_op jit(solution)/shard_map/ppermute | solution.py:314
  54.7 15.0 %collective-permute-start.10 = (bf16[128,2688]{1,0:T(8,128)(2,1)S(1)}, bf16[128,2688]{1,0:T(8,128)(2,1)S(1)}, u32[]{:S(2)}, u32[]{:S(2)}) collective-permute-start(bf16[128,2688]{1,0:T(8,128)(2,1)S(1)} %collective-permute-done.3.refs_1_), channel_id=1, source_target_pairs={{0,16},{16,0},{1,17},{17,1},{2,18},{18,2},{3,19},{19,3},{4,20},{20... | collective-permute-start | bytes 2064392 | tf_op jit(solution)/shard_map/ppermute | solution.py:314
  56.1 15.6 %collective-permute-start.8 = (bf16[128,2688]{1,0:T(8,128)(2,1)S(1)}, bf16[128,2688]{1,0:T(8,128)(2,1)S(1)}, u32[]{:S(2)}, u32[]{:S(2)}) collective-permute-start(bf16[128,2688]{1,0:T(8,128)(2,1)S(1)} %collective-permute-done.3.refs_1_), channel_id=1, source_target_pairs={{0,4},{4,12},{12,8},{8,0},{1,5},{5,13},{13,9},{9,1},{2,6},{6,14},{... | collective-permute-start | bytes 2064392 | tf_op jit(solution)/shard_map/ppermute | solution.py:352
  57.0 14.8 %collective-permute-start.9 = (bf16[128,2688]{1,0:T(8,128)(2,1)S(1)}, bf16[128,2688]{1,0:T(8,128)(2,1)S(1)}, u32[]{:S(2)}, u32[]{:S(2)}) collective-permute-start(bf16[128,2688]{1,0:T(8,128)(2,1)S(1)} %collective-permute-done.3.refs_1_), channel_id=1, source_target_pairs={{0,2},{2,0},{1,3},{3,1},{4,6},{6,4},{5,7},{7,5},{8,10},{10,8},{9,1... | collective-permute-start | bytes 2064392 | tf_op jit(solution)/shard_map/ppermute | solution.py:314
  57.5 54.6 %copy-start.5 = (f32[2688]{0:T(1024)S(1)}, f32[2688]{0:T(1024)}, u32[]{:S(2)}) copy-start(f32[2688]{0:T(1024)} %param.12) | copy-start | bytes 32260
  57.5 54.6 %copy-start.6 = (f32[2688]{0:T(1024)S(1)}, f32[2688]{0:T(1024)}, u32[]{:S(2)}) copy-start(f32[2688]{0:T(1024)} %param.13) | copy-start | bytes 32260
  71.7 20.6 %collective-permute-start.14 = (bf16[8,512,128]{2,1,0:T(8,128)(2,1)S(1)}, bf16[8,512,128]{2,1,0:T(8,128)(2,1)S(1)}, u32[]{:S(2)}, u32[]{:S(2)}) collective-permute-start(bf16[8,512,128]{2,1,0:T(8,128)(2,1)S(1)} %shard_map.82.own_ref), channel_id=1, source_target_pairs={{0,1},{1,0},{2,3},{3,2},{4,5},{5,4},{6,7},{7,6},{8,9},{9,8},{10,11... | collective-permute-start | bytes 3145736 | tf_op jit(solution)/shard_map/ppermute | solution.py:314
  71.7 18.7 %collective-permute-start.11 = (bf16[128,2688]{1,0:T(8,128)(2,1)S(1)}, bf16[128,2688]{1,0:T(8,128)(2,1)S(1)}, u32[]{:S(2)}, u32[]{:S(2)}) collective-permute-start(bf16[128,2688]{1,0:T(8,128)(2,1)S(1)} %collective-permute-done.8.refs_2_), channel_id=1, source_target_pairs={{0,4},{4,12},{12,8},{8,0},{1,5},{5,13},{13,9},{9,1},{2,6},{6,14},{... | collective-permute-start | bytes 2064392 | tf_op jit(solution)/shard_map/ppermute | solution.py:352
  74.5 17.6 %collective-permute-start.12 = (bf16[128,2688]{1,0:T(8,128)(2,1)S(1)}, bf16[128,2688]{1,0:T(8,128)(2,1)S(1)}, u32[]{:S(2)}, u32[]{:S(2)}) collective-permute-start(bf16[128,2688]{1,0:T(8,128)(2,1)S(1)} %collective-permute-done.8.refs_2_), channel_id=1, source_target_pairs={{0,2},{2,0},{1,3},{3,1},{4,6},{6,4},{5,7},{7,5},{8,10},{10,8},{9,1... | collective-permute-start | bytes 2064392 | tf_op jit(solution)/shard_map/ppermute | solution.py:314
  75.0 17.3 %collective-permute-start.13 = (bf16[128,2688]{1,0:T(8,128)(2,1)S(1)}, bf16[128,2688]{1,0:T(8,128)(2,1)S(1)}, u32[]{:S(2)}, u32[]{:S(2)}) collective-permute-start(bf16[128,2688]{1,0:T(8,128)(2,1)S(1)} %collective-permute-done.9.refs_5_), channel_id=1, source_target_pairs={{0,16},{16,0},{1,17},{17,1},{2,18},{18,2},{3,19},{19,3},{4,20},{20... | collective-permute-start | bytes 2064392 | tf_op jit(solution)/shard_map/ppermute | solution.py:314
  92.3 17.4 %collective-permute-start.15 = (bf16[128,2688]{1,0:T(8,128)(2,1)S(1)}, bf16[128,2688]{1,0:T(8,128)(2,1)S(1)}, u32[]{:S(2)}, u32[]{:S(2)}) collective-permute-start(bf16[128,2688]{1,0:T(8,128)(2,1)S(1)} %collective-permute-done.10.refs_9_), channel_id=1, source_target_pairs={{0,4},{4,12},{12,8},{8,0},{1,5},{5,13},{13,9},{9,1},{2,6},{6,14},{... | collective-permute-start | bytes 2064392 | tf_op jit(solution)/shard_map/ppermute | solution.py:352
  93.5 16.2 %collective-permute-start.16 = (bf16[128,2688]{1,0:T(8,128)(2,1)S(1)}, bf16[128,2688]{1,0:T(8,128)(2,1)S(1)}, u32[]{:S(2)}, u32[]{:S(2)}) collective-permute-start(bf16[128,2688]{1,0:T(8,128)(2,1)S(1)} %collective-permute-done.11.refs_3_), channel_id=1, source_target_pairs={{0,2},{2,0},{1,3},{3,1},{4,6},{6,4},{5,7},{7,5},{8,10},{10,8},{9,1... | collective-permute-start | bytes 2064392 | tf_op jit(solution)/shard_map/ppermute | solution.py:314
  95.0 15.9 %collective-permute-start.17 = (bf16[128,2688]{1,0:T(8,128)(2,1)S(1)}, bf16[128,2688]{1,0:T(8,128)(2,1)S(1)}, u32[]{:S(2)}, u32[]{:S(2)}) collective-permute-start(bf16[128,2688]{1,0:T(8,128)(2,1)S(1)} %collective-permute-done.12.refs_6_), channel_id=1, source_target_pairs={{0,16},{16,0},{1,17},{17,1},{2,18},{18,2},{3,19},{19,3},{4,20},{20... | collective-permute-start | bytes 2064392 | tf_op jit(solution)/shard_map/ppermute | solution.py:314
  110.9 15.8 %collective-permute-start.18 = (bf16[128,2688]{1,0:T(8,128)(2,1)S(1)}, bf16[128,2688]{1,0:T(8,128)(2,1)S(1)}, u32[]{:S(2)}, u32[]{:S(2)}) collective-permute-start(bf16[128,2688]{1,0:T(8,128)(2,1)S(1)} %collective-permute-done.15.refs_10_), channel_id=1, source_target_pairs={{0,4},{4,12},{12,8},{8,0},{1,5},{5,13},{13,9},{9,1},{2,6},{6,14},{... | collective-permute-start | bytes 2064392 | tf_op jit(solution)/shard_map/ppermute | solution.py:352
  111.5 15.4 %collective-permute-start.19 = (bf16[128,2688]{1,0:T(8,128)(2,1)S(1)}, bf16[128,2688]{1,0:T(8,128)(2,1)S(1)}, u32[]{:S(2)}, u32[]{:S(2)}) collective-permute-start(bf16[128,2688]{1,0:T(8,128)(2,1)S(1)} %collective-permute-done.16.refs_7_), channel_id=1, source_target_pairs={{0,16},{16,0},{1,17},{17,1},{2,18},{18,2},{3,19},{19,3},{4,20},{20... | collective-permute-start | bytes 2064392 | tf_op jit(solution)/shard_map/ppermute | solution.py:314
  131.5 1.6 %collective-permute-start.20 = (f32[520,128]{1,0:T(8,128)S(1)}, f32[520,128]{1,0:T(8,128)S(1)}, u32[]{:S(2)}, u32[]{:S(2)}) collective-permute-start(f32[520,128]{1,0:T(8,128)S(1)} %get-tuple-element.57.own_ref), channel_id=1, source_target_pairs={{0,1},{1,0},{2,3},{3,2},{4,5},{5,4},{6,7},{7,6},{8,9},{9,8},{10,11... | collective-permute-start | bytes 798728 | tf_op jit(solution)/shard_map/ppermute | solution.py:314
  (4 other events, 45.6 us)

commit v7 on v6

--- a/solution.py
+++ b/solution.py
@@ -112,7 +112,7 @@
         out_shape=jax.ShapeDtypeStruct(out_shape, jnp.bfloat16),
         compiler_params=pltpu.CompilerParams(vmem_limit_bytes=VMEM_LIMIT),
         cost_estimate=pl.CostEstimate(
-            flops=heads * tok * 10 * tok * HD, bytes_accessed=6 * 2**20, transcendentals=heads * tok * 2 * tok
+            flops=4 * heads * tok * 10 * tok * HD, bytes_accessed=6 * 2**20, transcendentals=heads * tok * 2 * tok
         ),
     )(row, queries, *key_blocks, *val_blocks, cos, sin)
 
@@ -135,9 +135,13 @@
     return other * slots + from_far * 2 + side
 
 
+def parts_of(kinds):
+    return sum(1 if kind is None else 2 for kind, _ in kinds)
+
+
 def project_kernel(kinds, first, last, where_ref, own_ref, other_ref, *refs):
-    count = len(kinds)
-    weights, refs = refs[:count], refs[count:]
+    count, parts = len(kinds), parts_of(kinds)
+    weights, refs = refs[:parts], refs[parts:]
     if not first:
         partial_ref, refs = refs[0], refs[1:]
     if last:
@@ -147,7 +151,8 @@
         stat_ref, refs = refs[0], refs[1:]
     heads, sems = refs[:2]
     step = pl.program_id(0)
-    depth = weights[0].shape[0]
+    share = weights[0].shape[0]
+    depth = parts // count * share
     if not last:
         blocks, block_sems = refs[2:]
         steps = pl.num_programs(0)
@@ -156,7 +161,7 @@
             slot = lax.rem(at, 2)
             for n, piece in enumerate(weights):
                 source = piece.at[:, pl.ds(pl.multiple_of(at * TILE, TILE), TILE)]
-                act(pltpu.make_async_copy(source, blocks.at[slot, n * depth : (n + 1) * depth], block_sems.at[slot, n]))
+                act(pltpu.make_async_copy(source, blocks.at[slot, n * share : (n + 1) * share], block_sems.at[slot, n]))
 
         @pl.when(step == 0)
         def _():
@@ -226,15 +231,16 @@
 
 def project(where, kinds, own, other, weights, partial=None, last_terms=None):
     tok = own.shape[1]
-    depth, width = weights[0].shape
-    count = len(weights)
+    share, width = weights[0].shape
+    parts, count = len(weights), len(kinds)
+    depth = parts // count * share
     first, last = partial is None, last_terms is not None
     columns = lambda rows: pl.BlockSpec((rows, TILE), lambda j, r: (0, j))
     in_hbm = pl.BlockSpec(memory_space=pltpu.HBM)
-    in_specs = [in_hbm] * 2 + [columns(depth) if last else in_hbm] * count
+    in_specs = [in_hbm] * 2 + [columns(share) if last else in_hbm] * parts
     scratch = [pltpu.VMEM((tok, count * depth), jnp.bfloat16), pltpu.SemaphoreType.DMA((count,))]
     if not last:
-        scratch += [pltpu.VMEM((2, count * depth, TILE), jnp.bfloat16), pltpu.SemaphoreType.DMA((2, count))]
+        scratch += [pltpu.VMEM((2, count * depth, TILE), jnp.bfloat16), pltpu.SemaphoreType.DMA((2, parts))]
     operands = [where, own, other, *weights]
     out_specs = [columns(tok)]
     out_shape = [jax.ShapeDtypeStruct((tok, width), jnp.float32)]
@@ -349,41 +355,49 @@
     if direct:
         order = ring_order(outer)
         hops = [(order[i], order[(i + 1) % outer]) for i in range(outer)]
-        ring = lambda block: lax.ppermute(block, "far", hops)
-        beyond = lambda block: swapped(block, "near")
-        facing = lambda block: swapped(block, "grp")
+        queues = {"far": [], "near": [], "grp": []}
+
+        def send(axis, block, *earlier, route=((0, 1), (1, 0))):
+            queue = queues[axis]
+            waits = (*earlier, *queue[-2:-1])
+            queue.append(lax.ppermute(after(block, *waits) if waits else block, axis, route))
+            return queue[-1]
+
+        ring = lambda block, *earlier: send("far", block, *earlier, route=hops)
+        beyond = lambda block, *earlier: send("near", block, *earlier)
+        facing = lambda block, *earlier: send("grp", block, *earlier)
         main, beside, across, corner = ({} for _ in range(4))
-        main[0] = jnp.where(is_mine, mine, theirs)
-        across[0] = jnp.where(is_mine, theirs, mine)
-        beside[0] = beyond(main[0])
-        second_keys = from_behind(after(keys, main[0]))
-        second_values = from_behind(after(values, second_keys))
-        first_keys = for_next(keys, after(second_keys, beside[0]))
-        corner[0] = facing(beside[0])
-        main[1] = ring(after(main[0], second_values))
-        first_values = for_next(values, after(second_values, first_keys))
-        cos, sin = rope_tables((after(row, beside[0]) - 2) * tok, 3 * tok)
-        main[1], first_keys, first_values, corner[0], cos, sin, where = hold(
-            (main[1], first_keys, first_values, corner[0], cos, sin, where)
-        )
-        main[2], beside[1], across[1] = ring(main[1]), beyond(main[1]), facing(main[1])
+        rows = [slice(0, depth // 2), slice(depth // 2, depth)]
+        main[0] = [jnp.where(is_mine, mine[r], theirs[r]) for r in rows]
+        across[0] = [jnp.where(is_mine, theirs[r], mine[r]) for r in rows]
+        beside[0] = [beyond(half) for half in main[0]]
+        second_keys = send("far", keys, main[0], route=ahead)
+        second_values = send("far", values, beside[0][0], route=ahead)
+        cos, sin = rope_tables((after(row, beside[0], second_keys) - 2) * tok, 3 * tok)
+        first_keys = beyond(jnp.where(near == 0, keys, after(second_keys, beside[0])))
+        corner[0] = [facing(half) for half in beside[0]]
+        main[1] = [ring(main[0][0], beside[0]), ring(main[0][1])]
+        first_values = beyond(jnp.where(near == 0, values, second_values))
+        beside[1] = [beyond(half) for half in main[1]]
+        across[1] = [facing(half) for half in main[1]]
+        main[2] = [ring(half) for half in main[1]]
+        corner[1] = [facing(half) for half in beside[1]]
         attended = attend(
             row[None], queries, (second_keys, first_keys, keys), (second_values, first_values, values), cos, sin, True
         )
-        main[2], beside[1], across[1], attended = hold((main[2], beside[1], across[1], attended))
-        main[3], beside[2], corner[1] = ring(main[2]), beyond(main[2]), facing(beside[1])
+        main[3] = [ring(main[2][0], attended), ring(main[2][1])]
+        beside[2] = [beyond(half) for half in main[2]]
+        corner[2] = [facing(half) for half in beside[2]]
         att_other = swapped(attended, "col")
-        main[3], beside[2], corner[1], att_other, across[1] = hold(
-            (main[3], beside[2], corner[1], att_other, across[1])
-        )
-        across[2], beside[3], corner[2] = ring(across[1]), beyond(main[3]), facing(beside[2])
-        across[2], beside[3], corner[2] = hold((across[2], beside[3], corner[2]))
-        across[3], corner[3] = ring(across[2]), facing(beside[3])
+        beside[3] = [beyond(half) for half in main[3]]
+        across[2] = [ring(half) for half in across[1]]
+        across[3] = [ring(half) for half in across[2]]
+        corner[3] = [facing(half) for half in beside[3]]
         weights, kinds, late, late_kinds = [], [], [], []
         for name, pieces in (("main", main), ("beside", beside), ("across", across), ("corner", corner)):
             for k in range(outer):
                 is_late = k == 3 and name in ("across", "corner")
-                (late if is_late else weights).append(pieces[k])
+                (late if is_late else weights).extend(pieces[k])
                 (late_kinds if is_late else kinds).append((name, k))
     else:
         second_keys, second_values = from_behind(keys), from_behind(values)

time: 137 us -> 150 us (1.095)
  waiting for transfers between devices: 72.6 us -> 45.8 us
  starting transfers between devices: 27.6 us -> 49.2 us
  local copies, waits for them, and re-layouts: 1.28 us -> 18.2 us
    ppermute x7 -> x32, starting transfers between devices: 15.8 us -> 48.6 us  [send(): lax.ppermute(after(block, *waits) if waits else block, axis, route)]
    ppermute x7 -> x32, waiting for transfers between devices: 64.8 us -> 42.5 us  [send(): lax.ppermute(after(block, *waits) if waits else block, axis, route)]
    unnamed x14 -> x60, local copies, waits for them, and re-layouts: 0.03 us -> 17 us
    ppermute x14 -> x3, starting transfers between devices: 11.8 us -> 0.66 us  [swapped(): return lax.ppermute(block, axis, [(0, 1), (1, 0)])]
    ppermute x14 -> x3, waiting for transfers between devices: 7.83 us -> 3.3 us  [swapped(): return lax.ppermute(block, axis, [(0, 1), (1, 0)])]
  transfers between devices with their start and end apart: 21 -> 35, of which waited for: 15 -> 15; matrix products, arithmetic and copies ran while one was open for 3% -> 3% of each run, Pallas kernels for 16% -> 14%
where the time goes in v7:
time: 150 us
  starting transfers between devices  49.2 us (33%)
  waiting for transfers between devices  45.8 us (31%)
  Pallas kernels  29.6 us (20%)
  local copies, waits for them, and re-layouts  18.2 us (12%)
  other arithmetic  6.33 us (4%)
    ppermute x32, starting transfers between devices, send(): lax.ppermute(after(block, *waits) if waits else block, axis, route)  48.6 us
    ppermute x32, waiting for transfers between devices, send(): lax.ppermute(after(block, *waits) if waits else block, axis, route)  42.5 us
    unnamed x60, local copies, waits for them, and re-layouts  17 us
    pallas_call x2, Pallas kernels, project(): pl.pallas_call(functools.partial(project_kernel, kinds, first, last), gri...  14.7 us
    pallas_call x1, Pallas kernels, attend(): pl.pallas_call(functools.partial(attend_kernel, tok, group, direct), grid...  11.7 us
    ppermute x3, waiting for transfers between devices, swapped(): return lax.ppermute(block, axis, [(0, 1), (1, 0)])  3.3 us
    pallas_call x1, Pallas kernels, finish(): pl.pallas_call(functools.partial(finish_kernel, model_width), grid=(width...  3.25 us
  transfers between devices with their start and end apart: 35, of which 15 were waited for; matrix products, arithmetic and copies ran while one was open for 3% of the time, Pallas kernels for 14%

profile of v7, /device:TPU:0, one launch (start us, length us, event | category | flops | bytes accessed | tf_op | source)
XLA Modules:
  0.0 149.5 jit_solution(8749637776230464269)
XLA Ops:
  1.8 1.8 %collective-permute-done = bf16[128,2688]{1,0:T(8,128)(2,1)S(1)} collective-permute-done((bf16[128,2688]{1,0:T(8,128)(2,1)S(1)}, bf16[128,2688]{1,0:T(8,128)(2,1)S(1)}, u32[]{:S(2)}, u32[]{:S(2)}) %collective-permute-start) | collective-permute-done | bytes 688160 | tf_op jit(solution)/shard_map/ppermute | solution.py:320
  3.5 2.0 %broadcast_select_fusion.2 = (bf16[64,2688]{1,0:T(8,128)(2,1)S(1)}, bf16[64,2688]{1,0:T(8,128)(2,1)S(1)}, bf16[64,2688]{1,0:T(8,128)(2,1)}, bf16[64,2688]{1,0:T(8,128)(2,1)S(1)}) fusion(pred[]{:T(512)S(6)} %eq.7, bf16[128,2688]{1,0:T(8,128)(2,1)S(1)} %collective-permute-done, bf16[128,5376]{1,0:T(8,128)(2,1)} %param.11, s32[]{:T(128)S(6)} %add.28, ...), kind=kLoop, calls=%fused_computation.6 | loop fusion | flops 688128 | bytes 2752521 | tf_op jit(solution)/shard_map/jit(_where)/select_n | solution.py:372
  5.6 4.9 %collective-permute-start.1 = (bf16[512,512]{1,0:T(8,128)(2,1)S(1)}, bf16[512,512]{1,0:T(8,128)(2,1)S(1)}, u32[]{:S(2)}, u32[]{:S(2)}) collective-permute-start(bf16[512,512]{1,0:T(8,128)(2,1)S(1)} %copy-done.2), channel_id=1, source_target_pairs={{0,4},{4,8},{8,12},{1,5},{5,9},{9,13},{2,6},{6,10},{10,14},{3,7},{... | collective-permute-start | bytes 1572872 | tf_op jit(solution)/shard_map/ppermute | solution.py:363
  12.6 8.9 %collective-permute-done.2.refs_8_ = bf16[64,2688]{1,0:T(8,128)(2,1)S(1)} collective-permute-done((bf16[64,2688]{1,0:T(8,128)(2,1)S(1)}, bf16[64,2688]{1,0:T(8,128)(2,1)S(1)}, u32[]{:S(2)}, u32[]{:S(2)}) %collective-permute-start.2) | collective-permute-done | bytes 344096 | tf_op jit(solution)/shard_map/ppermute | solution.py:363
  21.5 3.5 %collective-permute-start.5 = (bf16[512,512]{1,0:T(8,128)(2,1)S(1)}, bf16[512,512]{1,0:T(8,128)(2,1)S(1)}, u32[]{:S(2)}, u32[]{:S(2)}) collective-permute-start(bf16[512,512]{1,0:T(8,128)(2,1)S(1)} %copy-done.3), channel_id=1, source_target_pairs={{0,4},{4,8},{8,12},{1,5},{5,9},{9,13},{2,6},{6,10},{10,14},{3,7},{... | collective-permute-start | bytes 1572872 | tf_op jit(solution)/shard_map/ppermute | solution.py:363
  33.2 2.4 %collective-permute-done.9.refs_22_ = bf16[64,2688]{1,0:T(8,128)(2,1)} collective-permute-done((bf16[64,2688]{1,0:T(8,128)(2,1)S(1)}, bf16[64,2688]{1,0:T(8,128)(2,1)}, u32[]{:S(2)}, u32[]{:S(2)}) %collective-permute-start.9) | collective-permute-done | bytes 344096 | tf_op jit(solution)/shard_map/ppermute | solution.py:363
  35.7 5.8 %collective-permute-done.8.refs_2_ = bf16[64,2688]{1,0:T(8,128)(2,1)} collective-permute-done((bf16[64,2688]{1,0:T(8,128)(2,1)S(1)}, bf16[64,2688]{1,0:T(8,128)(2,1)}, u32[]{:S(2)}, u32[]{:S(2)}) %collective-permute-start.8) | collective-permute-done | bytes 344096 | tf_op jit(solution)/shard_map/ppermute | solution.py:363
  44.6 2.6 %collective-permute-start.15 = (bf16[64,2688]{1,0:T(8,128)(2,1)S(1)}, bf16[64,2688]{1,0:T(8,128)(2,1)S(1)}, u32[]{:S(2)}, u32[]{:S(2)}) collective-permute-start(bf16[64,2688]{1,0:T(8,128)(2,1)S(1)} %get-tuple-element.49.refs_1_), channel_id=1, source_target_pairs={{0,4},{4,12},{12,8},{8,0},{1,5},{5,13},{13,9},{9,1},{2,6},{6,14},{... | collective-permute-start | bytes 1032200 | tf_op jit(solution)/shard_map/ppermute | solution.py:363
  47.2 2.8 %fusion = (f32[1536,64]{1,0:T(8,128)S(1)}, f32[1536,64]{1,0:T(8,128)S(1)}, f32[1536,64]{1,0:T(8,128)S(1)}) fusion(f32[64]{0:T(128)S(1)} %multiply_exponential_fusion, f32[1536]{0:T(1024)S(1)} %add_convert_fusion), kind=kLoop, calls=%fused_computation.10 | loop fusion | flops 196608 | bytes 1186048 | tf_op jit(solution)/shard_map/neg | solution.py:34
  50.6 2.5 %collective-permute-start.11 = (bf16[64,2688]{1,0:T(8,128)(2,1)}, bf16[64,2688]{1,0:T(8,128)(2,1)S(1)}, u32[]{:S(2)}, u32[]{:S(2)}) collective-permute-start(bf16[64,2688]{1,0:T(8,128)(2,1)} %collective-permute-done.8.refs_2_), channel_id=1, source_target_pairs={{0,4},{4,12},{12,8},{8,0},{1,5},{5,13},{13,9},{9,1},{2,6},{6,14},{... | collective-permute-start | bytes 1032200 | tf_op jit(solution)/shard_map/ppermute | solution.py:363
  55.7 2.3 %collective-permute-done.6.v1 = bf16[512,512]{1,0:T(8,128)(2,1)S(1)} collective-permute-done((bf16[512,512]{1,0:T(8,128)(2,1)S(1)}, bf16[512,512]{1,0:T(8,128)(2,1)S(1)}, u32[]{:S(2)}, u32[]{:S(2)}) %collective-permute-start.6) | collective-permute-done | bytes 524320 | tf_op jit(solution)/shard_map/ppermute | solution.py:363
  58.0 2.6 %collective-permute-start.18 = (bf16[64,2688]{1,0:T(8,128)(2,1)S(1)}, bf16[64,2688]{1,0:T(8,128)(2,1)S(1)}, u32[]{:S(2)}, u32[]{:S(2)}) collective-permute-start(bf16[64,2688]{1,0:T(8,128)(2,1)S(1)} %collective-permute-done.15.refs_3_), channel_id=1, source_target_pairs={{0,4},{4,12},{12,8},{8,0},{1,5},{5,13},{13,9},{9,1},{2,6},{6,14},{... | collective-permute-start | bytes 1032200 | tf_op jit(solution)/shard_map/ppermute | solution.py:363
  62.1 11.7 %shard_map.82.own_ref = bf16[8,512,128]{2,1,0:T(8,128)(2,1)S(1)} custom-call(s32[1]{0:T(128)} %bitcast.3.row_ref, bf16[512,1024]{1,0:T(8,128)(2,1)S(1)} %copy-done.9, bf16[512,512]{1,0:T(8,128)(2,1)S(1)} %collective-permute-done.1.k0, bf16[512,512]{1,0:T(8,128)(2,1)} %collective-permute-done.4.k1, bf16[512,512]{1,0:T(8,128)(2,1)S(1)} %copy-done.2, ...), custom_call_target="tpu_custom_call" | custom-call | flops 10737418240 | bytes 6291456 | tf_op jit(solution)/shard_map/pallas_call | solution.py:104
  75.8 2.5 %collective-permute-start.12 = (bf16[64,2688]{1,0:T(8,128)(2,1)S(1)}, bf16[64,2688]{1,0:T(8,128)(2,1)S(1)}, u32[]{:S(2)}, u32[]{:S(2)}) collective-permute-start(bf16[64,2688]{1,0:T(8,128)(2,1)S(1)} %collective-permute-done.11.refs_4_), channel_id=1, source_target_pairs={{0,4},{4,12},{12,8},{8,0},{1,5},{5,13},{13,9},{9,1},{2,6},{6,14},{... | collective-permute-start | bytes 1032200 | tf_op jit(solution)/shard_map/ppermute | solution.py:363
  79.1 5.3 %collective-permute-done.25.refs_24_ = bf16[64,2688]{1,0:T(8,128)(2,1)S(1)} collective-permute-done((bf16[64,2688]{1,0:T(8,128)(2,1)S(1)}, bf16[64,2688]{1,0:T(8,128)(2,1)S(1)}, u32[]{:S(2)}, u32[]{:S(2)}) %collective-permute-start.25) | collective-permute-done | bytes 344096 | tf_op jit(solution)/shard_map/ppermute | solution.py:363
  89.1 4.9 %collective-permute-done.19.refs_7_ = bf16[64,2688]{1,0:T(8,128)(2,1)} collective-permute-done((bf16[64,2688]{1,0:T(8,128)(2,1)S(1)}, bf16[64,2688]{1,0:T(8,128)(2,1)}, u32[]{:S(2)}, u32[]{:S(2)}) %collective-permute-start.19) | collective-permute-done | bytes 344096 | tf_op jit(solution)/shard_map/ppermute | solution.py:363
  96.2 2.3 %collective-permute-start.13 = (bf16[64,2688]{1,0:T(8,128)(2,1)}, bf16[64,2688]{1,0:T(8,128)(2,1)}, u32[]{:S(2)}, u32[]{:S(2)}) collective-permute-start(bf16[64,2688]{1,0:T(8,128)(2,1)} %collective-permute-done.10.refs_18_), channel_id=1, source_target_pairs={{0,4},{4,12},{12,8},{8,0},{1,5},{5,13},{13,9},{9,1},{2,6},{6,14},{... | collective-permute-start | bytes 1032200 | tf_op jit(solution)/shard_map/ppermute | solution.py:363
  99.0 2.3 %collective-permute-done.26.refs_26_ = bf16[64,2688]{1,0:T(8,128)(2,1)S(1)} collective-permute-done((bf16[64,2688]{1,0:T(8,128)(2,1)S(1)}, bf16[64,2688]{1,0:T(8,128)(2,1)S(1)}, u32[]{:S(2)}, u32[]{:S(2)}) %collective-permute-start.26) | collective-permute-done | bytes 344096 | tf_op jit(solution)/shard_map/ppermute | solution.py:363
  105.3 3.1 %collective-permute-done.13.refs_20_ = bf16[64,2688]{1,0:T(8,128)(2,1)} collective-permute-done((bf16[64,2688]{1,0:T(8,128)(2,1)}, bf16[64,2688]{1,0:T(8,128)(2,1)}, u32[]{:S(2)}, u32[]{:S(2)}) %collective-permute-start.13) | collective-permute-done | bytes 344096 | tf_op jit(solution)/shard_map/ppermute | solution.py:363
  110.0 3.6 %collective-permute-done.20.refs_21_ = bf16[64,2688]{1,0:T(8,128)(2,1)} collective-permute-done((bf16[64,2688]{1,0:T(8,128)(2,1)}, bf16[64,2688]{1,0:T(8,128)(2,1)}, u32[]{:S(2)}, u32[]{:S(2)}) %collective-permute-start.20) | collective-permute-done | bytes 344096 | tf_op jit(solution)/shard_map/ppermute | solution.py:363
  114.2 2.4 %collective-permute-start.21 = (bf16[64,2688]{1,0:T(8,128)(2,1)}, bf16[64,2688]{1,0:T(8,128)(2,1)S(1)}, u32[]{:S(2)}, u32[]{:S(2)}) collective-permute-start(bf16[64,2688]{1,0:T(8,128)(2,1)} %collective-permute-done.20.refs_21_), channel_id=1, source_target_pairs={{0,4},{4,12},{12,8},{8,0},{1,5},{5,13},{13,9},{9,1},{2,6},{6,14},{... | collective-permute-start | bytes 1032200 | tf_op jit(solution)/shard_map/ppermute | solution.py:363
  129.9 10.0 %shard_map.83.refs_4_ = f32[512,2688]{1,0:T(8,128)S(1)} custom-call(s32[4]{0:T(128)S(1)} %pad_add_fusion.where_ref, bf16[8,512,128]{2,1,0:T(8,128)(2,1)S(1)} %shard_map.82.own_ref, bf16[8,512,128]{2,1,0:T(8,128)(2,1)S(1)} %collective-permute-done.7.other_ref, bf16[64,2688]{1,0:T(8,128)(2,1)S(1)} %copy-done.8, bf16[64,2688]{1,0:T(8,128)(2,1)S(1)} %copy-done.5, ...), custom_call_target="tpu_custom_call" | custom-call | flops 4932501504 | bytes 9633792 | tf_op jit(solution)/shard_map/pallas_call | solution.py:256
  139.9 4.7 %shard_map.84 = (f32[512,2688]{1,0:T(8,128)S(1)}, f32[520,128]{1,0:T(8,128)S(1)}) custom-call(s32[4]{0:T(128)S(1)} %pad_add_fusion.where_ref, bf16[8,512,128]{2,1,0:T(8,128)(2,1)S(1)} %shard_map.82.own_ref, bf16[8,512,128]{2,1,0:T(8,128)(2,1)S(1)} %collective-permute-done.7.other_ref, bf16[64,2688]{1,0:T(8,128)(2,1)S(1)} %collective-permute-done.14.refs_0_, ...), custom_call_target="tpu_custom_call" | custom-call | flops 704643072 | bytes 1376256 | tf_op jit(solution)/shard_map/pallas_call | solution.py:256
  146.3 3.2 %shard_map.85 = bf16[512,2688]{1,0:T(8,128)(2,1)} custom-call(f32[520,128]{1,0:T(8,128)S(1)} %get-tuple-element.67.own_ref, f32[520,128]{1,0:T(8,128)S(1)} %collective-permute-done.34.other_ref, f32[1,2688]{1,0:T(1,128)S(1)} %broadcast_in_dim.12.refs_5_.gain_ref, f32[64,2688]{1,0:T(8,128)S(1)} %bitcast.7, f32[512,2688]{1,0:T(8,128)S(1)} %get-tuple-element.68.hidden_ref), custom_call_target="tpu_custom_call" | custom-call | flops 704643072 | bytes 8257536 | tf_op jit(solution)/shard_map/pallas_call | solution.py:299
  (121 shorter events, 51.0 us)
Async XLA Ops:
  5.6 23.7 %collective-permute-start.1 = (bf16[512,512]{1,0:T(8,128)(2,1)S(1)}, bf16[512,512]{1,0:T(8,128)(2,1)S(1)}, u32[]{:S(2)}, u32[]{:S(2)}) collective-permute-start(bf16[512,512]{1,0:T(8,128)(2,1)S(1)} %copy-done.2), channel_id=1, source_target_pairs={{0,4},{4,8},{8,12},{1,5},{5,9},{9,13},{2,6},{6,10},{10,14},{3,7},{... | collective-permute-start | bytes 1572872 | tf_op jit(solution)/shard_map/ppermute | solution.py:363
  12.0 15.8 %collective-permute-start.3 = (bf16[64,2688]{1,0:T(8,128)(2,1)S(1)}, bf16[64,2688]{1,0:T(8,128)(2,1)}, u32[]{:S(2)}, u32[]{:S(2)}) collective-permute-start(bf16[64,2688]{1,0:T(8,128)(2,1)S(1)} %get-tuple-element.49.refs_1_), channel_id=1, source_target_pairs={{0,2},{2,0},{1,3},{3,1},{4,6},{6,4},{5,7},{7,5},{8,10},{10,8},{9,1... | collective-permute-start | bytes 1032200 | tf_op jit(solution)/shard_map/ppermute | solution.py:363
  21.5 21.5 %collective-permute-start.5 = (bf16[512,512]{1,0:T(8,128)(2,1)S(1)}, bf16[512,512]{1,0:T(8,128)(2,1)S(1)}, u32[]{:S(2)}, u32[]{:S(2)}) collective-permute-start(bf16[512,512]{1,0:T(8,128)(2,1)S(1)} %copy-done.3), channel_id=1, source_target_pairs={{0,4},{4,8},{8,12},{1,5},{5,9},{9,13},{2,6},{6,10},{10,14},{3,7},{... | collective-permute-start | bytes 1572872 | tf_op jit(solution)/shard_map/ppermute | solution.py:363
  27.8 25.3 %collective-permute-start.16 = (bf16[64,2688]{1,0:T(8,128)(2,1)}, bf16[64,2688]{1,0:T(8,128)(2,1)}, u32[]{:S(2)}, u32[]{:S(2)}) collective-permute-start(bf16[64,2688]{1,0:T(8,128)(2,1)} %collective-permute-done.3.refs_9_), channel_id=1, source_target_pairs={{0,16},{16,0},{1,17},{17,1},{2,18},{18,2},{3,19},{19,3},{4,20},{20... | collective-permute-start | bytes 1032200 | tf_op jit(solution)/shard_map/ppermute | solution.py:363
  29.3 12.2 %collective-permute-start.8 = (bf16[64,2688]{1,0:T(8,128)(2,1)S(1)}, bf16[64,2688]{1,0:T(8,128)(2,1)}, u32[]{:S(2)}, u32[]{:S(2)}) collective-permute-start(bf16[64,2688]{1,0:T(8,128)(2,1)S(1)} %get-tuple-element.43.refs_0_), channel_id=1, source_target_pairs={{0,4},{4,12},{12,8},{8,0},{1,5},{5,13},{13,9},{9,1},{2,6},{6,14},{... | collective-permute-start | bytes 1032200 | tf_op jit(solution)/shard_map/ppermute | solution.py:363
  31.7 18.8 %collective-permute-start.4 = (bf16[512,512]{1,0:T(8,128)(2,1)}, bf16[512,512]{1,0:T(8,128)(2,1)}, u32[]{:S(2)}, u32[]{:S(2)}) collective-permute-start(bf16[512,512]{1,0:T(8,128)(2,1)} %broadcast_select_fusion.1), channel_id=1, source_target_pairs={{0,2},{2,0},{1,3},{3,1},{4,6},{6,4},{5,7},{7,5},{8,10},{10,8},{9,1... | collective-permute-start | bytes 1572872 | tf_op jit(solution)/shard_map/ppermute | solution.py:363
  41.5 19.1 %collective-permute-start.10 = (bf16[64,2688]{1,0:T(8,128)(2,1)}, bf16[64,2688]{1,0:T(8,128)(2,1)}, u32[]{:S(2)}, u32[]{:S(2)}) collective-permute-start(bf16[64,2688]{1,0:T(8,128)(2,1)} %collective-permute-done.8.refs_2_), channel_id=1, source_target_pairs={{0,16},{16,0},{1,17},{17,1},{2,18},{18,2},{3,19},{19,3},{4,20},{20... | collective-permute-start | bytes 1032200 | tf_op jit(solution)/shard_map/ppermute | solution.py:363
  43.1 14.9 %collective-permute-start.6 = (bf16[512,512]{1,0:T(8,128)(2,1)S(1)}, bf16[512,512]{1,0:T(8,128)(2,1)S(1)}, u32[]{:S(2)}, u32[]{:S(2)}) collective-permute-start(bf16[512,512]{1,0:T(8,128)(2,1)S(1)} %broadcast_select_fusion), channel_id=1, source_target_pairs={{0,2},{2,0},{1,3},{3,1},{4,6},{6,4},{5,7},{7,5},{8,10},{10,8},{9,1... | collective-permute-start | bytes 1572872 | tf_op jit(solution)/shard_map/ppermute | solution.py:363
  50.6 23.3 %collective-permute-start.11 = (bf16[64,2688]{1,0:T(8,128)(2,1)}, bf16[64,2688]{1,0:T(8,128)(2,1)S(1)}, u32[]{:S(2)}, u32[]{:S(2)}) collective-permute-start(bf16[64,2688]{1,0:T(8,128)(2,1)} %collective-permute-done.8.refs_2_), channel_id=1, source_target_pairs={{0,4},{4,12},{12,8},{8,0},{1,5},{5,13},{13,9},{9,1},{2,6},{6,14},{... | collective-permute-start | bytes 1032200 | tf_op jit(solution)/shard_map/ppermute | solution.py:363
  53.1 20.7 %collective-permute-start.22 = (bf16[64,2688]{1,0:T(8,128)(2,1)}, bf16[64,2688]{1,0:T(8,128)(2,1)S(1)}, u32[]{:S(2)}, u32[]{:S(2)}) collective-permute-start(bf16[64,2688]{1,0:T(8,128)(2,1)} %collective-permute-done.8.refs_2_), channel_id=1, source_target_pairs={{0,2},{2,0},{1,3},{3,1},{4,6},{6,4},{5,7},{7,5},{8,10},{10,8},{9,1... | collective-permute-start | bytes 1032200 | tf_op jit(solution)/shard_map/ppermute | solution.py:363
  55.1 20.1 %collective-permute-start.17 = (bf16[64,2688]{1,0:T(8,128)(2,1)S(1)}, bf16[64,2688]{1,0:T(8,128)(2,1)}, u32[]{:S(2)}, u32[]{:S(2)}) collective-permute-start(bf16[64,2688]{1,0:T(8,128)(2,1)S(1)} %collective-permute-done.15.refs_3_), channel_id=1, source_target_pairs={{0,16},{16,0},{1,17},{17,1},{2,18},{18,2},{3,19},{19,3},{4,20},{20... | collective-permute-start | bytes 1032200 | tf_op jit(solution)/shard_map/ppermute | solution.py:363
  58.0 17.8 %collective-permute-start.18 = (bf16[64,2688]{1,0:T(8,128)(2,1)S(1)}, bf16[64,2688]{1,0:T(8,128)(2,1)S(1)}, u32[]{:S(2)}, u32[]{:S(2)}) collective-permute-start(bf16[64,2688]{1,0:T(8,128)(2,1)S(1)} %collective-permute-done.15.refs_3_), channel_id=1, source_target_pairs={{0,4},{4,12},{12,8},{8,0},{1,5},{5,13},{13,9},{9,1},{2,6},{6,14},{... | collective-permute-start | bytes 1032200 | tf_op jit(solution)/shard_map/ppermute | solution.py:363
  60.6 18.5 %collective-permute-start.28 = (bf16[64,2688]{1,0:T(8,128)(2,1)S(1)}, bf16[64,2688]{1,0:T(8,128)(2,1)S(1)}, u32[]{:S(2)}, u32[]{:S(2)}) collective-permute-start(bf16[64,2688]{1,0:T(8,128)(2,1)S(1)} %collective-permute-done.15.refs_3_), channel_id=1, source_target_pairs={{0,2},{2,0},{1,3},{3,1},{4,6},{6,4},{5,7},{7,5},{8,10},{10,8},{9,1... | collective-permute-start | bytes 1032200 | tf_op jit(solution)/shard_map/ppermute | solution.py:363
  73.8 44.3 %collective-permute-start.7 = (bf16[8,512,128]{2,1,0:T(8,128)(2,1)S(1)}, bf16[8,512,128]{2,1,0:T(8,128)(2,1)S(1)}, u32[]{:S(2)}, u32[]{:S(2)}) collective-permute-start(bf16[8,512,128]{2,1,0:T(8,128)(2,1)S(1)} %shard_map.82.own_ref), channel_id=1, source_target_pairs={{0,1},{1,0},{2,3},{3,2},{4,5},{5,4},{6,7},{7,6},{8,9},{9,8},{10,11... | collective-permute-start | bytes 3145736 | tf_op jit(solution)/shard_map/ppermute | solution.py:320
  79.0 14.9 %collective-permute-start.19 = (bf16[64,2688]{1,0:T(8,128)(2,1)S(1)}, bf16[64,2688]{1,0:T(8,128)(2,1)}, u32[]{:S(2)}, u32[]{:S(2)}) collective-permute-start(bf16[64,2688]{1,0:T(8,128)(2,1)S(1)} %collective-permute-done.18.refs_5_), channel_id=1, source_target_pairs={{0,4},{4,12},{12,8},{8,0},{1,5},{5,13},{13,9},{9,1},{2,6},{6,14},{... | collective-permute-start | bytes 1032200 | tf_op jit(solution)/shard_map/ppermute | solution.py:363
  85.6 12.9 %collective-permute-start.29 = (bf16[64,2688]{1,0:T(8,128)(2,1)S(1)}, bf16[64,2688]{1,0:T(8,128)(2,1)}, u32[]{:S(2)}, u32[]{:S(2)}) collective-permute-start(bf16[64,2688]{1,0:T(8,128)(2,1)S(1)} %collective-permute-done.18.refs_5_), channel_id=1, source_target_pairs={{0,2},{2,0},{1,3},{3,1},{4,6},{6,4},{5,7},{7,5},{8,10},{10,8},{9,1... | collective-permute-start | bytes 1032200 | tf_op jit(solution)/shard_map/ppermute | solution.py:363
  87.6 13.8 %collective-permute-start.26 = (bf16[64,2688]{1,0:T(8,128)(2,1)S(1)}, bf16[64,2688]{1,0:T(8,128)(2,1)S(1)}, u32[]{:S(2)}, u32[]{:S(2)}) collective-permute-start(bf16[64,2688]{1,0:T(8,128)(2,1)S(1)} %collective-permute-done.23.refs_12_), channel_id=1, source_target_pairs={{0,16},{16,0},{1,17},{17,1},{2,18},{18,2},{3,19},{19,3},{4,20},{20... | collective-permute-start | bytes 1032200 | tf_op jit(solution)/shard_map/ppermute | solution.py:363
  96.2 12.2 %collective-permute-start.13 = (bf16[64,2688]{1,0:T(8,128)(2,1)}, bf16[64,2688]{1,0:T(8,128)(2,1)}, u32[]{:S(2)}, u32[]{:S(2)}) collective-permute-start(bf16[64,2688]{1,0:T(8,128)(2,1)} %collective-permute-done.10.refs_18_), channel_id=1, source_target_pairs={{0,4},{4,12},{12,8},{8,0},{1,5},{5,13},{13,9},{9,1},{2,6},{6,14},{... | collective-permute-start | bytes 1032200 | tf_op jit(solution)/shard_map/ppermute | solution.py:363
  98.6 15.0 %collective-permute-start.20 = (bf16[64,2688]{1,0:T(8,128)(2,1)}, bf16[64,2688]{1,0:T(8,128)(2,1)}, u32[]{:S(2)}, u32[]{:S(2)}) collective-permute-start(bf16[64,2688]{1,0:T(8,128)(2,1)} %collective-permute-done.17.refs_19_), channel_id=1, source_target_pairs={{0,4},{4,12},{12,8},{8,0},{1,5},{5,13},{13,9},{9,1},{2,6},{6,14},{... | collective-permute-start | bytes 1032200 | tf_op jit(solution)/shard_map/ppermute | solution.py:363
  103.7 12.9 %collective-permute-start.30 = (bf16[64,2688]{1,0:T(8,128)(2,1)}, bf16[64,2688]{1,0:T(8,128)(2,1)}, u32[]{:S(2)}, u32[]{:S(2)}) collective-permute-start(bf16[64,2688]{1,0:T(8,128)(2,1)} %collective-permute-done.19.refs_7_), channel_id=1, source_target_pairs={{0,2},{2,0},{1,3},{3,1},{4,6},{6,4},{5,7},{7,5},{8,10},{10,8},{9,1... | collective-permute-start | bytes 1032200 | tf_op jit(solution)/shard_map/ppermute | solution.py:363
  108.5 31.4 %collective-permute-start.27 = (bf16[64,2688]{1,0:T(8,128)(2,1)}, bf16[64,2688]{1,0:T(8,128)(2,1)S(1)}, u32[]{:S(2)}, u32[]{:S(2)}) collective-permute-start(bf16[64,2688]{1,0:T(8,128)(2,1)} %copy-done.26), channel_id=1, source_target_pairs={{0,16},{16,0},{1,17},{17,1},{2,18},{18,2},{3,19},{19,3},{4,20},{20... | collective-permute-start | bytes 1032200 | tf_op jit(solution)/shard_map/ppermute | solution.py:363
  113.5 26.3 %collective-permute-start.14 = (bf16[64,2688]{1,0:T(8,128)(2,1)}, bf16[64,2688]{1,0:T(8,128)(2,1)S(1)}, u32[]{:S(2)}, u32[]{:S(2)}) collective-permute-start(bf16[64,2688]{1,0:T(8,128)(2,1)} %collective-permute-done.13.refs_20_), channel_id=1, source_target_pairs={{0,4},{4,12},{12,8},{8,0},{1,5},{5,13},{13,9},{9,1},{2,6},{6,14},{... | collective-permute-start | bytes 1032200 | tf_op jit(solution)/shard_map/ppermute | solution.py:363
  114.2 25.7 %collective-permute-start.21 = (bf16[64,2688]{1,0:T(8,128)(2,1)}, bf16[64,2688]{1,0:T(8,128)(2,1)S(1)}, u32[]{:S(2)}, u32[]{:S(2)}) collective-permute-start(bf16[64,2688]{1,0:T(8,128)(2,1)} %collective-permute-done.20.refs_21_), channel_id=1, source_target_pairs={{0,4},{4,12},{12,8},{8,0},{1,5},{5,13},{13,9},{9,1},{2,6},{6,14},{... | collective-permute-start | bytes 1032200 | tf_op jit(solution)/shard_map/ppermute | solution.py:363
  116.6 23.3 %collective-permute-start.33 = (bf16[64,2688]{1,0:T(8,128)(2,1)}, bf16[64,2688]{1,0:T(8,128)(2,1)S(1)}, u32[]{:S(2)}, u32[]{:S(2)}) collective-permute-start(bf16[64,2688]{1,0:T(8,128)(2,1)} %collective-permute-done.30.refs_15_), channel_id=1, source_target_pairs={{0,16},{16,0},{1,17},{17,1},{2,18},{18,2},{3,19},{19,3},{4,20},{20... | collective-permute-start | bytes 1032200 | tf_op jit(solution)/shard_map/ppermute | solution.py:363
  (41 other events, 402.9 us)

commit v8 on v6

--- a/solution.py
+++ b/solution.py
@@ -89,30 +89,31 @@
                 out_ref[lo:hi, h * HD : (h + 1) * HD] = block
 
 
-def attend(row, queries, key_blocks, val_blocks, cos, sin, direct):
+def attend(row, queries, key_blocks, val_blocks, cos, sin, direct, first=0, count=None):
     tok, kv_local = queries.shape[0], key_blocks[0].shape[1] // HD
     group = queries.shape[1] // HD // kv_local
-    head_block = pl.BlockSpec((tok, HD), lambda g, r: (0, g))
+    count = kv_local if count is None else count
+    head_block = pl.BlockSpec((tok, HD), lambda g, r: (0, g + first))
     table = pl.BlockSpec((3 * tok, HD), lambda g, r: (0, 0))
     if direct:
-        out_shape = (kv_local * group, tok, HD)
+        out_shape = (count * group, tok, HD)
         out_spec = pl.BlockSpec((group, tok, HD), lambda g, r: (g, 0, 0))
     else:
         out_shape = queries.shape
         out_spec = pl.BlockSpec((tok, group * HD), lambda g, r: (0, g))
-    heads = kv_local * group
+    heads = count * group
     return pl.pallas_call(
         functools.partial(attend_kernel, tok, group, direct),
         grid_spec=pltpu.PrefetchScalarGridSpec(
             num_scalar_prefetch=1,
-            grid=(kv_local,),
-            in_specs=[pl.BlockSpec((tok, group * HD), lambda g, r: (0, g))] + [head_block] * 6 + [table] * 2,
+            grid=(count,),
+            in_specs=[pl.BlockSpec((tok, group * HD), lambda g, r: (0, g + first))] + [head_block] * 6 + [table] * 2,
             out_specs=out_spec,
         ),
         out_shape=jax.ShapeDtypeStruct(out_shape, jnp.bfloat16),
         compiler_params=pltpu.CompilerParams(vmem_limit_bytes=VMEM_LIMIT),
         cost_estimate=pl.CostEstimate(
-            flops=heads * tok * 10 * tok * HD, bytes_accessed=6 * 2**20, transcendentals=heads * tok * 2 * tok
+            flops=4 * heads * tok * 10 * tok * HD, bytes_accessed=6 * 2**20, transcendentals=heads * tok * 2 * tok
         ),
     )(row, queries, *key_blocks, *val_blocks, cos, sin)
 
@@ -135,9 +136,10 @@
     return other * slots + from_far * 2 + side
 
 
-def project_kernel(kinds, first, last, where_ref, own_ref, other_ref, *refs):
+def project_kernel(kinds, sources, parts, first, last, where_ref, *refs):
     count = len(kinds)
-    weights, refs = refs[:count], refs[count:]
+    sources, refs = refs[:sources], refs[sources:]
+    weights, refs = refs[: len(parts)], refs[len(parts) :]
     if not first:
         partial_ref, refs = refs[0], refs[1:]
     if last:
@@ -147,16 +149,17 @@
         stat_ref, refs = refs[0], refs[1:]
     heads, sems = refs[:2]
     step = pl.program_id(0)
-    depth = weights[0].shape[0]
+    depth = sum(parts) // count
     if not last:
         blocks, block_sems = refs[2:]
         steps = pl.num_programs(0)
 
         def columns_of(at, act):
             slot = lax.rem(at, 2)
-            for n, piece in enumerate(weights):
+            for n, (piece, share) in enumerate(zip(weights, parts)):
+                rows = slice(sum(parts[:n]), sum(parts[: n + 1]))
                 source = piece.at[:, pl.ds(pl.multiple_of(at * TILE, TILE), TILE)]
-                act(pltpu.make_async_copy(source, blocks.at[slot, n * depth : (n + 1) * depth], block_sems.at[slot, n]))
+                act(pltpu.make_async_copy(source, blocks.at[slot, rows], block_sems.at[slot, n]))
 
         @pl.when(step == 0)
         def _():
@@ -166,25 +169,22 @@
         def _():
             columns_of(step + 1, lambda copy: copy.start())
 
-    slots = own_ref.shape[0]
+    slots = sources[0].shape[0]
 
     @pl.when(step == 0)
     def _():
         for n, (kind, k) in enumerate(kinds):
-            slot = slot_of(kind, k, where_ref, slots)
+            slot = slot_of(kind, k, where_ref, slots * len(sources) // 2)
             place = heads.at[:, n * depth : (n + 1) * depth]
-
-            @pl.when(slot < slots)
-            def _():
-                pltpu.make_async_copy(own_ref.at[slot], place, sems.at[n]).start()
-
-            @pl.when(slot >= slots)
-            def _():
-                pltpu.make_async_copy(other_ref.at[slot - slots], place, sems.at[n]).start()
+            for i, source in enumerate(sources):
+
+                @pl.when((slot >= i * slots) & (slot < (i + 1) * slots))
+                def _():
+                    pltpu.make_async_copy(source.at[slot - i * slots], place, sems.at[n]).start()
 
         for n in range(count):
             place = heads.at[:, n * depth : (n + 1) * depth]
-            pltpu.make_async_copy(own_ref.at[0], place, sems.at[n]).wait()
+            pltpu.make_async_copy(sources[0].at[0], place, sems.at[n]).wait()
 
     if last:
         weight = jnp.concatenate([w[...] for w in weights], 0)
@@ -224,18 +224,19 @@
             stat_ref[tok:, :] += mean_code
 
 
-def project(where, kinds, own, other, weights, partial=None, last_terms=None):
-    tok = own.shape[1]
-    depth, width = weights[0].shape
-    count = len(weights)
+def project(where, kinds, sources, weights, partial=None, last_terms=None):
+    tok = sources[0].shape[1]
+    width = weights[0].shape[1]
+    parts = [w.shape[0] for w in weights]
+    count, total = len(kinds), sum(parts)
     first, last = partial is None, last_terms is not None
     columns = lambda rows: pl.BlockSpec((rows, TILE), lambda j, r: (0, j))
     in_hbm = pl.BlockSpec(memory_space=pltpu.HBM)
-    in_specs = [in_hbm] * 2 + [columns(depth) if last else in_hbm] * count
-    scratch = [pltpu.VMEM((tok, count * depth), jnp.bfloat16), pltpu.SemaphoreType.DMA((count,))]
+    in_specs = [in_hbm] * len(sources) + [columns(rows) if last else in_hbm for rows in parts]
+    scratch = [pltpu.VMEM((tok, total), jnp.bfloat16), pltpu.SemaphoreType.DMA((count,))]
     if not last:
-        scratch += [pltpu.VMEM((2, count * depth, TILE), jnp.bfloat16), pltpu.SemaphoreType.DMA((2, count))]
-    operands = [where, own, other, *weights]
+        scratch += [pltpu.VMEM((2, total, TILE), jnp.bfloat16), pltpu.SemaphoreType.DMA((2, len(parts)))]
+    operands = [where, *sources, *weights]
     out_specs = [columns(tok)]
     out_shape = [jax.ShapeDtypeStruct((tok, width), jnp.float32)]
     if not first:
@@ -248,7 +249,7 @@
         out_specs.append(pl.BlockSpec((tok + 8, 2 * RANK), lambda j, r: (0, 0)))
         out_shape.append(jax.ShapeDtypeStruct((tok + 8, 2 * RANK), jnp.float32))
     return pl.pallas_call(
-        functools.partial(project_kernel, kinds, first, last),
+        functools.partial(project_kernel, kinds, len(sources), parts, first, last),
         grid_spec=pltpu.PrefetchScalarGridSpec(
             num_scalar_prefetch=1,
             grid=(width // TILE,),
@@ -259,7 +260,7 @@
         out_shape=out_shape,
         compiler_params=pltpu.CompilerParams(vmem_limit_bytes=VMEM_LIMIT),
         cost_estimate=pl.CostEstimate(
-            flops=2 * tok * count * depth * width, bytes_accessed=2 * count * depth * width, transcendentals=0
+            flops=4 * tok * total * width, bytes_accessed=2 * total * width, transcendentals=0
         ),
     )(*operands)
 
@@ -358,33 +359,41 @@
         beside[0] = beyond(main[0])
         second_keys = from_behind(after(keys, main[0]))
         second_values = from_behind(after(values, second_keys))
+        main[1] = ring(after(main[0], second_keys))
         first_keys = for_next(keys, after(second_keys, beside[0]))
         corner[0] = facing(beside[0])
-        main[1] = ring(after(main[0], second_values))
+        cos, sin = rope_tables((after(row, beside[0], second_keys) - 2) * tok, 3 * tok)
         first_values = for_next(values, after(second_values, first_keys))
-        cos, sin = rope_tables((after(row, beside[0]) - 2) * tok, 3 * tok)
-        main[1], first_keys, first_values, corner[0], cos, sin, where = hold(
-            (main[1], first_keys, first_values, corner[0], cos, sin, where)
-        )
-        main[2], beside[1], across[1] = ring(main[1]), beyond(main[1]), facing(main[1])
-        attended = attend(
-            row[None], queries, (second_keys, first_keys, keys), (second_values, first_values, values), cos, sin, True
-        )
-        main[2], beside[1], across[1], attended = hold((main[2], beside[1], across[1], attended))
-        main[3], beside[2], corner[1] = ring(main[2]), beyond(main[2]), facing(beside[1])
-        att_other = swapped(attended, "col")
-        main[3], beside[2], corner[1], att_other, across[1] = hold(
-            (main[3], beside[2], corner[1], att_other, across[1])
-        )
-        across[2], beside[3], corner[2] = ring(across[1]), beyond(main[3]), facing(beside[2])
-        across[2], beside[3], corner[2] = hold((across[2], beside[3], corner[2]))
-        across[3], corner[3] = ring(across[2]), facing(beside[3])
+        main[2] = ring(after(main[1], cos, sin))
+        across[1] = facing(after(main[1], corner[0]))
+        beside[1] = beyond(after(main[1], second_values))
+        key_blocks, val_blocks = (second_keys, first_keys, keys), (second_values, first_values, values)
+        some = kv_local // 2
+        early = attend(row[None], queries, key_blocks, val_blocks, cos, sin, True, 0, some)
+        main[3] = ring(after(main[2], early))
+        across[2] = facing(after(main[2], across[1], early))
+        beside[2] = beyond(after(main[2], beside[1], early))
+        corner[1] = facing(after(beside[1], early))
+        rest = attend(after(row, beside[1])[None], queries, key_blocks, val_blocks, cos, sin, True, some, kv_local - some)
+        attended = [early, rest]
+        att_other = [swapped(after(early, rest), "col"), swapped(rest, "col")]
+        across[3] = ring(after(across[2], main[3]))
+        beside[3] = beyond(after(main[3], beside[2], rest))
+        corner[2] = facing(after(beside[2], corner[1]))
         weights, kinds, late, late_kinds = [], [], [], []
+        last_ones = (("beside", 3), ("across", 3), ("corner", 2))
         for name, pieces in (("main", main), ("beside", beside), ("across", across), ("corner", corner)):
             for k in range(outer):
-                is_late = k == 3 and name in ("across", "corner")
+                if (name, k) == ("corner", 3):
+                    continue
+                is_late = (name, k) in last_ones
                 (late if is_late else weights).append(pieces[k])
                 (late_kinds if is_late else kinds).append((name, k))
+        (partial,) = project(where, kinds, attended + att_other, weights)
+        half = depth // 2
+        late.append(facing(after(beside[3][:half], corner[2], partial)))
+        late.append(beyond(after(across[3][half:], beside[3], partial)))
+        late_kinds.append(("corner", 3))
     else:
         second_keys, second_values = from_behind(keys), from_behind(values)
         first_keys, first_values = for_next(keys, second_keys), for_next(values, second_values)
@@ -392,13 +401,13 @@
         attended = attend(
             row[None], queries, (second_keys, first_keys, keys), (second_values, first_values, values), cos, sin, False
         )
-        attended = attended[None]
-        att_other = swapped(attended, "col")
+        attended = [attended[None]]
+        att_other = [swapped(attended[0], "col")]
         weights, late = ([lax.all_gather(w, ("far", "near"), axis=0, tiled=True)] for w in (mine, theirs))
         kinds, late_kinds = [(None, 0)], [(None, 1)]
-
-    (partial,) = project(where, kinds, attended, att_other, weights)
-    hidden, stat = project(where, late_kinds, attended, att_other, late, partial, (gain, erase_in, mean))
+        (partial,) = project(where, kinds, attended + att_other, weights)
+
+    hidden, stat = project(where, late_kinds, attended + att_other, late, partial, (gain, erase_in, mean))
     return finish(model_width, stat, swapped(stat, "col"), gain, erase_out, hidden)
 
 

time: 137 us -> 138 us (level)
  waiting for transfers between devices: 72.6 us -> 61.8 us
  starting transfers between devices: 27.6 us -> 33.5 us
  local copies, waits for them, and re-layouts: 1.28 us -> 6.48 us
    ppermute x5 -> x4, waiting for transfers between devices: 46.2 us -> 11.8 us  [on_device(): ring = lambda block: lax.ppermute(block, 'far', hops)]
    ppermute x14 -> x17, waiting for transfers between devices: 7.83 us -> 31 us  [swapped(): return lax.ppermute(block, axis, [(0, 1), (1, 0)])]
    unnamed x14 -> x32, local copies, waits for them, and re-layouts: 0.03 us -> 5.18 us
    ppermute x14 -> x17, starting transfers between devices: 11.8 us -> 16.5 us  [swapped(): return lax.ppermute(block, axis, [(0, 1), (1, 0)])]
    ppermute x5 -> x4, starting transfers between devices: 7.9 us -> 9.1 us  [on_device(): ring = lambda block: lax.ppermute(block, 'far', hops)]
    pallas_call x1 -> x2, Pallas kernels: 11.7 us -> 12.4 us  [attend(): pl.pallas_call(functools.partial(attend_kernel, tok, group, direct), grid...]
  transfers between devices with their start and end apart: 21 -> 23, of which waited for: 15 -> 14; matrix products, arithmetic and copies ran while one was open for 3% -> 3% of each run, Pallas kernels for 16% -> 15%
where the time goes in v8:
time: 138 us; the launch traced here: 137 us
  waiting for transfers between devices  61.8 us (45%)
  starting transfers between devices  33.5 us (24%)
  Pallas kernels  29.8 us (22%)
  local copies, waits for them, and re-layouts  6.48 us (5%)
  other arithmetic  5.61 us (4%)
    ppermute x17, waiting for transfers between devices, swapped(): return lax.ppermute(block, axis, [(0, 1), (1, 0)])  31 us
    ppermute x2, waiting for transfers between devices, on_device(): from_behind = lambda block: lax.ppermute(block, 'far', ahead)  19 us
    ppermute x17, starting transfers between devices, swapped(): return lax.ppermute(block, axis, [(0, 1), (1, 0)])  16.5 us
    pallas_call x2, Pallas kernels, project(): pl.pallas_call(functools.partial(project_kernel, kinds, len(sources), par...  14.2 us
    pallas_call x2, Pallas kernels, attend(): pl.pallas_call(functools.partial(attend_kernel, tok, group, direct), grid...  12.4 us
    ppermute x4, waiting for transfers between devices, on_device(): ring = lambda block: lax.ppermute(block, 'far', hops)  11.8 us
    ppermute x4, starting transfers between devices, on_device(): ring = lambda block: lax.ppermute(block, 'far', hops)  9.1 us
    ppermute x2, starting transfers between devices, on_device(): from_behind = lambda block: lax.ppermute(block, 'far', ahead)  7.91 us
  transfers between devices with their start and end apart: 23, of which 14 were waited for; matrix products, arithmetic and copies ran while one was open for 3% of the time, Pallas kernels for 15%

profile of v8, /device:TPU:0, one launch (start us, length us, event | category | flops | bytes accessed | tf_op | source)
XLA Modules:
  0.0 137.4 jit_solution(16490264635128603571)
XLA Ops:
  1.8 1.8 %collective-permute-done = bf16[128,2688]{1,0:T(8,128)(2,1)S(1)} collective-permute-done((bf16[128,2688]{1,0:T(8,128)(2,1)S(1)}, bf16[128,2688]{1,0:T(8,128)(2,1)S(1)}, u32[]{:S(2)}, u32[]{:S(2)}) %collective-permute-start) | collective-permute-done | bytes 688160 | tf_op jit(solution)/shard_map/ppermute | solution.py:315
  4.9 3.0 %collective-permute-start.2 = (bf16[128,2688]{1,0:T(8,128)(2,1)S(1)}, bf16[128,2688]{1,0:T(8,128)(2,1)}, u32[]{:S(2)}, u32[]{:S(2)}) collective-permute-start(bf16[128,2688]{1,0:T(8,128)(2,1)S(1)} %get-tuple-element.32.refs_4_), channel_id=1, source_target_pairs={{0,2},{2,0},{1,3},{3,1},{4,6},{6,4},{5,7},{7,5},{8,10},{10,8},{9,1... | collective-permute-start | bytes 2064392 | tf_op jit(solution)/shard_map/ppermute | solution.py:315
  7.8 3.5 %collective-permute-start.1 = (bf16[512,512]{1,0:T(8,128)(2,1)S(1)}, bf16[512,512]{1,0:T(8,128)(2,1)S(1)}, u32[]{:S(2)}, u32[]{:S(2)}) collective-permute-start(bf16[512,512]{1,0:T(8,128)(2,1)S(1)} %copy-done.2), channel_id=1, source_target_pairs={{0,4},{4,8},{8,12},{1,5},{5,9},{9,13},{2,6},{6,10},{10,14},{3,7},{... | collective-permute-start | bytes 1572872 | tf_op jit(solution)/shard_map/ppermute | solution.py:334
  11.3 11.1 %collective-permute-done.1.k0 = bf16[512,512]{1,0:T(8,128)(2,1)S(1)} collective-permute-done((bf16[512,512]{1,0:T(8,128)(2,1)S(1)}, bf16[512,512]{1,0:T(8,128)(2,1)S(1)}, u32[]{:S(2)}, u32[]{:S(2)}) %collective-permute-start.1) | collective-permute-done | bytes 524320 | tf_op jit(solution)/shard_map/ppermute | solution.py:334
  22.5 4.4 %collective-permute-start.4 = (bf16[512,512]{1,0:T(8,128)(2,1)S(1)}, bf16[512,512]{1,0:T(8,128)(2,1)S(1)}, u32[]{:S(2)}, u32[]{:S(2)}) collective-permute-start(bf16[512,512]{1,0:T(8,128)(2,1)S(1)} %copy-done.3), channel_id=1, source_target_pairs={{0,4},{4,8},{8,12},{1,5},{5,9},{9,13},{2,6},{6,10},{10,14},{3,7},{... | collective-permute-start | bytes 1572872 | tf_op jit(solution)/shard_map/ppermute | solution.py:334
  28.3 1.6 %collective-permute-start.6 = (bf16[128,2688]{1,0:T(8,128)(2,1)S(1)}, bf16[128,2688]{1,0:T(8,128)(2,1)}, u32[]{:S(2)}, u32[]{:S(2)}) collective-permute-start(bf16[128,2688]{1,0:T(8,128)(2,1)S(1)} %get-tuple-element.32.refs_4_), channel_id=1, source_target_pairs={{0,4},{4,12},{12,8},{8,0},{1,5},{5,13},{13,9},{9,1},{2,6},{6,14},{... | collective-permute-start | bytes 2064392 | tf_op jit(solution)/shard_map/ppermute | solution.py:353
  31.3 7.9 %collective-permute-done.4.v0 = bf16[512,512]{1,0:T(8,128)(2,1)S(1)} collective-permute-done((bf16[512,512]{1,0:T(8,128)(2,1)S(1)}, bf16[512,512]{1,0:T(8,128)(2,1)S(1)}, u32[]{:S(2)}, u32[]{:S(2)}) %collective-permute-start.4) | collective-permute-done | bytes 524320 | tf_op jit(solution)/shard_map/ppermute | solution.py:334
  41.4 2.8 %fusion = (f32[1536,64]{1,0:T(8,128)S(1)}, f32[1536,64]{1,0:T(8,128)S(1)}, f32[1536,64]{1,0:T(8,128)S(1)}) fusion(f32[64]{0:T(128)S(1)} %multiply_exponential_fusion, f32[1536]{0:T(1024)S(1)} %add_convert_fusion), kind=kLoop, calls=%fused_computation.8 | loop fusion | flops 196608 | bytes 1186048 | tf_op jit(solution)/shard_map/neg | solution.py:34
  44.7 7.4 %collective-permute-done.6.refs_5_ = bf16[128,2688]{1,0:T(8,128)(2,1)} collective-permute-done((bf16[128,2688]{1,0:T(8,128)(2,1)S(1)}, bf16[128,2688]{1,0:T(8,128)(2,1)}, u32[]{:S(2)}, u32[]{:S(2)}) %collective-permute-start.6) | collective-permute-done | bytes 688160 | tf_op jit(solution)/shard_map/ppermute | solution.py:353
  52.5 2.6 %collective-permute-start.10 = (bf16[128,2688]{1,0:T(8,128)(2,1)}, bf16[128,2688]{1,0:T(8,128)(2,1)}, u32[]{:S(2)}, u32[]{:S(2)}) collective-permute-start(bf16[128,2688]{1,0:T(8,128)(2,1)} %collective-permute-done.6.refs_5_), channel_id=1, source_target_pairs={{0,4},{4,12},{12,8},{8,0},{1,5},{5,13},{13,9},{9,1},{2,6},{6,14},{... | collective-permute-start | bytes 2064392 | tf_op jit(solution)/shard_map/ppermute | solution.py:353
  58.5 6.2 %shard_map.82.refs_0_ = bf16[4,512,128]{2,1,0:T(8,128)(2,1)S(1)} custom-call(s32[1]{0:T(128)} %bitcast.3.row_ref, bf16[512,1024]{1,0:T(8,128)(2,1)S(1)} %copy-done.9, bf16[512,512]{1,0:T(8,128)(2,1)S(1)} %collective-permute-done.1.k0, bf16[512,512]{1,0:T(8,128)(2,1)} %collective-permute-done.3.k1, bf16[512,512]{1,0:T(8,128)(2,1)S(1)} %copy-done.2, ...), custom_call_target="tpu_custom_call" | custom-call | flops 5368709120 | bytes 6291456 | tf_op jit(solution)/shard_map/pallas_call | solution.py:105
  64.7 3.1 %collective-permute-done.7.refs_9_ = bf16[128,2688]{1,0:T(8,128)(2,1)} collective-permute-done((bf16[128,2688]{1,0:T(8,128)(2,1)}, bf16[128,2688]{1,0:T(8,128)(2,1)}, u32[]{:S(2)}, u32[]{:S(2)}) %collective-permute-start.7) | collective-permute-done | bytes 688160 | tf_op jit(solution)/shard_map/ppermute | solution.py:315
  72.0 1.7 %collective-permute-start.11 = (bf16[128,2688]{1,0:T(8,128)(2,1)}, bf16[128,2688]{1,0:T(8,128)(2,1)}, u32[]{:S(2)}, u32[]{:S(2)}) collective-permute-start(bf16[128,2688]{1,0:T(8,128)(2,1)} %collective-permute-done.10.refs_6_), channel_id=1, source_target_pairs={{0,4},{4,12},{12,8},{8,0},{1,5},{5,13},{13,9},{9,1},{2,6},{6,14},{... | collective-permute-start | bytes 2064392 | tf_op jit(solution)/shard_map/ppermute | solution.py:353
  75.9 6.2 %shard_map.83.refs_1_ = bf16[4,512,128]{2,1,0:T(8,128)(2,1)S(1)} custom-call(s32[1]{0:T(128)} %bitcast.4.row_ref, bf16[512,1024]{1,0:T(8,128)(2,1)S(1)} %copy-done.9, bf16[512,512]{1,0:T(8,128)(2,1)S(1)} %copy-done.5, bf16[512,512]{1,0:T(8,128)(2,1)} %collective-permute-done.3.k1, bf16[512,512]{1,0:T(8,128)(2,1)S(1)} %copy-done.2, ...), custom_call_target="tpu_custom_call" | custom-call | flops 5368709120 | bytes 6291456 | tf_op jit(solution)/shard_map/pallas_call | solution.py:105
  83.7 3.3 %collective-permute-done.11.refs_7_ = bf16[128,2688]{1,0:T(8,128)(2,1)} collective-permute-done((bf16[128,2688]{1,0:T(8,128)(2,1)}, bf16[128,2688]{1,0:T(8,128)(2,1)}, u32[]{:S(2)}, u32[]{:S(2)}) %collective-permute-start.11) | collective-permute-done | bytes 688160 | tf_op jit(solution)/shard_map/ppermute | solution.py:353
  87.5 1.7 %collective-permute-done.18.refs_15_ = bf16[128,2688]{1,0:T(8,128)(2,1)} collective-permute-done((bf16[128,2688]{1,0:T(8,128)(2,1)}, bf16[128,2688]{1,0:T(8,128)(2,1)}, u32[]{:S(2)}, u32[]{:S(2)}) %collective-permute-start.18) | collective-permute-done | bytes 688160 | tf_op jit(solution)/shard_map/ppermute | solution.py:315
  90.7 13.3 %collective-permute-done.16.refs_13_ = bf16[128,2688]{1,0:T(8,128)(2,1)} collective-permute-done((bf16[128,2688]{1,0:T(8,128)(2,1)}, bf16[128,2688]{1,0:T(8,128)(2,1)}, u32[]{:S(2)}, u32[]{:S(2)}) %collective-permute-start.16) | collective-permute-done | bytes 688160 | tf_op jit(solution)/shard_map/ppermute | solution.py:315
  103.9 3.2 %collective-permute-start.17 = (bf16[128,2688]{1,0:T(8,128)(2,1)}, bf16[128,2688]{1,0:T(8,128)(2,1)S(1)}, u32[]{:S(2)}, u32[]{:S(2)}) collective-permute-start(bf16[128,2688]{1,0:T(8,128)(2,1)} %collective-permute-done.16.refs_13_), channel_id=1, source_target_pairs={{0,4},{4,12},{12,8},{8,0},{1,5},{5,13},{13,9},{9,1},{2,6},{6,14},{... | collective-permute-start | bytes 2064392 | tf_op jit(solution)/shard_map/ppermute | solution.py:353
  109.4 8.4 %shard_map.84.refs_9_ = f32[512,2688]{1,0:T(8,128)S(1)} custom-call(s32[4]{0:T(128)S(1)} %pad_add_fusion.where_ref, bf16[4,512,128]{2,1,0:T(8,128)(2,1)S(1)} %shard_map.82.refs_0_, bf16[4,512,128]{2,1,0:T(8,128)(2,1)S(1)} %shard_map.83.refs_1_, bf16[4,512,128]{2,1,0:T(8,128)(2,1)S(1)} %collective-permute-done.8.refs_2_, ...), custom_call_target="tpu_custom_call" | custom-call | flops 8455716864 | bytes 8257536 | tf_op jit(solution)/shard_map/pallas_call | solution.py:251
  117.9 1.6 %collective-permute-start.20 = (bf16[64,2688]{1,0:T(8,128)(2,1)S(1)}, bf16[64,2688]{1,0:T(8,128)(2,1)S(1)}, u32[]{:S(2)}, u32[]{:S(2)}) collective-permute-start(bf16[64,2688]{1,0:T(8,128)(2,1)S(1)} %slice.8), channel_id=1, source_target_pairs={{0,16},{16,0},{1,17},{17,1},{2,18},{18,2},{3,19},{19,3},{4,20},{20... | collective-permute-start | bytes 1032200 | tf_op jit(solution)/shard_map/ppermute | solution.py:315
  120.1 5.1 %collective-permute-done.20.refs_7_ = bf16[64,2688]{1,0:T(8,128)(2,1)S(1)} collective-permute-done((bf16[64,2688]{1,0:T(8,128)(2,1)S(1)}, bf16[64,2688]{1,0:T(8,128)(2,1)S(1)}, u32[]{:S(2)}, u32[]{:S(2)}) %collective-permute-start.20) | collective-permute-done | bytes 344096 | tf_op jit(solution)/shard_map/ppermute | solution.py:315
  125.2 1.6 %collective-permute-done.21.refs_8_ = bf16[64,2688]{1,0:T(8,128)(2,1)S(1)} collective-permute-done((bf16[64,2688]{1,0:T(8,128)(2,1)S(1)}, bf16[64,2688]{1,0:T(8,128)(2,1)S(1)}, u32[]{:S(2)}, u32[]{:S(2)}) %collective-permute-start.21) | collective-permute-done | bytes 344096 | tf_op jit(solution)/shard_map/ppermute | solution.py:315
  126.8 5.8 %shard_map.85 = (f32[512,2688]{1,0:T(8,128)S(1)}, f32[520,128]{1,0:T(8,128)S(1)}) custom-call(s32[4]{0:T(128)S(1)} %pad_add_fusion.where_ref, bf16[4,512,128]{2,1,0:T(8,128)(2,1)S(1)} %shard_map.82.refs_0_, bf16[4,512,128]{2,1,0:T(8,128)(2,1)S(1)} %shard_map.83.refs_1_, bf16[4,512,128]{2,1,0:T(8,128)(2,1)S(1)} %collective-permute-done.8.refs_2_, ...), custom_call_target="tpu_custom_call" | custom-call | flops 2818572288 | bytes 2752512 | tf_op jit(solution)/shard_map/pallas_call | solution.py:251
  134.2 3.2 %shard_map.86 = bf16[512,2688]{1,0:T(8,128)(2,1)} custom-call(f32[520,128]{1,0:T(8,128)S(1)} %get-tuple-element.47.own_ref, f32[520,128]{1,0:T(8,128)S(1)} %collective-permute-done.22.other_ref, f32[1,2688]{1,0:T(1,128)S(1)} %broadcast_in_dim.16.refs_10_.gain_ref, f32[64,2688]{1,0:T(8,128)S(1)} %bitcast.8, f32[512,2688]{1,0:T(8,128)S(1)} %get-tuple-element.48.hidden_ref), custom_call_target="tpu_custom_call" | custom-call | flops 704643072 | bytes 8257536 | tf_op jit(solution)/shard_map/pallas_call | solution.py:294
  (72 shorter events, 26.8 us)
Async XLA Ops:
  1.2 2.3 %collective-permute-start = (bf16[128,2688]{1,0:T(8,128)(2,1)S(1)}, bf16[128,2688]{1,0:T(8,128)(2,1)S(1)}, u32[]{:S(2)}, u32[]{:S(2)}) collective-permute-start(bf16[128,2688]{1,0:T(8,128)(2,1)S(1)} %constant_dynamic-slice_fusion), channel_id=1, source_target_pairs={{0,1},{1,0},{2,3},{3,2},{4,5},{5,4},{6,7},{7,6},{8,9},{9,8},{10,11... | collective-permute-start | bytes 2064392 | tf_op jit(solution)/shard_map/ppermute | solution.py:315
  4.9 22.0 %collective-permute-start.2 = (bf16[128,2688]{1,0:T(8,128)(2,1)S(1)}, bf16[128,2688]{1,0:T(8,128)(2,1)}, u32[]{:S(2)}, u32[]{:S(2)}) collective-permute-start(bf16[128,2688]{1,0:T(8,128)(2,1)S(1)} %get-tuple-element.32.refs_4_), channel_id=1, source_target_pairs={{0,2},{2,0},{1,3},{3,1},{4,6},{6,4},{5,7},{7,5},{8,10},{10,8},{9,1... | collective-permute-start | bytes 2064392 | tf_op jit(solution)/shard_map/ppermute | solution.py:315
  7.8 14.7 %collective-permute-start.1 = (bf16[512,512]{1,0:T(8,128)(2,1)S(1)}, bf16[512,512]{1,0:T(8,128)(2,1)S(1)}, u32[]{:S(2)}, u32[]{:S(2)}) collective-permute-start(bf16[512,512]{1,0:T(8,128)(2,1)S(1)} %copy-done.2), channel_id=1, source_target_pairs={{0,4},{4,8},{8,12},{1,5},{5,9},{9,13},{2,6},{6,10},{10,14},{3,7},{... | collective-permute-start | bytes 1572872 | tf_op jit(solution)/shard_map/ppermute | solution.py:334
  22.5 35.0 %copy-start.4 = (bf16[512,512]{1,0:T(8,128)(2,1)}, bf16[512,512]{1,0:T(8,128)(2,1)S(1)}, u32[]{:S(2)}) copy-start(bf16[512,512]{1,0:T(8,128)(2,1)S(1)} %collective-permute-done.1.k0) | copy-start | bytes 1572868
  22.5 16.7 %collective-permute-start.4 = (bf16[512,512]{1,0:T(8,128)(2,1)S(1)}, bf16[512,512]{1,0:T(8,128)(2,1)S(1)}, u32[]{:S(2)}, u32[]{:S(2)}) collective-permute-start(bf16[512,512]{1,0:T(8,128)(2,1)S(1)} %copy-done.3), channel_id=1, source_target_pairs={{0,4},{4,8},{8,12},{1,5},{5,9},{9,13},{2,6},{6,10},{10,14},{3,7},{... | collective-permute-start | bytes 1572872 | tf_op jit(solution)/shard_map/ppermute | solution.py:334
  27.8 13.0 %collective-permute-start.3 = (bf16[512,512]{1,0:T(8,128)(2,1)}, bf16[512,512]{1,0:T(8,128)(2,1)}, u32[]{:S(2)}, u32[]{:S(2)}) collective-permute-start(bf16[512,512]{1,0:T(8,128)(2,1)} %broadcast_select_fusion.3), channel_id=1, source_target_pairs={{0,2},{2,0},{1,3},{3,1},{4,6},{6,4},{5,7},{7,5},{8,10},{10,8},{9,1... | collective-permute-start | bytes 1572872 | tf_op jit(solution)/shard_map/ppermute | solution.py:315
  28.3 23.8 %collective-permute-start.6 = (bf16[128,2688]{1,0:T(8,128)(2,1)S(1)}, bf16[128,2688]{1,0:T(8,128)(2,1)}, u32[]{:S(2)}, u32[]{:S(2)}) collective-permute-start(bf16[128,2688]{1,0:T(8,128)(2,1)S(1)} %get-tuple-element.32.refs_4_), channel_id=1, source_target_pairs={{0,4},{4,12},{12,8},{8,0},{1,5},{5,13},{13,9},{9,1},{2,6},{6,14},{... | collective-permute-start | bytes 2064392 | tf_op jit(solution)/shard_map/ppermute | solution.py:353
  29.8 25.3 %collective-permute-start.14 = (bf16[128,2688]{1,0:T(8,128)(2,1)}, bf16[128,2688]{1,0:T(8,128)(2,1)S(1)}, u32[]{:S(2)}, u32[]{:S(2)}) collective-permute-start(bf16[128,2688]{1,0:T(8,128)(2,1)} %collective-permute-done.2.refs_8_), channel_id=1, source_target_pairs={{0,16},{16,0},{1,17},{17,1},{2,18},{18,2},{3,19},{19,3},{4,20},{20... | collective-permute-start | bytes 2064392 | tf_op jit(solution)/shard_map/ppermute | solution.py:315
  40.8 16.7 %collective-permute-start.5 = (bf16[512,512]{1,0:T(8,128)(2,1)S(1)}, bf16[512,512]{1,0:T(8,128)(2,1)S(1)}, u32[]{:S(2)}, u32[]{:S(2)}) collective-permute-start(bf16[512,512]{1,0:T(8,128)(2,1)S(1)} %broadcast_select_fusion.2), channel_id=1, source_target_pairs={{0,2},{2,0},{1,3},{3,1},{4,6},{6,4},{5,7},{7,5},{8,10},{10,8},{9,1... | collective-permute-start | bytes 1572872 | tf_op jit(solution)/shard_map/ppermute | solution.py:315
  52.0 15.8 %collective-permute-start.7 = (bf16[128,2688]{1,0:T(8,128)(2,1)}, bf16[128,2688]{1,0:T(8,128)(2,1)}, u32[]{:S(2)}, u32[]{:S(2)}) collective-permute-start(bf16[128,2688]{1,0:T(8,128)(2,1)} %collective-permute-done.6.refs_5_), channel_id=1, source_target_pairs={{0,2},{2,0},{1,3},{3,1},{4,6},{6,4},{5,7},{7,5},{8,10},{10,8},{9,1... | collective-permute-start | bytes 2064392 | tf_op jit(solution)/shard_map/ppermute | solution.py:315
  52.5 16.4 %collective-permute-start.10 = (bf16[128,2688]{1,0:T(8,128)(2,1)}, bf16[128,2688]{1,0:T(8,128)(2,1)}, u32[]{:S(2)}, u32[]{:S(2)}) collective-permute-start(bf16[128,2688]{1,0:T(8,128)(2,1)} %collective-permute-done.6.refs_5_), channel_id=1, source_target_pairs={{0,4},{4,12},{12,8},{8,0},{1,5},{5,13},{13,9},{9,1},{2,6},{6,14},{... | collective-permute-start | bytes 2064392 | tf_op jit(solution)/shard_map/ppermute | solution.py:353
  56.0 17.7 %collective-permute-start.15 = (bf16[128,2688]{1,0:T(8,128)(2,1)}, bf16[128,2688]{1,0:T(8,128)(2,1)S(1)}, u32[]{:S(2)}, u32[]{:S(2)}) collective-permute-start(bf16[128,2688]{1,0:T(8,128)(2,1)} %collective-permute-done.6.refs_5_), channel_id=1, source_target_pairs={{0,16},{16,0},{1,17},{17,1},{2,18},{18,2},{3,19},{19,3},{4,20},{20... | collective-permute-start | bytes 2064392 | tf_op jit(solution)/shard_map/ppermute | solution.py:315
  69.0 14.6 %collective-permute-start.12 = (bf16[128,2688]{1,0:T(8,128)(2,1)}, bf16[128,2688]{1,0:T(8,128)(2,1)}, u32[]{:S(2)}, u32[]{:S(2)}) collective-permute-start(bf16[128,2688]{1,0:T(8,128)(2,1)} %collective-permute-done.10.refs_6_), channel_id=1, source_target_pairs={{0,2},{2,0},{1,3},{3,1},{4,6},{6,4},{5,7},{7,5},{8,10},{10,8},{9,1... | collective-permute-start | bytes 2064392 | tf_op jit(solution)/shard_map/ppermute | solution.py:315
  70.5 18.7 %collective-permute-start.18 = (bf16[128,2688]{1,0:T(8,128)(2,1)}, bf16[128,2688]{1,0:T(8,128)(2,1)}, u32[]{:S(2)}, u32[]{:S(2)}) collective-permute-start(bf16[128,2688]{1,0:T(8,128)(2,1)} %collective-permute-done.7.refs_9_), channel_id=1, source_target_pairs={{0,16},{16,0},{1,17},{17,1},{2,18},{18,2},{3,19},{19,3},{4,20},{20... | collective-permute-start | bytes 2064392 | tf_op jit(solution)/shard_map/ppermute | solution.py:315
  72.0 15.0 %collective-permute-start.11 = (bf16[128,2688]{1,0:T(8,128)(2,1)}, bf16[128,2688]{1,0:T(8,128)(2,1)}, u32[]{:S(2)}, u32[]{:S(2)}) collective-permute-start(bf16[128,2688]{1,0:T(8,128)(2,1)} %collective-permute-done.10.refs_6_), channel_id=1, source_target_pairs={{0,4},{4,12},{12,8},{8,0},{1,5},{5,13},{13,9},{9,1},{2,6},{6,14},{... | collective-permute-start | bytes 2064392 | tf_op jit(solution)/shard_map/ppermute | solution.py:353
  73.7 30.2 %collective-permute-start.16 = (bf16[128,2688]{1,0:T(8,128)(2,1)}, bf16[128,2688]{1,0:T(8,128)(2,1)}, u32[]{:S(2)}, u32[]{:S(2)}) collective-permute-start(bf16[128,2688]{1,0:T(8,128)(2,1)} %collective-permute-done.10.refs_6_), channel_id=1, source_target_pairs={{0,16},{16,0},{1,17},{17,1},{2,18},{18,2},{3,19},{19,3},{4,20},{20... | collective-permute-start | bytes 2064392 | tf_op jit(solution)/shard_map/ppermute | solution.py:315
  82.1 25.1 %collective-permute-start.8 = (bf16[4,512,128]{2,1,0:T(8,128)(2,1)S(1)}, bf16[4,512,128]{2,1,0:T(8,128)(2,1)S(1)}, u32[]{:S(2)}, u32[]{:S(2)}) collective-permute-start(bf16[4,512,128]{2,1,0:T(8,128)(2,1)S(1)} %shard_map.82.refs_0_), channel_id=1, source_target_pairs={{0,1},{1,0},{2,3},{3,2},{4,5},{5,4},{6,7},{7,6},{8,9},{9,8},{10,11... | collective-permute-start | bytes 1572872 | tf_op jit(solution)/shard_map/ppermute | solution.py:315
  83.6 23.6 %collective-permute-start.9 = (bf16[4,512,128]{2,1,0:T(8,128)(2,1)S(1)}, bf16[4,512,128]{2,1,0:T(8,128)(2,1)S(1)}, u32[]{:S(2)}, u32[]{:S(2)}) collective-permute-start(bf16[4,512,128]{2,1,0:T(8,128)(2,1)S(1)} %shard_map.83.refs_1_), channel_id=1, source_target_pairs={{0,1},{1,0},{2,3},{3,2},{4,5},{5,4},{6,7},{7,6},{8,9},{9,8},{10,11... | collective-permute-start | bytes 1572872 | tf_op jit(solution)/shard_map/ppermute | solution.py:315
  87.0 30.9 %collective-permute-start.13 = (bf16[128,2688]{1,0:T(8,128)(2,1)}, bf16[128,2688]{1,0:T(8,128)(2,1)S(1)}, u32[]{:S(2)}, u32[]{:S(2)}) collective-permute-start(bf16[128,2688]{1,0:T(8,128)(2,1)} %collective-permute-done.11.refs_7_), channel_id=1, source_target_pairs={{0,2},{2,0},{1,3},{3,1},{4,6},{6,4},{5,7},{7,5},{8,10},{10,8},{9,1... | collective-permute-start | bytes 2064392 | tf_op jit(solution)/shard_map/ppermute | solution.py:315
  89.2 28.7 %collective-permute-start.19 = (bf16[128,2688]{1,0:T(8,128)(2,1)}, bf16[128,2688]{1,0:T(8,128)(2,1)S(1)}, u32[]{:S(2)}, u32[]{:S(2)}) collective-permute-start(bf16[128,2688]{1,0:T(8,128)(2,1)} %collective-permute-done.12.refs_10_), channel_id=1, source_target_pairs={{0,16},{16,0},{1,17},{17,1},{2,18},{18,2},{3,19},{19,3},{4,20},{20... | collective-permute-start | bytes 2064392 | tf_op jit(solution)/shard_map/ppermute | solution.py:315
  103.9 15.5 %collective-permute-start.17 = (bf16[128,2688]{1,0:T(8,128)(2,1)}, bf16[128,2688]{1,0:T(8,128)(2,1)S(1)}, u32[]{:S(2)}, u32[]{:S(2)}) collective-permute-start(bf16[128,2688]{1,0:T(8,128)(2,1)} %collective-permute-done.16.refs_13_), channel_id=1, source_target_pairs={{0,4},{4,12},{12,8},{8,0},{1,5},{5,13},{13,9},{9,1},{2,6},{6,14},{... | collective-permute-start | bytes 2064392 | tf_op jit(solution)/shard_map/ppermute | solution.py:353
  117.9 7.3 %collective-permute-start.20 = (bf16[64,2688]{1,0:T(8,128)(2,1)S(1)}, bf16[64,2688]{1,0:T(8,128)(2,1)S(1)}, u32[]{:S(2)}, u32[]{:S(2)}) collective-permute-start(bf16[64,2688]{1,0:T(8,128)(2,1)S(1)} %slice.8), channel_id=1, source_target_pairs={{0,16},{16,0},{1,17},{17,1},{2,18},{18,2},{3,19},{19,3},{4,20},{20... | collective-permute-start | bytes 1032200 | tf_op jit(solution)/shard_map/ppermute | solution.py:315
  119.5 7.3 %collective-permute-start.21 = (bf16[64,2688]{1,0:T(8,128)(2,1)S(1)}, bf16[64,2688]{1,0:T(8,128)(2,1)S(1)}, u32[]{:S(2)}, u32[]{:S(2)}) collective-permute-start(bf16[64,2688]{1,0:T(8,128)(2,1)S(1)} %slice.9), channel_id=1, source_target_pairs={{0,2},{2,0},{1,3},{3,1},{4,6},{6,4},{5,7},{7,5},{8,10},{10,8},{9,1... | collective-permute-start | bytes 1032200 | tf_op jit(solution)/shard_map/ppermute | solution.py:315
  132.5 1.6 %collective-permute-start.22 = (f32[520,128]{1,0:T(8,128)S(1)}, f32[520,128]{1,0:T(8,128)S(1)}, u32[]{:S(2)}, u32[]{:S(2)}) collective-permute-start(f32[520,128]{1,0:T(8,128)S(1)} %get-tuple-element.47.own_ref), channel_id=1, source_target_pairs={{0,1},{1,0},{2,3},{3,2},{4,5},{5,4},{6,7},{7,6},{8,9},{9,8},{10,11... | collective-permute-start | bytes 798728 | tf_op jit(solution)/shard_map/ppermute | solution.py:315
  (15 other events, 128.4 us)

commit v9 on v8

--- a/solution.py
+++ b/solution.py
@@ -18,7 +18,7 @@
 log2_e = 1.4426950408889634
 
 TILE = 896
-VMEM_LIMIT = 32 * 2**20
+VMEM_LIMIT = 20 * 2**20
 
 NT = (((1,), (1,)), ((), ()))
 
@@ -350,50 +350,53 @@
     if direct:
         order = ring_order(outer)
         hops = [(order[i], order[(i + 1) % outer]) for i in range(outer)]
-        ring = lambda block: lax.ppermute(block, "far", hops)
-        beyond = lambda block: swapped(block, "near")
-        facing = lambda block: swapped(block, "grp")
+        queues = {"far": [], "near": [], "grp": []}
+
+        def send(axis, block, *earlier, route=((0, 1), (1, 0))):
+            queue = queues[axis]
+            waits = (*earlier, *queue[-2:-1])
+            queue.append(lax.ppermute(after(block, *waits) if waits else block, axis, route))
+            return queue[-1]
+
+        ring = lambda block, *earlier: send("far", block, *earlier, route=hops)
+        beyond = lambda block, *earlier: send("near", block, *earlier)
+        facing = lambda block, *earlier: send("grp", block, *earlier)
         main, beside, across, corner = ({} for _ in range(4))
-        main[0] = jnp.where(is_mine, mine, theirs)
-        across[0] = jnp.where(is_mine, theirs, mine)
-        beside[0] = beyond(main[0])
-        second_keys = from_behind(after(keys, main[0]))
-        second_values = from_behind(after(values, second_keys))
-        main[1] = ring(after(main[0], second_keys))
-        first_keys = for_next(keys, after(second_keys, beside[0]))
-        corner[0] = facing(beside[0])
+        rows = [slice(0, depth // 2), slice(depth // 2, depth)]
+        main[0] = [jnp.where(is_mine, mine[r], theirs[r]) for r in rows]
+        across[0] = [jnp.where(is_mine, theirs[r], mine[r]) for r in rows]
+        beside[0] = [beyond(half) for half in main[0]]
+        second_keys = send("far", keys, main[0], route=ahead)
+        second_values = send("far", values, beside[0][0], route=ahead)
         cos, sin = rope_tables((after(row, beside[0], second_keys) - 2) * tok, 3 * tok)
-        first_values = for_next(values, after(second_values, first_keys))
-        main[2] = ring(after(main[1], cos, sin))
-        across[1] = facing(after(main[1], corner[0]))
-        beside[1] = beyond(after(main[1], second_values))
+        first_keys = beyond(jnp.where(near == 0, keys, after(second_keys, beside[0])))
+        corner[0] = [facing(half) for half in beside[0]]
+        main[1] = [ring(main[0][0], beside[0]), ring(main[0][1])]
+        first_values = beyond(jnp.where(near == 0, values, second_values))
+        beside[1] = [beyond(half) for half in main[1]]
+        across[1] = [facing(half) for half in main[1]]
+        main[2] = [ring(half) for half in main[1]]
+        corner[1] = [facing(half) for half in beside[1]]
         key_blocks, val_blocks = (second_keys, first_keys, keys), (second_values, first_values, values)
         some = kv_local // 2
         early = attend(row[None], queries, key_blocks, val_blocks, cos, sin, True, 0, some)
-        main[3] = ring(after(main[2], early))
-        across[2] = facing(after(main[2], across[1], early))
-        beside[2] = beyond(after(main[2], beside[1], early))
-        corner[1] = facing(after(beside[1], early))
-        rest = attend(after(row, beside[1])[None], queries, key_blocks, val_blocks, cos, sin, True, some, kv_local - some)
+        main[3] = [ring(main[2][0], early), ring(main[2][1])]
+        rest = attend(after(row, main[2][0])[None], queries, key_blocks, val_blocks, cos, sin, True, some, kv_local - some)
+        beside[2] = [beyond(main[2][0], early), beyond(main[2][1], rest)]
+        corner[2] = [facing(half) for half in beside[2]]
         attended = [early, rest]
         att_other = [swapped(after(early, rest), "col"), swapped(rest, "col")]
-        across[3] = ring(after(across[2], main[3]))
-        beside[3] = beyond(after(main[3], beside[2], rest))
-        corner[2] = facing(after(beside[2], corner[1]))
+        beside[3] = [beyond(half) for half in main[3]]
+        across[2] = [ring(half) for half in across[1]]
+        across[3] = [ring(half) for half in across[2]]
+        corner[3] = [facing(half) for half in beside[3]]
         weights, kinds, late, late_kinds = [], [], [], []
-        last_ones = (("beside", 3), ("across", 3), ("corner", 2))
         for name, pieces in (("main", main), ("beside", beside), ("across", across), ("corner", corner)):
             for k in range(outer):
-                if (name, k) == ("corner", 3):
-                    continue
-                is_late = (name, k) in last_ones
-                (late if is_late else weights).append(pieces[k])
+                is_late = k == 3 and name in ("across", "corner")
+                (late if is_late else weights).extend(pieces[k])
                 (late_kinds if is_late else kinds).append((name, k))
         (partial,) = project(where, kinds, attended + att_other, weights)
-        half = depth // 2
-        late.append(facing(after(beside[3][:half], corner[2], partial)))
-        late.append(beyond(after(across[3][half:], beside[3], partial)))
-        late_kinds.append(("corner", 3))
     else:
         second_keys, second_values = from_behind(keys), from_behind(values)
         first_keys, first_values = for_next(keys, second_keys), for_next(values, second_values)

time: 138 us -> 143 us (1.036)
  waiting for transfers between devices: 61.8 us -> 42 us
  starting transfers between devices: 33.5 us -> 45.9 us
  local copies, waits for them, and re-layouts: 6.48 us -> 17.1 us
    ppermute x6 -> x32, starting transfers between devices: 17 us -> 45.3 us  [send(): lax.ppermute(after(block, *waits) if waits else block, axis, route)]
    ppermute x17 -> x4, waiting for transfers between devices: 31 us -> 3.3 us  [swapped(): return lax.ppermute(block, axis, [(0, 1), (1, 0)])]
    ppermute x17 -> x4, starting transfers between devices: 16.5 us -> 0.59 us  [swapped(): return lax.ppermute(block, axis, [(0, 1), (1, 0)])]
    unnamed x32 -> x64, local copies, waits for them, and re-layouts: 5.18 us -> 15.8 us
    ppermute x6 -> x32, waiting for transfers between devices: 30.8 us -> 38.7 us  [send(): lax.ppermute(after(block, *waits) if waits else block, axis, route)]
  transfers between devices with their start and end apart: 23 -> 36, of which waited for: 14 -> 13; matrix products, arithmetic and copies ran while one was open for 3% -> 3% of each run, Pallas kernels for 15% -> 16%
where the time goes in v9:
time: 143 us; the launch traced here: 142 us
  starting transfers between devices  45.9 us (32%)
  waiting for transfers between devices  42 us (29%)
  Pallas kernels  30.6 us (21%)
  local copies, waits for them, and re-layouts  17.1 us (12%)
  other arithmetic  6.34 us (4%)
    ppermute x32, starting transfers between devices, send(): lax.ppermute(after(block, *waits) if waits else block, axis, route)  45.3 us
    ppermute x32, waiting for transfers between devices, send(): lax.ppermute(after(block, *waits) if waits else block, axis, route)  38.7 us
    unnamed x64, local copies, waits for them, and re-layouts  15.8 us
    pallas_call x2, Pallas kernels, project(): pl.pallas_call(functools.partial(project_kernel, kinds, len(sources), par...  15 us
    pallas_call x2, Pallas kernels, attend(): pl.pallas_call(functools.partial(attend_kernel, tok, group, direct), grid...  12.4 us
    ppermute x4, waiting for transfers between devices, swapped(): return lax.ppermute(block, axis, [(0, 1), (1, 0)])  3.3 us
    pallas_call x1, Pallas kernels, finish(): pl.pallas_call(functools.partial(finish_kernel, model_width), grid=(width...  3.24 us
  transfers between devices with their start and end apart: 36, of which 13 were waited for; matrix products, arithmetic and copies ran while one was open for 3% of the time, Pallas kernels for 16%

profile of v9, /device:TPU:0, one launch (start us, length us, event | category | flops | bytes accessed | tf_op | source)
XLA Modules:
  0.0 142.1 jit_solution(2078219934429222617)
XLA Ops:
  1.8 1.8 %collective-permute-done = bf16[128,2688]{1,0:T(8,128)(2,1)S(1)} collective-permute-done((bf16[128,2688]{1,0:T(8,128)(2,1)S(1)}, bf16[128,2688]{1,0:T(8,128)(2,1)S(1)}, u32[]{:S(2)}, u32[]{:S(2)}) %collective-permute-start) | collective-permute-done | bytes 688160 | tf_op jit(solution)/shard_map/ppermute | solution.py:315
  3.5 2.1 %broadcast_select_fusion.2 = (bf16[64,2688]{1,0:T(8,128)(2,1)S(1)}, bf16[64,2688]{1,0:T(8,128)(2,1)S(1)}, bf16[64,2688]{1,0:T(8,128)(2,1)}, bf16[64,2688]{1,0:T(8,128)(2,1)S(1)}) fusion(pred[]{:T(512)S(6)} %eq.7, bf16[128,2688]{1,0:T(8,128)(2,1)S(1)} %collective-permute-done, bf16[128,5376]{1,0:T(8,128)(2,1)} %param.11, s32[]{:T(128)S(6)} %add.28, ...), kind=kLoop, calls=%fused_computation.6 | loop fusion | flops 688128 | bytes 2752521 | tf_op jit(solution)/shard_map/jit(_where)/select_n | solution.py:367
  5.6 4.9 %collective-permute-start.1 = (bf16[512,512]{1,0:T(8,128)(2,1)S(1)}, bf16[512,512]{1,0:T(8,128)(2,1)S(1)}, u32[]{:S(2)}, u32[]{:S(2)}) collective-permute-start(bf16[512,512]{1,0:T(8,128)(2,1)S(1)} %copy-done.2), channel_id=1, source_target_pairs={{0,4},{4,8},{8,12},{1,5},{5,9},{9,13},{2,6},{6,10},{10,14},{3,7},{... | collective-permute-start | bytes 1572872 | tf_op jit(solution)/shard_map/ppermute | solution.py:358
  12.6 8.9 %collective-permute-done.2.refs_12_ = bf16[64,2688]{1,0:T(8,128)(2,1)S(1)} collective-permute-done((bf16[64,2688]{1,0:T(8,128)(2,1)S(1)}, bf16[64,2688]{1,0:T(8,128)(2,1)S(1)}, u32[]{:S(2)}, u32[]{:S(2)}) %collective-permute-start.2) | collective-permute-done | bytes 344096 | tf_op jit(solution)/shard_map/ppermute | solution.py:358
  21.5 3.5 %collective-permute-start.5 = (bf16[512,512]{1,0:T(8,128)(2,1)S(1)}, bf16[512,512]{1,0:T(8,128)(2,1)S(1)}, u32[]{:S(2)}, u32[]{:S(2)}) collective-permute-start(bf16[512,512]{1,0:T(8,128)(2,1)S(1)} %copy-done.3), channel_id=1, source_target_pairs={{0,4},{4,8},{8,12},{1,5},{5,9},{9,13},{2,6},{6,10},{10,14},{3,7},{... | collective-permute-start | bytes 1572872 | tf_op jit(solution)/shard_map/ppermute | solution.py:358
  33.3 8.3 %collective-permute-done.7.refs_6_ = bf16[64,2688]{1,0:T(8,128)(2,1)} collective-permute-done((bf16[64,2688]{1,0:T(8,128)(2,1)S(1)}, bf16[64,2688]{1,0:T(8,128)(2,1)}, u32[]{:S(2)}, u32[]{:S(2)}) %collective-permute-start.7) | collective-permute-done | bytes 344096 | tf_op jit(solution)/shard_map/ppermute | solution.py:358
  41.6 2.6 %collective-permute-start.8 = (bf16[64,2688]{1,0:T(8,128)(2,1)}, bf16[64,2688]{1,0:T(8,128)(2,1)S(1)}, u32[]{:S(2)}, u32[]{:S(2)}) collective-permute-start(bf16[64,2688]{1,0:T(8,128)(2,1)} %collective-permute-done.7.refs_6_), channel_id=1, source_target_pairs={{0,4},{4,12},{12,8},{8,0},{1,5},{5,13},{13,9},{9,1},{2,6},{6,14},{... | collective-permute-start | bytes 1032200 | tf_op jit(solution)/shard_map/ppermute | solution.py:358
  47.3 2.4 %collective-permute-start.16 = (bf16[64,2688]{1,0:T(8,128)(2,1)S(1)}, bf16[64,2688]{1,0:T(8,128)(2,1)S(1)}, u32[]{:S(2)}, u32[]{:S(2)}) collective-permute-start(bf16[64,2688]{1,0:T(8,128)(2,1)S(1)} %get-tuple-element.53.refs_5_), channel_id=1, source_target_pairs={{0,4},{4,12},{12,8},{8,0},{1,5},{5,13},{13,9},{9,1},{2,6},{6,14},{... | collective-permute-start | bytes 1032200 | tf_op jit(solution)/shard_map/ppermute | solution.py:358
  49.7 3.4 %collective-permute-done.8.refs_8_ = bf16[64,2688]{1,0:T(8,128)(2,1)S(1)} collective-permute-done((bf16[64,2688]{1,0:T(8,128)(2,1)}, bf16[64,2688]{1,0:T(8,128)(2,1)S(1)}, u32[]{:S(2)}, u32[]{:S(2)}) %collective-permute-start.8) | collective-permute-done | bytes 344096 | tf_op jit(solution)/shard_map/ppermute | solution.py:358
  53.1 1.6 %collective-permute-start.23 = (bf16[64,2688]{1,0:T(8,128)(2,1)}, bf16[64,2688]{1,0:T(8,128)(2,1)S(1)}, u32[]{:S(2)}, u32[]{:S(2)}) collective-permute-start(bf16[64,2688]{1,0:T(8,128)(2,1)} %collective-permute-done.7.refs_6_), channel_id=1, source_target_pairs={{0,2},{2,0},{1,3},{3,1},{4,6},{6,4},{5,7},{7,5},{8,10},{10,8},{9,1... | collective-permute-start | bytes 1032200 | tf_op jit(solution)/shard_map/ppermute | solution.py:358
  54.7 2.8 %fusion = (f32[1536,64]{1,0:T(8,128)S(1)}, f32[1536,64]{1,0:T(8,128)S(1)}, f32[1536,64]{1,0:T(8,128)S(1)}) fusion(f32[64]{0:T(128)S(1)} %multiply_exponential_fusion, f32[1536]{0:T(1024)S(1)} %add_convert_fusion), kind=kLoop, calls=%fused_computation.10 | loop fusion | flops 196608 | bytes 1186048 | tf_op jit(solution)/shard_map/neg | solution.py:34
  59.6 1.8 %collective-permute-start.19 = (bf16[64,2688]{1,0:T(8,128)(2,1)S(1)}, bf16[64,2688]{1,0:T(8,128)(2,1)S(1)}, u32[]{:S(2)}, u32[]{:S(2)}) collective-permute-start(bf16[64,2688]{1,0:T(8,128)(2,1)S(1)} %collective-permute-done.16.refs_7_), channel_id=1, source_target_pairs={{0,4},{4,12},{12,8},{8,0},{1,5},{5,13},{13,9},{9,1},{2,6},{6,14},{... | collective-permute-start | bytes 1032200 | tf_op jit(solution)/shard_map/ppermute | solution.py:358
  61.5 3.5 %collective-permute-done.23.refs_14_ = bf16[64,2688]{1,0:T(8,128)(2,1)S(1)} collective-permute-done((bf16[64,2688]{1,0:T(8,128)(2,1)}, bf16[64,2688]{1,0:T(8,128)(2,1)S(1)}, u32[]{:S(2)}, u32[]{:S(2)}) %collective-permute-start.23) | collective-permute-done | bytes 344096 | tf_op jit(solution)/shard_map/ppermute | solution.py:358
  65.0 1.6 %collective-permute-start.29 = (bf16[64,2688]{1,0:T(8,128)(2,1)S(1)}, bf16[64,2688]{1,0:T(8,128)(2,1)S(1)}, u32[]{:S(2)}, u32[]{:S(2)}) collective-permute-start(bf16[64,2688]{1,0:T(8,128)(2,1)S(1)} %collective-permute-done.16.refs_7_), channel_id=1, source_target_pairs={{0,2},{2,0},{1,3},{3,1},{4,6},{6,4},{5,7},{7,5},{8,10},{10,8},{9,1... | collective-permute-start | bytes 1032200 | tf_op jit(solution)/shard_map/ppermute | solution.py:358
  66.7 6.2 %shard_map.82.refs_0_ = bf16[4,512,128]{2,1,0:T(8,128)(2,1)S(1)} custom-call(s32[1]{0:T(128)} %bitcast.3.row_ref, bf16[512,1024]{1,0:T(8,128)(2,1)S(1)} %copy-done.9, bf16[512,512]{1,0:T(8,128)(2,1)S(1)} %collective-permute-done.1.k0, bf16[512,512]{1,0:T(8,128)(2,1)} %collective-permute-done.4.k1, bf16[512,512]{1,0:T(8,128)(2,1)S(1)} %copy-done.2, ...), custom_call_target="tpu_custom_call" | custom-call | flops 5368709120 | bytes 6291456 | tf_op jit(solution)/shard_map/pallas_call | solution.py:105
  73.4 2.4 %collective-permute-start.13 = (bf16[64,2688]{1,0:T(8,128)(2,1)S(1)}, bf16[64,2688]{1,0:T(8,128)(2,1)S(1)}, u32[]{:S(2)}, u32[]{:S(2)}) collective-permute-start(bf16[64,2688]{1,0:T(8,128)(2,1)S(1)} %collective-permute-done.8.refs_8_), channel_id=1, source_target_pairs={{0,4},{4,12},{12,8},{8,0},{1,5},{5,13},{13,9},{9,1},{2,6},{6,14},{... | collective-permute-start | bytes 1032200 | tf_op jit(solution)/shard_map/ppermute | solution.py:358
  76.6 6.2 %shard_map.83.refs_1_ = bf16[4,512,128]{2,1,0:T(8,128)(2,1)S(1)} custom-call(s32[1]{0:T(128)} %bitcast.4.row_ref, bf16[512,1024]{1,0:T(8,128)(2,1)S(1)} %copy-done.9, bf16[512,512]{1,0:T(8,128)(2,1)S(1)} %collective-permute-done.1.k0, bf16[512,512]{1,0:T(8,128)(2,1)} %collective-permute-done.4.k1, bf16[512,512]{1,0:T(8,128)(2,1)S(1)} %copy-done.2, ...), custom_call_target="tpu_custom_call" | custom-call | flops 5368709120 | bytes 6291456 | tf_op jit(solution)/shard_map/pallas_call | solution.py:105
  90.1 2.8 %collective-permute-done.30.refs_17_ = bf16[64,2688]{1,0:T(8,128)(2,1)S(1)} collective-permute-done((bf16[64,2688]{1,0:T(8,128)(2,1)S(1)}, bf16[64,2688]{1,0:T(8,128)(2,1)S(1)}, u32[]{:S(2)}, u32[]{:S(2)}) %collective-permute-start.30) | collective-permute-done | bytes 344096 | tf_op jit(solution)/shard_map/ppermute | solution.py:358
  94.5 2.2 %collective-permute-done.25.refs_18_ = bf16[64,2688]{1,0:T(8,128)(2,1)} collective-permute-done((bf16[64,2688]{1,0:T(8,128)(2,1)S(1)}, bf16[64,2688]{1,0:T(8,128)(2,1)}, u32[]{:S(2)}, u32[]{:S(2)}) %collective-permute-start.25) | collective-permute-done | bytes 344096 | tf_op jit(solution)/shard_map/ppermute | solution.py:358
  100.5 5.1 %collective-permute-done.21.refs_25_ = bf16[64,2688]{1,0:T(8,128)(2,1)} collective-permute-done((bf16[64,2688]{1,0:T(8,128)(2,1)}, bf16[64,2688]{1,0:T(8,128)(2,1)}, u32[]{:S(2)}, u32[]{:S(2)}) %collective-permute-start.21) | collective-permute-done | bytes 344096 | tf_op jit(solution)/shard_map/ppermute | solution.py:358
  107.0 2.5 %collective-permute-start.22 = (bf16[64,2688]{1,0:T(8,128)(2,1)}, bf16[64,2688]{1,0:T(8,128)(2,1)S(1)}, u32[]{:S(2)}, u32[]{:S(2)}) collective-permute-start(bf16[64,2688]{1,0:T(8,128)(2,1)} %collective-permute-done.21.refs_25_), channel_id=1, source_target_pairs={{0,4},{4,12},{12,8},{8,0},{1,5},{5,13},{13,9},{9,1},{2,6},{6,14},{... | collective-permute-start | bytes 1032200 | tf_op jit(solution)/shard_map/ppermute | solution.py:358
  122.2 10.2 %shard_map.84.refs_8_ = f32[512,2688]{1,0:T(8,128)S(1)} custom-call(s32[4]{0:T(128)S(1)} %pad_add_fusion.where_ref, bf16[4,512,128]{2,1,0:T(8,128)(2,1)S(1)} %shard_map.82.refs_0_, bf16[4,512,128]{2,1,0:T(8,128)(2,1)S(1)} %shard_map.83.refs_1_, bf16[4,512,128]{2,1,0:T(8,128)(2,1)S(1)} %collective-permute-done.9.refs_2_, ...), custom_call_target="tpu_custom_call" | custom-call | flops 9865003008 | bytes 9633792 | tf_op jit(solution)/shard_map/pallas_call | solution.py:251
  132.5 4.8 %shard_map.85 = (f32[512,2688]{1,0:T(8,128)S(1)}, f32[520,128]{1,0:T(8,128)S(1)}) custom-call(s32[4]{0:T(128)S(1)} %pad_add_fusion.where_ref, bf16[4,512,128]{2,1,0:T(8,128)(2,1)S(1)} %shard_map.82.refs_0_, bf16[4,512,128]{2,1,0:T(8,128)(2,1)S(1)} %shard_map.83.refs_1_, bf16[4,512,128]{2,1,0:T(8,128)(2,1)S(1)} %collective-permute-done.9.refs_2_, ...), custom_call_target="tpu_custom_call" | custom-call | flops 1409286144 | bytes 1376256 | tf_op jit(solution)/shard_map/pallas_call | solution.py:251
  138.9 3.2 %shard_map.86 = bf16[512,2688]{1,0:T(8,128)(2,1)} custom-call(f32[520,128]{1,0:T(8,128)S(1)} %get-tuple-element.71.own_ref, f32[520,128]{1,0:T(8,128)S(1)} %collective-permute-done.35.other_ref, f32[1,2688]{1,0:T(1,128)S(1)} %broadcast_in_dim.16.refs_9_.gain_ref, f32[64,2688]{1,0:T(8,128)S(1)} %bitcast.8, f32[512,2688]{1,0:T(8,128)S(1)} %get-tuple-element.72.hidden_ref), custom_call_target="tpu_custom_call" | custom-call | flops 704643072 | bytes 8257536 | tf_op jit(solution)/shard_map/pallas_call | solution.py:294
  (128 shorter events, 47.0 us)
Async XLA Ops:
  5.6 22.3 %collective-permute-start.1 = (bf16[512,512]{1,0:T(8,128)(2,1)S(1)}, bf16[512,512]{1,0:T(8,128)(2,1)S(1)}, u32[]{:S(2)}, u32[]{:S(2)}) collective-permute-start(bf16[512,512]{1,0:T(8,128)(2,1)S(1)} %copy-done.2), channel_id=1, source_target_pairs={{0,4},{4,8},{8,12},{1,5},{5,9},{9,13},{2,6},{6,10},{10,14},{3,7},{... | collective-permute-start | bytes 1572872 | tf_op jit(solution)/shard_map/ppermute | solution.py:358
  12.1 15.8 %collective-permute-start.3 = (bf16[64,2688]{1,0:T(8,128)(2,1)S(1)}, bf16[64,2688]{1,0:T(8,128)(2,1)}, u32[]{:S(2)}, u32[]{:S(2)}) collective-permute-start(bf16[64,2688]{1,0:T(8,128)(2,1)S(1)} %get-tuple-element.53.refs_5_), channel_id=1, source_target_pairs={{0,2},{2,0},{1,3},{3,1},{4,6},{6,4},{5,7},{7,5},{8,10},{10,8},{9,1... | collective-permute-start | bytes 1032200 | tf_op jit(solution)/shard_map/ppermute | solution.py:358
  21.5 24.2 %collective-permute-start.5 = (bf16[512,512]{1,0:T(8,128)(2,1)S(1)}, bf16[512,512]{1,0:T(8,128)(2,1)S(1)}, u32[]{:S(2)}, u32[]{:S(2)}) collective-permute-start(bf16[512,512]{1,0:T(8,128)(2,1)S(1)} %copy-done.3), channel_id=1, source_target_pairs={{0,4},{4,8},{8,12},{1,5},{5,9},{9,13},{2,6},{6,10},{10,14},{3,7},{... | collective-permute-start | bytes 1572872 | tf_op jit(solution)/shard_map/ppermute | solution.py:358
  25.0 19.2 %collective-permute-start.11 = (bf16[64,2688]{1,0:T(8,128)(2,1)S(1)}, bf16[64,2688]{1,0:T(8,128)(2,1)}, u32[]{:S(2)}, u32[]{:S(2)}) collective-permute-start(bf16[64,2688]{1,0:T(8,128)(2,1)S(1)} %collective-permute-done.2.refs_12_), channel_id=1, source_target_pairs={{0,16},{16,0},{1,17},{17,1},{2,18},{18,2},{3,19},{19,3},{4,20},{20... | collective-permute-start | bytes 1032200 | tf_op jit(solution)/shard_map/ppermute | solution.py:358
  27.9 13.7 %collective-permute-start.7 = (bf16[64,2688]{1,0:T(8,128)(2,1)S(1)}, bf16[64,2688]{1,0:T(8,128)(2,1)}, u32[]{:S(2)}, u32[]{:S(2)}) collective-permute-start(bf16[64,2688]{1,0:T(8,128)(2,1)S(1)} %get-tuple-element.45.refs_4_), channel_id=1, source_target_pairs={{0,4},{4,12},{12,8},{8,0},{1,5},{5,13},{13,9},{9,1},{2,6},{6,14},{... | collective-permute-start | bytes 1032200 | tf_op jit(solution)/shard_map/ppermute | solution.py:358
  30.3 17.1 %collective-permute-start.4 = (bf16[512,512]{1,0:T(8,128)(2,1)}, bf16[512,512]{1,0:T(8,128)(2,1)}, u32[]{:S(2)}, u32[]{:S(2)}) collective-permute-start(bf16[512,512]{1,0:T(8,128)(2,1)} %broadcast_select_fusion.1), channel_id=1, source_target_pairs={{0,2},{2,0},{1,3},{3,1},{4,6},{6,4},{5,7},{7,5},{8,10},{10,8},{9,1... | collective-permute-start | bytes 1572872 | tf_op jit(solution)/shard_map/ppermute | solution.py:358
  31.8 26.3 %collective-permute-start.17 = (bf16[64,2688]{1,0:T(8,128)(2,1)}, bf16[64,2688]{1,0:T(8,128)(2,1)}, u32[]{:S(2)}, u32[]{:S(2)}) collective-permute-start(bf16[64,2688]{1,0:T(8,128)(2,1)} %collective-permute-done.3.refs_13_), channel_id=1, source_target_pairs={{0,16},{16,0},{1,17},{17,1},{2,18},{18,2},{3,19},{19,3},{4,20},{20... | collective-permute-start | bytes 1032200 | tf_op jit(solution)/shard_map/ppermute | solution.py:358
  41.6 11.5 %collective-permute-start.8 = (bf16[64,2688]{1,0:T(8,128)(2,1)}, bf16[64,2688]{1,0:T(8,128)(2,1)S(1)}, u32[]{:S(2)}, u32[]{:S(2)}) collective-permute-start(bf16[64,2688]{1,0:T(8,128)(2,1)} %collective-permute-done.7.refs_6_), channel_id=1, source_target_pairs={{0,4},{4,12},{12,8},{8,0},{1,5},{5,13},{13,9},{9,1},{2,6},{6,14},{... | collective-permute-start | bytes 1032200 | tf_op jit(solution)/shard_map/ppermute | solution.py:358
  44.2 17.3 %collective-permute-start.12 = (bf16[64,2688]{1,0:T(8,128)(2,1)}, bf16[64,2688]{1,0:T(8,128)(2,1)S(1)}, u32[]{:S(2)}, u32[]{:S(2)}) collective-permute-start(bf16[64,2688]{1,0:T(8,128)(2,1)} %collective-permute-done.7.refs_6_), channel_id=1, source_target_pairs={{0,16},{16,0},{1,17},{17,1},{2,18},{18,2},{3,19},{19,3},{4,20},{20... | collective-permute-start | bytes 1032200 | tf_op jit(solution)/shard_map/ppermute | solution.py:358
  45.8 19.3 %collective-permute-start.6 = (bf16[512,512]{1,0:T(8,128)(2,1)S(1)}, bf16[512,512]{1,0:T(8,128)(2,1)S(1)}, u32[]{:S(2)}, u32[]{:S(2)}) collective-permute-start(bf16[512,512]{1,0:T(8,128)(2,1)S(1)} %broadcast_select_fusion), channel_id=1, source_target_pairs={{0,2},{2,0},{1,3},{3,1},{4,6},{6,4},{5,7},{7,5},{8,10},{10,8},{9,1... | collective-permute-start | bytes 1572872 | tf_op jit(solution)/shard_map/ppermute | solution.py:358
  53.1 11.9 %collective-permute-start.23 = (bf16[64,2688]{1,0:T(8,128)(2,1)}, bf16[64,2688]{1,0:T(8,128)(2,1)S(1)}, u32[]{:S(2)}, u32[]{:S(2)}) collective-permute-start(bf16[64,2688]{1,0:T(8,128)(2,1)} %collective-permute-done.7.refs_6_), channel_id=1, source_target_pairs={{0,2},{2,0},{1,3},{3,1},{4,6},{6,4},{5,7},{7,5},{8,10},{10,8},{9,1... | collective-permute-start | bytes 1032200 | tf_op jit(solution)/shard_map/ppermute | solution.py:358
  58.1 17.8 %collective-permute-start.18 = (bf16[64,2688]{1,0:T(8,128)(2,1)S(1)}, bf16[64,2688]{1,0:T(8,128)(2,1)}, u32[]{:S(2)}, u32[]{:S(2)}) collective-permute-start(bf16[64,2688]{1,0:T(8,128)(2,1)S(1)} %collective-permute-done.16.refs_7_), channel_id=1, source_target_pairs={{0,16},{16,0},{1,17},{17,1},{2,18},{18,2},{3,19},{19,3},{4,20},{20... | collective-permute-start | bytes 1032200 | tf_op jit(solution)/shard_map/ppermute | solution.py:358
  59.6 13.8 %collective-permute-start.19 = (bf16[64,2688]{1,0:T(8,128)(2,1)S(1)}, bf16[64,2688]{1,0:T(8,128)(2,1)S(1)}, u32[]{:S(2)}, u32[]{:S(2)}) collective-permute-start(bf16[64,2688]{1,0:T(8,128)(2,1)S(1)} %collective-permute-done.16.refs_7_), channel_id=1, source_target_pairs={{0,4},{4,12},{12,8},{8,0},{1,5},{5,13},{13,9},{9,1},{2,6},{6,14},{... | collective-permute-start | bytes 1032200 | tf_op jit(solution)/shard_map/ppermute | solution.py:358
  65.0 19.9 %collective-permute-start.26 = (bf16[64,2688]{1,0:T(8,128)(2,1)S(1)}, bf16[64,2688]{1,0:T(8,128)(2,1)S(1)}, u32[]{:S(2)}, u32[]{:S(2)}) collective-permute-start(bf16[64,2688]{1,0:T(8,128)(2,1)S(1)} %collective-permute-done.23.refs_14_), channel_id=1, source_target_pairs={{0,16},{16,0},{1,17},{17,1},{2,18},{18,2},{3,19},{19,3},{4,20},{20... | collective-permute-start | bytes 1032200 | tf_op jit(solution)/shard_map/ppermute | solution.py:358
  65.0 17.8 %collective-permute-start.29 = (bf16[64,2688]{1,0:T(8,128)(2,1)S(1)}, bf16[64,2688]{1,0:T(8,128)(2,1)S(1)}, u32[]{:S(2)}, u32[]{:S(2)}) collective-permute-start(bf16[64,2688]{1,0:T(8,128)(2,1)S(1)} %collective-permute-done.16.refs_7_), channel_id=1, source_target_pairs={{0,2},{2,0},{1,3},{3,1},{4,6},{6,4},{5,7},{7,5},{8,10},{10,8},{9,1... | collective-permute-start | bytes 1032200 | tf_op jit(solution)/shard_map/ppermute | solution.py:358
  72.9 14.3 %collective-permute-start.24 = (bf16[64,2688]{1,0:T(8,128)(2,1)S(1)}, bf16[64,2688]{1,0:T(8,128)(2,1)S(1)}, u32[]{:S(2)}, u32[]{:S(2)}) collective-permute-start(bf16[64,2688]{1,0:T(8,128)(2,1)S(1)} %collective-permute-done.8.refs_8_), channel_id=1, source_target_pairs={{0,2},{2,0},{1,3},{3,1},{4,6},{6,4},{5,7},{7,5},{8,10},{10,8},{9,1... | collective-permute-start | bytes 1032200 | tf_op jit(solution)/shard_map/ppermute | solution.py:358
  73.4 15.2 %collective-permute-start.13 = (bf16[64,2688]{1,0:T(8,128)(2,1)S(1)}, bf16[64,2688]{1,0:T(8,128)(2,1)S(1)}, u32[]{:S(2)}, u32[]{:S(2)}) collective-permute-start(bf16[64,2688]{1,0:T(8,128)(2,1)S(1)} %collective-permute-done.8.refs_8_), channel_id=1, source_target_pairs={{0,4},{4,12},{12,8},{8,0},{1,5},{5,13},{13,9},{9,1},{2,6},{6,14},{... | collective-permute-start | bytes 1032200 | tf_op jit(solution)/shard_map/ppermute | solution.py:358
  75.9 14.1 %collective-permute-start.20 = (bf16[64,2688]{1,0:T(8,128)(2,1)S(1)}, bf16[64,2688]{1,0:T(8,128)(2,1)}, u32[]{:S(2)}, u32[]{:S(2)}) collective-permute-start(bf16[64,2688]{1,0:T(8,128)(2,1)S(1)} %collective-permute-done.19.refs_9_), channel_id=1, source_target_pairs={{0,4},{4,12},{12,8},{8,0},{1,5},{5,13},{13,9},{9,1},{2,6},{6,14},{... | collective-permute-start | bytes 1032200 | tf_op jit(solution)/shard_map/ppermute | solution.py:358
  90.1 19.3 %collective-permute-start.9 = (bf16[4,512,128]{2,1,0:T(8,128)(2,1)S(1)}, bf16[4,512,128]{2,1,0:T(8,128)(2,1)S(1)}, u32[]{:S(2)}, u32[]{:S(2)}) collective-permute-start(bf16[4,512,128]{2,1,0:T(8,128)(2,1)S(1)} %shard_map.82.refs_0_), channel_id=1, source_target_pairs={{0,1},{1,0},{2,3},{3,2},{4,5},{5,4},{6,7},{7,6},{8,9},{9,8},{10,11... | collective-permute-start | bytes 1572872 | tf_op jit(solution)/shard_map/ppermute | solution.py:315
  93.0 16.6 %collective-permute-start.10 = (bf16[4,512,128]{2,1,0:T(8,128)(2,1)S(1)}, bf16[4,512,128]{2,1,0:T(8,128)(2,1)S(1)}, u32[]{:S(2)}, u32[]{:S(2)}) collective-permute-start(bf16[4,512,128]{2,1,0:T(8,128)(2,1)S(1)} %shard_map.83.refs_1_), channel_id=1, source_target_pairs={{0,1},{1,0},{2,3},{3,2},{4,5},{5,4},{6,7},{7,6},{8,9},{9,8},{10,11... | collective-permute-start | bytes 1572872 | tf_op jit(solution)/shard_map/ppermute | solution.py:315
  105.6 26.9 %collective-permute-start.28 = (bf16[64,2688]{1,0:T(8,128)(2,1)}, bf16[64,2688]{1,0:T(8,128)(2,1)S(1)}, u32[]{:S(2)}, u32[]{:S(2)}) collective-permute-start(bf16[64,2688]{1,0:T(8,128)(2,1)} %collective-permute-done.25.refs_18_), channel_id=1, source_target_pairs={{0,16},{16,0},{1,17},{17,1},{2,18},{18,2},{3,19},{19,3},{4,20},{20... | collective-permute-start | bytes 1032200 | tf_op jit(solution)/shard_map/ppermute | solution.py:358
  106.9 25.5 %collective-permute-start.15 = (bf16[64,2688]{1,0:T(8,128)(2,1)}, bf16[64,2688]{1,0:T(8,128)(2,1)S(1)}, u32[]{:S(2)}, u32[]{:S(2)}) collective-permute-start(bf16[64,2688]{1,0:T(8,128)(2,1)} %collective-permute-done.14.refs_24_), channel_id=1, source_target_pairs={{0,4},{4,12},{12,8},{8,0},{1,5},{5,13},{13,9},{9,1},{2,6},{6,14},{... | collective-permute-start | bytes 1032200 | tf_op jit(solution)/shard_map/ppermute | solution.py:358
  107.0 25.5 %collective-permute-start.22 = (bf16[64,2688]{1,0:T(8,128)(2,1)}, bf16[64,2688]{1,0:T(8,128)(2,1)S(1)}, u32[]{:S(2)}, u32[]{:S(2)}) collective-permute-start(bf16[64,2688]{1,0:T(8,128)(2,1)} %collective-permute-done.21.refs_25_), channel_id=1, source_target_pairs={{0,4},{4,12},{12,8},{8,0},{1,5},{5,13},{13,9},{9,1},{2,6},{6,14},{... | collective-permute-start | bytes 1032200 | tf_op jit(solution)/shard_map/ppermute | solution.py:358
  109.4 23.1 %collective-permute-start.34 = (bf16[64,2688]{1,0:T(8,128)(2,1)}, bf16[64,2688]{1,0:T(8,128)(2,1)S(1)}, u32[]{:S(2)}, u32[]{:S(2)}) collective-permute-start(bf16[64,2688]{1,0:T(8,128)(2,1)} %collective-permute-done.31.refs_19_), channel_id=1, source_target_pairs={{0,16},{16,0},{1,17},{17,1},{2,18},{18,2},{3,19},{19,3},{4,20},{20... | collective-permute-start | bytes 1032200 | tf_op jit(solution)/shard_map/ppermute | solution.py:358
  (44 other events, 444.9 us)

commit v10 on v4

v10 whole, which is shorter than its diff:
```python
import functools

import jax
import jax.numpy as jnp
from jax import lax
from jax.experimental import pallas as pl
from jax.experimental.pallas import tpu as pltpu
from jax.sharding import Mesh
from jax.sharding import PartitionSpec as P

HD = 128
WINDOW = 1024
RANK = 64

query_scale = 168.0 ** (-0.5)
norm_eps = 1e-06
rope_base = 10000.0
log2_e = 1.4426950408889634

TILE = 896
VMEM_LIMIT = 32 * 2**20

NT = (((1,), (1,)), ((), ()))


def rope_tables(first_position, count):
    half_dim = HD // 2
    inverse = jnp.exp(
        -(2.0 * jnp.arange(half_dim, dtype=jnp.float32) / HD) * jnp.log(jnp.float32(rope_base))
    )
    positions = (first_position + jnp.arange(count, dtype=jnp.int32)).astype(jnp.float32)
    angles = positions[:, None] * inverse[None, :]
    cosine, sine = jnp.cos(angles), jnp.sin(angles)
    return jnp.concatenate([cosine, cosine], 1), jnp.concatenate([-sine, sine], 1)


def attend_kernel(tok, group, direct, row_ref, q_ref, k0, k1, k2, v0, v1, v2, cos_ref, sin_ref, out_ref):
    tile = 256

    def turned(field, at):
        wide = field.astype(jnp.float32)
        cos, sin = cos_ref[at : at + tok, :], sin_ref[at : at + tok, :]
        return (wide * cos + pltpu.roll(wide, HD // 2, 1) * sin).astype(jnp.bfloat16)

    row = row_ref[0]
    bias0 = jnp.where(row >= 2, 0.0, -1e30).astype(jnp.float32)
    bias1 = jnp.where(row >= 1, 0.0, -1e30).astype(jnp.float32)
    key0, key1, key2 = turned(k0[...], 0), turned(k1[...], tok), turned(k2[...], 2 * tok)
    heads = [turned(q_ref[:, h * HD : (h + 1) * HD], 2 * tok) for h in range(group)]
    scale = query_scale * log2_e
    stacked = group * tile
    inner = lax.rem(lax.broadcasted_iota(jnp.int32, (stacked, tile), 0), tile)
    newer = lax.broadcasted_iota(jnp.int32, (stacked, tile), 1) > inner

    def dot_nt(a, b):
        return lax.dot_general(a, b, NT, preferred_element_type=jnp.float32)

    def dot(a, b):
        return jnp.dot(a, b, preferred_element_type=jnp.float32)

    for t in range(tok // tile):
        lo, hi = t * tile, (t + 1) * tile
        query = jnp.concatenate([h[lo:hi] for h in heads], 0)
        parts = [(dot_nt(query, key1) + bias1, v1[...])]
        if hi < tok:
            parts.append((dot_nt(query, key0[hi:]) + bias0, v0[hi:, :]))
        if lo > 0:
            parts.append((dot_nt(query, key2[:lo]), v2[:lo, :]))
        mixed = jnp.where(newer, dot_nt(query, key0[lo:hi]) + bias0, dot_nt(query, key2[lo:hi]))
        top = jnp.max(mixed, axis=1, keepdims=True)
        for part, _ in parts:
            top = jnp.maximum(top, jnp.max(part, axis=1, keepdims=True))
        top = top * scale
        weights = jnp.exp2(mixed * scale - top)
        total = jnp.sum(weights, axis=1, keepdims=True)
        older = jnp.where(newer, weights, 0.0)
        result = dot(older.astype(jnp.bfloat16), v0[lo:hi, :])
        result += dot((weights - older).astype(jnp.bfloat16), v2[lo:hi, :])
        for part, value in parts:
            weights = jnp.exp2(part * scale - top)
            total += jnp.sum(weights, axis=1, keepdims=True)
            result += dot(weights.astype(jnp.bfloat16), value)
        result = (result / total).astype(jnp.bfloat16)
        for h in range(group):
            block = result[h * tile : (h + 1) * tile]
            if direct:
                out_ref[h, lo:hi, :] = block
            else:
                out_ref[lo:hi, h * HD : (h + 1) * HD] = block


def attend(row, queries, key_blocks, val_blocks, cos, sin, direct, first=0, count=None):
    tok, kv_local = queries.shape[0], key_blocks[-1].shape[1] // HD
    group = queries.shape[1] // HD // kv_local
    count = kv_local if count is None else count
    head_block = pl.BlockSpec((tok, HD), lambda g, r: (0, g + first))
    table = pl.BlockSpec((3 * tok, HD), lambda g, r: (0, 0))
    if direct:
        out_shape = (count * group, tok, HD)
        out_spec = pl.BlockSpec((group, tok, HD), lambda g, r: (g, 0, 0))
    else:
        out_shape = queries.shape
        out_spec = pl.BlockSpec((tok, group * HD), lambda g, r: (0, g))
    heads = count * group
    return pl.pallas_call(
        functools.partial(attend_kernel, tok, group, direct),
        grid_spec=pltpu.PrefetchScalarGridSpec(
            num_scalar_prefetch=1,
            grid=(count,),
            in_specs=[pl.BlockSpec((tok, group * HD), lambda g, r: (0, g + first))] + [head_block] * 3
            + [
                pl.BlockSpec((tok, HD), lambda g, r, skip=v.shape[1] // HD - kv_local: (0, g + first + skip))
                for v in val_blocks
            ]
            + [table] * 2,
            out_specs=out_spec,
        ),
        out_shape=jax.ShapeDtypeStruct(out_shape, jnp.bfloat16),
        compiler_params=pltpu.CompilerParams(vmem_limit_bytes=VMEM_LIMIT),
        cost_estimate=pl.CostEstimate(
            flops=4 * heads * tok * 10 * tok * HD, bytes_accessed=6 * 2**20, transcendentals=heads * tok * 2 * tok
        ),
    )(row, queries, *key_blocks, *val_blocks, cos, sin)


def ring_place(position, size):
    return jnp.where(position <= size // 2, jnp.maximum(2 * position - 1, 0), 2 * (size - position))


def ring_position(place, size):
    return jnp.where(place % 2 == 1, (place + 1) // 2, (size - place // 2) % size)


def slot_of(kind, step, where_ref, slots):
    if kind is None:
        return step * slots
    is_mine, far, near, outer = where_ref[0], where_ref[1], where_ref[2], where_ref[3]
    from_far = ring_place((ring_position(far, outer) - step + outer) % outer, outer)
    side = near if kind in ("main", "across") else 1 - near
    other = 1 - is_mine if kind in ("main", "beside") else is_mine
    return other * slots + from_far * 2 + side


def gather_heads(kinds, where_ref, sources, heads, sems):
    slots = sources[0].shape[0]
    depth = sources[0].shape[2]
    places = [heads.at[:, n * depth : (n + 1) * depth] for n in range(len(kinds))]
    for n, (kind, k) in enumerate(kinds):
        slot = slot_of(kind, k, where_ref, slots * len(sources) // 2)
        for i, source in enumerate(sources):

            @pl.when((slot >= i * slots) & (slot < (i + 1) * slots))
            def _():
                pltpu.make_async_copy(source.at[slot - i * slots], places[n], sems.at[n]).start()

    for n, place in enumerate(places):
        pltpu.make_async_copy(sources[0].at[0], place, sems.at[n]).wait()


def project_kernel(kinds, sources, where_ref, *refs):
    sources, refs = refs[:sources], refs[sources:]
    weights, (partial_ref, heads, sems, blocks, block_sems) = refs[:-5], refs[-5:]
    step = pl.program_id(0)
    steps = pl.num_programs(0)
    depth = weights[0].shape[0]

    def columns_of(at, act):
        slot = lax.rem(at, 2)
        for n, piece in enumerate(weights):
            source = piece.at[:, pl.ds(pl.multiple_of(at * TILE, TILE), TILE)]
            act(pltpu.make_async_copy(source, blocks.at[slot, n * depth : (n + 1) * depth], block_sems.at[slot, n]))

    @pl.when(step == 0)
    def _():
        columns_of(step, lambda copy: copy.start())

    @pl.when(step + 1 < steps)
    def _():
        columns_of(step + 1, lambda copy: copy.start())

    @pl.when(step == 0)
    def _():
        gather_heads(kinds, where_ref, sources, heads, sems)

    columns_of(step, lambda copy: copy.wait())
    partial_ref[...] = jnp.dot(heads[...], blocks[lax.rem(step, 2)], preferred_element_type=jnp.float32)


def project(where, kinds, sources, weights):
    tok = sources[0].shape[1]
    depth, width = weights[0].shape
    count = len(kinds)
    in_hbm = pl.BlockSpec(memory_space=pltpu.HBM)
    return pl.pallas_call(
        functools.partial(project_kernel, kinds, len(sources)),
        grid_spec=pltpu.PrefetchScalarGridSpec(
            num_scalar_prefetch=1,
            grid=(width // TILE,),
            in_specs=[in_hbm] * (len(sources) + count),
            out_specs=pl.BlockSpec((tok, TILE), lambda j, r: (0, j)),
            scratch_shapes=[
                pltpu.VMEM((tok, count * depth), jnp.bfloat16),
                pltpu.SemaphoreType.DMA((count,)),
                pltpu.VMEM((2, count * depth, TILE), jnp.bfloat16),
                pltpu.SemaphoreType.DMA((2, count)),
            ],
        ),
        out_shape=jax.ShapeDtypeStruct((tok, width), jnp.float32),
        compiler_params=pltpu.CompilerParams(vmem_limit_bytes=VMEM_LIMIT),
        cost_estimate=pl.CostEstimate(
            flops=2 * tok * count * depth * width, bytes_accessed=2 * count * depth * width, transcendentals=0
        ),
    )(where, *sources, *weights)


def close_kernel(kinds, sources, where_ref, *refs):
    sources, refs = refs[:sources], refs[sources:]
    weights, (partial_ref, gain_ref, in_ref, mean_ref, hidden_ref, stat_ref, heads, sems) = refs[:-8], refs[-8:]
    gather_heads(kinds, where_ref, sources, heads, sems)
    tok, width = hidden_ref.shape
    code = square = mean_code = 0.0
    for at in range(0, width, TILE):
        here = slice(at, at + TILE)
        weight = jnp.concatenate([w[:, here] for w in weights], 0)
        total = partial_ref[:, here] + jnp.dot(heads[...], weight, preferred_element_type=jnp.float32)
        hidden_ref[:, here] = total
        in_high = in_ref[:, here].astype(jnp.bfloat16)
        in_low = (in_ref[:, here] - in_high.astype(jnp.float32)).astype(jnp.bfloat16)
        in_parts = jnp.concatenate([in_high, in_low], 0)

        def coded(field):
            return lax.dot_general(field.astype(jnp.bfloat16), in_parts, NT, preferred_element_type=jnp.float32)

        code += coded(total * gain_ref[:, here])
        square += jnp.sum(total * total, axis=1, keepdims=True)
        mean = jnp.broadcast_to(mean_ref[:, here], (8, TILE))
        mean_high = mean.astype(jnp.bfloat16).astype(jnp.float32)
        mean_code += coded(mean_high) + coded(mean - mean_high)
    lane = lax.broadcasted_iota(jnp.int32, code.shape, 1)
    stat_ref[:tok, :] = jnp.where(lane < RANK, code + pltpu.roll(code, RANK, 1), square)
    stat_ref[tok:, :] = mean_code + pltpu.roll(mean_code, RANK, 1)


def close(where, kinds, sources, weights, partial, gain, erase_in, mean):
    tok, width = partial.shape
    depth = weights[0].shape[0]
    count = len(kinds)
    in_vmem = pl.BlockSpec(memory_space=pltpu.VMEM)
    in_hbm = pl.BlockSpec(memory_space=pltpu.HBM)
    return pl.pallas_call(
        functools.partial(close_kernel, kinds, len(sources)),
        in_specs=[pl.BlockSpec(memory_space=pltpu.SMEM)] + [in_hbm] * len(sources) + [in_vmem] * (count + 4),
        out_specs=[in_vmem] * 2,
        out_shape=[
            jax.ShapeDtypeStruct((tok, width), jnp.float32),
            jax.ShapeDtypeStruct((tok + 8, 2 * RANK), jnp.float32),
        ],
        scratch_shapes=[pltpu.VMEM((tok, count * depth), jnp.bfloat16), pltpu.SemaphoreType.DMA((count,))],
        input_output_aliases={1 + len(sources) + count: 0},
        compiler_params=pltpu.CompilerParams(vmem_limit_bytes=VMEM_LIMIT),
        cost_estimate=pl.CostEstimate(
            flops=2 * tok * count * depth * width, bytes_accessed=2 * count * depth * width, transcendentals=0
        ),
    )(where, *sources, *weights, partial, gain, erase_in, mean)


def finish_kernel(model_width, own_ref, other_ref, gain_ref, out_ref, hidden_ref, erased_ref, tiles, sems):
    tok, width = hidden_ref.shape
    stat = own_ref[:tok, :] + other_ref[:tok, :]
    mean_code = own_ref[tok : tok + 1, :] + other_ref[tok : tok + 1, :]
    inv_rms = lax.rsqrt(stat[:, RANK : RANK + 1] / model_width + norm_eps)
    lane = lax.broadcasted_iota(jnp.int32, stat.shape, 1)
    code = jnp.where(lane < RANK, stat * inv_rms - mean_code, 0.0)
    high = code.astype(jnp.bfloat16).astype(jnp.float32)
    low = code - high
    packed = jnp.concatenate([high + pltpu.roll(low, RANK, 1), high], 1).astype(jnp.bfloat16)
    copies = []
    for n, at in enumerate(range(0, width, TILE)):
        here = slice(at, at + TILE)
        out_high = out_ref[:, here].astype(jnp.bfloat16)
        out_low = (out_ref[:, here] - out_high.astype(jnp.float32)).astype(jnp.bfloat16)
        out_parts = jnp.concatenate([out_high, out_high, out_low, jnp.zeros_like(out_low)], 0)
        removed = jnp.dot(packed, out_parts, preferred_element_type=jnp.float32)
        normed = hidden_ref[:, here] * inv_rms * gain_ref[:, here]
        tiles[:, here] = (normed - removed).astype(jnp.bfloat16)
        copies.append(pltpu.make_async_copy(tiles.at[:, here], erased_ref.at[:, here], sems.at[n]))
        copies[-1].start()
    for copy in copies:
        copy.wait()


def finish(model_width, stat, stat_other, gain, erase_out, hidden):
    tok, width = hidden.shape
    in_vmem = pl.BlockSpec(memory_space=pltpu.VMEM)
    return pl.pallas_call(
        functools.partial(finish_kernel, model_width),
        in_specs=[in_vmem] * 5,
        out_specs=pl.BlockSpec(memory_space=pltpu.HBM),
        out_shape=jax.ShapeDtypeStruct((tok, width), jnp.bfloat16),
        scratch_shapes=[pltpu.VMEM((tok, width), jnp.bfloat16), pltpu.SemaphoreType.DMA((width // TILE,))],
        compiler_params=pltpu.CompilerParams(vmem_limit_bytes=VMEM_LIMIT),
        cost_estimate=pl.CostEstimate(
            flops=2 * tok * 256 * width, bytes_accessed=6 * tok * width, transcendentals=0
        ),
    )(stat, stat_other, gain, erase_out, hidden)


def swapped(block, axis):
    return lax.ppermute(block, axis, [(0, 1), (1, 0)])


def ring_order(size):
    return list(range(0, 1)) + list(range(1, size, 2)) + [i for i in range(size - 1, 0, -1) if i % 2 == 0]


def on_device(queries, keys, values, out_proj, post_gain, mean_vec, erase_in, erase_out):
    tok = queries.shape[0]
    outer, inner = lax.axis_size("far"), lax.axis_size("near")
    grp, far, near, col = (lax.axis_index(a) for a in ("grp", "far", "near", "col"))
    row = far * inner + near
    depth, model_width = out_proj.shape
    width = model_width // 2
    kv_local = keys.shape[1] // HD
    heads = queries.shape[1] // HD
    direct = depth == HD and outer * inner == heads and outer == 4

    ahead = [(i, i + 1) for i in range(outer - 1)]
    from_behind = lambda block: lax.ppermute(block, "far", ahead)
    hold = lax.optimization_barrier

    def for_next(own, second):
        return swapped(jnp.where(near == 0, own, second), "near")

    def after(block, *earlier):
        return hold((block, earlier))[0]

    theirs = swapped(lax.dynamic_slice_in_dim(out_proj, (1 - col) * width, width, 1), "col")
    mine = lax.dynamic_slice_in_dim(out_proj, col * width, width, 1)
    gain, mean = post_gain[None, :], mean_vec[None, :]
    erase_in, erase_out = erase_in.T, erase_out.T
    is_mine = grp == col
    where = jnp.stack([is_mine.astype(jnp.int32), far, near, jnp.int32(outer)])

    if direct:
        order = ring_order(outer)
        hops = [(order[i], order[(i + 1) % outer]) for i in range(outer)]
        ring = lambda block: lax.ppermute(block, "far", hops)
        beyond = lambda block: swapped(block, "near")
        facing = lambda block: swapped(block, "grp")
        main, beside, across, corner = ({} for _ in range(4))
        main[0] = jnp.where(is_mine, mine, theirs)
        across[0] = jnp.where(is_mine, theirs, mine)
        beside[0] = beyond(main[0])
        second_keys, second_values = from_behind(keys), from_behind(values)
        corner[0] = facing(beside[0])
        cos, sin = rope_tables((after(row, beside[0]) - 2) * tok, 3 * tok)
        main[1] = ring(after(main[0], second_keys, second_values))
        own_both = jnp.concatenate([keys, values], 1)
        old_both = jnp.concatenate(after((second_keys, second_values), beside[0]), 1)
        first_both = for_next(own_both, old_both)
        main[1], corner[0], cos, sin = hold((main[1], corner[0], cos, sin))
        main[2], across[1] = ring(main[1]), facing(main[1])
        beside[1] = beyond(main[1])
        attended = attend(
            row[None], queries, (second_keys, first_both, keys), (second_values, first_both, values), cos, sin, True
        )
        main[2], beside[1], across[1], attended = hold((main[2], beside[1], across[1], attended))
        main[3], beside[2], corner[1] = ring(main[2]), beyond(main[2]), facing(beside[1])
        att_other = swapped(attended, "col")
        main[3], beside[2], corner[1], att_other, across[1] = hold((main[3], beside[2], corner[1], att_other, across[1]))
        across[2], beside[3], corner[2] = ring(across[1]), beyond(main[3]), facing(beside[2])
        across[2], beside[3], corner[2] = hold((across[2], beside[3], corner[2]))
        across[3], corner[3] = ring(across[2]), facing(beside[3])
        attended, att_other = [attended], [att_other]
        weights, kinds, late, late_kinds = [], [], [], []
        for name, pieces in (("main", main), ("beside", beside), ("across", across), ("corner", corner)):
            for k in range(outer):
                is_late = k == 3 and name in ("across", "corner")
                (late if is_late else weights).append(pieces[k])
                (late_kinds if is_late else kinds).append((name, k))
        partial = project(where, kinds, attended + att_other, weights)
    else:
        second_keys, second_values = from_behind(keys), from_behind(values)
        first_keys, first_values = for_next(keys, second_keys), for_next(values, second_values)
        cos, sin = rope_tables((row - 2) * tok, 3 * tok)
        attended = attend(
            row[None], queries, (second_keys, first_keys, keys), (second_values, first_values, values), cos, sin, False
        )
        attended = [attended[None]]
        att_other = [swapped(attended[0], "col")]
        weights, late = ([lax.all_gather(w, ("far", "near"), axis=0, tiled=True)] for w in (mine, theirs))
        kinds, late_kinds = [(None, 0)], [(None, 1)]
        partial = project(where, kinds, attended + att_other, weights)

    hidden, stat = close(where, late_kinds, attended + att_other, late, partial, gain, erase_in, mean)
    return finish(model_width, stat, swapped(stat, "col"), gain, erase_out, hidden)


def solution(mesh):
    grp, row, col = (mesh.shape[a] for a in ("grp", "row", "col"))
    fine = Mesh(mesh.devices.reshape(grp, row // 2, 2, col), ("grp", "far", "near", "col"))
    tokens = P(("grp", "far", "near"), "col")
    placed = (tokens, tokens, tokens, P(("col", "far", "near"), None), P("col"), P("col"), P("col", None), P("col", None))
    return jax.shard_map(on_device, mesh=fine, in_specs=placed, out_specs=tokens, check_vma=False)
```

time: 165 us -> 149 us (0.903)
  local copies, waits for them, and re-layouts: 32.4 us -> 17 us
  starting transfers between devices: 27.4 us -> 32.6 us
  waiting for transfers between devices: 67.6 us -> 63.5 us
    ppermute x14 -> x13, waiting for transfers between devices: 51.8 us -> 11.4 us  [swapped(): return lax.ppermute(block, axis, [(0, 1), (1, 0)])]
    ppermute x5, waiting for transfers between devices: 12.4 us -> 33.2 us  [on_device(): ring = lambda block: lax.ppermute(block, 'far', hops)]
    ppermute x2, waiting for transfers between devices: 3.46 us -> 18.9 us  [on_device(): from_behind = lambda block: lax.ppermute(block, 'far', ahead)]
    unnamed x69 -> x54, local copies, waits for them, and re-layouts: 26.1 us -> 15.7 us
    ppermute x5, starting transfers between devices: 4.93 us -> 10.6 us  [on_device(): ring = lambda block: lax.ppermute(block, 'far', hops)]
    reduce_precision x1 -> x0, local copies, waits for them, and re-layouts: 2.62 us -> none  [split_high_low(): high = lax.reduce_precision(value, 8, 7)]
    ppermute x14 -> x13, starting transfers between devices: 13.9 us -> 15.1 us  [swapped(): return lax.ppermute(block, axis, [(0, 1), (1, 0)])]
  transfers between devices with their start and end apart: 21 -> 20, of which waited for: 14 -> 14; matrix products, arithmetic and copies ran while one was open for 8% -> 2% of each run, Pallas kernels for 13% -> 14%
where the time goes in v10:
time: 149 us; the launch traced here: 148 us
  waiting for transfers between devices  63.5 us (43%)
  starting transfers between devices  32.6 us (22%)
  Pallas kernels  28.4 us (19%)
  local copies, waits for them, and re-layouts  17 us (11%)
  other arithmetic  5.97 us (4%)
    ppermute x5, waiting for transfers between devices, on_device(): ring = lambda block: lax.ppermute(block, 'far', hops)  33.2 us
    ppermute x2, waiting for transfers between devices, on_device(): from_behind = lambda block: lax.ppermute(block, 'far', ahead)  18.9 us
    unnamed x54, local copies, waits for them, and re-layouts  15.7 us
    ppermute x13, starting transfers between devices, swapped(): return lax.ppermute(block, axis, [(0, 1), (1, 0)])  15.1 us
    pallas_call x1, Pallas kernels, attend(): pl.pallas_call(functools.partial(attend_kernel, tok, group, direct), grid...  11.8 us
    ppermute x13, waiting for transfers between devices, swapped(): return lax.ppermute(block, axis, [(0, 1), (1, 0)])  11.4 us
    ppermute x5, starting transfers between devices, on_device(): ring = lambda block: lax.ppermute(block, 'far', hops)  10.6 us
    pallas_call x1, Pallas kernels, project(): pl.pallas_call(functools.partial(project_kernel, kinds, len(sources)), gr...  9.42 us
  transfers between devices with their start and end apart: 20, of which 14 were waited for; matrix products, arithmetic and copies ran while one was open for 2% of the time, Pallas kernels for 14%

profile of v10, /device:TPU:0, one launch (start us, length us, event | category | flops | bytes accessed | tf_op | source)
XLA Modules:
  0.0 147.9 jit_solution(8109686574818438551)
XLA Ops:
  1.8 1.8 %collective-permute-done = bf16[128,2688]{1,0:T(8,128)(2,1)S(1)} collective-permute-done((bf16[128,2688]{1,0:T(8,128)(2,1)S(1)}, bf16[128,2688]{1,0:T(8,128)(2,1)S(1)}, u32[]{:S(2)}, u32[]{:S(2)}) %collective-permute-start) | collective-permute-done | bytes 688160 | tf_op jit(solution)/shard_map/ppermute | solution.py:309
  4.9 3.0 %collective-permute-start.4 = (bf16[128,2688]{1,0:T(8,128)(2,1)S(1)}, bf16[128,2688]{1,0:T(8,128)(2,1)}, u32[]{:S(2)}, u32[]{:S(2)}) collective-permute-start(bf16[128,2688]{1,0:T(8,128)(2,1)S(1)} %get-tuple-element.27.refs_2_), channel_id=1, source_target_pairs={{0,2},{2,0},{1,3},{3,1},{4,6},{6,4},{5,7},{7,5},{8,10},{10,8},{9,1... | collective-permute-start | bytes 2064392 | tf_op jit(solution)/shard_map/ppermute | solution.py:309
  7.8 3.5 %collective-permute-start.1 = (bf16[512,512]{1,0:T(8,128)(2,1)S(1)}, bf16[512,512]{1,0:T(8,128)(2,1)S(1)}, u32[]{:S(2)}, u32[]{:S(2)}) collective-permute-start(bf16[512,512]{1,0:T(8,128)(2,1)S(1)} %copy-done.2), channel_id=1, source_target_pairs={{0,4},{4,8},{8,12},{1,5},{5,9},{9,13},{2,6},{6,10},{10,14},{3,7},{... | collective-permute-start | bytes 1572872 | tf_op jit(solution)/shard_map/ppermute | solution.py:328
  11.3 3.5 %collective-permute-start.2 = (bf16[512,512]{1,0:T(8,128)(2,1)S(1)}, bf16[512,512]{1,0:T(8,128)(2,1)S(1)}, u32[]{:S(2)}, u32[]{:S(2)}) collective-permute-start(bf16[512,512]{1,0:T(8,128)(2,1)S(1)} %copy-done.3), channel_id=1, source_target_pairs={{0,4},{4,8},{8,12},{1,5},{5,9},{9,13},{2,6},{6,10},{10,14},{3,7},{... | collective-permute-start | bytes 1572872 | tf_op jit(solution)/shard_map/ppermute | solution.py:328
  14.8 8.8 %collective-permute-done.1.k0 = bf16[512,512]{1,0:T(8,128)(2,1)S(1)} collective-permute-done((bf16[512,512]{1,0:T(8,128)(2,1)S(1)}, bf16[512,512]{1,0:T(8,128)(2,1)S(1)}, u32[]{:S(2)}, u32[]{:S(2)}) %collective-permute-start.1) | collective-permute-done | bytes 524320 | tf_op jit(solution)/shard_map/ppermute | solution.py:328
  23.6 10.1 %collective-permute-done.2.v0 = bf16[512,512]{1,0:T(8,128)(2,1)S(1)} collective-permute-done((bf16[512,512]{1,0:T(8,128)(2,1)S(1)}, bf16[512,512]{1,0:T(8,128)(2,1)S(1)}, u32[]{:S(2)}, u32[]{:S(2)}) %collective-permute-start.2) | collective-permute-done | bytes 524320 | tf_op jit(solution)/shard_map/ppermute | solution.py:328
  35.5 2.5 %collective-permute-start.3 = (bf16[128,2688]{1,0:T(8,128)(2,1)S(1)}, bf16[128,2688]{1,0:T(8,128)(2,1)}, u32[]{:S(2)}, u32[]{:S(2)}) collective-permute-start(bf16[128,2688]{1,0:T(8,128)(2,1)S(1)} %get-tuple-element.27.refs_2_), channel_id=1, source_target_pairs={{0,4},{4,12},{12,8},{8,0},{1,5},{5,13},{13,9},{9,1},{2,6},{6,14},{... | collective-permute-start | bytes 2064392 | tf_op jit(solution)/shard_map/ppermute | solution.py:347
  38.0 1.5 %collective-permute-start.5 = (bf16[128,2688]{1,0:T(8,128)(2,1)}, bf16[128,2688]{1,0:T(8,128)(2,1)S(1)}, u32[]{:S(2)}, u32[]{:S(2)}) collective-permute-start(bf16[128,2688]{1,0:T(8,128)(2,1)} %collective-permute-done.4.refs_6_), channel_id=1, source_target_pairs={{0,16},{16,0},{1,17},{17,1},{2,18},{18,2},{3,19},{19,3},{4,20},{20... | collective-permute-start | bytes 2064392 | tf_op jit(solution)/shard_map/ppermute | solution.py:309
  39.5 2.8 %fusion = (f32[1536,64]{1,0:T(8,128)S(1)}, f32[1536,64]{1,0:T(8,128)S(1)}, f32[1536,64]{1,0:T(8,128)S(1)}) fusion(f32[64]{0:T(128)S(1)} %multiply_exponential_fusion, f32[1536]{0:T(1024)S(1)} %add_convert_fusion), kind=kLoop, calls=%fused_computation.7 | loop fusion | flops 196608 | bytes 1186048 | tf_op jit(solution)/shard_map/neg | solution.py:34
  42.8 10.6 %collective-permute-done.3.refs_3_ = bf16[128,2688]{1,0:T(8,128)(2,1)} collective-permute-done((bf16[128,2688]{1,0:T(8,128)(2,1)S(1)}, bf16[128,2688]{1,0:T(8,128)(2,1)}, u32[]{:S(2)}, u32[]{:S(2)}) %collective-permute-start.3) | collective-permute-done | bytes 688160 | tf_op jit(solution)/shard_map/ppermute | solution.py:347
  54.8 2.6 %collective-permute-start.6 = (bf16[128,2688]{1,0:T(8,128)(2,1)}, bf16[128,2688]{1,0:T(8,128)(2,1)S(1)}, u32[]{:S(2)}, u32[]{:S(2)}) collective-permute-start(bf16[128,2688]{1,0:T(8,128)(2,1)} %collective-permute-done.3.refs_3_), channel_id=1, source_target_pairs={{0,4},{4,12},{12,8},{8,0},{1,5},{5,13},{13,9},{9,1},{2,6},{6,14},{... | collective-permute-start | bytes 2064392 | tf_op jit(solution)/shard_map/ppermute | solution.py:347
  57.4 1.5 %collective-permute-start.7 = (bf16[128,2688]{1,0:T(8,128)(2,1)}, bf16[128,2688]{1,0:T(8,128)(2,1)S(1)}, u32[]{:S(2)}, u32[]{:S(2)}) collective-permute-start(bf16[128,2688]{1,0:T(8,128)(2,1)} %collective-permute-done.3.refs_3_), channel_id=1, source_target_pairs={{0,2},{2,0},{1,3},{3,1},{4,6},{6,4},{5,7},{7,5},{8,10},{10,8},{9,1... | collective-permute-start | bytes 2064392 | tf_op jit(solution)/shard_map/ppermute | solution.py:309
  61.0 11.8 %shard_map.82.refs_0_ = bf16[8,512,128]{2,1,0:T(8,128)(2,1)S(1)} custom-call(s32[1]{0:T(128)} %bitcast.3.row_ref, bf16[512,1024]{1,0:T(8,128)(2,1)S(1)} %copy-done.8, bf16[512,512]{1,0:T(8,128)(2,1)S(1)} %copy-done.5, bf16[512,1024]{1,0:T(8,128)(2,1)} %collective-permute-done.9.k1.v1, bf16[512,512]{1,0:T(8,128)(2,1)S(1)} %copy-done.2, ...), custom_call_target="tpu_custom_call" | custom-call | flops 10737418240 | bytes 6291456 | tf_op jit(solution)/shard_map/pallas_call | solution.py:105
  74.0 2.5 %collective-permute-start.10 = (bf16[128,2688]{1,0:T(8,128)(2,1)S(1)}, bf16[128,2688]{1,0:T(8,128)(2,1)S(1)}, u32[]{:S(2)}, u32[]{:S(2)}) collective-permute-start(bf16[128,2688]{1,0:T(8,128)(2,1)S(1)} %collective-permute-done.6.refs_4_), channel_id=1, source_target_pairs={{0,4},{4,12},{12,8},{8,0},{1,5},{5,13},{13,9},{9,1},{2,6},{6,14},{... | collective-permute-start | bytes 2064392 | tf_op jit(solution)/shard_map/ppermute | solution.py:347
  80.2 13.4 %collective-permute-done.10.refs_5_ = bf16[128,2688]{1,0:T(8,128)(2,1)S(1)} collective-permute-done((bf16[128,2688]{1,0:T(8,128)(2,1)S(1)}, bf16[128,2688]{1,0:T(8,128)(2,1)S(1)}, u32[]{:S(2)}, u32[]{:S(2)}) %collective-permute-start.10) | collective-permute-done | bytes 688160 | tf_op jit(solution)/shard_map/ppermute | solution.py:347
  96.0 2.6 %collective-permute-start.14 = (bf16[128,2688]{1,0:T(8,128)(2,1)S(1)}, bf16[128,2688]{1,0:T(8,128)(2,1)}, u32[]{:S(2)}, u32[]{:S(2)}) collective-permute-start(bf16[128,2688]{1,0:T(8,128)(2,1)S(1)} %collective-permute-done.8.refs_11_), channel_id=1, source_target_pairs={{0,4},{4,12},{12,8},{8,0},{1,5},{5,13},{13,9},{9,1},{2,6},{6,14},{... | collective-permute-start | bytes 2064392 | tf_op jit(solution)/shard_map/ppermute | solution.py:347
  99.4 1.5 %collective-permute-start.15 = (bf16[128,2688]{1,0:T(8,128)(2,1)S(1)}, bf16[128,2688]{1,0:T(8,128)(2,1)}, u32[]{:S(2)}, u32[]{:S(2)}) collective-permute-start(bf16[128,2688]{1,0:T(8,128)(2,1)S(1)} %collective-permute-done.10.refs_5_), channel_id=1, source_target_pairs={{0,2},{2,0},{1,3},{3,1},{4,6},{6,4},{5,7},{7,5},{8,10},{10,8},{9,1... | collective-permute-start | bytes 2064392 | tf_op jit(solution)/shard_map/ppermute | solution.py:309
  104.2 9.2 %collective-permute-done.14.refs_12_ = bf16[128,2688]{1,0:T(8,128)(2,1)} collective-permute-done((bf16[128,2688]{1,0:T(8,128)(2,1)S(1)}, bf16[128,2688]{1,0:T(8,128)(2,1)}, u32[]{:S(2)}, u32[]{:S(2)}) %collective-permute-start.14) | collective-permute-done | bytes 688160 | tf_op jit(solution)/shard_map/ppermute | solution.py:347
  113.4 2.3 %collective-permute-done.15.refs_9_ = bf16[128,2688]{1,0:T(8,128)(2,1)} collective-permute-done((bf16[128,2688]{1,0:T(8,128)(2,1)S(1)}, bf16[128,2688]{1,0:T(8,128)(2,1)}, u32[]{:S(2)}, u32[]{:S(2)}) %collective-permute-start.15) | collective-permute-done | bytes 688160 | tf_op jit(solution)/shard_map/ppermute | solution.py:309
  115.7 2.0 %collective-permute-done.16.refs_15_ = bf16[128,2688]{1,0:T(8,128)(2,1)S(1)} collective-permute-done((bf16[128,2688]{1,0:T(8,128)(2,1)S(1)}, bf16[128,2688]{1,0:T(8,128)(2,1)S(1)}, u32[]{:S(2)}, u32[]{:S(2)}) %collective-permute-start.16) | collective-permute-done | bytes 688160 | tf_op jit(solution)/shard_map/ppermute | solution.py:309
  129.5 9.4 %shard_map.83.refs_4_ = f32[512,2688]{1,0:T(8,128)S(1)} custom-call(s32[4]{0:T(128)S(1)} %pad_add_fusion.where_ref, bf16[8,512,128]{2,1,0:T(8,128)(2,1)S(1)} %shard_map.82.refs_0_, bf16[8,512,128]{2,1,0:T(8,128)(2,1)S(1)} %collective-permute-done.13.refs_1_, bf16[128,2688]{1,0:T(8,128)(2,1)S(1)} %get-tuple-element.27.refs_2_, ...), custom_call_target="tpu_custom_call" | custom-call | flops 4932501504 | bytes 9633792 | tf_op jit(solution)/shard_map/pallas_call | solution.py:194
  138.9 4.9 %shard_map.84 = (f32[512,2688]{1,0:T(8,128)S(1)}, f32[520,128]{1,0:T(8,128)S(1)}) custom-call(s32[4]{0:T(128)S(1)} %pad_add_fusion.where_ref, bf16[8,512,128]{2,1,0:T(8,128)(2,1)S(1)} %shard_map.82.refs_0_, bf16[8,512,128]{2,1,0:T(8,128)(2,1)S(1)} %collective-permute-done.13.refs_1_, ...), custom_call_target="tpu_custom_call", output_to_operand_aliasing={{0}: (5, {})} | custom-call | flops 704643072 | bytes 1376256 | tf_op jit(solution)/shard_map/pallas_call | solution.py:250
  143.9 1.5 %collective-permute-done.19.other_ref = f32[520,128]{1,0:T(8,128)S(1)} collective-permute-done((f32[520,128]{1,0:T(8,128)S(1)}, f32[520,128]{1,0:T(8,128)S(1)}, u32[]{:S(2)}, u32[]{:S(2)}) %collective-permute-start.19) | collective-permute-done | bytes 266272 | tf_op jit(solution)/shard_map/ppermute | solution.py:309
  145.5 2.3 %shard_map.85 = bf16[512,2688]{1,0:T(8,128)(2,1)} custom-call(f32[520,128]{1,0:T(8,128)S(1)} %get-tuple-element.47.own_ref, f32[520,128]{1,0:T(8,128)S(1)} %collective-permute-done.19.other_ref, f32[1,2688]{1,0:T(1,128)S(1)} %broadcast_in_dim.12.refs_5_.gain_ref, f32[64,2688]{1,0:T(8,128)S(1)} %bitcast.7, f32[512,2688]{1,0:T(8,128)S(1)} %get-tuple-element.48.hidden_ref), custom_call_target="tpu_custom_call" | custom-call | flops 704643072 | bytes 8257536 | tf_op jit(solution)/shard_map/pallas_call | solution.py:295
  (84 shorter events, 32.0 us)
Async XLA Ops:
  1.2 2.3 %collective-permute-start = (bf16[128,2688]{1,0:T(8,128)(2,1)S(1)}, bf16[128,2688]{1,0:T(8,128)(2,1)S(1)}, u32[]{:S(2)}, u32[]{:S(2)}) collective-permute-start(bf16[128,2688]{1,0:T(8,128)(2,1)S(1)} %constant_dynamic-slice_fusion), channel_id=1, source_target_pairs={{0,1},{1,0},{2,3},{3,2},{4,5},{5,4},{6,7},{7,6},{8,9},{9,8},{10,11... | collective-permute-start | bytes 2064392 | tf_op jit(solution)/shard_map/ppermute | solution.py:309
  4.9 28.9 %collective-permute-start.4 = (bf16[128,2688]{1,0:T(8,128)(2,1)S(1)}, bf16[128,2688]{1,0:T(8,128)(2,1)}, u32[]{:S(2)}, u32[]{:S(2)}) collective-permute-start(bf16[128,2688]{1,0:T(8,128)(2,1)S(1)} %get-tuple-element.27.refs_2_), channel_id=1, source_target_pairs={{0,2},{2,0},{1,3},{3,1},{4,6},{6,4},{5,7},{7,5},{8,10},{10,8},{9,1... | collective-permute-start | bytes 2064392 | tf_op jit(solution)/shard_map/ppermute | solution.py:309
  7.8 15.8 %collective-permute-start.1 = (bf16[512,512]{1,0:T(8,128)(2,1)S(1)}, bf16[512,512]{1,0:T(8,128)(2,1)S(1)}, u32[]{:S(2)}, u32[]{:S(2)}) collective-permute-start(bf16[512,512]{1,0:T(8,128)(2,1)S(1)} %copy-done.2), channel_id=1, source_target_pairs={{0,4},{4,8},{8,12},{1,5},{5,9},{9,13},{2,6},{6,10},{10,14},{3,7},{... | collective-permute-start | bytes 1572872 | tf_op jit(solution)/shard_map/ppermute | solution.py:328
  11.3 22.4 %collective-permute-start.2 = (bf16[512,512]{1,0:T(8,128)(2,1)S(1)}, bf16[512,512]{1,0:T(8,128)(2,1)S(1)}, u32[]{:S(2)}, u32[]{:S(2)}) collective-permute-start(bf16[512,512]{1,0:T(8,128)(2,1)S(1)} %copy-done.3), channel_id=1, source_target_pairs={{0,4},{4,8},{8,12},{1,5},{5,9},{9,13},{2,6},{6,10},{10,14},{3,7},{... | collective-permute-start | bytes 1572872 | tf_op jit(solution)/shard_map/ppermute | solution.py:328
  23.6 18.7 %copy-start.4 = (bf16[512,512]{1,0:T(8,128)(2,1)}, bf16[512,512]{1,0:T(8,128)(2,1)S(1)}, u32[]{:S(2)}) copy-start(bf16[512,512]{1,0:T(8,128)(2,1)S(1)} %collective-permute-done.1.k0) | copy-start | bytes 1572868
  35.0 26.0 %collective-permute-start.9 = (bf16[512,1024]{1,0:T(8,128)(2,1)}, bf16[512,1024]{1,0:T(8,128)(2,1)}, u32[]{:S(2)}, u32[]{:S(2)}) collective-permute-start(bf16[512,1024]{1,0:T(8,128)(2,1)} %maximum_select_fusion), channel_id=1, source_target_pairs={{0,2},{2,0},{1,3},{3,1},{4,6},{6,4},{5,7},{7,5},{8,10},{10,8},{9,1... | collective-permute-start | bytes 3145736 | tf_op jit(solution)/shard_map/ppermute | solution.py:309
  35.5 17.9 %collective-permute-start.3 = (bf16[128,2688]{1,0:T(8,128)(2,1)S(1)}, bf16[128,2688]{1,0:T(8,128)(2,1)}, u32[]{:S(2)}, u32[]{:S(2)}) collective-permute-start(bf16[128,2688]{1,0:T(8,128)(2,1)S(1)} %get-tuple-element.27.refs_2_), channel_id=1, source_target_pairs={{0,4},{4,12},{12,8},{8,0},{1,5},{5,13},{13,9},{9,1},{2,6},{6,14},{... | collective-permute-start | bytes 2064392 | tf_op jit(solution)/shard_map/ppermute | solution.py:347
  38.0 16.0 %collective-permute-start.5 = (bf16[128,2688]{1,0:T(8,128)(2,1)}, bf16[128,2688]{1,0:T(8,128)(2,1)S(1)}, u32[]{:S(2)}, u32[]{:S(2)}) collective-permute-start(bf16[128,2688]{1,0:T(8,128)(2,1)} %collective-permute-done.4.refs_6_), channel_id=1, source_target_pairs={{0,16},{16,0},{1,17},{17,1},{2,18},{18,2},{3,19},{19,3},{4,20},{20... | collective-permute-start | bytes 2064392 | tf_op jit(solution)/shard_map/ppermute | solution.py:309
  42.3 18.7 %copy-start.8 = (bf16[512,1024]{1,0:T(8,128)(2,1)S(1)}, bf16[512,1024]{1,0:T(8,128)(2,1)}, u32[]{:S(2)}) copy-start(bf16[512,1024]{1,0:T(8,128)(2,1)} %q_ref.1) | copy-start | bytes 3145732
  54.8 18.0 %collective-permute-start.6 = (bf16[128,2688]{1,0:T(8,128)(2,1)}, bf16[128,2688]{1,0:T(8,128)(2,1)S(1)}, u32[]{:S(2)}, u32[]{:S(2)}) collective-permute-start(bf16[128,2688]{1,0:T(8,128)(2,1)} %collective-permute-done.3.refs_3_), channel_id=1, source_target_pairs={{0,4},{4,12},{12,8},{8,0},{1,5},{5,13},{13,9},{9,1},{2,6},{6,14},{... | collective-permute-start | bytes 2064392 | tf_op jit(solution)/shard_map/ppermute | solution.py:347
  57.4 16.6 %collective-permute-start.7 = (bf16[128,2688]{1,0:T(8,128)(2,1)}, bf16[128,2688]{1,0:T(8,128)(2,1)S(1)}, u32[]{:S(2)}, u32[]{:S(2)}) collective-permute-start(bf16[128,2688]{1,0:T(8,128)(2,1)} %collective-permute-done.3.refs_3_), channel_id=1, source_target_pairs={{0,2},{2,0},{1,3},{3,1},{4,6},{6,4},{5,7},{7,5},{8,10},{10,8},{9,1... | collective-permute-start | bytes 2064392 | tf_op jit(solution)/shard_map/ppermute | solution.py:309
  58.9 15.1 %collective-permute-start.8 = (bf16[128,2688]{1,0:T(8,128)(2,1)}, bf16[128,2688]{1,0:T(8,128)(2,1)S(1)}, u32[]{:S(2)}, u32[]{:S(2)}) collective-permute-start(bf16[128,2688]{1,0:T(8,128)(2,1)} %collective-permute-done.3.refs_3_), channel_id=1, source_target_pairs={{0,16},{16,0},{1,17},{17,1},{2,18},{18,2},{3,19},{19,3},{4,20},{20... | collective-permute-start | bytes 2064392 | tf_op jit(solution)/shard_map/ppermute | solution.py:309
  61.0 59.5 %copy-start.25 = (f32[2688]{0:T(1024)S(1)}, f32[2688]{0:T(1024)}, u32[]{:S(2)}) copy-start(f32[2688]{0:T(1024)} %param.12) | copy-start | bytes 32260
  61.0 59.5 %copy-start.26 = (f32[2688]{0:T(1024)S(1)}, f32[2688]{0:T(1024)}, u32[]{:S(2)}) copy-start(f32[2688]{0:T(1024)} %param.13) | copy-start | bytes 32260
  74.0 22.0 %collective-permute-start.13 = (bf16[8,512,128]{2,1,0:T(8,128)(2,1)S(1)}, bf16[8,512,128]{2,1,0:T(8,128)(2,1)S(1)}, u32[]{:S(2)}, u32[]{:S(2)}) collective-permute-start(bf16[8,512,128]{2,1,0:T(8,128)(2,1)S(1)} %shard_map.82.refs_0_), channel_id=1, source_target_pairs={{0,1},{1,0},{2,3},{3,2},{4,5},{5,4},{6,7},{7,6},{8,9},{9,8},{10,11... | collective-permute-start | bytes 3145736 | tf_op jit(solution)/shard_map/ppermute | solution.py:309
  74.0 19.6 %collective-permute-start.10 = (bf16[128,2688]{1,0:T(8,128)(2,1)S(1)}, bf16[128,2688]{1,0:T(8,128)(2,1)S(1)}, u32[]{:S(2)}, u32[]{:S(2)}) collective-permute-start(bf16[128,2688]{1,0:T(8,128)(2,1)S(1)} %collective-permute-done.6.refs_4_), channel_id=1, source_target_pairs={{0,4},{4,12},{12,8},{8,0},{1,5},{5,13},{13,9},{9,1},{2,6},{6,14},{... | collective-permute-start | bytes 2064392 | tf_op jit(solution)/shard_map/ppermute | solution.py:347
  76.5 17.6 %collective-permute-start.11 = (bf16[128,2688]{1,0:T(8,128)(2,1)S(1)}, bf16[128,2688]{1,0:T(8,128)(2,1)S(1)}, u32[]{:S(2)}, u32[]{:S(2)}) collective-permute-start(bf16[128,2688]{1,0:T(8,128)(2,1)S(1)} %collective-permute-done.6.refs_4_), channel_id=1, source_target_pairs={{0,2},{2,0},{1,3},{3,1},{4,6},{6,4},{5,7},{7,5},{8,10},{10,8},{9,1... | collective-permute-start | bytes 2064392 | tf_op jit(solution)/shard_map/ppermute | solution.py:309
  77.8 17.3 %collective-permute-start.12 = (bf16[128,2688]{1,0:T(8,128)(2,1)S(1)}, bf16[128,2688]{1,0:T(8,128)(2,1)S(1)}, u32[]{:S(2)}, u32[]{:S(2)}) collective-permute-start(bf16[128,2688]{1,0:T(8,128)(2,1)S(1)} %collective-permute-done.7.refs_7_), channel_id=1, source_target_pairs={{0,16},{16,0},{1,17},{17,1},{2,18},{18,2},{3,19},{19,3},{4,20},{20... | collective-permute-start | bytes 2064392 | tf_op jit(solution)/shard_map/ppermute | solution.py:309
  96.0 17.4 %collective-permute-start.14 = (bf16[128,2688]{1,0:T(8,128)(2,1)S(1)}, bf16[128,2688]{1,0:T(8,128)(2,1)}, u32[]{:S(2)}, u32[]{:S(2)}) collective-permute-start(bf16[128,2688]{1,0:T(8,128)(2,1)S(1)} %collective-permute-done.8.refs_11_), channel_id=1, source_target_pairs={{0,4},{4,12},{12,8},{8,0},{1,5},{5,13},{13,9},{9,1},{2,6},{6,14},{... | collective-permute-start | bytes 2064392 | tf_op jit(solution)/shard_map/ppermute | solution.py:347
  99.4 16.3 %collective-permute-start.15 = (bf16[128,2688]{1,0:T(8,128)(2,1)S(1)}, bf16[128,2688]{1,0:T(8,128)(2,1)}, u32[]{:S(2)}, u32[]{:S(2)}) collective-permute-start(bf16[128,2688]{1,0:T(8,128)(2,1)S(1)} %collective-permute-done.10.refs_5_), channel_id=1, source_target_pairs={{0,2},{2,0},{1,3},{3,1},{4,6},{6,4},{5,7},{7,5},{8,10},{10,8},{9,1... | collective-permute-start | bytes 2064392 | tf_op jit(solution)/shard_map/ppermute | solution.py:309
  101.8 15.9 %collective-permute-start.16 = (bf16[128,2688]{1,0:T(8,128)(2,1)S(1)}, bf16[128,2688]{1,0:T(8,128)(2,1)S(1)}, u32[]{:S(2)}, u32[]{:S(2)}) collective-permute-start(bf16[128,2688]{1,0:T(8,128)(2,1)S(1)} %collective-permute-done.11.refs_8_), channel_id=1, source_target_pairs={{0,16},{16,0},{1,17},{17,1},{2,18},{18,2},{3,19},{19,3},{4,20},{20... | collective-permute-start | bytes 2064392 | tf_op jit(solution)/shard_map/ppermute | solution.py:309
  118.6 20.3 %collective-permute-start.17 = (bf16[128,2688]{1,0:T(8,128)(2,1)}, bf16[128,2688]{1,0:T(8,128)(2,1)}, u32[]{:S(2)}, u32[]{:S(2)}) collective-permute-start(bf16[128,2688]{1,0:T(8,128)(2,1)} %collective-permute-done.14.refs_12_), channel_id=1, source_target_pairs={{0,4},{4,12},{12,8},{8,0},{1,5},{5,13},{13,9},{9,1},{2,6},{6,14},{... | collective-permute-start | bytes 2064392 | tf_op jit(solution)/shard_map/ppermute | solution.py:347
  119.0 19.9 %collective-permute-start.18 = (bf16[128,2688]{1,0:T(8,128)(2,1)}, bf16[128,2688]{1,0:T(8,128)(2,1)}, u32[]{:S(2)}, u32[]{:S(2)}) collective-permute-start(bf16[128,2688]{1,0:T(8,128)(2,1)} %collective-permute-done.15.refs_9_), channel_id=1, source_target_pairs={{0,16},{16,0},{1,17},{17,1},{2,18},{18,2},{3,19},{19,3},{4,20},{20... | collective-permute-start | bytes 2064392 | tf_op jit(solution)/shard_map/ppermute | solution.py:309
  143.8 1.6 %collective-permute-start.19 = (f32[520,128]{1,0:T(8,128)S(1)}, f32[520,128]{1,0:T(8,128)S(1)}, u32[]{:S(2)}, u32[]{:S(2)}) collective-permute-start(f32[520,128]{1,0:T(8,128)S(1)} %get-tuple-element.47.own_ref), channel_id=1, source_target_pairs={{0,1},{1,0},{2,3},{3,2},{4,5},{5,4},{6,7},{7,6},{8,9},{9,8},{10,11... | collective-permute-start | bytes 798728 | tf_op jit(solution)/shard_map/ppermute | solution.py:309
  (23 other events, 96.7 us)

commit v11 on v10

--- a/solution.py
+++ b/solution.py
@@ -157,9 +157,21 @@
         pltpu.make_async_copy(sources[0].at[0], place, sems.at[n]).wait()
 
 
-def project_kernel(kinds, sources, where_ref, *refs):
+def split_in(in_ref):
+    high = in_ref[...].astype(jnp.bfloat16)
+    low = (in_ref[...] - high.astype(jnp.float32)).astype(jnp.bfloat16)
+    return jnp.concatenate([high, low], 0)
+
+
+def coded(field, in_parts):
+    code = lax.dot_general(field.astype(jnp.bfloat16), in_parts, NT, preferred_element_type=jnp.float32)
+    return code + pltpu.roll(code, RANK, 1)
+
+
+def project_kernel(kinds, late_kinds, sources, where_ref, *refs):
     sources, refs = refs[:sources], refs[sources:]
-    weights, (partial_ref, heads, sems, blocks, block_sems) = refs[:-5], refs[-5:]
+    weights, refs = refs[: len(kinds)], refs[len(kinds) :]
+    in_ref, mean_ref, partial_ref, late_ref, code_ref, heads, sems, late_sems, blocks, block_sems = refs
     step = pl.program_id(0)
     steps = pl.num_programs(0)
     depth = weights[0].shape[0]
@@ -181,87 +193,103 @@
     @pl.when(step == 0)
     def _():
         gather_heads(kinds, where_ref, sources, heads, sems)
+        gather_heads(late_kinds, where_ref, sources, late_ref, late_sems)
+
+    mean = jnp.broadcast_to(mean_ref[...], (8, mean_ref.shape[1]))
+    mean_high = mean.astype(jnp.bfloat16).astype(jnp.float32)
+    in_parts = split_in(in_ref)
+    code = coded(mean_high, in_parts) + coded(mean - mean_high, in_parts)
+
+    @pl.when(step == 0)
+    def _():
+        code_ref[...] = code
+
+    @pl.when(step > 0)
+    def _():
+        code_ref[...] += code
 
     columns_of(step, lambda copy: copy.wait())
     partial_ref[...] = jnp.dot(heads[...], blocks[lax.rem(step, 2)], preferred_element_type=jnp.float32)
 
 
-def project(where, kinds, sources, weights):
+def project(where, kinds, late_kinds, sources, weights, erase_in, mean):
     tok = sources[0].shape[1]
     depth, width = weights[0].shape
-    count = len(kinds)
+    count, late = len(kinds), len(late_kinds)
     in_hbm = pl.BlockSpec(memory_space=pltpu.HBM)
+    columns = lambda rows: pl.BlockSpec((rows, TILE), lambda j, r: (0, j))
+    whole = lambda *shape: pl.BlockSpec(shape, lambda j, r: (0, 0))
     return pl.pallas_call(
-        functools.partial(project_kernel, kinds, len(sources)),
+        functools.partial(project_kernel, kinds, late_kinds, len(sources)),
         grid_spec=pltpu.PrefetchScalarGridSpec(
             num_scalar_prefetch=1,
             grid=(width // TILE,),
-            in_specs=[in_hbm] * (len(sources) + count),
-            out_specs=pl.BlockSpec((tok, TILE), lambda j, r: (0, j)),
+            in_specs=[in_hbm] * (len(sources) + count) + [columns(RANK), columns(1)],
+            out_specs=[columns(tok), whole(tok, late * depth), whole(8, 2 * RANK)],
             scratch_shapes=[
                 pltpu.VMEM((tok, count * depth), jnp.bfloat16),
                 pltpu.SemaphoreType.DMA((count,)),
+                pltpu.SemaphoreType.DMA((late,)),
                 pltpu.VMEM((2, count * depth, TILE), jnp.bfloat16),
                 pltpu.SemaphoreType.DMA((2, count)),
             ],
         ),
-        out_shape=jax.ShapeDtypeStruct((tok, width), jnp.float32),
+        out_shape=[
+            jax.ShapeDtypeStruct((tok, width), jnp.float32),
+            jax.ShapeDtypeStruct((tok, late * depth), jnp.bfloat16),
+            jax.ShapeDtypeStruct((8, 2 * RANK), jnp.float32),
+        ],
         compiler_params=pltpu.CompilerParams(vmem_limit_bytes=VMEM_LIMIT),
         cost_estimate=pl.CostEstimate(
             flops=2 * tok * count * depth * width, bytes_accessed=2 * count * depth * width, transcendentals=0
         ),
-    )(where, *sources, *weights)
-
-
-def close_kernel(kinds, sources, where_ref, *refs):
-    sources, refs = refs[:sources], refs[sources:]
-    weights, (partial_ref, gain_ref, in_ref, mean_ref, hidden_ref, stat_ref, heads, sems) = refs[:-8], refs[-8:]
-    gather_heads(kinds, where_ref, sources, heads, sems)
-    tok, width = hidden_ref.shape
-    code = square = mean_code = 0.0
-    for at in range(0, width, TILE):
-        here = slice(at, at + TILE)
-        weight = jnp.concatenate([w[:, here] for w in weights], 0)
-        total = partial_ref[:, here] + jnp.dot(heads[...], weight, preferred_element_type=jnp.float32)
-        hidden_ref[:, here] = total
-        in_high = in_ref[:, here].astype(jnp.bfloat16)
-        in_low = (in_ref[:, here] - in_high.astype(jnp.float32)).astype(jnp.bfloat16)
-        in_parts = jnp.concatenate([in_high, in_low], 0)
-
-        def coded(field):
-            return lax.dot_general(field.astype(jnp.bfloat16), in_parts, NT, preferred_element_type=jnp.float32)
-
-        code += coded(total * gain_ref[:, here])
-        square += jnp.sum(total * total, axis=1, keepdims=True)
-        mean = jnp.broadcast_to(mean_ref[:, here], (8, TILE))
-        mean_high = mean.astype(jnp.bfloat16).astype(jnp.float32)
-        mean_code += coded(mean_high) + coded(mean - mean_high)
+    )(where, *sources, *weights, erase_in, mean)
+
+
+def close_kernel(heads_ref, *refs):
+    weights, (partial_ref, mean_code_ref, gain_ref, in_ref, hidden_ref, stat_ref) = refs[:-6], refs[-6:]
+    step = pl.program_id(0)
+    tok = hidden_ref.shape[0]
+    weight = jnp.concatenate([w[...] for w in weights], 0)
+    total = partial_ref[...] + jnp.dot(heads_ref[...], weight, preferred_element_type=jnp.float32)
+    hidden_ref[...] = total
+    code = coded(total * gain_ref[...], split_in(in_ref))
+    square = jnp.sum(total * total, axis=1, keepdims=True)
     lane = lax.broadcasted_iota(jnp.int32, code.shape, 1)
-    stat_ref[:tok, :] = jnp.where(lane < RANK, code + pltpu.roll(code, RANK, 1), square)
-    stat_ref[tok:, :] = mean_code + pltpu.roll(mean_code, RANK, 1)
-
-
-def close(where, kinds, sources, weights, partial, gain, erase_in, mean):
+    stat = jnp.where(lane < RANK, code, square)
+
+    @pl.when(step == 0)
+    def _():
+        stat_ref[:tok, :] = stat
+        stat_ref[tok:, :] = mean_code_ref[...]
+
+    @pl.when(step > 0)
+    def _():
+        stat_ref[:tok, :] += stat
+
+
+def close(heads, weights, partial, mean_code, gain, erase_in):
     tok, width = partial.shape
     depth = weights[0].shape[0]
-    count = len(kinds)
-    in_vmem = pl.BlockSpec(memory_space=pltpu.VMEM)
-    in_hbm = pl.BlockSpec(memory_space=pltpu.HBM)
+    count = len(weights)
+    columns = lambda rows: pl.BlockSpec((rows, TILE), lambda j: (0, j))
+    whole = lambda *shape: pl.BlockSpec(shape, lambda j: (0, 0))
     return pl.pallas_call(
-        functools.partial(close_kernel, kinds, len(sources)),
-        in_specs=[pl.BlockSpec(memory_space=pltpu.SMEM)] + [in_hbm] * len(sources) + [in_vmem] * (count + 4),
-        out_specs=[in_vmem] * 2,
+        close_kernel,
+        grid=(width // TILE,),
+        in_specs=[whole(*heads.shape)]
+        + [columns(depth)] * count
+        + [columns(tok), whole(*mean_code.shape), columns(1), columns(RANK)],
+        out_specs=[columns(tok), whole(tok + 8, 2 * RANK)],
         out_shape=[
             jax.ShapeDtypeStruct((tok, width), jnp.float32),
             jax.ShapeDtypeStruct((tok + 8, 2 * RANK), jnp.float32),
         ],
-        scratch_shapes=[pltpu.VMEM((tok, count * depth), jnp.bfloat16), pltpu.SemaphoreType.DMA((count,))],
-        input_output_aliases={1 + len(sources) + count: 0},
         compiler_params=pltpu.CompilerParams(vmem_limit_bytes=VMEM_LIMIT),
         cost_estimate=pl.CostEstimate(
             flops=2 * tok * count * depth * width, bytes_accessed=2 * count * depth * width, transcendentals=0
         ),
-    )(where, *sources, *weights, partial, gain, erase_in, mean)
+    )(heads, *weights, partial, mean_code, gain, erase_in)
 
 
 def finish_kernel(model_width, own_ref, other_ref, gain_ref, out_ref, hidden_ref, erased_ref, tiles, sems):
@@ -351,34 +379,33 @@
         main[0] = jnp.where(is_mine, mine, theirs)
         across[0] = jnp.where(is_mine, theirs, mine)
         beside[0] = beyond(main[0])
-        second_keys, second_values = from_behind(keys), from_behind(values)
+        second_keys = from_behind(after(keys, main[0]))
+        second_values = from_behind(after(values, second_keys))
+        first_keys = for_next(keys, after(second_keys, beside[0]))
         corner[0] = facing(beside[0])
+        main[1] = ring(after(main[0], second_values))
+        first_values = for_next(values, after(second_values, first_keys))
         cos, sin = rope_tables((after(row, beside[0]) - 2) * tok, 3 * tok)
-        main[1] = ring(after(main[0], second_keys, second_values))
-        own_both = jnp.concatenate([keys, values], 1)
-        old_both = jnp.concatenate(after((second_keys, second_values), beside[0]), 1)
-        first_both = for_next(own_both, old_both)
-        main[1], corner[0], cos, sin = hold((main[1], corner[0], cos, sin))
-        main[2], across[1] = ring(main[1]), facing(main[1])
-        beside[1] = beyond(main[1])
+        main[1], first_keys, first_values, corner[0], cos, sin, where = hold(
+            (main[1], first_keys, first_values, corner[0], cos, sin, where)
+        )
+        main[2], beside[1], across[1] = ring(main[1]), beyond(main[1]), facing(main[1])
         attended = attend(
-            row[None], queries, (second_keys, first_both, keys), (second_values, first_both, values), cos, sin, True
+            row[None], queries, (second_keys, first_keys, keys), (second_values, first_values, values), cos, sin, True
         )
         main[2], beside[1], across[1], attended = hold((main[2], beside[1], across[1], attended))
         main[3], beside[2], corner[1] = ring(main[2]), beyond(main[2]), facing(beside[1])
-        att_other = swapped(attended, "col")
-        main[3], beside[2], corner[1], att_other, across[1] = hold((main[3], beside[2], corner[1], att_other, across[1]))
+        main[3], beside[2], corner[1], across[1], attended = hold((main[3], beside[2], corner[1], across[1], attended))
         across[2], beside[3], corner[2] = ring(across[1]), beyond(main[3]), facing(beside[2])
-        across[2], beside[3], corner[2] = hold((across[2], beside[3], corner[2]))
+        across[2], beside[3], corner[2], attended = hold((across[2], beside[3], corner[2], attended))
         across[3], corner[3] = ring(across[2]), facing(beside[3])
-        attended, att_other = [attended], [att_other]
+        attended, att_other = [attended], [swapped(attended, "col")]
         weights, kinds, late, late_kinds = [], [], [], []
         for name, pieces in (("main", main), ("beside", beside), ("across", across), ("corner", corner)):
             for k in range(outer):
                 is_late = k == 3 and name in ("across", "corner")
                 (late if is_late else weights).append(pieces[k])
                 (late_kinds if is_late else kinds).append((name, k))
-        partial = project(where, kinds, attended + att_other, weights)
     else:
         second_keys, second_values = from_behind(keys), from_behind(values)
         first_keys, first_values = for_next(keys, second_keys), for_next(values, second_values)
@@ -390,9 +417,9 @@
         att_other = [swapped(attended[0], "col")]
         weights, late = ([lax.all_gather(w, ("far", "near"), axis=0, tiled=True)] for w in (mine, theirs))
         kinds, late_kinds = [(None, 0)], [(None, 1)]
-        partial = project(where, kinds, attended + att_other, weights)
-
-    hidden, stat = close(where, late_kinds, attended + att_other, late, partial, gain, erase_in, mean)
+
+    partial, late_heads, mean_code = project(where, kinds, late_kinds, attended + att_other, weights, erase_in, mean)
+    hidden, stat = close(late_heads, late, partial, mean_code, gain, erase_in)
     return finish(model_width, stat, swapped(stat, "col"), gain, erase_out, hidden)
 
 

time: 149 us -> 129 us (0.87)
  local copies, waits for them, and re-layouts: 17 us -> 1.28 us
  starting transfers between devices: 32.6 us -> 29.3 us
    unnamed x54 -> x14, local copies, waits for them, and re-layouts: 15.7 us -> 0.03 us
    ppermute x5, waiting for transfers between devices: 33.2 us -> 38.1 us  [on_device(): ring = lambda block: lax.ppermute(block, 'far', hops)]
    ppermute x13 -> x14, waiting for transfers between devices: 11.4 us -> 7.57 us  [swapped(): return lax.ppermute(block, axis, [(0, 1), (1, 0)])]
    ppermute x13 -> x14, starting transfers between devices: 15.1 us -> 11.3 us  [swapped(): return lax.ppermute(block, axis, [(0, 1), (1, 0)])]
  transfers between devices with their start and end apart: 20 -> 21, of which waited for: 14 -> 16; matrix products, arithmetic and copies ran while one was open for 2% -> 3% of each run, Pallas kernels for 14% -> 17%
where the time goes in v11:
time: 129 us
  waiting for transfers between devices  64.2 us (50%)
  starting transfers between devices  29.3 us (23%)
  Pallas kernels  28.4 us (22%)
  other arithmetic  5.64 us (4%)
    ppermute x5, waiting for transfers between devices, on_device(): ring = lambda block: lax.ppermute(block, 'far', hops)  38.1 us
    ppermute x2, waiting for transfers between devices, on_device(): from_behind = lambda block: lax.ppermute(block, 'far', ahead)  18.6 us
    pallas_call x1, Pallas kernels, attend(): pl.pallas_call(functools.partial(attend_kernel, tok, group, direct), grid...  11.8 us
    ppermute x14, starting transfers between devices, swapped(): return lax.ppermute(block, axis, [(0, 1), (1, 0)])  11.3 us
    pallas_call x1, Pallas kernels, project(): pl.pallas_call(functools.partial(project_kernel, kinds, late_kinds, len(s...  10.8 us
    ppermute x5, starting transfers between devices, on_device(): ring = lambda block: lax.ppermute(block, 'far', hops)  10.1 us
    ppermute x2, starting transfers between devices, on_device(): from_behind = lambda block: lax.ppermute(block, 'far', ahead)  7.91 us
    ppermute x14, waiting for transfers between devices, swapped(): return lax.ppermute(block, axis, [(0, 1), (1, 0)])  7.57 us
  transfers between devices with their start and end apart: 21, of which 16 were waited for; matrix products, arithmetic and copies ran while one was open for 3% of the time, Pallas kernels for 17%

profile of v11, /device:TPU:0, one launch (start us, length us, event | category | flops | bytes accessed | tf_op | source)
XLA Modules:
  0.0 129.2 jit_solution(3290056479764711980)
XLA Ops:
  1.8 1.8 %collective-permute-done = bf16[128,2688]{1,0:T(8,128)(2,1)S(1)} collective-permute-done((bf16[128,2688]{1,0:T(8,128)(2,1)S(1)}, bf16[128,2688]{1,0:T(8,128)(2,1)S(1)}, u32[]{:S(2)}, u32[]{:S(2)}) %collective-permute-start) | collective-permute-done | bytes 688160 | tf_op jit(solution)/shard_map/ppermute | solution.py:337
  3.5 1.3 %broadcast_select_fusion = (bf16[128,2688]{1,0:T(8,128)(2,1)S(1)}, bf16[128,2688]{1,0:T(8,128)(2,1)S(1)}) fusion(bf16[128,2688]{1,0:T(8,128)(2,1)S(1)} %collective-permute-done, pred[]{:T(512)S(6)} %eq.7, bf16[128,5376]{1,0:T(8,128)(2,1)} %param.11, s32[]{:T(128)S(6)} %select_n.31), kind=kLoop, calls=%fused_computation.4 | loop fusion | flops 688128 | bytes 2752517 | tf_op jit(solution)/shard_map/jit(_where)/select_n | solution.py:380
  4.9 3.0 %collective-permute-start.4 = (bf16[128,2688]{1,0:T(8,128)(2,1)S(1)}, bf16[128,2688]{1,0:T(8,128)(2,1)}, u32[]{:S(2)}, u32[]{:S(2)}) collective-permute-start(bf16[128,2688]{1,0:T(8,128)(2,1)S(1)} %get-tuple-element.38.refs_2_), channel_id=1, source_target_pairs={{0,2},{2,0},{1,3},{3,1},{4,6},{6,4},{5,7},{7,5},{8,10},{10,8},{9,1... | collective-permute-start | bytes 2064392 | tf_op jit(solution)/shard_map/ppermute | solution.py:337
  7.8 3.5 %collective-permute-start.1 = (bf16[512,512]{1,0:T(8,128)(2,1)S(1)}, bf16[512,512]{1,0:T(8,128)(2,1)S(1)}, u32[]{:S(2)}, u32[]{:S(2)}) collective-permute-start(bf16[512,512]{1,0:T(8,128)(2,1)S(1)} %copy-done.2), channel_id=1, source_target_pairs={{0,4},{4,8},{8,12},{1,5},{5,9},{9,13},{2,6},{6,10},{10,14},{3,7},{... | collective-permute-start | bytes 1572872 | tf_op jit(solution)/shard_map/ppermute | solution.py:356
  11.3 11.1 %collective-permute-done.1.k0 = bf16[512,512]{1,0:T(8,128)(2,1)S(1)} collective-permute-done((bf16[512,512]{1,0:T(8,128)(2,1)S(1)}, bf16[512,512]{1,0:T(8,128)(2,1)S(1)}, u32[]{:S(2)}, u32[]{:S(2)}) %collective-permute-start.1) | collective-permute-done | bytes 524320 | tf_op jit(solution)/shard_map/ppermute | solution.py:356
  22.5 4.4 %collective-permute-start.2 = (bf16[512,512]{1,0:T(8,128)(2,1)S(1)}, bf16[512,512]{1,0:T(8,128)(2,1)S(1)}, u32[]{:S(2)}, u32[]{:S(2)}) collective-permute-start(bf16[512,512]{1,0:T(8,128)(2,1)S(1)} %copy-done.3), channel_id=1, source_target_pairs={{0,4},{4,8},{8,12},{1,5},{5,9},{9,13},{2,6},{6,10},{10,14},{3,7},{... | collective-permute-start | bytes 1572872 | tf_op jit(solution)/shard_map/ppermute | solution.py:356
  28.4 1.5 %collective-permute-start.7 = (bf16[128,2688]{1,0:T(8,128)(2,1)}, bf16[128,2688]{1,0:T(8,128)(2,1)S(1)}, u32[]{:S(2)}, u32[]{:S(2)}) collective-permute-start(bf16[128,2688]{1,0:T(8,128)(2,1)} %collective-permute-done.4.refs_6_), channel_id=1, source_target_pairs={{0,16},{16,0},{1,17},{17,1},{2,18},{18,2},{3,19},{19,3},{4,20},{20... | collective-permute-start | bytes 2064392 | tf_op jit(solution)/shard_map/ppermute | solution.py:337
  29.9 7.4 %collective-permute-done.2.v0 = bf16[512,512]{1,0:T(8,128)(2,1)S(1)} collective-permute-done((bf16[512,512]{1,0:T(8,128)(2,1)S(1)}, bf16[512,512]{1,0:T(8,128)(2,1)S(1)}, u32[]{:S(2)}, u32[]{:S(2)}) %collective-permute-start.2) | collective-permute-done | bytes 524320 | tf_op jit(solution)/shard_map/ppermute | solution.py:356
  37.3 2.5 %collective-permute-start.3 = (bf16[128,2688]{1,0:T(8,128)(2,1)S(1)}, bf16[128,2688]{1,0:T(8,128)(2,1)S(1)}, u32[]{:S(2)}, u32[]{:S(2)}) collective-permute-start(bf16[128,2688]{1,0:T(8,128)(2,1)S(1)} %get-tuple-element.38.refs_2_), channel_id=1, source_target_pairs={{0,4},{4,12},{12,8},{8,0},{1,5},{5,13},{13,9},{9,1},{2,6},{6,14},{... | collective-permute-start | bytes 2064392 | tf_op jit(solution)/shard_map/ppermute | solution.py:375
  41.4 2.8 %fusion = (f32[1536,64]{1,0:T(8,128)S(1)}, f32[1536,64]{1,0:T(8,128)S(1)}, f32[1536,64]{1,0:T(8,128)S(1)}) fusion(f32[64]{0:T(128)S(1)} %multiply_exponential_fusion, f32[1536]{0:T(1024)S(1)} %add_convert_fusion), kind=kLoop, calls=%fused_computation.8 | loop fusion | flops 196608 | bytes 1186048 | tf_op jit(solution)/shard_map/neg | solution.py:34
  44.7 10.0 %collective-permute-done.3.refs_3_ = bf16[128,2688]{1,0:T(8,128)(2,1)S(1)} collective-permute-done((bf16[128,2688]{1,0:T(8,128)(2,1)S(1)}, bf16[128,2688]{1,0:T(8,128)(2,1)S(1)}, u32[]{:S(2)}, u32[]{:S(2)}) %collective-permute-start.3) | collective-permute-done | bytes 688160 | tf_op jit(solution)/shard_map/ppermute | solution.py:375
  54.7 1.5 %collective-permute-start.10 = (bf16[128,2688]{1,0:T(8,128)(2,1)S(1)}, bf16[128,2688]{1,0:T(8,128)(2,1)S(1)}, u32[]{:S(2)}, u32[]{:S(2)}) collective-permute-start(bf16[128,2688]{1,0:T(8,128)(2,1)S(1)} %collective-permute-done.3.refs_3_), channel_id=1, source_target_pairs={{0,16},{16,0},{1,17},{17,1},{2,18},{18,2},{3,19},{19,3},{4,20},{20... | collective-permute-start | bytes 2064392 | tf_op jit(solution)/shard_map/ppermute | solution.py:337
  57.5 11.8 %shard_map.82.refs_0_ = bf16[8,512,128]{2,1,0:T(8,128)(2,1)S(1)} custom-call(s32[1]{0:T(128)} %bitcast.3.row_ref, bf16[512,1024]{1,0:T(8,128)(2,1)S(1)} %copy-done.4, bf16[512,512]{1,0:T(8,128)(2,1)S(1)} %collective-permute-done.1.k0, bf16[512,512]{1,0:T(8,128)(2,1)} %collective-permute-done.5.k1, bf16[512,512]{1,0:T(8,128)(2,1)S(1)} %copy-done.2, ...), custom_call_target="tpu_custom_call" | custom-call | flops 10737418240 | bytes 6291456 | tf_op jit(solution)/shard_map/pallas_call | solution.py:105
  69.6 2.1 %collective-permute-done.8.refs_4_ = bf16[128,2688]{1,0:T(8,128)(2,1)S(1)} collective-permute-done((bf16[128,2688]{1,0:T(8,128)(2,1)S(1)}, bf16[128,2688]{1,0:T(8,128)(2,1)S(1)}, u32[]{:S(2)}, u32[]{:S(2)}) %collective-permute-start.8) | collective-permute-done | bytes 688160 | tf_op jit(solution)/shard_map/ppermute | solution.py:375
  71.7 3.0 %collective-permute-start.11 = (bf16[128,2688]{1,0:T(8,128)(2,1)S(1)}, bf16[128,2688]{1,0:T(8,128)(2,1)S(1)}, u32[]{:S(2)}, u32[]{:S(2)}) collective-permute-start(bf16[128,2688]{1,0:T(8,128)(2,1)S(1)} %collective-permute-done.8.refs_4_), channel_id=1, source_target_pairs={{0,4},{4,12},{12,8},{8,0},{1,5},{5,13},{13,9},{9,1},{2,6},{6,14},{... | collective-permute-start | bytes 2064392 | tf_op jit(solution)/shard_map/ppermute | solution.py:375
  75.8 11.5 %collective-permute-done.11.refs_5_ = bf16[128,2688]{1,0:T(8,128)(2,1)S(1)} collective-permute-done((bf16[128,2688]{1,0:T(8,128)(2,1)S(1)}, bf16[128,2688]{1,0:T(8,128)(2,1)S(1)}, u32[]{:S(2)}, u32[]{:S(2)}) %collective-permute-start.11) | collective-permute-done | bytes 688160 | tf_op jit(solution)/shard_map/ppermute | solution.py:375
  88.2 2.2 %collective-permute-start.14 = (bf16[128,2688]{1,0:T(8,128)(2,1)S(1)}, bf16[128,2688]{1,0:T(8,128)(2,1)S(1)}, u32[]{:S(2)}, u32[]{:S(2)}) collective-permute-start(bf16[128,2688]{1,0:T(8,128)(2,1)S(1)} %collective-permute-done.10.refs_11_), channel_id=1, source_target_pairs={{0,4},{4,12},{12,8},{8,0},{1,5},{5,13},{13,9},{9,1},{2,6},{6,14},{... | collective-permute-start | bytes 2064392 | tf_op jit(solution)/shard_map/ppermute | solution.py:375
  92.0 9.3 %collective-permute-done.14.refs_12_ = bf16[128,2688]{1,0:T(8,128)(2,1)S(1)} collective-permute-done((bf16[128,2688]{1,0:T(8,128)(2,1)S(1)}, bf16[128,2688]{1,0:T(8,128)(2,1)S(1)}, u32[]{:S(2)}, u32[]{:S(2)}) %collective-permute-start.14) | collective-permute-done | bytes 688160 | tf_op jit(solution)/shard_map/ppermute | solution.py:375
  102.4 1.6 %collective-permute-start.18 = (bf16[128,2688]{1,0:T(8,128)(2,1)S(1)}, bf16[128,2688]{1,0:T(8,128)(2,1)S(1)}, u32[]{:S(2)}, u32[]{:S(2)}) collective-permute-start(bf16[128,2688]{1,0:T(8,128)(2,1)S(1)} %collective-permute-done.14.refs_12_), channel_id=1, source_target_pairs={{0,4},{4,12},{12,8},{8,0},{1,5},{5,13},{13,9},{9,1},{2,6},{6,14},{... | collective-permute-start | bytes 2064392 | tf_op jit(solution)/shard_map/ppermute | solution.py:375
  105.1 10.8 %shard_map.83 = (f32[512,2688]{1,0:T(8,128)S(1)}, bf16[512,256]{1,0:T(8,128)(2,1)S(1)}, f32[8,128]{1,0:T(8,128)S(1)}) custom-call(s32[4]{0:T(128)S(1)} %pad_add_fusion.where_ref, bf16[8,512,128]{2,1,0:T(8,128)(2,1)S(1)} %shard_map.82.refs_0_, bf16[8,512,128]{2,1,0:T(8,128)(2,1)S(1)} %collective-permute-done.17.refs_1_, ...), custom_call_target="tpu_custom_call" | custom-call | flops 4932501504 | bytes 9633792 | tf_op jit(solution)/shard_map/pallas_call | solution.py:222
  115.9 5.2 %collective-permute-done.18.refs_0_ = bf16[128,2688]{1,0:T(8,128)(2,1)S(1)} collective-permute-done((bf16[128,2688]{1,0:T(8,128)(2,1)S(1)}, bf16[128,2688]{1,0:T(8,128)(2,1)S(1)}, u32[]{:S(2)}, u32[]{:S(2)}) %collective-permute-start.18) | collective-permute-done | bytes 688160 | tf_op jit(solution)/shard_map/ppermute | solution.py:375
  121.6 3.5 %shard_map.84 = (f32[512,2688]{1,0:T(8,128)S(1)}, f32[520,128]{1,0:T(8,128)S(1)}) custom-call(bf16[512,256]{1,0:T(8,128)(2,1)S(1)} %get-tuple-element.62.heads_ref, bf16[128,2688]{1,0:T(8,128)(2,1)S(1)} %collective-permute-done.18.refs_0_, bf16[128,2688]{1,0:T(8,128)(2,1)S(1)} %collective-permute-done.19.refs_1_, f32[512,2688]{1,0:T(8,128)S(1)} %get-tuple-element.63.refs_2_, ...), custom_call_target="tpu_custom_call" | custom-call | flops 704643072 | bytes 1376256 | tf_op jit(solution)/shard_map/pallas_call | solution.py:277
  125.2 1.5 %collective-permute-done.20.other_ref = f32[520,128]{1,0:T(8,128)S(1)} collective-permute-done((f32[520,128]{1,0:T(8,128)S(1)}, f32[520,128]{1,0:T(8,128)S(1)}, u32[]{:S(2)}, u32[]{:S(2)}) %collective-permute-start.20) | collective-permute-done | bytes 266272 | tf_op jit(solution)/shard_map/ppermute | solution.py:337
  126.7 2.3 %shard_map.85 = bf16[512,2688]{1,0:T(8,128)(2,1)} custom-call(f32[520,128]{1,0:T(8,128)S(1)} %get-tuple-element.65.own_ref, f32[520,128]{1,0:T(8,128)S(1)} %collective-permute-done.20.other_ref, f32[1,2688]{1,0:T(1,128)S(1)} %broadcast_in_dim.13.refs_4_.gain_ref, f32[64,2688]{1,0:T(8,128)S(1)} %bitcast.8, f32[512,2688]{1,0:T(8,128)S(1)} %get-tuple-element.66.hidden_ref), custom_call_target="tpu_custom_call" | custom-call | flops 704643072 | bytes 8257536 | tf_op jit(solution)/shard_map/pallas_call | solution.py:323
  (47 shorter events, 13.2 us)
Async XLA Ops:
  1.2 2.3 %collective-permute-start = (bf16[128,2688]{1,0:T(8,128)(2,1)S(1)}, bf16[128,2688]{1,0:T(8,128)(2,1)S(1)}, u32[]{:S(2)}, u32[]{:S(2)}) collective-permute-start(bf16[128,2688]{1,0:T(8,128)(2,1)S(1)} %constant_dynamic-slice_fusion), channel_id=1, source_target_pairs={{0,1},{1,0},{2,3},{3,2},{4,5},{5,4},{6,7},{7,6},{8,9},{9,8},{10,11... | collective-permute-start | bytes 2064392 | tf_op jit(solution)/shard_map/ppermute | solution.py:337
  4.9 22.0 %collective-permute-start.4 = (bf16[128,2688]{1,0:T(8,128)(2,1)S(1)}, bf16[128,2688]{1,0:T(8,128)(2,1)}, u32[]{:S(2)}, u32[]{:S(2)}) collective-permute-start(bf16[128,2688]{1,0:T(8,128)(2,1)S(1)} %get-tuple-element.38.refs_2_), channel_id=1, source_target_pairs={{0,2},{2,0},{1,3},{3,1},{4,6},{6,4},{5,7},{7,5},{8,10},{10,8},{9,1... | collective-permute-start | bytes 2064392 | tf_op jit(solution)/shard_map/ppermute | solution.py:337
  7.8 14.7 %collective-permute-start.1 = (bf16[512,512]{1,0:T(8,128)(2,1)S(1)}, bf16[512,512]{1,0:T(8,128)(2,1)S(1)}, u32[]{:S(2)}, u32[]{:S(2)}) collective-permute-start(bf16[512,512]{1,0:T(8,128)(2,1)S(1)} %copy-done.2), channel_id=1, source_target_pairs={{0,4},{4,8},{8,12},{1,5},{5,9},{9,13},{2,6},{6,10},{10,14},{3,7},{... | collective-permute-start | bytes 1572872 | tf_op jit(solution)/shard_map/ppermute | solution.py:356
  22.5 14.8 %collective-permute-start.2 = (bf16[512,512]{1,0:T(8,128)(2,1)S(1)}, bf16[512,512]{1,0:T(8,128)(2,1)S(1)}, u32[]{:S(2)}, u32[]{:S(2)}) collective-permute-start(bf16[512,512]{1,0:T(8,128)(2,1)S(1)} %copy-done.3), channel_id=1, source_target_pairs={{0,4},{4,8},{8,12},{1,5},{5,9},{9,13},{2,6},{6,10},{10,14},{3,7},{... | collective-permute-start | bytes 1572872 | tf_op jit(solution)/shard_map/ppermute | solution.py:356
  27.8 13.0 %collective-permute-start.5 = (bf16[512,512]{1,0:T(8,128)(2,1)}, bf16[512,512]{1,0:T(8,128)(2,1)}, u32[]{:S(2)}, u32[]{:S(2)}) collective-permute-start(bf16[512,512]{1,0:T(8,128)(2,1)} %broadcast_select_fusion.3), channel_id=1, source_target_pairs={{0,2},{2,0},{1,3},{3,1},{4,6},{6,4},{5,7},{7,5},{8,10},{10,8},{9,1... | collective-permute-start | bytes 1572872 | tf_op jit(solution)/shard_map/ppermute | solution.py:337
  28.4 16.3 %collective-permute-start.7 = (bf16[128,2688]{1,0:T(8,128)(2,1)}, bf16[128,2688]{1,0:T(8,128)(2,1)S(1)}, u32[]{:S(2)}, u32[]{:S(2)}) collective-permute-start(bf16[128,2688]{1,0:T(8,128)(2,1)} %collective-permute-done.4.refs_6_), channel_id=1, source_target_pairs={{0,16},{16,0},{1,17},{17,1},{2,18},{18,2},{3,19},{19,3},{4,20},{20... | collective-permute-start | bytes 2064392 | tf_op jit(solution)/shard_map/ppermute | solution.py:337
  37.3 17.4 %collective-permute-start.3 = (bf16[128,2688]{1,0:T(8,128)(2,1)S(1)}, bf16[128,2688]{1,0:T(8,128)(2,1)S(1)}, u32[]{:S(2)}, u32[]{:S(2)}) collective-permute-start(bf16[128,2688]{1,0:T(8,128)(2,1)S(1)} %get-tuple-element.38.refs_2_), channel_id=1, source_target_pairs={{0,4},{4,12},{12,8},{8,0},{1,5},{5,13},{13,9},{9,1},{2,6},{6,14},{... | collective-permute-start | bytes 2064392 | tf_op jit(solution)/shard_map/ppermute | solution.py:375
  40.8 13.8 %collective-permute-start.6 = (bf16[512,512]{1,0:T(8,128)(2,1)S(1)}, bf16[512,512]{1,0:T(8,128)(2,1)S(1)}, u32[]{:S(2)}, u32[]{:S(2)}) collective-permute-start(bf16[512,512]{1,0:T(8,128)(2,1)S(1)} %broadcast_select_fusion.2), channel_id=1, source_target_pairs={{0,2},{2,0},{1,3},{3,1},{4,6},{6,4},{5,7},{7,5},{8,10},{10,8},{9,1... | collective-permute-start | bytes 1572872 | tf_op jit(solution)/shard_map/ppermute | solution.py:337
  54.7 15.0 %collective-permute-start.10 = (bf16[128,2688]{1,0:T(8,128)(2,1)S(1)}, bf16[128,2688]{1,0:T(8,128)(2,1)S(1)}, u32[]{:S(2)}, u32[]{:S(2)}) collective-permute-start(bf16[128,2688]{1,0:T(8,128)(2,1)S(1)} %collective-permute-done.3.refs_3_), channel_id=1, source_target_pairs={{0,16},{16,0},{1,17},{17,1},{2,18},{18,2},{3,19},{19,3},{4,20},{20... | collective-permute-start | bytes 2064392 | tf_op jit(solution)/shard_map/ppermute | solution.py:337
  56.1 15.6 %collective-permute-start.8 = (bf16[128,2688]{1,0:T(8,128)(2,1)S(1)}, bf16[128,2688]{1,0:T(8,128)(2,1)S(1)}, u32[]{:S(2)}, u32[]{:S(2)}) collective-permute-start(bf16[128,2688]{1,0:T(8,128)(2,1)S(1)} %collective-permute-done.3.refs_3_), channel_id=1, source_target_pairs={{0,4},{4,12},{12,8},{8,0},{1,5},{5,13},{13,9},{9,1},{2,6},{6,14},{... | collective-permute-start | bytes 2064392 | tf_op jit(solution)/shard_map/ppermute | solution.py:375
  57.0 14.8 %collective-permute-start.9 = (bf16[128,2688]{1,0:T(8,128)(2,1)S(1)}, bf16[128,2688]{1,0:T(8,128)(2,1)S(1)}, u32[]{:S(2)}, u32[]{:S(2)}) collective-permute-start(bf16[128,2688]{1,0:T(8,128)(2,1)S(1)} %collective-permute-done.3.refs_3_), channel_id=1, source_target_pairs={{0,2},{2,0},{1,3},{3,1},{4,6},{6,4},{5,7},{7,5},{8,10},{10,8},{9,1... | collective-permute-start | bytes 2064392 | tf_op jit(solution)/shard_map/ppermute | solution.py:337
  57.5 47.0 %copy-start.5 = (f32[2688]{0:T(1024)S(1)}, f32[2688]{0:T(1024)}, u32[]{:S(2)}) copy-start(f32[2688]{0:T(1024)} %param.13) | copy-start | bytes 32260
  57.5 47.1 %copy-start.6 = (f32[2688]{0:T(1024)S(1)}, f32[2688]{0:T(1024)}, u32[]{:S(2)}) copy-start(f32[2688]{0:T(1024)} %param.12) | copy-start | bytes 32260
  57.5 47.6 %copy-start = (f32[2688,64]{0,1:T(8,128)S(1)}, f32[2688,64]{0,1:T(8,128)}, u32[]{:S(2)}) copy-start(f32[2688,64]{0,1:T(8,128)} %param.14) | copy-start | bytes 2064388
  71.7 15.6 %collective-permute-start.11 = (bf16[128,2688]{1,0:T(8,128)(2,1)S(1)}, bf16[128,2688]{1,0:T(8,128)(2,1)S(1)}, u32[]{:S(2)}, u32[]{:S(2)}) collective-permute-start(bf16[128,2688]{1,0:T(8,128)(2,1)S(1)} %collective-permute-done.8.refs_4_), channel_id=1, source_target_pairs={{0,4},{4,12},{12,8},{8,0},{1,5},{5,13},{13,9},{9,1},{2,6},{6,14},{... | collective-permute-start | bytes 2064392 | tf_op jit(solution)/shard_map/ppermute | solution.py:375
  74.8 13.4 %collective-permute-start.12 = (bf16[128,2688]{1,0:T(8,128)(2,1)S(1)}, bf16[128,2688]{1,0:T(8,128)(2,1)S(1)}, u32[]{:S(2)}, u32[]{:S(2)}) collective-permute-start(bf16[128,2688]{1,0:T(8,128)(2,1)S(1)} %collective-permute-done.8.refs_4_), channel_id=1, source_target_pairs={{0,2},{2,0},{1,3},{3,1},{4,6},{6,4},{5,7},{7,5},{8,10},{10,8},{9,1... | collective-permute-start | bytes 2064392 | tf_op jit(solution)/shard_map/ppermute | solution.py:337
  75.3 12.9 %collective-permute-start.13 = (bf16[128,2688]{1,0:T(8,128)(2,1)S(1)}, bf16[128,2688]{1,0:T(8,128)(2,1)S(1)}, u32[]{:S(2)}, u32[]{:S(2)}) collective-permute-start(bf16[128,2688]{1,0:T(8,128)(2,1)S(1)} %collective-permute-done.9.refs_7_), channel_id=1, source_target_pairs={{0,16},{16,0},{1,17},{17,1},{2,18},{18,2},{3,19},{19,3},{4,20},{20... | collective-permute-start | bytes 2064392 | tf_op jit(solution)/shard_map/ppermute | solution.py:337
  88.2 13.0 %collective-permute-start.14 = (bf16[128,2688]{1,0:T(8,128)(2,1)S(1)}, bf16[128,2688]{1,0:T(8,128)(2,1)S(1)}, u32[]{:S(2)}, u32[]{:S(2)}) collective-permute-start(bf16[128,2688]{1,0:T(8,128)(2,1)S(1)} %collective-permute-done.10.refs_11_), channel_id=1, source_target_pairs={{0,4},{4,12},{12,8},{8,0},{1,5},{5,13},{13,9},{9,1},{2,6},{6,14},{... | collective-permute-start | bytes 2064392 | tf_op jit(solution)/shard_map/ppermute | solution.py:375
  90.4 11.8 %collective-permute-start.15 = (bf16[128,2688]{1,0:T(8,128)(2,1)S(1)}, bf16[128,2688]{1,0:T(8,128)(2,1)S(1)}, u32[]{:S(2)}, u32[]{:S(2)}) collective-permute-start(bf16[128,2688]{1,0:T(8,128)(2,1)S(1)} %collective-permute-done.11.refs_5_), channel_id=1, source_target_pairs={{0,2},{2,0},{1,3},{3,1},{4,6},{6,4},{5,7},{7,5},{8,10},{10,8},{9,1... | collective-permute-start | bytes 2064392 | tf_op jit(solution)/shard_map/ppermute | solution.py:337
  91.4 11.0 %collective-permute-start.16 = (bf16[128,2688]{1,0:T(8,128)(2,1)S(1)}, bf16[128,2688]{1,0:T(8,128)(2,1)S(1)}, u32[]{:S(2)}, u32[]{:S(2)}) collective-permute-start(bf16[128,2688]{1,0:T(8,128)(2,1)S(1)} %collective-permute-done.12.refs_8_), channel_id=1, source_target_pairs={{0,16},{16,0},{1,17},{17,1},{2,18},{18,2},{3,19},{19,3},{4,20},{20... | collective-permute-start | bytes 2064392 | tf_op jit(solution)/shard_map/ppermute | solution.py:337
  102.4 2.7 %collective-permute-start.17 = (bf16[8,512,128]{2,1,0:T(8,128)(2,1)S(1)}, bf16[8,512,128]{2,1,0:T(8,128)(2,1)S(1)}, u32[]{:S(2)}, u32[]{:S(2)}) collective-permute-start(bf16[8,512,128]{2,1,0:T(8,128)(2,1)S(1)} %shard_map.82.refs_0_), channel_id=1, source_target_pairs={{0,1},{1,0},{2,3},{3,2},{4,5},{5,4},{6,7},{7,6},{8,9},{9,8},{10,11... | collective-permute-start | bytes 3145736 | tf_op jit(solution)/shard_map/ppermute | solution.py:337
  102.4 18.7 %collective-permute-start.18 = (bf16[128,2688]{1,0:T(8,128)(2,1)S(1)}, bf16[128,2688]{1,0:T(8,128)(2,1)S(1)}, u32[]{:S(2)}, u32[]{:S(2)}) collective-permute-start(bf16[128,2688]{1,0:T(8,128)(2,1)S(1)} %collective-permute-done.14.refs_12_), channel_id=1, source_target_pairs={{0,4},{4,12},{12,8},{8,0},{1,5},{5,13},{13,9},{9,1},{2,6},{6,14},{... | collective-permute-start | bytes 2064392 | tf_op jit(solution)/shard_map/ppermute | solution.py:375
  104.0 17.6 %collective-permute-start.19 = (bf16[128,2688]{1,0:T(8,128)(2,1)S(1)}, bf16[128,2688]{1,0:T(8,128)(2,1)S(1)}, u32[]{:S(2)}, u32[]{:S(2)}) collective-permute-start(bf16[128,2688]{1,0:T(8,128)(2,1)S(1)} %collective-permute-done.15.refs_9_), channel_id=1, source_target_pairs={{0,16},{16,0},{1,17},{17,1},{2,18},{18,2},{3,19},{19,3},{4,20},{20... | collective-permute-start | bytes 2064392 | tf_op jit(solution)/shard_map/ppermute | solution.py:337
  125.1 1.6 %collective-permute-start.20 = (f32[520,128]{1,0:T(8,128)S(1)}, f32[520,128]{1,0:T(8,128)S(1)}, u32[]{:S(2)}, u32[]{:S(2)}) collective-permute-start(f32[520,128]{1,0:T(8,128)S(1)} %get-tuple-element.65.own_ref), channel_id=1, source_target_pairs={{0,1},{1,0},{2,3},{3,2},{4,5},{5,4},{6,7},{7,6},{8,9},{9,8},{10,11... | collective-permute-start | bytes 798728 | tf_op jit(solution)/shard_map/ppermute | solution.py:337
  (4 other events, 52.1 us)

commit v12 on v11

--- a/solution.py
+++ b/solution.py
@@ -380,7 +380,7 @@
         across[0] = jnp.where(is_mine, theirs, mine)
         beside[0] = beyond(main[0])
         second_keys = from_behind(after(keys, main[0]))
-        second_values = from_behind(after(values, second_keys))
+        second_values = from_behind(after(values, main[0]))
         first_keys = for_next(keys, after(second_keys, beside[0]))
         corner[0] = facing(beside[0])
         main[1] = ring(after(main[0], second_values))

time: 129 us -> 129 us (level)
  waiting for transfers between devices: 64.2 us -> 62.9 us
    ppermute x14, starting transfers between devices: 11.3 us -> 13.9 us  [swapped(): return lax.ppermute(block, axis, [(0, 1), (1, 0)])]
    ppermute x2, waiting for transfers between devices: 18.6 us -> 16.1 us  [on_device(): from_behind = lambda block: lax.ppermute(block, 'far', ahead)]
  transfers between devices with their start and end apart: 21 -> 21, of which waited for: 16 -> 17; matrix products, arithmetic and copies ran while one was open for 3% -> 3% of each run, Pallas kernels for 17% -> 18%
where the time goes in v12:
time: 129 us; the launch traced here: 128 us
  waiting for transfers between devices  62.9 us (49%)
  starting transfers between devices  29.9 us (23%)
  Pallas kernels  28.3 us (22%)
  other arithmetic  5.64 us (4%)
    ppermute x5, waiting for transfers between devices, on_device(): ring = lambda block: lax.ppermute(block, 'far', hops)  38.3 us
    ppermute x2, waiting for transfers between devices, on_device(): from_behind = lambda block: lax.ppermute(block, 'far', ahead)  16.1 us
    ppermute x14, starting transfers between devices, swapped(): return lax.ppermute(block, axis, [(0, 1), (1, 0)])  13.9 us
    pallas_call x1, Pallas kernels, attend(): pl.pallas_call(functools.partial(attend_kernel, tok, group, direct), grid...  11.8 us
    pallas_call x1, Pallas kernels, project(): pl.pallas_call(functools.partial(project_kernel, kinds, late_kinds, len(s...  10.8 us
    ppermute x5, starting transfers between devices, on_device(): ring = lambda block: lax.ppermute(block, 'far', hops)  9.02 us
    ppermute x14, waiting for transfers between devices, swapped(): return lax.ppermute(block, axis, [(0, 1), (1, 0)])  8.47 us
    ppermute x2, starting transfers between devices, on_device(): from_behind = lambda block: lax.ppermute(block, 'far', ahead)  6.99 us
  transfers between devices with their start and end apart: 21, of which 17 were waited for; matrix products, arithmetic and copies ran while one was open for 3% of the time, Pallas kernels for 18%

profile of v12, /device:TPU:0, one launch (start us, length us, event | category | flops | bytes accessed | tf_op | source)
XLA Modules:
  0.0 128.4 jit_solution(17688423836295626599)
XLA Ops:
  1.8 1.8 %collective-permute-done = bf16[128,2688]{1,0:T(8,128)(2,1)S(1)} collective-permute-done((bf16[128,2688]{1,0:T(8,128)(2,1)S(1)}, bf16[128,2688]{1,0:T(8,128)(2,1)S(1)}, u32[]{:S(2)}, u32[]{:S(2)}) %collective-permute-start) | collective-permute-done | bytes 688160 | tf_op jit(solution)/shard_map/ppermute | solution.py:337
  4.9 3.0 %collective-permute-start.4 = (bf16[128,2688]{1,0:T(8,128)(2,1)S(1)}, bf16[128,2688]{1,0:T(8,128)(2,1)}, u32[]{:S(2)}, u32[]{:S(2)}) collective-permute-start(bf16[128,2688]{1,0:T(8,128)(2,1)S(1)} %get-tuple-element.37.refs_2_), channel_id=1, source_target_pairs={{0,2},{2,0},{1,3},{3,1},{4,6},{6,4},{5,7},{7,5},{8,10},{10,8},{9,1... | collective-permute-start | bytes 2064392 | tf_op jit(solution)/shard_map/ppermute | solution.py:337
  7.8 3.5 %collective-permute-start.3 = (bf16[512,512]{1,0:T(8,128)(2,1)S(1)}, bf16[512,512]{1,0:T(8,128)(2,1)S(1)}, u32[]{:S(2)}, u32[]{:S(2)}) collective-permute-start(bf16[512,512]{1,0:T(8,128)(2,1)S(1)} %copy-done.2), channel_id=1, source_target_pairs={{0,4},{4,8},{8,12},{1,5},{5,9},{9,13},{2,6},{6,10},{10,14},{3,7},{... | collective-permute-start | bytes 1572872 | tf_op jit(solution)/shard_map/ppermute | solution.py:356
  11.3 3.5 %collective-permute-start.1 = (bf16[512,512]{1,0:T(8,128)(2,1)S(1)}, bf16[512,512]{1,0:T(8,128)(2,1)S(1)}, u32[]{:S(2)}, u32[]{:S(2)}) collective-permute-start(bf16[512,512]{1,0:T(8,128)(2,1)S(1)} %copy-done.3), channel_id=1, source_target_pairs={{0,4},{4,8},{8,12},{1,5},{5,9},{9,13},{2,6},{6,10},{10,14},{3,7},{... | collective-permute-start | bytes 1572872 | tf_op jit(solution)/shard_map/ppermute | solution.py:356
  14.8 8.8 %collective-permute-done.3.k0 = bf16[512,512]{1,0:T(8,128)(2,1)S(1)} collective-permute-done((bf16[512,512]{1,0:T(8,128)(2,1)S(1)}, bf16[512,512]{1,0:T(8,128)(2,1)S(1)}, u32[]{:S(2)}, u32[]{:S(2)}) %collective-permute-start.3) | collective-permute-done | bytes 524320 | tf_op jit(solution)/shard_map/ppermute | solution.py:356
  24.5 1.7 %collective-permute-start.5 = (bf16[512,512]{1,0:T(8,128)(2,1)}, bf16[512,512]{1,0:T(8,128)(2,1)}, u32[]{:S(2)}, u32[]{:S(2)}) collective-permute-start(bf16[512,512]{1,0:T(8,128)(2,1)} %broadcast_select_fusion.3), channel_id=1, source_target_pairs={{0,2},{2,0},{1,3},{3,1},{4,6},{6,4},{5,7},{7,5},{8,10},{10,8},{9,1... | collective-permute-start | bytes 1572872 | tf_op jit(solution)/shard_map/ppermute | solution.py:337
  26.4 7.4 %collective-permute-done.1.v0 = bf16[512,512]{1,0:T(8,128)(2,1)S(1)} collective-permute-done((bf16[512,512]{1,0:T(8,128)(2,1)S(1)}, bf16[512,512]{1,0:T(8,128)(2,1)S(1)}, u32[]{:S(2)}, u32[]{:S(2)}) %collective-permute-start.1) | collective-permute-done | bytes 524320 | tf_op jit(solution)/shard_map/ppermute | solution.py:356
  33.7 2.5 %collective-permute-start.2 = (bf16[128,2688]{1,0:T(8,128)(2,1)S(1)}, bf16[128,2688]{1,0:T(8,128)(2,1)}, u32[]{:S(2)}, u32[]{:S(2)}) collective-permute-start(bf16[128,2688]{1,0:T(8,128)(2,1)S(1)} %get-tuple-element.37.refs_2_), channel_id=1, source_target_pairs={{0,4},{4,12},{12,8},{8,0},{1,5},{5,13},{13,9},{9,1},{2,6},{6,14},{... | collective-permute-start | bytes 2064392 | tf_op jit(solution)/shard_map/ppermute | solution.py:375
  36.2 1.5 %collective-permute-start.7 = (bf16[128,2688]{1,0:T(8,128)(2,1)}, bf16[128,2688]{1,0:T(8,128)(2,1)S(1)}, u32[]{:S(2)}, u32[]{:S(2)}) collective-permute-start(bf16[128,2688]{1,0:T(8,128)(2,1)} %collective-permute-done.4.refs_6_), channel_id=1, source_target_pairs={{0,16},{16,0},{1,17},{17,1},{2,18},{18,2},{3,19},{19,3},{4,20},{20... | collective-permute-start | bytes 2064392 | tf_op jit(solution)/shard_map/ppermute | solution.py:337
  38.4 1.5 %collective-permute-start.6 = (bf16[512,512]{1,0:T(8,128)(2,1)S(1)}, bf16[512,512]{1,0:T(8,128)(2,1)S(1)}, u32[]{:S(2)}, u32[]{:S(2)}) collective-permute-start(bf16[512,512]{1,0:T(8,128)(2,1)S(1)} %broadcast_select_fusion.2), channel_id=1, source_target_pairs={{0,2},{2,0},{1,3},{3,1},{4,6},{6,4},{5,7},{7,5},{8,10},{10,8},{9,1... | collective-permute-start | bytes 1572872 | tf_op jit(solution)/shard_map/ppermute | solution.py:337
  39.9 2.8 %fusion = (f32[1536,64]{1,0:T(8,128)S(1)}, f32[1536,64]{1,0:T(8,128)S(1)}, f32[1536,64]{1,0:T(8,128)S(1)}) fusion(f32[64]{0:T(128)S(1)} %multiply_exponential_fusion, f32[1536]{0:T(1024)S(1)} %add_convert_fusion), kind=kLoop, calls=%fused_computation.8 | loop fusion | flops 196608 | bytes 1186048 | tf_op jit(solution)/shard_map/neg | solution.py:34
  43.2 8.8 %collective-permute-done.2.refs_3_ = bf16[128,2688]{1,0:T(8,128)(2,1)} collective-permute-done((bf16[128,2688]{1,0:T(8,128)(2,1)S(1)}, bf16[128,2688]{1,0:T(8,128)(2,1)}, u32[]{:S(2)}, u32[]{:S(2)}) %collective-permute-start.2) | collective-permute-done | bytes 688160 | tf_op jit(solution)/shard_map/ppermute | solution.py:375
  52.6 1.5 %collective-permute-start.10 = (bf16[128,2688]{1,0:T(8,128)(2,1)}, bf16[128,2688]{1,0:T(8,128)(2,1)S(1)}, u32[]{:S(2)}, u32[]{:S(2)}) collective-permute-start(bf16[128,2688]{1,0:T(8,128)(2,1)} %collective-permute-done.2.refs_3_), channel_id=1, source_target_pairs={{0,16},{16,0},{1,17},{17,1},{2,18},{18,2},{3,19},{19,3},{4,20},{20... | collective-permute-start | bytes 2064392 | tf_op jit(solution)/shard_map/ppermute | solution.py:337
  54.1 2.6 %collective-permute-start.8 = (bf16[128,2688]{1,0:T(8,128)(2,1)}, bf16[128,2688]{1,0:T(8,128)(2,1)S(1)}, u32[]{:S(2)}, u32[]{:S(2)}) collective-permute-start(bf16[128,2688]{1,0:T(8,128)(2,1)} %collective-permute-done.2.refs_3_), channel_id=1, source_target_pairs={{0,4},{4,12},{12,8},{8,0},{1,5},{5,13},{13,9},{9,1},{2,6},{6,14},{... | collective-permute-start | bytes 2064392 | tf_op jit(solution)/shard_map/ppermute | solution.py:375
  57.2 11.8 %shard_map.82.refs_0_ = bf16[8,512,128]{2,1,0:T(8,128)(2,1)S(1)} custom-call(s32[1]{0:T(128)} %bitcast.3.row_ref, bf16[512,1024]{1,0:T(8,128)(2,1)S(1)} %copy-done.4, bf16[512,512]{1,0:T(8,128)(2,1)S(1)} %collective-permute-done.3.k0, bf16[512,512]{1,0:T(8,128)(2,1)} %collective-permute-done.5.k1, bf16[512,512]{1,0:T(8,128)(2,1)S(1)} %copy-done.2, ...), custom_call_target="tpu_custom_call" | custom-call | flops 10737418240 | bytes 6291456 | tf_op jit(solution)/shard_map/pallas_call | solution.py:105
  73.9 12.7 %collective-permute-done.11.refs_5_ = bf16[128,2688]{1,0:T(8,128)(2,1)S(1)} collective-permute-done((bf16[128,2688]{1,0:T(8,128)(2,1)S(1)}, bf16[128,2688]{1,0:T(8,128)(2,1)S(1)}, u32[]{:S(2)}, u32[]{:S(2)}) %collective-permute-start.11) | collective-permute-done | bytes 688160 | tf_op jit(solution)/shard_map/ppermute | solution.py:375
  87.0 1.6 %collective-permute-start.14 = (bf16[128,2688]{1,0:T(8,128)(2,1)S(1)}, bf16[128,2688]{1,0:T(8,128)(2,1)S(1)}, u32[]{:S(2)}, u32[]{:S(2)}) collective-permute-start(bf16[128,2688]{1,0:T(8,128)(2,1)S(1)} %collective-permute-done.10.refs_11_), channel_id=1, source_target_pairs={{0,4},{4,12},{12,8},{8,0},{1,5},{5,13},{13,9},{9,1},{2,6},{6,14},{... | collective-permute-start | bytes 2064392 | tf_op jit(solution)/shard_map/ppermute | solution.py:375
  88.6 1.6 %collective-permute-start.15 = (bf16[128,2688]{1,0:T(8,128)(2,1)S(1)}, bf16[128,2688]{1,0:T(8,128)(2,1)S(1)}, u32[]{:S(2)}, u32[]{:S(2)}) collective-permute-start(bf16[128,2688]{1,0:T(8,128)(2,1)S(1)} %collective-permute-done.11.refs_5_), channel_id=1, source_target_pairs={{0,2},{2,0},{1,3},{3,1},{4,6},{6,4},{5,7},{7,5},{8,10},{10,8},{9,1... | collective-permute-start | bytes 2064392 | tf_op jit(solution)/shard_map/ppermute | solution.py:337
  90.8 10.2 %collective-permute-done.14.refs_12_ = bf16[128,2688]{1,0:T(8,128)(2,1)S(1)} collective-permute-done((bf16[128,2688]{1,0:T(8,128)(2,1)S(1)}, bf16[128,2688]{1,0:T(8,128)(2,1)S(1)}, u32[]{:S(2)}, u32[]{:S(2)}) %collective-permute-start.14) | collective-permute-done | bytes 688160 | tf_op jit(solution)/shard_map/ppermute | solution.py:375
  104.8 10.8 %shard_map.83 = (f32[512,2688]{1,0:T(8,128)S(1)}, bf16[512,256]{1,0:T(8,128)(2,1)S(1)}, f32[8,128]{1,0:T(8,128)S(1)}) custom-call(s32[4]{0:T(128)S(1)} %pad_add_fusion.where_ref, bf16[8,512,128]{2,1,0:T(8,128)(2,1)S(1)} %shard_map.82.refs_0_, bf16[8,512,128]{2,1,0:T(8,128)(2,1)S(1)} %collective-permute-done.17.refs_1_, ...), custom_call_target="tpu_custom_call" | custom-call | flops 4932501504 | bytes 9633792 | tf_op jit(solution)/shard_map/pallas_call | solution.py:222
  115.5 5.3 %collective-permute-done.18.refs_0_ = bf16[128,2688]{1,0:T(8,128)(2,1)S(1)} collective-permute-done((bf16[128,2688]{1,0:T(8,128)(2,1)S(1)}, bf16[128,2688]{1,0:T(8,128)(2,1)S(1)}, u32[]{:S(2)}, u32[]{:S(2)}) %collective-permute-start.18) | collective-permute-done | bytes 688160 | tf_op jit(solution)/shard_map/ppermute | solution.py:375
  120.9 3.5 %shard_map.84 = (f32[512,2688]{1,0:T(8,128)S(1)}, f32[520,128]{1,0:T(8,128)S(1)}) custom-call(bf16[512,256]{1,0:T(8,128)(2,1)S(1)} %get-tuple-element.62.heads_ref, bf16[128,2688]{1,0:T(8,128)(2,1)S(1)} %collective-permute-done.18.refs_0_, bf16[128,2688]{1,0:T(8,128)(2,1)S(1)} %collective-permute-done.19.refs_1_, f32[512,2688]{1,0:T(8,128)S(1)} %get-tuple-element.63.refs_2_, ...), custom_call_target="tpu_custom_call" | custom-call | flops 704643072 | bytes 1376256 | tf_op jit(solution)/shard_map/pallas_call | solution.py:277
  124.5 1.5 %collective-permute-done.20.other_ref = f32[520,128]{1,0:T(8,128)S(1)} collective-permute-done((f32[520,128]{1,0:T(8,128)S(1)}, f32[520,128]{1,0:T(8,128)S(1)}, u32[]{:S(2)}, u32[]{:S(2)}) %collective-permute-start.20) | collective-permute-done | bytes 266272 | tf_op jit(solution)/shard_map/ppermute | solution.py:337
  126.0 2.3 %shard_map.85 = bf16[512,2688]{1,0:T(8,128)(2,1)} custom-call(f32[520,128]{1,0:T(8,128)S(1)} %get-tuple-element.65.own_ref, f32[520,128]{1,0:T(8,128)S(1)} %collective-permute-done.20.other_ref, f32[1,2688]{1,0:T(1,128)S(1)} %broadcast_in_dim.13.refs_4_.gain_ref, f32[64,2688]{1,0:T(8,128)S(1)} %bitcast.8, f32[512,2688]{1,0:T(8,128)S(1)} %get-tuple-element.66.hidden_ref), custom_call_target="tpu_custom_call" | custom-call | flops 704643072 | bytes 8257536 | tf_op jit(solution)/shard_map/pallas_call | solution.py:323
  (47 shorter events, 16.1 us)
Async XLA Ops:
  1.2 2.3 %collective-permute-start = (bf16[128,2688]{1,0:T(8,128)(2,1)S(1)}, bf16[128,2688]{1,0:T(8,128)(2,1)S(1)}, u32[]{:S(2)}, u32[]{:S(2)}) collective-permute-start(bf16[128,2688]{1,0:T(8,128)(2,1)S(1)} %constant_dynamic-slice_fusion), channel_id=1, source_target_pairs={{0,1},{1,0},{2,3},{3,2},{4,5},{5,4},{6,7},{7,6},{8,9},{9,8},{10,11... | collective-permute-start | bytes 2064392 | tf_op jit(solution)/shard_map/ppermute | solution.py:337
  4.9 18.8 %collective-permute-start.4 = (bf16[128,2688]{1,0:T(8,128)(2,1)S(1)}, bf16[128,2688]{1,0:T(8,128)(2,1)}, u32[]{:S(2)}, u32[]{:S(2)}) collective-permute-start(bf16[128,2688]{1,0:T(8,128)(2,1)S(1)} %get-tuple-element.37.refs_2_), channel_id=1, source_target_pairs={{0,2},{2,0},{1,3},{3,1},{4,6},{6,4},{5,7},{7,5},{8,10},{10,8},{9,1... | collective-permute-start | bytes 2064392 | tf_op jit(solution)/shard_map/ppermute | solution.py:337
  7.8 15.8 %collective-permute-start.3 = (bf16[512,512]{1,0:T(8,128)(2,1)S(1)}, bf16[512,512]{1,0:T(8,128)(2,1)S(1)}, u32[]{:S(2)}, u32[]{:S(2)}) collective-permute-start(bf16[512,512]{1,0:T(8,128)(2,1)S(1)} %copy-done.2), channel_id=1, source_target_pairs={{0,4},{4,8},{8,12},{1,5},{5,9},{9,13},{2,6},{6,10},{10,14},{3,7},{... | collective-permute-start | bytes 1572872 | tf_op jit(solution)/shard_map/ppermute | solution.py:356
  11.3 22.4 %collective-permute-start.1 = (bf16[512,512]{1,0:T(8,128)(2,1)S(1)}, bf16[512,512]{1,0:T(8,128)(2,1)S(1)}, u32[]{:S(2)}, u32[]{:S(2)}) collective-permute-start(bf16[512,512]{1,0:T(8,128)(2,1)S(1)} %copy-done.3), channel_id=1, source_target_pairs={{0,4},{4,8},{8,12},{1,5},{5,9},{9,13},{2,6},{6,10},{10,14},{3,7},{... | collective-permute-start | bytes 1572872 | tf_op jit(solution)/shard_map/ppermute | solution.py:356
  24.5 13.8 %collective-permute-start.5 = (bf16[512,512]{1,0:T(8,128)(2,1)}, bf16[512,512]{1,0:T(8,128)(2,1)}, u32[]{:S(2)}, u32[]{:S(2)}) collective-permute-start(bf16[512,512]{1,0:T(8,128)(2,1)} %broadcast_select_fusion.3), channel_id=1, source_target_pairs={{0,2},{2,0},{1,3},{3,1},{4,6},{6,4},{5,7},{7,5},{8,10},{10,8},{9,1... | collective-permute-start | bytes 1572872 | tf_op jit(solution)/shard_map/ppermute | solution.py:337
  33.7 18.3 %collective-permute-start.2 = (bf16[128,2688]{1,0:T(8,128)(2,1)S(1)}, bf16[128,2688]{1,0:T(8,128)(2,1)}, u32[]{:S(2)}, u32[]{:S(2)}) collective-permute-start(bf16[128,2688]{1,0:T(8,128)(2,1)S(1)} %get-tuple-element.37.refs_2_), channel_id=1, source_target_pairs={{0,4},{4,12},{12,8},{8,0},{1,5},{5,13},{13,9},{9,1},{2,6},{6,14},{... | collective-permute-start | bytes 2064392 | tf_op jit(solution)/shard_map/ppermute | solution.py:375
  36.2 16.4 %collective-permute-start.7 = (bf16[128,2688]{1,0:T(8,128)(2,1)}, bf16[128,2688]{1,0:T(8,128)(2,1)S(1)}, u32[]{:S(2)}, u32[]{:S(2)}) collective-permute-start(bf16[128,2688]{1,0:T(8,128)(2,1)} %collective-permute-done.4.refs_6_), channel_id=1, source_target_pairs={{0,16},{16,0},{1,17},{17,1},{2,18},{18,2},{3,19},{19,3},{4,20},{20... | collective-permute-start | bytes 2064392 | tf_op jit(solution)/shard_map/ppermute | solution.py:337
  38.4 14.2 %collective-permute-start.6 = (bf16[512,512]{1,0:T(8,128)(2,1)S(1)}, bf16[512,512]{1,0:T(8,128)(2,1)S(1)}, u32[]{:S(2)}, u32[]{:S(2)}) collective-permute-start(bf16[512,512]{1,0:T(8,128)(2,1)S(1)} %broadcast_select_fusion.2), channel_id=1, source_target_pairs={{0,2},{2,0},{1,3},{3,1},{4,6},{6,4},{5,7},{7,5},{8,10},{10,8},{9,1... | collective-permute-start | bytes 1572872 | tf_op jit(solution)/shard_map/ppermute | solution.py:337
  52.6 16.4 %collective-permute-start.10 = (bf16[128,2688]{1,0:T(8,128)(2,1)}, bf16[128,2688]{1,0:T(8,128)(2,1)S(1)}, u32[]{:S(2)}, u32[]{:S(2)}) collective-permute-start(bf16[128,2688]{1,0:T(8,128)(2,1)} %collective-permute-done.2.refs_3_), channel_id=1, source_target_pairs={{0,16},{16,0},{1,17},{17,1},{2,18},{18,2},{3,19},{19,3},{4,20},{20... | collective-permute-start | bytes 2064392 | tf_op jit(solution)/shard_map/ppermute | solution.py:337
  54.1 16.2 %collective-permute-start.8 = (bf16[128,2688]{1,0:T(8,128)(2,1)}, bf16[128,2688]{1,0:T(8,128)(2,1)S(1)}, u32[]{:S(2)}, u32[]{:S(2)}) collective-permute-start(bf16[128,2688]{1,0:T(8,128)(2,1)} %collective-permute-done.2.refs_3_), channel_id=1, source_target_pairs={{0,4},{4,12},{12,8},{8,0},{1,5},{5,13},{13,9},{9,1},{2,6},{6,14},{... | collective-permute-start | bytes 2064392 | tf_op jit(solution)/shard_map/ppermute | solution.py:375
  56.6 14.9 %collective-permute-start.9 = (bf16[128,2688]{1,0:T(8,128)(2,1)}, bf16[128,2688]{1,0:T(8,128)(2,1)S(1)}, u32[]{:S(2)}, u32[]{:S(2)}) collective-permute-start(bf16[128,2688]{1,0:T(8,128)(2,1)} %collective-permute-done.2.refs_3_), channel_id=1, source_target_pairs={{0,2},{2,0},{1,3},{3,1},{4,6},{6,4},{5,7},{7,5},{8,10},{10,8},{9,1... | collective-permute-start | bytes 2064392 | tf_op jit(solution)/shard_map/ppermute | solution.py:337
  57.2 46.5 %copy-start.5 = (f32[2688]{0:T(1024)S(1)}, f32[2688]{0:T(1024)}, u32[]{:S(2)}) copy-start(f32[2688]{0:T(1024)} %param.13) | copy-start | bytes 32260
  57.2 46.5 %copy-start.6 = (f32[2688]{0:T(1024)S(1)}, f32[2688]{0:T(1024)}, u32[]{:S(2)}) copy-start(f32[2688]{0:T(1024)} %param.12) | copy-start | bytes 32260
  57.2 47.6 %copy-start = (f32[2688,64]{0,1:T(8,128)S(1)}, f32[2688,64]{0,1:T(8,128)}, u32[]{:S(2)}) copy-start(f32[2688,64]{0,1:T(8,128)} %param.14) | copy-start | bytes 2064388
  71.5 15.1 %collective-permute-start.11 = (bf16[128,2688]{1,0:T(8,128)(2,1)S(1)}, bf16[128,2688]{1,0:T(8,128)(2,1)S(1)}, u32[]{:S(2)}, u32[]{:S(2)}) collective-permute-start(bf16[128,2688]{1,0:T(8,128)(2,1)S(1)} %collective-permute-done.8.refs_4_), channel_id=1, source_target_pairs={{0,4},{4,12},{12,8},{8,0},{1,5},{5,13},{13,9},{9,1},{2,6},{6,14},{... | collective-permute-start | bytes 2064392 | tf_op jit(solution)/shard_map/ppermute | solution.py:375
  72.9 14.1 %collective-permute-start.12 = (bf16[128,2688]{1,0:T(8,128)(2,1)S(1)}, bf16[128,2688]{1,0:T(8,128)(2,1)S(1)}, u32[]{:S(2)}, u32[]{:S(2)}) collective-permute-start(bf16[128,2688]{1,0:T(8,128)(2,1)S(1)} %collective-permute-done.8.refs_4_), channel_id=1, source_target_pairs={{0,2},{2,0},{1,3},{3,1},{4,6},{6,4},{5,7},{7,5},{8,10},{10,8},{9,1... | collective-permute-start | bytes 2064392 | tf_op jit(solution)/shard_map/ppermute | solution.py:337
  73.4 13.6 %collective-permute-start.13 = (bf16[128,2688]{1,0:T(8,128)(2,1)S(1)}, bf16[128,2688]{1,0:T(8,128)(2,1)S(1)}, u32[]{:S(2)}, u32[]{:S(2)}) collective-permute-start(bf16[128,2688]{1,0:T(8,128)(2,1)S(1)} %collective-permute-done.9.refs_7_), channel_id=1, source_target_pairs={{0,16},{16,0},{1,17},{17,1},{2,18},{18,2},{3,19},{19,3},{4,20},{20... | collective-permute-start | bytes 2064392 | tf_op jit(solution)/shard_map/ppermute | solution.py:337
  87.0 13.9 %collective-permute-start.14 = (bf16[128,2688]{1,0:T(8,128)(2,1)S(1)}, bf16[128,2688]{1,0:T(8,128)(2,1)S(1)}, u32[]{:S(2)}, u32[]{:S(2)}) collective-permute-start(bf16[128,2688]{1,0:T(8,128)(2,1)S(1)} %collective-permute-done.10.refs_11_), channel_id=1, source_target_pairs={{0,4},{4,12},{12,8},{8,0},{1,5},{5,13},{13,9},{9,1},{2,6},{6,14},{... | collective-permute-start | bytes 2064392 | tf_op jit(solution)/shard_map/ppermute | solution.py:375
  88.6 12.7 %collective-permute-start.15 = (bf16[128,2688]{1,0:T(8,128)(2,1)S(1)}, bf16[128,2688]{1,0:T(8,128)(2,1)S(1)}, u32[]{:S(2)}, u32[]{:S(2)}) collective-permute-start(bf16[128,2688]{1,0:T(8,128)(2,1)S(1)} %collective-permute-done.11.refs_5_), channel_id=1, source_target_pairs={{0,2},{2,0},{1,3},{3,1},{4,6},{6,4},{5,7},{7,5},{8,10},{10,8},{9,1... | collective-permute-start | bytes 2064392 | tf_op jit(solution)/shard_map/ppermute | solution.py:337
  90.2 11.9 %collective-permute-start.16 = (bf16[128,2688]{1,0:T(8,128)(2,1)S(1)}, bf16[128,2688]{1,0:T(8,128)(2,1)S(1)}, u32[]{:S(2)}, u32[]{:S(2)}) collective-permute-start(bf16[128,2688]{1,0:T(8,128)(2,1)S(1)} %collective-permute-done.12.refs_8_), channel_id=1, source_target_pairs={{0,16},{16,0},{1,17},{17,1},{2,18},{18,2},{3,19},{19,3},{4,20},{20... | collective-permute-start | bytes 2064392 | tf_op jit(solution)/shard_map/ppermute | solution.py:337
  102.1 2.7 %collective-permute-start.17 = (bf16[8,512,128]{2,1,0:T(8,128)(2,1)S(1)}, bf16[8,512,128]{2,1,0:T(8,128)(2,1)S(1)}, u32[]{:S(2)}, u32[]{:S(2)}) collective-permute-start(bf16[8,512,128]{2,1,0:T(8,128)(2,1)S(1)} %shard_map.82.refs_0_), channel_id=1, source_target_pairs={{0,1},{1,0},{2,3},{3,2},{4,5},{5,4},{6,7},{7,6},{8,9},{9,8},{10,11... | collective-permute-start | bytes 3145736 | tf_op jit(solution)/shard_map/ppermute | solution.py:337
  102.1 18.7 %collective-permute-start.18 = (bf16[128,2688]{1,0:T(8,128)(2,1)S(1)}, bf16[128,2688]{1,0:T(8,128)(2,1)S(1)}, u32[]{:S(2)}, u32[]{:S(2)}) collective-permute-start(bf16[128,2688]{1,0:T(8,128)(2,1)S(1)} %collective-permute-done.14.refs_12_), channel_id=1, source_target_pairs={{0,4},{4,12},{12,8},{8,0},{1,5},{5,13},{13,9},{9,1},{2,6},{6,14},{... | collective-permute-start | bytes 2064392 | tf_op jit(solution)/shard_map/ppermute | solution.py:375
  103.1 17.8 %collective-permute-start.19 = (bf16[128,2688]{1,0:T(8,128)(2,1)S(1)}, bf16[128,2688]{1,0:T(8,128)(2,1)S(1)}, u32[]{:S(2)}, u32[]{:S(2)}) collective-permute-start(bf16[128,2688]{1,0:T(8,128)(2,1)S(1)} %collective-permute-done.15.refs_9_), channel_id=1, source_target_pairs={{0,16},{16,0},{1,17},{17,1},{2,18},{18,2},{3,19},{19,3},{4,20},{20... | collective-permute-start | bytes 2064392 | tf_op jit(solution)/shard_map/ppermute | solution.py:337
  124.4 1.6 %collective-permute-start.20 = (f32[520,128]{1,0:T(8,128)S(1)}, f32[520,128]{1,0:T(8,128)S(1)}, u32[]{:S(2)}, u32[]{:S(2)}) collective-permute-start(f32[520,128]{1,0:T(8,128)S(1)} %get-tuple-element.65.own_ref), channel_id=1, source_target_pairs={{0,1},{1,0},{2,3},{3,2},{4,5},{5,4},{6,7},{7,6},{8,9},{9,8},{10,11... | collective-permute-start | bytes 798728 | tf_op jit(solution)/shard_map/ppermute | solution.py:337
  (4 other events, 43.1 us)

commit v13 on v12

--- a/solution.py
+++ b/solution.py
@@ -144,14 +144,16 @@
 def gather_heads(kinds, where_ref, sources, heads, sems):
     slots = sources[0].shape[0]
     depth = sources[0].shape[2]
+    ends = [sum(source.shape[0] for source in sources[: i + 1]) for i in range(len(sources))]
     places = [heads.at[:, n * depth : (n + 1) * depth] for n in range(len(kinds))]
     for n, (kind, k) in enumerate(kinds):
-        slot = slot_of(kind, k, where_ref, slots * len(sources) // 2)
-        for i, source in enumerate(sources):
-
-            @pl.when((slot >= i * slots) & (slot < (i + 1) * slots))
+        slot = slot_of(kind, k, where_ref, slots)
+        for source, end in zip(sources, ends):
+            begin = end - source.shape[0]
+
+            @pl.when((slot >= begin) & (slot < end))
             def _():
-                pltpu.make_async_copy(source.at[slot - i * slots], places[n], sems.at[n]).start()
+                pltpu.make_async_copy(source.at[slot - begin], places[n], sems.at[n]).start()
 
     for n, place in enumerate(places):
         pltpu.make_async_copy(sources[0].at[0], place, sems.at[n]).wait()
@@ -241,7 +243,7 @@
         ],
         compiler_params=pltpu.CompilerParams(vmem_limit_bytes=VMEM_LIMIT),
         cost_estimate=pl.CostEstimate(
-            flops=2 * tok * count * depth * width, bytes_accessed=2 * count * depth * width, transcendentals=0
+            flops=tok * depth * width, bytes_accessed=depth * width, transcendentals=0
         ),
     )(where, *sources, *weights, erase_in, mean)
 
@@ -399,7 +401,8 @@
         across[2], beside[3], corner[2] = ring(across[1]), beyond(main[3]), facing(beside[2])
         across[2], beside[3], corner[2], attended = hold((across[2], beside[3], corner[2], attended))
         across[3], corner[3] = ring(across[2]), facing(beside[3])
-        attended, att_other = [attended], [swapped(attended, "col")]
+        some = heads // 2
+        attended, att_other = [attended], [swapped(part, "col") for part in (attended[:some], attended[some:])]
         weights, kinds, late, late_kinds = [], [], [], []
         for name, pieces in (("main", main), ("beside", beside), ("across", across), ("corner", corner)):
             for k in range(outer):

time: 129 us -> 129 us (level)
  waiting for transfers between devices: 62.9 us -> 56.8 us
  starting transfers between devices: 29.9 us -> 34.9 us
    ppermute x5, waiting for transfers between devices: 38.3 us -> 29.4 us  [on_device(): ring = lambda block: lax.ppermute(block, 'far', hops)]
    ppermute x14 -> x15, waiting for transfers between devices: 8.47 us -> 13 us  [swapped(): return lax.ppermute(block, axis, [(0, 1), (1, 0)])]
    ppermute x14 -> x15, starting transfers between devices: 13.9 us -> 16.5 us  [swapped(): return lax.ppermute(block, axis, [(0, 1), (1, 0)])]
    ppermute x2, waiting for transfers between devices: 16.1 us -> 14.5 us  [on_device(): from_behind = lambda block: lax.ppermute(block, 'far', ahead)]
    ppermute x5, starting transfers between devices: 9.02 us -> 10.6 us  [on_device(): ring = lambda block: lax.ppermute(block, 'far', hops)]
  transfers between devices with their start and end apart: 21 -> 22, of which waited for: 17 -> 16; matrix products, arithmetic and copies ran while one was open for 3% -> 4% of each run, Pallas kernels for 18% -> 18%
where the time goes in v13:
time: 129 us
  waiting for transfers between devices  56.8 us (44%)
  starting transfers between devices  34.9 us (27%)
  Pallas kernels  28.5 us (22%)
  other arithmetic  6.65 us (5%)
  local copies, waits for them, and re-layouts  1.36 us (1%)
    ppermute x5, waiting for transfers between devices, on_device(): ring = lambda block: lax.ppermute(block, 'far', hops)  29.4 us
    ppermute x15, starting transfers between devices, swapped(): return lax.ppermute(block, axis, [(0, 1), (1, 0)])  16.5 us
    ppermute x2, waiting for transfers between devices, on_device(): from_behind = lambda block: lax.ppermute(block, 'far', ahead)  14.5 us
    ppermute x15, waiting for transfers between devices, swapped(): return lax.ppermute(block, axis, [(0, 1), (1, 0)])  13 us
    pallas_call x1, Pallas kernels, attend(): pl.pallas_call(functools.partial(attend_kernel, tok, group, direct), grid...  11.8 us
    pallas_call x1, Pallas kernels, project(): pl.pallas_call(functools.partial(project_kernel, kinds, late_kinds, len(s...  11 us
    ppermute x5, starting transfers between devices, on_device(): ring = lambda block: lax.ppermute(block, 'far', hops)  10.6 us
    ppermute x2, starting transfers between devices, on_device(): from_behind = lambda block: lax.ppermute(block, 'far', ahead)  7.77 us
  transfers between devices with their start and end apart: 22, of which 16 were waited for; matrix products, arithmetic and copies ran while one was open for 4% of the time, Pallas kernels for 18%

profile of v13, /device:TPU:0, one launch (start us, length us, event | category | flops | bytes accessed | tf_op | source)
XLA Modules:
  0.0 128.6 jit_solution(8096868965418165525)
XLA Ops:
  1.8 1.8 %collective-permute-done = bf16[128,2688]{1,0:T(8,128)(2,1)S(1)} collective-permute-done((bf16[128,2688]{1,0:T(8,128)(2,1)S(1)}, bf16[128,2688]{1,0:T(8,128)(2,1)S(1)}, u32[]{:S(2)}, u32[]{:S(2)}) %collective-permute-start) | collective-permute-done | bytes 688160 | tf_op jit(solution)/shard_map/ppermute | solution.py:339
  4.9 3.0 %collective-permute-start.4 = (bf16[128,2688]{1,0:T(8,128)(2,1)S(1)}, bf16[128,2688]{1,0:T(8,128)(2,1)S(1)}, u32[]{:S(2)}, u32[]{:S(2)}) collective-permute-start(bf16[128,2688]{1,0:T(8,128)(2,1)S(1)} %get-tuple-element.37.refs_3_), channel_id=1, source_target_pairs={{0,2},{2,0},{1,3},{3,1},{4,6},{6,4},{5,7},{7,5},{8,10},{10,8},{9,1... | collective-permute-start | bytes 2064392 | tf_op jit(solution)/shard_map/ppermute | solution.py:339
  7.8 4.3 %collective-permute-start.3 = (bf16[512,512]{1,0:T(8,128)(2,1)S(1)}, bf16[512,512]{1,0:T(8,128)(2,1)}, u32[]{:S(2)}, u32[]{:S(2)}) collective-permute-start(bf16[512,512]{1,0:T(8,128)(2,1)S(1)} %copy-done.2), channel_id=1, source_target_pairs={{0,4},{4,8},{8,12},{1,5},{5,9},{9,13},{2,6},{6,10},{10,14},{3,7},{... | collective-permute-start | bytes 1572872 | tf_op jit(solution)/shard_map/ppermute | solution.py:358
  12.1 3.5 %collective-permute-start.1 = (bf16[512,512]{1,0:T(8,128)(2,1)S(1)}, bf16[512,512]{1,0:T(8,128)(2,1)}, u32[]{:S(2)}, u32[]{:S(2)}) collective-permute-start(bf16[512,512]{1,0:T(8,128)(2,1)S(1)} %copy-done.3), channel_id=1, source_target_pairs={{0,4},{4,8},{8,12},{1,5},{5,9},{9,13},{2,6},{6,10},{10,14},{3,7},{... | collective-permute-start | bytes 1572872 | tf_op jit(solution)/shard_map/ppermute | solution.py:358
  15.6 8.0 %collective-permute-done.3.k0 = bf16[512,512]{1,0:T(8,128)(2,1)} collective-permute-done((bf16[512,512]{1,0:T(8,128)(2,1)S(1)}, bf16[512,512]{1,0:T(8,128)(2,1)}, u32[]{:S(2)}, u32[]{:S(2)}) %collective-permute-start.3) | collective-permute-done | bytes 524320 | tf_op jit(solution)/shard_map/ppermute | solution.py:358
  24.5 2.7 %collective-permute-start.5 = (bf16[512,512]{1,0:T(8,128)(2,1)}, bf16[512,512]{1,0:T(8,128)(2,1)}, u32[]{:S(2)}, u32[]{:S(2)}) collective-permute-start(bf16[512,512]{1,0:T(8,128)(2,1)} %broadcast_select_fusion.3), channel_id=1, source_target_pairs={{0,2},{2,0},{1,3},{3,1},{4,6},{6,4},{5,7},{7,5},{8,10},{10,8},{9,1... | collective-permute-start | bytes 1572872 | tf_op jit(solution)/shard_map/ppermute | solution.py:339
  27.3 6.4 %collective-permute-done.1.v0 = bf16[512,512]{1,0:T(8,128)(2,1)} collective-permute-done((bf16[512,512]{1,0:T(8,128)(2,1)S(1)}, bf16[512,512]{1,0:T(8,128)(2,1)}, u32[]{:S(2)}, u32[]{:S(2)}) %collective-permute-start.1) | collective-permute-done | bytes 524320 | tf_op jit(solution)/shard_map/ppermute | solution.py:358
  33.7 2.6 %collective-permute-start.2 = (bf16[128,2688]{1,0:T(8,128)(2,1)S(1)}, bf16[128,2688]{1,0:T(8,128)(2,1)S(1)}, u32[]{:S(2)}, u32[]{:S(2)}) collective-permute-start(bf16[128,2688]{1,0:T(8,128)(2,1)S(1)} %get-tuple-element.37.refs_3_), channel_id=1, source_target_pairs={{0,4},{4,12},{12,8},{8,0},{1,5},{5,13},{13,9},{9,1},{2,6},{6,14},{... | collective-permute-start | bytes 2064392 | tf_op jit(solution)/shard_map/ppermute | solution.py:377
  36.3 1.5 %collective-permute-start.7 = (bf16[128,2688]{1,0:T(8,128)(2,1)S(1)}, bf16[128,2688]{1,0:T(8,128)(2,1)S(1)}, u32[]{:S(2)}, u32[]{:S(2)}) collective-permute-start(bf16[128,2688]{1,0:T(8,128)(2,1)S(1)} %collective-permute-done.4.refs_7_), channel_id=1, source_target_pairs={{0,16},{16,0},{1,17},{17,1},{2,18},{18,2},{3,19},{19,3},{4,20},{20... | collective-permute-start | bytes 2064392 | tf_op jit(solution)/shard_map/ppermute | solution.py:339
  40.0 1.8 %collective-permute-start.6 = (bf16[512,512]{1,0:T(8,128)(2,1)S(1)}, bf16[512,512]{1,0:T(8,128)(2,1)S(1)}, u32[]{:S(2)}, u32[]{:S(2)}) collective-permute-start(bf16[512,512]{1,0:T(8,128)(2,1)S(1)} %broadcast_select_fusion.2), channel_id=1, source_target_pairs={{0,2},{2,0},{1,3},{3,1},{4,6},{6,4},{5,7},{7,5},{8,10},{10,8},{9,1... | collective-permute-start | bytes 1572872 | tf_op jit(solution)/shard_map/ppermute | solution.py:339
  41.8 2.8 %fusion = (f32[1536,64]{1,0:T(8,128)S(1)}, f32[1536,64]{1,0:T(8,128)S(1)}, f32[1536,64]{1,0:T(8,128)S(1)}) fusion(f32[64]{0:T(128)S(1)} %multiply_exponential_fusion, f32[1536]{0:T(1024)S(1)} %add_convert_fusion), kind=kLoop, calls=%fused_computation.8 | loop fusion | flops 196608 | bytes 1186048 | tf_op jit(solution)/shard_map/neg | solution.py:34
  45.1 6.8 %collective-permute-done.2.refs_4_ = bf16[128,2688]{1,0:T(8,128)(2,1)S(1)} collective-permute-done((bf16[128,2688]{1,0:T(8,128)(2,1)S(1)}, bf16[128,2688]{1,0:T(8,128)(2,1)S(1)}, u32[]{:S(2)}, u32[]{:S(2)}) %collective-permute-start.2) | collective-permute-done | bytes 688160 | tf_op jit(solution)/shard_map/ppermute | solution.py:377
  54.1 2.3 %collective-permute-start.8 = (bf16[128,2688]{1,0:T(8,128)(2,1)S(1)}, bf16[128,2688]{1,0:T(8,128)(2,1)S(1)}, u32[]{:S(2)}, u32[]{:S(2)}) collective-permute-start(bf16[128,2688]{1,0:T(8,128)(2,1)S(1)} %collective-permute-done.2.refs_4_), channel_id=1, source_target_pairs={{0,4},{4,12},{12,8},{8,0},{1,5},{5,13},{13,9},{9,1},{2,6},{6,14},{... | collective-permute-start | bytes 2064392 | tf_op jit(solution)/shard_map/ppermute | solution.py:377
  57.4 11.8 %shard_map.82.refs_0_ = bf16[8,512,128]{2,1,0:T(8,128)(2,1)S(1)} custom-call(s32[1]{0:T(128)} %bitcast.3.row_ref, bf16[512,1024]{1,0:T(8,128)(2,1)S(1)} %copy-done.5, bf16[512,512]{1,0:T(8,128)(2,1)} %collective-permute-done.3.k0, bf16[512,512]{1,0:T(8,128)(2,1)} %collective-permute-done.5.k1, bf16[512,512]{1,0:T(8,128)(2,1)S(1)} %copy-done.2, ...), custom_call_target="tpu_custom_call" | custom-call | flops 10737418240 | bytes 6291456 | tf_op jit(solution)/shard_map/pallas_call | solution.py:105
  71.0 1.6 %collective-permute-start.11 = (bf16[128,2688]{1,0:T(8,128)(2,1)S(1)}, bf16[128,2688]{1,0:T(8,128)(2,1)S(1)}, u32[]{:S(2)}, u32[]{:S(2)}) collective-permute-start(bf16[128,2688]{1,0:T(8,128)(2,1)S(1)} %collective-permute-done.8.refs_5_), channel_id=1, source_target_pairs={{0,4},{4,12},{12,8},{8,0},{1,5},{5,13},{13,9},{9,1},{2,6},{6,14},{... | collective-permute-start | bytes 2064392 | tf_op jit(solution)/shard_map/ppermute | solution.py:377
  72.6 1.7 %collective-permute-start.12 = (bf16[128,2688]{1,0:T(8,128)(2,1)S(1)}, bf16[128,2688]{1,0:T(8,128)(2,1)S(1)}, u32[]{:S(2)}, u32[]{:S(2)}) collective-permute-start(bf16[128,2688]{1,0:T(8,128)(2,1)S(1)} %collective-permute-done.8.refs_5_), channel_id=1, source_target_pairs={{0,2},{2,0},{1,3},{3,1},{4,6},{6,4},{5,7},{7,5},{8,10},{10,8},{9,1... | collective-permute-start | bytes 2064392 | tf_op jit(solution)/shard_map/ppermute | solution.py:339
  74.9 11.0 %collective-permute-done.11.refs_6_ = bf16[128,2688]{1,0:T(8,128)(2,1)S(1)} collective-permute-done((bf16[128,2688]{1,0:T(8,128)(2,1)S(1)}, bf16[128,2688]{1,0:T(8,128)(2,1)S(1)}, u32[]{:S(2)}, u32[]{:S(2)}) %collective-permute-start.11) | collective-permute-done | bytes 688160 | tf_op jit(solution)/shard_map/ppermute | solution.py:377
  85.9 2.1 %collective-permute-done.13.refs_15_ = bf16[128,2688]{1,0:T(8,128)(2,1)S(1)} collective-permute-done((bf16[128,2688]{1,0:T(8,128)(2,1)S(1)}, bf16[128,2688]{1,0:T(8,128)(2,1)S(1)}, u32[]{:S(2)}, u32[]{:S(2)}) %collective-permute-start.13) | collective-permute-done | bytes 688160 | tf_op jit(solution)/shard_map/ppermute | solution.py:339
  90.5 11.0 %collective-permute-done.14.refs_13_ = bf16[128,2688]{1,0:T(8,128)(2,1)S(1)} collective-permute-done((bf16[128,2688]{1,0:T(8,128)(2,1)S(1)}, bf16[128,2688]{1,0:T(8,128)(2,1)S(1)}, u32[]{:S(2)}, u32[]{:S(2)}) %collective-permute-start.14) | collective-permute-done | bytes 688160 | tf_op jit(solution)/shard_map/ppermute | solution.py:377
  101.5 2.6 %collective-permute-done.16.refs_16_ = bf16[128,2688]{1,0:T(8,128)(2,1)S(1)} collective-permute-done((bf16[128,2688]{1,0:T(8,128)(2,1)S(1)}, bf16[128,2688]{1,0:T(8,128)(2,1)S(1)}, u32[]{:S(2)}, u32[]{:S(2)}) %collective-permute-start.16) | collective-permute-done | bytes 688160 | tf_op jit(solution)/shard_map/ppermute | solution.py:339
  104.1 2.6 %collective-permute-start.19 = (bf16[128,2688]{1,0:T(8,128)(2,1)S(1)}, bf16[128,2688]{1,0:T(8,128)(2,1)S(1)}, u32[]{:S(2)}, u32[]{:S(2)}) collective-permute-start(bf16[128,2688]{1,0:T(8,128)(2,1)S(1)} %collective-permute-done.14.refs_13_), channel_id=1, source_target_pairs={{0,4},{4,12},{12,8},{8,0},{1,5},{5,13},{13,9},{9,1},{2,6},{6,14},{... | collective-permute-start | bytes 2064392 | tf_op jit(solution)/shard_map/ppermute | solution.py:377
  110.0 11.0 %shard_map.83 = (f32[512,2688]{1,0:T(8,128)S(1)}, bf16[512,256]{1,0:T(8,128)(2,1)S(1)}, f32[8,128]{1,0:T(8,128)S(1)}) custom-call(s32[4]{0:T(128)S(1)} %pad_add_fusion.where_ref, bf16[8,512,128]{2,1,0:T(8,128)(2,1)S(1)} %shard_map.82.refs_0_, bf16[4,512,128]{2,1,0:T(8,128)(2,1)S(1)} %collective-permute-done.17.refs_1_, ...), custom_call_target="tpu_custom_call" | custom-call | flops 176160768 | bytes 344064 | tf_op jit(solution)/shard_map/pallas_call | solution.py:224
  121.0 3.5 %shard_map.84 = (f32[512,2688]{1,0:T(8,128)S(1)}, f32[520,128]{1,0:T(8,128)S(1)}) custom-call(bf16[512,256]{1,0:T(8,128)(2,1)S(1)} %get-tuple-element.62.heads_ref, bf16[128,2688]{1,0:T(8,128)(2,1)S(1)} %collective-permute-done.19.refs_0_, bf16[128,2688]{1,0:T(8,128)(2,1)S(1)} %collective-permute-done.20.refs_1_, f32[512,2688]{1,0:T(8,128)S(1)} %get-tuple-element.63.refs_2_, ...), custom_call_target="tpu_custom_call" | custom-call | flops 704643072 | bytes 1376256 | tf_op jit(solution)/shard_map/pallas_call | solution.py:279
  126.2 2.3 %shard_map.85 = bf16[512,2688]{1,0:T(8,128)(2,1)} custom-call(f32[520,128]{1,0:T(8,128)S(1)} %get-tuple-element.65.own_ref, f32[520,128]{1,0:T(8,128)S(1)} %collective-permute-done.21.other_ref, f32[1,2688]{1,0:T(1,128)S(1)} %broadcast_in_dim.13.refs_4_.gain_ref, f32[64,2688]{1,0:T(8,128)S(1)} %bitcast.8, f32[512,2688]{1,0:T(8,128)S(1)} %get-tuple-element.66.hidden_ref), custom_call_target="tpu_custom_call" | custom-call | flops 704643072 | bytes 8257536 | tf_op jit(solution)/shard_map/pallas_call | solution.py:325
  (52 shorter events, 19.7 us)
Async XLA Ops:
  1.2 2.3 %collective-permute-start = (bf16[128,2688]{1,0:T(8,128)(2,1)S(1)}, bf16[128,2688]{1,0:T(8,128)(2,1)S(1)}, u32[]{:S(2)}, u32[]{:S(2)}) collective-permute-start(bf16[128,2688]{1,0:T(8,128)(2,1)S(1)} %constant_dynamic-slice_fusion), channel_id=1, source_target_pairs={{0,1},{1,0},{2,3},{3,2},{4,5},{5,4},{6,7},{7,6},{8,9},{9,8},{10,11... | collective-permute-start | bytes 2064392 | tf_op jit(solution)/shard_map/ppermute | solution.py:339
  4.9 18.7 %collective-permute-start.4 = (bf16[128,2688]{1,0:T(8,128)(2,1)S(1)}, bf16[128,2688]{1,0:T(8,128)(2,1)S(1)}, u32[]{:S(2)}, u32[]{:S(2)}) collective-permute-start(bf16[128,2688]{1,0:T(8,128)(2,1)S(1)} %get-tuple-element.37.refs_3_), channel_id=1, source_target_pairs={{0,2},{2,0},{1,3},{3,1},{4,6},{6,4},{5,7},{7,5},{8,10},{10,8},{9,1... | collective-permute-start | bytes 2064392 | tf_op jit(solution)/shard_map/ppermute | solution.py:339
  7.8 15.8 %collective-permute-start.3 = (bf16[512,512]{1,0:T(8,128)(2,1)S(1)}, bf16[512,512]{1,0:T(8,128)(2,1)}, u32[]{:S(2)}, u32[]{:S(2)}) collective-permute-start(bf16[512,512]{1,0:T(8,128)(2,1)S(1)} %copy-done.2), channel_id=1, source_target_pairs={{0,4},{4,8},{8,12},{1,5},{5,9},{9,13},{2,6},{6,10},{10,14},{3,7},{... | collective-permute-start | bytes 1572872 | tf_op jit(solution)/shard_map/ppermute | solution.py:358
  12.1 21.6 %collective-permute-start.1 = (bf16[512,512]{1,0:T(8,128)(2,1)S(1)}, bf16[512,512]{1,0:T(8,128)(2,1)}, u32[]{:S(2)}, u32[]{:S(2)}) collective-permute-start(bf16[512,512]{1,0:T(8,128)(2,1)S(1)} %copy-done.3), channel_id=1, source_target_pairs={{0,4},{4,8},{8,12},{1,5},{5,9},{9,13},{2,6},{6,10},{10,14},{3,7},{... | collective-permute-start | bytes 1572872 | tf_op jit(solution)/shard_map/ppermute | solution.py:358
  24.5 14.4 %collective-permute-start.5 = (bf16[512,512]{1,0:T(8,128)(2,1)}, bf16[512,512]{1,0:T(8,128)(2,1)}, u32[]{:S(2)}, u32[]{:S(2)}) collective-permute-start(bf16[512,512]{1,0:T(8,128)(2,1)} %broadcast_select_fusion.3), channel_id=1, source_target_pairs={{0,2},{2,0},{1,3},{3,1},{4,6},{6,4},{5,7},{7,5},{8,10},{10,8},{9,1... | collective-permute-start | bytes 1572872 | tf_op jit(solution)/shard_map/ppermute | solution.py:339
  33.7 18.2 %collective-permute-start.2 = (bf16[128,2688]{1,0:T(8,128)(2,1)S(1)}, bf16[128,2688]{1,0:T(8,128)(2,1)S(1)}, u32[]{:S(2)}, u32[]{:S(2)}) collective-permute-start(bf16[128,2688]{1,0:T(8,128)(2,1)S(1)} %get-tuple-element.37.refs_3_), channel_id=1, source_target_pairs={{0,4},{4,12},{12,8},{8,0},{1,5},{5,13},{13,9},{9,1},{2,6},{6,14},{... | collective-permute-start | bytes 2064392 | tf_op jit(solution)/shard_map/ppermute | solution.py:377
  36.3 16.0 %collective-permute-start.7 = (bf16[128,2688]{1,0:T(8,128)(2,1)S(1)}, bf16[128,2688]{1,0:T(8,128)(2,1)S(1)}, u32[]{:S(2)}, u32[]{:S(2)}) collective-permute-start(bf16[128,2688]{1,0:T(8,128)(2,1)S(1)} %collective-permute-done.4.refs_7_), channel_id=1, source_target_pairs={{0,16},{16,0},{1,17},{17,1},{2,18},{18,2},{3,19},{19,3},{4,20},{20... | collective-permute-start | bytes 2064392 | tf_op jit(solution)/shard_map/ppermute | solution.py:339
  40.0 12.6 %collective-permute-start.6 = (bf16[512,512]{1,0:T(8,128)(2,1)S(1)}, bf16[512,512]{1,0:T(8,128)(2,1)S(1)}, u32[]{:S(2)}, u32[]{:S(2)}) collective-permute-start(bf16[512,512]{1,0:T(8,128)(2,1)S(1)} %broadcast_select_fusion.2), channel_id=1, source_target_pairs={{0,2},{2,0},{1,3},{3,1},{4,6},{6,4},{5,7},{7,5},{8,10},{10,8},{9,1... | collective-permute-start | bytes 1572872 | tf_op jit(solution)/shard_map/ppermute | solution.py:339
  52.6 16.5 %collective-permute-start.10 = (bf16[128,2688]{1,0:T(8,128)(2,1)S(1)}, bf16[128,2688]{1,0:T(8,128)(2,1)S(1)}, u32[]{:S(2)}, u32[]{:S(2)}) collective-permute-start(bf16[128,2688]{1,0:T(8,128)(2,1)S(1)} %collective-permute-done.2.refs_4_), channel_id=1, source_target_pairs={{0,16},{16,0},{1,17},{17,1},{2,18},{18,2},{3,19},{19,3},{4,20},{20... | collective-permute-start | bytes 2064392 | tf_op jit(solution)/shard_map/ppermute | solution.py:339
  54.1 15.7 %collective-permute-start.8 = (bf16[128,2688]{1,0:T(8,128)(2,1)S(1)}, bf16[128,2688]{1,0:T(8,128)(2,1)S(1)}, u32[]{:S(2)}, u32[]{:S(2)}) collective-permute-start(bf16[128,2688]{1,0:T(8,128)(2,1)S(1)} %collective-permute-done.2.refs_4_), channel_id=1, source_target_pairs={{0,4},{4,12},{12,8},{8,0},{1,5},{5,13},{13,9},{9,1},{2,6},{6,14},{... | collective-permute-start | bytes 2064392 | tf_op jit(solution)/shard_map/ppermute | solution.py:377
  56.4 14.6 %collective-permute-start.9 = (bf16[128,2688]{1,0:T(8,128)(2,1)S(1)}, bf16[128,2688]{1,0:T(8,128)(2,1)S(1)}, u32[]{:S(2)}, u32[]{:S(2)}) collective-permute-start(bf16[128,2688]{1,0:T(8,128)(2,1)S(1)} %collective-permute-done.2.refs_4_), channel_id=1, source_target_pairs={{0,2},{2,0},{1,3},{3,1},{4,6},{6,4},{5,7},{7,5},{8,10},{10,8},{9,1... | collective-permute-start | bytes 2064392 | tf_op jit(solution)/shard_map/ppermute | solution.py:339
  57.3 50.5 %copy-start.7 = (f32[2688]{0:T(1024)S(1)}, f32[2688]{0:T(1024)}, u32[]{:S(2)}) copy-start(f32[2688]{0:T(1024)} %param.12) | copy-start | bytes 32260
  57.3 52.7 %copy-start = (f32[2688,64]{0,1:T(8,128)S(1)}, f32[2688,64]{0,1:T(8,128)}, u32[]{:S(2)}) copy-start(f32[2688,64]{0,1:T(8,128)} %param.14) | copy-start | bytes 2064388
  71.0 14.8 %collective-permute-start.11 = (bf16[128,2688]{1,0:T(8,128)(2,1)S(1)}, bf16[128,2688]{1,0:T(8,128)(2,1)S(1)}, u32[]{:S(2)}, u32[]{:S(2)}) collective-permute-start(bf16[128,2688]{1,0:T(8,128)(2,1)S(1)} %collective-permute-done.8.refs_5_), channel_id=1, source_target_pairs={{0,4},{4,12},{12,8},{8,0},{1,5},{5,13},{13,9},{9,1},{2,6},{6,14},{... | collective-permute-start | bytes 2064392 | tf_op jit(solution)/shard_map/ppermute | solution.py:377
  72.6 13.3 %collective-permute-start.12 = (bf16[128,2688]{1,0:T(8,128)(2,1)S(1)}, bf16[128,2688]{1,0:T(8,128)(2,1)S(1)}, u32[]{:S(2)}, u32[]{:S(2)}) collective-permute-start(bf16[128,2688]{1,0:T(8,128)(2,1)S(1)} %collective-permute-done.8.refs_5_), channel_id=1, source_target_pairs={{0,2},{2,0},{1,3},{3,1},{4,6},{6,4},{5,7},{7,5},{8,10},{10,8},{9,1... | collective-permute-start | bytes 2064392 | tf_op jit(solution)/shard_map/ppermute | solution.py:339
  74.3 13.6 %collective-permute-start.13 = (bf16[128,2688]{1,0:T(8,128)(2,1)S(1)}, bf16[128,2688]{1,0:T(8,128)(2,1)S(1)}, u32[]{:S(2)}, u32[]{:S(2)}) collective-permute-start(bf16[128,2688]{1,0:T(8,128)(2,1)S(1)} %collective-permute-done.9.refs_8_), channel_id=1, source_target_pairs={{0,16},{16,0},{1,17},{17,1},{2,18},{18,2},{3,19},{19,3},{4,20},{20... | collective-permute-start | bytes 2064392 | tf_op jit(solution)/shard_map/ppermute | solution.py:339
  87.9 13.5 %collective-permute-start.14 = (bf16[128,2688]{1,0:T(8,128)(2,1)S(1)}, bf16[128,2688]{1,0:T(8,128)(2,1)S(1)}, u32[]{:S(2)}, u32[]{:S(2)}) collective-permute-start(bf16[128,2688]{1,0:T(8,128)(2,1)S(1)} %collective-permute-done.10.refs_12_), channel_id=1, source_target_pairs={{0,4},{4,12},{12,8},{8,0},{1,5},{5,13},{13,9},{9,1},{2,6},{6,14},{... | collective-permute-start | bytes 2064392 | tf_op jit(solution)/shard_map/ppermute | solution.py:377
  89.4 12.1 %collective-permute-start.15 = (bf16[128,2688]{1,0:T(8,128)(2,1)S(1)}, bf16[128,2688]{1,0:T(8,128)(2,1)S(1)}, u32[]{:S(2)}, u32[]{:S(2)}) collective-permute-start(bf16[128,2688]{1,0:T(8,128)(2,1)S(1)} %collective-permute-done.11.refs_6_), channel_id=1, source_target_pairs={{0,2},{2,0},{1,3},{3,1},{4,6},{6,4},{5,7},{7,5},{8,10},{10,8},{9,1... | collective-permute-start | bytes 2064392 | tf_op jit(solution)/shard_map/ppermute | solution.py:339
  89.9 14.1 %collective-permute-start.16 = (bf16[128,2688]{1,0:T(8,128)(2,1)S(1)}, bf16[128,2688]{1,0:T(8,128)(2,1)S(1)}, u32[]{:S(2)}, u32[]{:S(2)}) collective-permute-start(bf16[128,2688]{1,0:T(8,128)(2,1)S(1)} %collective-permute-done.12.refs_9_), channel_id=1, source_target_pairs={{0,16},{16,0},{1,17},{17,1},{2,18},{18,2},{3,19},{19,3},{4,20},{20... | collective-permute-start | bytes 2064392 | tf_op jit(solution)/shard_map/ppermute | solution.py:339
  104.1 16.9 %collective-permute-start.19 = (bf16[128,2688]{1,0:T(8,128)(2,1)S(1)}, bf16[128,2688]{1,0:T(8,128)(2,1)S(1)}, u32[]{:S(2)}, u32[]{:S(2)}) collective-permute-start(bf16[128,2688]{1,0:T(8,128)(2,1)S(1)} %collective-permute-done.14.refs_13_), channel_id=1, source_target_pairs={{0,4},{4,12},{12,8},{8,0},{1,5},{5,13},{13,9},{9,1},{2,6},{6,14},{... | collective-permute-start | bytes 2064392 | tf_op jit(solution)/shard_map/ppermute | solution.py:377
  106.7 14.4 %collective-permute-start.20 = (bf16[128,2688]{1,0:T(8,128)(2,1)S(1)}, bf16[128,2688]{1,0:T(8,128)(2,1)S(1)}, u32[]{:S(2)}, u32[]{:S(2)}) collective-permute-start(bf16[128,2688]{1,0:T(8,128)(2,1)S(1)} %collective-permute-done.15.refs_10_), channel_id=1, source_target_pairs={{0,16},{16,0},{1,17},{17,1},{2,18},{18,2},{3,19},{19,3},{4,20},{20... | collective-permute-start | bytes 2064392 | tf_op jit(solution)/shard_map/ppermute | solution.py:339
  107.3 2.0 %collective-permute-start.17 = (bf16[4,512,128]{2,1,0:T(8,128)(2,1)S(1)}, bf16[4,512,128]{2,1,0:T(8,128)(2,1)S(1)}, u32[]{:S(2)}, u32[]{:S(2)}) collective-permute-start(bf16[4,512,128]{2,1,0:T(8,128)(2,1)S(1)} %get-tuple-element.70), channel_id=1, source_target_pairs={{0,1},{1,0},{2,3},{3,2},{4,5},{5,4},{6,7},{7,6},{8,9},{9,8},{10,11... | collective-permute-start | bytes 1572872 | tf_op jit(solution)/shard_map/ppermute | solution.py:339
  107.3 2.6 %collective-permute-start.18 = (bf16[4,512,128]{2,1,0:T(8,128)(2,1)S(1)}, bf16[4,512,128]{2,1,0:T(8,128)(2,1)S(1)}, u32[]{:S(2)}, u32[]{:S(2)}) collective-permute-start(bf16[4,512,128]{2,1,0:T(8,128)(2,1)S(1)} %get-tuple-element.69), channel_id=1, source_target_pairs={{0,1},{1,0},{2,3},{3,2},{4,5},{5,4},{6,7},{7,6},{8,9},{9,8},{10,11... | collective-permute-start | bytes 1572872 | tf_op jit(solution)/shard_map/ppermute | solution.py:339
  124.5 1.6 %collective-permute-start.21 = (f32[520,128]{1,0:T(8,128)S(1)}, f32[520,128]{1,0:T(8,128)S(1)}, u32[]{:S(2)}, u32[]{:S(2)}) collective-permute-start(f32[520,128]{1,0:T(8,128)S(1)} %get-tuple-element.65.own_ref), channel_id=1, source_target_pairs={{0,1},{1,0},{2,3},{3,2},{4,5},{5,4},{6,7},{7,6},{8,9},{9,8},{10,11... | collective-permute-start | bytes 798728 | tf_op jit(solution)/shard_map/ppermute | solution.py:339
  (6 other events, 110.2 us)
